TPU v7x, 32 devices: a whole 2x2x4 slice. The times are simulated.
32 devices in a mesh: dp: 4 (over z), expert: 8 (over y, x, core).
Axes of the slice: x: 2, y: 2, z: 4, core: 2. Of those that a mesh axis runs over, the one named last changes fastest.
Arguments:
- tokens: bfloat16 [16384, 1280], P(('dp', 'expert')), may hold values from -6 to 6
- cotangent: bfloat16 [16384, 1280], P(('dp', 'expert')), may hold values from -6 to 6
- lengths: int32 [32], P(('dp', 'expert')), may hold values from 1 to 512, as said below
- choices: int32 [16384, 7], P(('dp', 'expert')), may hold values from 0 to 15, all different within a row; in each aligned block of 512 rows (0 to 511, 512 to 1023, ...) at most 256 rows name the same one
- attn_weight: float32 [4, 1280, 1280], P(None, ('dp', 'expert')), may hold values from -1 to 1
- attn_moment: float32 [4, 1280, 1280], P(None, ('dp', 'expert')), may hold values from -224 to 224
- attn_average: float32 [4, 1280, 1280], P(None, ('dp', 'expert')), may hold values from -0.15625 to 0.15625
- router_weight: float32 [1280, 16], P(('dp', 'expert')), may hold values from -0.078125 to 0.078125
- router_moment: float32 [1280, 16], P(('dp', 'expert')), may hold values from -4096 to 4096
- router_average: float32 [1280, 16], P(('dp', 'expert')), may hold values from -0.078125 to 0.078125
- shared_weight: float32 [3, 1280, 896], P(None, ('dp', 'expert')), may hold values from -4 to 4
- shared_moment: float32 [3, 1280, 896], P(None, ('dp', 'expert')), may hold values from -384 to 384
- shared_average: float32 [3, 1280, 896], P(None, ('dp', 'expert')), may hold values from -0.15625 to 0.15625
- routed_weight: float32 [16, 3, 1280, 896], P('expert', None, 'dp'), may hold values from -4 to 4
- routed_moment: float32 [16, 3, 1280, 896], P('expert', None, 'dp'), may hold values from -64 to 64
- routed_average: float32 [16, 3, 1280, 896], P('expert', None, 'dp'), may hold values from -0.15625 to 0.15625
- norm_gains: float32 [2, 1280], P(None, ('dp', 'expert')), may hold values from 0.5 to 1.5
- gain_moment: float32 [2, 1280], P(None, ('dp', 'expert')), may hold values from -384 to 384
- gain_average: float32 [2, 1280], P(None, ('dp', 'expert')), may hold values from 0.5 to 1.5
Outputs:
- block_out: bfloat16 [16384, 1280], P(('dp', 'expert'))
- input_grad: float32 [16384, 1280], P(('dp', 'expert'))
- masked_rms: float32 [2], replicated
- attn_grad: float32 [4, 1280, 1280], P(None, ('dp', 'expert'))
- attn_new: float32 [4, 1280, 1280], P(None, ('dp', 'expert'))
- attn_moment_new: float32 [4, 1280, 1280], P(None, ('dp', 'expert'))
- attn_average_new: float32 [4, 1280, 1280], P(None, ('dp', 'expert'))
- attn_copy: bfloat16 [4, 1280, 1280], P(None, ('dp', 'expert'))
- router_grad: float32 [1280, 16], P(('dp', 'expert'))
- router_new: float32 [1280, 16], P(('dp', 'expert'))
- router_moment_new: float32 [1280, 16], P(('dp', 'expert'))
- router_average_new: float32 [1280, 16], P(('dp', 'expert'))
- router_copy: bfloat16 [1280, 16], P(('dp', 'expert'))
- shared_grad: float32 [3, 1280, 896], P(None, ('dp', 'expert'))
- shared_new: float32 [3, 1280, 896], P(None, ('dp', 'expert'))
- shared_moment_new: float32 [3, 1280, 896], P(None, ('dp', 'expert'))
- shared_average_new: float32 [3, 1280, 896], P(None, ('dp', 'expert'))
- shared_copy: bfloat16 [3, 1280, 896], P(None, ('dp', 'expert'))
- routed_grad: float32 [16, 3, 1280, 896], P('expert', None, 'dp')
- routed_new: float32 [16, 3, 1280, 896], P('expert', None, 'dp')
- routed_moment_new: float32 [16, 3, 1280, 896], P('expert', None, 'dp')
- routed_average_new: float32 [16, 3, 1280, 896], P('expert', None, 'dp')
- routed_copy: bfloat16 [16, 3, 1280, 896], P('expert', None, 'dp')
- gain_grad: float32 [2, 1280], P(None, ('dp', 'expert'))
- gain_new: float32 [2, 1280], P(None, ('dp', 'expert'))
- gain_moment_new: float32 [2, 1280], P(None, ('dp', 'expert'))
- gain_average_new: float32 [2, 1280], P(None, ('dp', 'expert'))
Inputs may be any that keep to these rules, and one draw needn't show every extreme that they name: `lengths`: one sequence has exactly 512 real tokens. `choices`: a token's 7 experts differ; in the rows of one sequence no expert is named more than 256 times, a bound that some block reaches.
All inputs are finite; a program needn't handle non-finite values.
Results may differ from a plain program's by a relative error of at most 0.018.
Values may be sent and summed in bfloat16 or wider, within the bound.
No kernel may reach another device: no remote copies, remote signals or barrier semaphores. Data moves between devices by JAX's collectives and lax.ppermute only.
A program may use at most 384 MiB of HBM per device.

v0:
```python
import math

import jax
import jax.numpy as jnp
from jax import lax
from jax.sharding import PartitionSpec as P

HEADS = 10
STEP = 3


highest_precision = lax.Precision.HIGHEST
eps_norm = 1e-06
momentum_rate = 0.9
decay_rate = 0.0001
rate_attention = 0.01
rate_router = 0.03
rate_shared = 0.01
rate_routed = 0.04
rate_gains = 0.2
masked_score = -1e30
block_limit = 512


def norm_forward(values, gain_row):
    inverse = lax.rsqrt(jnp.mean(values * values, axis=-1, keepdims=True) + eps_norm)
    normal_part = values * inverse
    return (normal_part * gain_row, normal_part, inverse)


def norm_backward(grad_out, normal_part, inverse, gain_row):
    grad_hat = grad_out * gain_row
    grad_in = inverse * (
        grad_hat - normal_part * jnp.mean(grad_hat * normal_part, axis=-1, keepdims=True)
    )
    return (grad_in, jnp.sum(grad_out * normal_part, axis=0))


def rotate(values, positions, direction):
    half_dim = values.shape[-1] // 2
    frequency = 10000.0 ** (-jnp.arange(half_dim, dtype=jnp.float32) / half_dim)
    angles = positions.astype(jnp.float32)[:, None] * frequency[None, :]
    cosine = jnp.cos(angles)[:, None, :]
    sine_part = direction * jnp.sin(angles)[:, None, :]
    first_half = values[..., :half_dim]
    second_half = values[..., half_dim:]
    return jnp.concatenate(
        [
            first_half * cosine - second_half * sine_part,
            second_half * cosine + first_half * sine_part,
        ],
        axis=-1,
    )


def silu_slope(pre_value):
    sigmoid_part = jax.nn.sigmoid(pre_value)
    return sigmoid_part * (1.0 + pre_value * (1.0 - sigmoid_part))


def update(weight, moment, average, gradient, step_rate):
    decayed = gradient + decay_rate * weight
    moment_new = momentum_rate * moment + decayed
    weight_new = weight - step_rate * (decayed + momentum_rate * moment_new)
    average_new = average + (weight_new - average) / (STEP + 1.0)
    return (gradient, weight_new, moment_new, average_new, weight_new.astype(jnp.bfloat16))


def local(
    tokens,
    cotangent,
    lengths,
    choices,
    attn_weight,
    attn_moment,
    attn_average,
    router_weight,
    router_moment,
    router_average,
    shared_weight,
    shared_moment,
    shared_average,
    routed_weight,
    routed_moment,
    routed_average,
    norm_gains,
    gain_moment,
    gain_average,
):
    seq_len, model_width = tokens.shape
    topk_count = choices.shape[1]
    head_dim = model_width // HEADS
    groups = lax.axis_size("expert")
    routed_count = routed_weight.shape[0] * groups
    capacity = (seq_len * topk_count * 8 // (7 * routed_count) + 7) // 8 * 8
    total_tokens = seq_len * groups * lax.axis_size("dp")
    step_root = 1.0 / math.sqrt(total_tokens)
    score_scale = 1.0 / math.sqrt(head_dim)
    block_rows = min(seq_len, block_limit)
    block_count = seq_len // block_rows
    attn16, shared16, router16, gains16 = (
        lax.all_gather(attn_weight.astype(jnp.bfloat16), ("dp", "expert"), axis=1, tiled=True),
        lax.all_gather(shared_weight.astype(jnp.bfloat16), ("dp", "expert"), axis=1, tiled=True),
        lax.all_gather(router_weight.astype(jnp.bfloat16), ("dp", "expert"), axis=0, tiled=True),
        lax.all_gather(norm_gains.astype(jnp.bfloat16), ("dp", "expert"), axis=1, tiled=True),
    )
    expert16 = lax.all_gather(routed_weight.astype(jnp.bfloat16), "dp", axis=2, tiled=True)
    gain_first = gains16[0].astype(jnp.float32)
    gain_second = gains16[1].astype(jnp.float32)
    positions = jnp.arange(seq_len, dtype=jnp.int32)
    length_here = lengths[0]
    valid_rows = (positions < length_here).astype(jnp.float32)[:, None]
    key_positions = positions[None, :]
    residual_in = tokens.astype(jnp.float32)
    normed_first, hat_first, inverse_first = norm_forward(residual_in, gain_first)
    first16 = normed_first.astype(jnp.bfloat16)
    query_linear = jnp.dot(first16, attn16[0], preferred_element_type=jnp.float32)
    key_linear = jnp.dot(first16, attn16[1], preferred_element_type=jnp.float32)
    value_linear = jnp.dot(first16, attn16[2], preferred_element_type=jnp.float32)
    query16 = rotate(query_linear.reshape(seq_len, HEADS, head_dim), positions, 1.0).astype(
        jnp.bfloat16
    )
    key16 = rotate(key_linear.reshape(seq_len, HEADS, head_dim), positions, 1.0).astype(
        jnp.bfloat16
    )
    value16 = value_linear.reshape(seq_len, HEADS, head_dim).astype(jnp.bfloat16)

    def block_scores(start_row):
        scores = (
            jnp.einsum("qhd,khd->hqk", query16, key16, preferred_element_type=jnp.float32)
            * score_scale
        )
        query_positions = start_row + jnp.arange(block_rows, dtype=jnp.int32)[:, None]
        allowed = (key_positions <= query_positions) & (key_positions < length_here)
        return (query16, jnp.where(allowed[None], scores, masked_score))

    def forward_block(block_index):
        query_block, masked = block_scores(block_index * block_rows)
        row_peak = jnp.max(masked, axis=-1, keepdims=True)
        exp_part = jnp.exp(masked - row_peak)
        row_total = jnp.sum(exp_part, axis=-1, keepdims=True)
        probs16 = (exp_part / row_total).astype(jnp.bfloat16)
        context = jnp.einsum("hqk,khd->qhd", probs16, value16, preferred_element_type=jnp.float32)
        return (context.astype(jnp.bfloat16), (row_peak + jnp.log(row_total))[..., 0])

    contexts, log_totals = lax.map(forward_block, jnp.arange(block_count))
    context16 = contexts.reshape(seq_len, model_width)
    attn_out = jnp.dot(context16, attn16[3], preferred_element_type=jnp.float32)
    hidden_state = residual_in + attn_out
    normed_second, hat_second, inverse_second = norm_forward(hidden_state, gain_second)
    second16 = normed_second.astype(jnp.bfloat16)
    logits = jnp.dot(second16, router16, preferred_element_type=jnp.float32)
    choice_table = (
        choices[:, :, None] == jnp.arange(routed_count, dtype=jnp.int32)[None, None, :]
    ).astype(jnp.float32)
    chosen = jnp.sum(logits[:, None, :] * choice_table, axis=2)
    chosen_exp = jnp.exp(chosen - jnp.max(chosen, axis=1, keepdims=True))
    gate_weights = chosen_exp / jnp.sum(chosen_exp, axis=1, keepdims=True)
    pair_count = seq_len * topk_count
    flat_choice = choices.reshape(-1)
    flat_onehot = (
        flat_choice[:, None] == jnp.arange(routed_count, dtype=jnp.int32)[None, :]
    ).astype(jnp.int32)
    earlier = jnp.cumsum(flat_onehot, axis=0) - flat_onehot
    slot_rank = jnp.sum(earlier * flat_onehot, axis=1)
    slot_place = flat_choice * capacity + slot_rank
    slot_owner = (
        jnp.full((routed_count * capacity,), pair_count, dtype=jnp.int32)
        .at[slot_place]
        .set(jnp.arange(pair_count, dtype=jnp.int32))
    )
    padded_second = jnp.concatenate([second16, jnp.zeros((1, model_width), jnp.bfloat16)], axis=0)
    send_rows = jnp.take(padded_second, slot_owner // topk_count, axis=0).reshape(
        routed_count, capacity, model_width
    )
    received = lax.all_to_all(send_rows, "expert", split_axis=0, concat_axis=1, tiled=True)
    pre_gate = jnp.einsum(
        "erd,edf->erf", received, expert16[:, 0], preferred_element_type=jnp.float32
    )
    pre_up = jnp.einsum(
        "erd,edf->erf", received, expert16[:, 1], preferred_element_type=jnp.float32
    )
    hidden16 = (jax.nn.silu(pre_gate) * pre_up).astype(jnp.bfloat16)
    expert_out = jnp.einsum(
        "erf,edf->erd", hidden16, expert16[:, 2], preferred_element_type=jnp.float32
    ).astype(jnp.bfloat16)
    returned = lax.all_to_all(
        expert_out, "expert", split_axis=1, concat_axis=0, tiled=True
    ).reshape(routed_count * capacity, model_width)
    picked = (
        jnp.take(returned, slot_place, axis=0)
        .reshape(seq_len, topk_count, model_width)
        .astype(jnp.float32)
    )
    routed_sum = jnp.sum(gate_weights[:, :, None] * picked, axis=1)
    shared_gate = jnp.dot(second16, shared16[0], preferred_element_type=jnp.float32)
    shared_up = jnp.dot(second16, shared16[1], preferred_element_type=jnp.float32)
    shared_hidden = (jax.nn.silu(shared_gate) * shared_up).astype(jnp.bfloat16)
    shared_out = jnp.einsum(
        "lf,df->ld", shared_hidden, shared16[2], preferred_element_type=jnp.float32
    )
    block_value = hidden_state + shared_out + routed_sum
    grad_out = cotangent.astype(jnp.float32) * valid_rows
    grad_out16 = grad_out.astype(jnp.bfloat16)
    grad_shared_hidden = jnp.dot(grad_out16, shared16[2], preferred_element_type=jnp.float32)
    grad_shared_gate16 = (grad_shared_hidden * shared_up * silu_slope(shared_gate)).astype(
        jnp.bfloat16
    )
    grad_shared_up16 = (grad_shared_hidden * jax.nn.silu(shared_gate)).astype(jnp.bfloat16)
    shared_grads = jnp.stack(
        [
            jnp.einsum(
                "ld,lf->df", second16, grad_shared_gate16, preferred_element_type=jnp.float32
            ),
            jnp.einsum("ld,lf->df", second16, grad_shared_up16, preferred_element_type=jnp.float32),
            jnp.einsum("ld,lf->df", grad_out16, shared_hidden, preferred_element_type=jnp.float32),
        ]
    )
    grad_second = jnp.einsum(
        "lf,df->ld", grad_shared_gate16, shared16[0], preferred_element_type=jnp.float32
    )
    grad_second = grad_second + jnp.einsum(
        "lf,df->ld", grad_shared_up16, shared16[1], preferred_element_type=jnp.float32
    )
    grad_picked16 = (gate_weights[:, :, None] * grad_out[:, None, :]).astype(jnp.bfloat16)
    grad_gate = jnp.sum(picked * grad_out[:, None, :], axis=2)
    padded_grads = jnp.concatenate(
        [grad_picked16.reshape(pair_count, model_width), jnp.zeros((1, model_width), jnp.bfloat16)],
        axis=0,
    )
    send_grads = jnp.take(padded_grads, slot_owner, axis=0).reshape(
        routed_count, capacity, model_width
    )
    grad_expert_out = lax.all_to_all(send_grads, "expert", split_axis=0, concat_axis=1, tiled=True)
    grad_hidden = jnp.einsum(
        "erd,edf->erf", grad_expert_out, expert16[:, 2], preferred_element_type=jnp.float32
    )
    grad_pre_gate16 = (grad_hidden * pre_up * silu_slope(pre_gate)).astype(jnp.bfloat16)
    grad_pre_up16 = (grad_hidden * jax.nn.silu(pre_gate)).astype(jnp.bfloat16)
    grad_rows = jnp.einsum(
        "erf,edf->erd", grad_pre_gate16, expert16[:, 0], preferred_element_type=jnp.float32
    )
    grad_rows = (
        grad_rows
        + jnp.einsum(
            "erf,edf->erd", grad_pre_up16, expert16[:, 1], preferred_element_type=jnp.float32
        )
    ).astype(jnp.bfloat16)
    grad_returned = lax.all_to_all(
        grad_rows, "expert", split_axis=1, concat_axis=0, tiled=True
    ).reshape(routed_count * capacity, model_width)
    grad_gate_w = jnp.einsum(
        "erd,erf->edf", received, grad_pre_gate16, preferred_element_type=jnp.float32
    )
    grad_up_w = jnp.einsum(
        "erd,erf->edf", received, grad_pre_up16, preferred_element_type=jnp.float32
    )
    grad_down_w = jnp.einsum(
        "erd,erf->edf", grad_expert_out, hidden16, preferred_element_type=jnp.float32
    )
    reduced_gate, reduced_up, reduced_down = (
        lax.psum_scatter(
            grad_gate_w.astype(jnp.bfloat16), "dp", scatter_dimension=1, tiled=True
        ).astype(jnp.float32),
        lax.psum_scatter(
            grad_up_w.astype(jnp.bfloat16), "dp", scatter_dimension=1, tiled=True
        ).astype(jnp.float32),
        lax.psum_scatter(
            grad_down_w.astype(jnp.bfloat16), "dp", scatter_dimension=1, tiled=True
        ).astype(jnp.float32),
    )
    routed_grad_shard = jnp.stack([reduced_gate, reduced_up, reduced_down], axis=1)
    picked_grads = (
        jnp.take(grad_returned, slot_place, axis=0)
        .reshape(seq_len, topk_count, model_width)
        .astype(jnp.float32)
    )
    grad_second = grad_second + jnp.sum(picked_grads, axis=1)
    gate_mean = jnp.sum(gate_weights * grad_gate, axis=1, keepdims=True)
    grad_chosen = gate_weights * (grad_gate - gate_mean)
    grad_logits = jnp.sum(grad_chosen[:, :, None] * choice_table, axis=1)
    router_float = router16.astype(jnp.float32)
    grad_second = grad_second + jnp.dot(grad_logits, router_float.T, precision=highest_precision)
    router_grad_full = jnp.dot(
        second16.astype(jnp.float32).T, grad_logits, precision=highest_precision
    )
    grad_norm_second, grad_gain_second = norm_backward(
        grad_second, hat_second, inverse_second, gain_second
    )
    grad_hidden_state = grad_out + grad_norm_second
    grad_attn16 = grad_hidden_state.astype(jnp.bfloat16)
    grad_out_proj = jnp.einsum(
        "ld,le->de", context16, grad_attn16, preferred_element_type=jnp.float32
    )
    grad_context16 = (
        jnp.einsum("le,de->ld", grad_attn16, attn16[3], preferred_element_type=jnp.float32)
        .astype(jnp.bfloat16)
        .reshape(seq_len, HEADS, head_dim)
    )

    def backward_block(carried, inputs):
        grad_keys, grad_values = carried
        block_index, log_block = inputs
        start_row = block_index * block_rows
        query_block, masked = block_scores(start_row)
        probability = jnp.exp(masked - log_block[..., None])
        grad_probs = jnp.einsum(
            "qhd,khd->hqk", grad_context16, value16, preferred_element_type=jnp.float32
        )
        row_delta = jnp.sum(probability * grad_probs, axis=-1, keepdims=True)
        grad_scores16 = (probability * (grad_probs - row_delta)).astype(jnp.bfloat16)
        grad_query = (
            jnp.einsum("hqk,khd->qhd", grad_scores16, key16, preferred_element_type=jnp.float32)
            * score_scale
        )
        grad_keys = (
            grad_keys
            + jnp.einsum(
                "hqk,qhd->khd", grad_scores16, query_block, preferred_element_type=jnp.float32
            )
            * score_scale
        )
        grad_values = grad_values + jnp.einsum(
            "hqk,qhd->khd",
            probability.astype(jnp.bfloat16),
            grad_context16,
            preferred_element_type=jnp.float32,
        )
        return ((grad_keys, grad_values), grad_query)

    zero_heads = jnp.zeros((seq_len, HEADS, head_dim), jnp.float32)
    (grad_keys, grad_values), grad_queries = lax.scan(
        backward_block, (zero_heads, zero_heads), (jnp.arange(block_count), log_totals)
    )
    grad_query16 = (
        rotate(grad_queries.reshape(seq_len, HEADS, head_dim), positions, -1.0)
        .reshape(seq_len, model_width)
        .astype(jnp.bfloat16)
    )
    grad_key16 = (
        rotate(grad_keys, positions, -1.0).reshape(seq_len, model_width).astype(jnp.bfloat16)
    )
    grad_value16 = grad_values.reshape(seq_len, model_width).astype(jnp.bfloat16)
    attn_grads = jnp.stack(
        [
            jnp.einsum("ld,le->de", first16, grad_query16, preferred_element_type=jnp.float32),
            jnp.einsum("ld,le->de", first16, grad_key16, preferred_element_type=jnp.float32),
            jnp.einsum("ld,le->de", first16, grad_value16, preferred_element_type=jnp.float32),
            grad_out_proj,
        ]
    )
    grad_first = jnp.einsum(
        "le,de->ld", grad_query16, attn16[0], preferred_element_type=jnp.float32
    )
    grad_first = grad_first + jnp.einsum(
        "le,de->ld", grad_key16, attn16[1], preferred_element_type=jnp.float32
    )
    grad_first = grad_first + jnp.einsum(
        "le,de->ld", grad_value16, attn16[2], preferred_element_type=jnp.float32
    )
    grad_norm_first, grad_gain_first = norm_backward(
        grad_first, hat_first, inverse_first, gain_first
    )
    input_grad = grad_hidden_state + grad_norm_first
    gain_grads = jnp.stack([grad_gain_first, grad_gain_second])
    attn_grad, shared_grad, router_grad, gain_grad = (
        lax.psum_scatter(attn_grads, ("dp", "expert"), scatter_dimension=1, tiled=True),
        lax.psum_scatter(shared_grads, ("dp", "expert"), scatter_dimension=1, tiled=True),
        lax.psum_scatter(router_grad_full, ("dp", "expert"), scatter_dimension=0, tiled=True),
        lax.psum_scatter(gain_grads, ("dp", "expert"), scatter_dimension=1, tiled=True),
    )
    row_sums = lax.psum(
        (
            jnp.sum(valid_rows * block_value * block_value),
            jnp.sum(valid_rows * input_grad * input_grad),
            length_here.astype(jnp.float32),
        ),
        ("dp", "expert"),
    )
    denominator = model_width * row_sums[2]
    masked_rms = jnp.stack(
        [jnp.sqrt(row_sums[0] / denominator), jnp.sqrt(row_sums[1] / denominator)]
    )
    attn_parts = update(
        attn_weight, attn_moment, attn_average, attn_grad, rate_attention * step_root
    )
    router_parts = update(
        router_weight, router_moment, router_average, router_grad, rate_router * step_root
    )
    shared_parts = update(
        shared_weight, shared_moment, shared_average, shared_grad, rate_shared * step_root
    )
    routed_parts = update(
        routed_weight, routed_moment, routed_average, routed_grad_shard, rate_routed * step_root
    )
    gain_parts = update(norm_gains, gain_moment, gain_average, gain_grad, rate_gains * step_root)
    return (
        block_value.astype(jnp.bfloat16),
        input_grad,
        masked_rms,
        attn_parts[0],
        attn_parts[1],
        attn_parts[2],
        attn_parts[3],
        attn_parts[4],
        router_parts[0],
        router_parts[1],
        router_parts[2],
        router_parts[3],
        router_parts[4],
        shared_parts[0],
        shared_parts[1],
        shared_parts[2],
        shared_parts[3],
        shared_parts[4],
        routed_parts[0],
        routed_parts[1],
        routed_parts[2],
        routed_parts[3],
        routed_parts[4],
        gain_parts[0],
        gain_parts[1],
        gain_parts[2],
        gain_parts[3],
    )


def solution(mesh):
    placed = (
        P(("dp", "expert"), None),
        P(("dp", "expert"), None),
        P(("dp", "expert")),
        P(("dp", "expert"), None),
        P(None, ("dp", "expert"), None),
        P(None, ("dp", "expert"), None),
        P(None, ("dp", "expert"), None),
        P(("dp", "expert"), None),
        P(("dp", "expert"), None),
        P(("dp", "expert"), None),
        P(None, ("dp", "expert"), None),
        P(None, ("dp", "expert"), None),
        P(None, ("dp", "expert"), None),
        P("expert", None, "dp", None),
        P("expert", None, "dp", None),
        P("expert", None, "dp", None),
        P(None, ("dp", "expert")),
        P(None, ("dp", "expert")),
        P(None, ("dp", "expert")),
    )
    return jax.shard_map(
        local,
        mesh=mesh,
        in_specs=placed,
        out_specs=(
            P(("dp", "expert"), None),
            P(("dp", "expert"), None),
            P(),
            P(None, ("dp", "expert"), None),
            P(None, ("dp", "expert"), None),
            P(None, ("dp", "expert"), None),
            P(None, ("dp", "expert"), None),
            P(None, ("dp", "expert"), None),
            P(("dp", "expert"), None),
            P(("dp", "expert"), None),
            P(("dp", "expert"), None),
            P(("dp", "expert"), None),
            P(("dp", "expert"), None),
            P(None, ("dp", "expert"), None),
            P(None, ("dp", "expert"), None),
            P(None, ("dp", "expert"), None),
            P(None, ("dp", "expert"), None),
            P(None, ("dp", "expert"), None),
            P("expert", None, "dp", None),
            P("expert", None, "dp", None),
            P("expert", None, "dp", None),
            P("expert", None, "dp", None),
            P("expert", None, "dp", None),
            P(None, ("dp", "expert")),
            P(None, ("dp", "expert")),
            P(None, ("dp", "expert")),
            P(None, ("dp", "expert")),
        ),
        check_vma=False,
    )
```

profile of v0, /device:TPU:0, one launch (start us, length us, event | category | flops | bytes accessed | tf_op | source)
XLA Modules:
  0.0 1615.0 jit_solution(7291214847206062660)
XLA Ops:
  9.3 5.2 copy.221
  16.4 43.3 %all-gather = bf16[32,40,2]{1,2,0:T(2,128)(2,1)S(1)} all-gather(bf16[1,40,2]{1,2,0:T(2,128)(2,1)S(1)} %convert_bitcast_fusion.1), channel_id=1, replica_groups=mesh['dp'=4,'expert'=8] {'dp','expert'}, dimensions={0}, use_global_device_ids=true | all-gather | bytes 5280 | tf_op jit(solution)/shard_map/all_gather | solution.py:105
  60.2 4.6 reduce-window.6
  65.9 14.2 scatter_custom_fusion
  84.9 27.5 %all-gather.6.cloned.1.call-done = bf16[4,1280,1280]{2,1,0:T(8,128)(2,1)} async-done(((bf16[4,40,1280]{2,1,0:T(8,128)(2,1)}), bf16[4,1280,1280]{2,1,0:T(8,128)(2,1)}) %all-gather.6.cloned.1.call-update) | async-done | bytes 13107216 | tf_op jit(solution)/shard_map/all_gather | solution.py:102
  112.4 6.2 slice_bitcast_fusion.13
  118.6 6.0 copy.153
  124.6 5.8 copy.154
  133.8 4.4 fusion.45
  150.5 4.6 multiply_reduce_fusion.5
  157.0 18.8 %gather_fusion = bf16[4096,1280]{1,0:T(8,128)(2,1)} fusion(bf16[513,1280]{1,0:T(8,128)(2,1)S(1)} %concatenate.22, s32[4096]{0:T(1024)S(1)} %copy-done.67), kind=kCustom, calls=%fused_computation.2 | custom fusion | bytes 20987904 | tf_op jit(solution)/shard_map/jit(_take)/gather | solution.py:173
  175.8 9.6 broadcast_select_fusion.1
  185.5 5.3 all-to-all-start
  191.6 115.7 %all-to-all-done = bf16[16,256,1280]{2,1,0:T(8,128)(2,1)} async-done(((bf16[16,256,1280]{2,1,0:T(8,128)(2,1)}), bf16[16,256,1280]{2,1,0:T(8,128)(2,1)}, u32[]{:S(2)}, u32[]{:S(2)}) %all-to-all-start) | async-done | bytes 10485792 | tf_op jit(solution)/shard_map/all_to_all | solution.py:176
  307.3 8.8 copy.165
  316.1 34.2 %all-gather.10.cloned.1.call-done = bf16[2,3,1280,896]{3,2,0,1:T(8,128)(2,1)} async-done(((bf16[2,3,320,896]{3,2,0,1:T(8,128)(2,1)}), bf16[2,3,1280,896]{3,2,0,1:T(8,128)(2,1)}) %all-gather.10.cloned.1.call-update) | async-done | bytes 13762576 | tf_op jit(solution)/shard_map/all_gather | solution.py:107
  350.3 18.0 %fusion.9 = f32[2,2048,896]{2,1,0:T(8,128)} fusion(bf16[2,2048,1280]{2,1,0:T(8,128)(2,1)} %bitcast.213, bf16[2,3,1280,896]{3,2,0,1:T(8,128)(2,1)} %all-gather.10.cloned.1.call-done), kind=kOutput, calls=%fused_computation.52 | convolution fusion | flops 9395240960 | bytes 29753344 | tf_op jit(solution)/shard_map/erd,edf->erf/dot_general | solution.py:177
  368.4 21.8 %multiply_convert_fusion.3 = (bf16[2,2048,896]{2,1,0:T(8,128)(2,1)}, f32[2,2048,896]{2,1,0:T(8,128)}) fusion(f32[2,2048,896]{2,1,0:T(8,128)} %fusion.9, bf16[2,2048,1280]{2,1,0:T(8,128)(2,1)} %bitcast.214, bf16[2,3,1280,896]{3,2,0,1:T(8,128)(2,1)} %all-gather.10.cloned.1.call-done), kind=kOutput, calls=%fused_computation.12 | convolution fusion | flops 9417261056 | bytes 51773440 | tf_op jit(solution)/shard_map/erd,edf->erf/dot_general | solution.py:180
  390.1 14.7 convolution_convert_fusion
  404.8 74.6 %copy.167 = bf16[2,2048,1280]{2,0,1:T(2,128)(2,1)} copy(bf16[2,2048,1280]{2,1,0:T(8,128)(2,1)S(1)} %convolution_convert_fusion) | data formatting | bytes 20971520 | tf_op jit(solution)/shard_map/convert_element_type | solution.py:186
  479.4 5.3 all-to-all-start.1
  485.0 7.7 mul.704
  492.7 19.5 %mul.705 = f32[3584,1280]{1,0:T(8,128)} reshape(f32[512,7,1280]{2,1,0:T(8,128)} %mul.704) | data formatting | bytes 36700160 | tf_op jit(solution)/shard_map/mul | solution.py:225
  512.2 118.5 %all-gather.1 = bf16[32,40,16]{1,2,0:T(8,128)(2,1)S(1)} all-gather(bf16[1,40,16]{1,2,0:T(8,128)(2,1)S(1)} %convert_bitcast_fusion), channel_id=1, replica_groups=mesh['dp'=4,'expert'=8] {'dp','expert'}, dimensions={0}, use_global_device_ids=true | all-gather | bytes 42240 | tf_op jit(solution)/shard_map/all_gather | solution.py:104
  646.4 3.8 convolution_bitcast_fusion.4
  650.2 9.8 copy.168
  660.1 24.6 %gather_fusion.2 = bf16[3584,1280]{1,0:T(8,128)(2,1)} fusion(bf16[4096,1280]{1,0:T(8,128)(2,1)} %bitcast.201, s32[4096]{0:T(1024)S(1)} %pad_clamp_fusion), kind=kCustom, calls=%fused_computation.clone | custom fusion | bytes 18364416 | tf_op jit(solution)/shard_map/jit(_take)/gather | solution.py:191
  684.7 10.2 multiply_reduce_fusion.1
  697.3 10.9 pad_maximum_fusion.1
  709.2 11.6 multiply_convert_fusion
  720.8 7.7 concatenate.23
  728.5 27.8 %gather_fusion.1 = bf16[4096,1280]{1,0:T(8,128)(2,1)} fusion(bf16[3585,1280]{1,0:T(8,128)(2,1)} %concatenate.23, s32[4096]{0:T(1024)S(1)} %copy-done.66), kind=kCustom, calls=%fused_computation.3 | custom fusion | bytes 20987904 | tf_op jit(solution)/shard_map/jit(_take)/gather | solution.py:231
  756.3 6.0 broadcast_select_fusion
  762.3 177.9 %all_to_all.66 = bf16[16,256,1280]{2,1,0:T(8,128)(2,1)} all-to-all(bf16[16,256,1280]{2,1,0:T(8,128)(2,1)S(1)} %broadcast_select_fusion), channel_id=1, replica_groups=mesh['dp'=4,'expert'=8] {'expert'}, dimensions={0} | all-to-all | bytes 20971520 | tf_op jit(solution)/shard_map/all_to_all | solution.py:234
  940.2 9.1 copy.170
  949.3 17.4 %convolution_convert_fusion.1 = bf16[2,1280,896]{2,1,0:T(8,128)(2,1)} fusion(bf16[2,2048,1280]{2,1,0:T(8,128)(2,1)} %bitcast.217, bf16[2,2048,896]{2,1,0:T(8,128)(2,1)} %get-tuple-element.261), kind=kOutput, calls=%fused_computation.42 | convolution fusion | flops 9397534720 | bytes 22413312 | tf_op jit(solution)/shard_map/erd,erf->edf/dot_general | solution.py:258
  966.8 27.0 %multiply_convert_fusion.1 = (bf16[2,2048,896]{2,1,0:T(8,128)(2,1)}, bf16[2,2048,896]{2,1,0:T(8,128)(2,1)}) fusion(f32[2,2048,896]{2,1,0:T(8,128)} %fusion.9, f32[2,2048,896]{2,1,0:T(8,128)} %get-tuple-element.262, bf16[2,2048,1280]{2,1,0:T(8,128)(2,1)} %bitcast.218, bf16[2,3,1280,896]{3,2,0,1:T(8,128)(2,1)} %all-gather.10.cloned.1.call-done), kind=kOutput, calls=%fused_computation.10 | convolution fusion | flops 9442951168 | bytes 59113472 | tf_op jit(solution)/shard_map/erd,edf->erf/dot_general | solution.py:235
  993.8 18.8 %fusion.8 = f32[2,2048,1280]{2,1,0:T(8,128)} fusion(bf16[2,2048,896]{2,1,0:T(8,128)(2,1)} %get-tuple-element.227, bf16[2,3,1280,896]{3,2,0,1:T(8,128)(2,1)} %all-gather.10.cloned.1.call-done), kind=kOutput, calls=%fused_computation.51 | convolution fusion | flops 9395240960 | bytes 32899072 | tf_op jit(solution)/shard_map/erf,edf->erd/dot_general | solution.py:240
  1012.6 18.2 %add_convert_fusion = bf16[2,2048,1280]{2,1,0:T(8,128)(2,1)} fusion(f32[2,2048,1280]{2,1,0:T(8,128)} %fusion.8, bf16[2,2048,896]{2,1,0:T(8,128)(2,1)S(1)} %copy-done.93, bf16[2,3,1280,896]{3,2,0,1:T(8,128)(2,1)} %all-gather.10.cloned.1.call-done), kind=kOutput, calls=%fused_computation.6 | convolution fusion | flops 9405726720 | bytes 43384832 | tf_op jit(solution)/shard_map/erf,edf->erd/dot_general | solution.py:245
  1030.8 20.2 %copy.171 = bf16[2,2048,1280]{2,0,1:T(2,128)(2,1)} copy(bf16[2,2048,1280]{2,1,0:T(8,128)(2,1)} %add_convert_fusion) | data formatting | bytes 20971520 | tf_op jit(solution)/shard_map/convert_element_type | solution.py:248
  1050.9 15.8 convolution_convert_fusion.2
  1066.8 5.3 all-to-all-start.3
  1072.2 4.7 fusion.34
  1076.9 17.6 %convolution_convert_fusion.3 = bf16[2,1280,896]{2,1,0:T(8,128)(2,1)} fusion(bf16[2,2048,1280]{2,1,0:T(8,128)(2,1)} %bitcast.216, bf16[2,2048,896]{2,1,0:T(8,128)(2,1)} %get-tuple-element.227), kind=kOutput, calls=%fused_computation.44 | convolution fusion | flops 9397534720 | bytes 22413312 | tf_op jit(solution)/shard_map/erd,erf->edf/dot_general | solution.py:252
  1094.6 94.1 %all-to-all-done.3 = bf16[2,2048,1280]{2,0,1:T(2,128)(2,1)} async-done(((bf16[2,2048,1280]{2,0,1:T(2,128)(2,1)}), bf16[2,2048,1280]{2,0,1:T(2,128)(2,1)}, u32[]{:S(2)}, u32[]{:S(2)}) %all-to-all-start.3) | async-done | bytes 10485792 | tf_op jit(solution)/shard_map/all_to_all | solution.py:249
  1188.7 9.8 copy.172
  1198.5 24.8 %gather_fusion.3 = bf16[3584,1280]{1,0:T(8,128)(2,1)} fusion(bf16[4096,1280]{1,0:T(8,128)(2,1)} %bitcast.200, s32[4096]{0:T(1024)S(1)} %copy-done.59), kind=kCustom, calls=%fused_computation.1.clone | custom fusion | bytes 18364416 | tf_op jit(solution)/shard_map/jit(_take)/gather | solution.py:274
  1223.3 18.8 %select_convert_fusion = (f32[3584,1280]{1,0:T(8,128)}, f32[3584,1280]{1,0:T(8,128)}) fusion(bf16[3584,1280]{1,0:T(8,128)(2,1)} %gather_fusion.3, pred[3584]{0:T(1024)(128)(4,1)S(1)} %copy-done.69, bf16[3584,1280]{1,0:T(8,128)(2,1)} %gather_fusion.2), kind=kLoop, calls=%fused_computation.26 | loop fusion | flops 18350080 | bytes 55053824 | tf_op jit(solution)/shard_map/convert_element_type | solution.py:276
  1242.1 19.1 %reshape.451 = f32[512,7,1280]{2,1,0:T(8,128)} reshape(f32[3584,1280]{1,0:T(8,128)} %get-tuple-element.252) | data formatting | bytes 36700160 | tf_op jit(solution)/shard_map/convert_element_type | solution.py:276
  1261.2 12.2 reduce_sum.176
  1273.4 5.3 fusion.16
  1283.2 4.9 convolution_convert_fusion.4
  1290.5 7.0 multiply_reduce_fusion.2
  1319.0 8.9 pad_maximum_fusion
  1335.3 19.3 %reshape.450 = f32[512,7,1280]{2,1,0:T(8,128)} reshape(f32[3584,1280]{1,0:T(8,128)} %get-tuple-element.253) | data formatting | bytes 36700160 | tf_op jit(solution)/shard_map/convert_element_type | solution.py:193
  1354.7 4.4 fusion.19
  1359.1 4.1 convolution_add_fusion.4
  1363.3 4.8 fusion.30
  1368.2 25.8 %multiply_reduce_fusion = f32[512,1280]{1,0:T(8,128)S(1)} fusion(f32[512,7,1280]{2,1,0:T(8,128)S(1)} %bitcast.205, f32[512,7]{1,0:T(8,128)S(1)} %copy-done.29), kind=kLoop, calls=%fused_computation.7 | loop fusion | flops 8519680 | bytes 20985856 | tf_op jit(solution)/shard_map/reduce_sum | solution.py:195
  1394.0 6.5 fusion.32
  1400.6 41.4 %all-reduce.4 = (f32[]{:T(128)}, f32[]{:T(128)}, f32[]{:T(128)}, f32[2,1280]{1,0:T(2,128)S(1)}) all-reduce(f32[]{:T(128)} %get-tuple-element.200, f32[]{:T(128)S(6)} %convert_element_type.275, f32[]{:T(128)} %get-tuple-element.199, f32[2,1280]{1,0:T(2,128)S(1)} %pad_maximum_fusion.8), channel_id=1, replica_groups=mesh['dp'=4,'expert'=8] {'dp','expert'}, use_global_device_ids=true, to_apply=%region_23.25 | all-reduce | flops 2563 | bytes 20504 | tf_op jit(solution)/shard_map/psum | solution.py:372
  1450.1 6.4 fusion.76
  1463.3 3.7 multiply_add_fusion
  1473.8 130.9 %reduce-scatter.8.cloned.1.call-done = f32[4,40,1280]{2,1,0:T(8,128)} async-done(((f32[4,1280,1280]{2,1,0:T(8,128)}), f32[4,40,1280]{2,1,0:T(8,128)}) %reduce-scatter.8.cloned.1.call-update) | async-done | bytes 819216 | tf_op jit(solution)/shard_map/reduce_scatter | solution.py:367
  (333 shorter events, 105.9 us)
Async XLA Ops:
  7.2 105.2 %all-gather.6.cloned.1.call-start = ((), (), s32[]{:S(2)}) async-start(), calls=%async_computation.9 | async-start | bytes 13516800 | tf_op jit(solution)/shard_map/all_gather | solution.py:102
  9.2 341.1 %all-gather.10.cloned.1.call-start = ((), (), s32[]{:S(2)}) async-start(), calls=%async_computation.11 | async-start | bytes 17203200 | tf_op jit(solution)/shard_map/all_gather | solution.py:107
  15.2 66.2 %copy-start.12 = (bf16[512,1280]{1,0:T(8,128)(2,1)S(1)}, bf16[512,1280]{1,0:T(8,128)(2,1)}, u32[]{:S(2)}) copy-start(bf16[512,1280]{1,0:T(8,128)(2,1)} %param.21) | copy-start | bytes 3932164
  15.7 69.2 %copy-start.54 = (s32[3584]{0:T(1024)}, s32[3584]{0:T(1024)S(1)}, u32[]{:S(2)}) copy-start(s32[3584]{0:T(1024)S(1)} %eq.41) | copy-start | bytes 43012
  65.8 19.1 %copy-start.56 = (s32[3584]{0:T(1024)}, s32[3584]{0:T(1024)S(1)}, u32[]{:S(2)}) copy-start(s32[3584]{0:T(1024)S(1)} %fusion.56) | copy-start | bytes 43012
  81.4 62.1 %copy-start.70 = (f32[1280]{0:T(1024)}, f32[1280]{0:T(1024)S(1)}, u32[]{:S(2)}) copy-start(f32[1280]{0:T(1024)S(1)} %get-tuple-element.198) | copy-start | bytes 15364
  81.4 73.8 %copy-start.64 = (f32[1280]{0:T(1024)}, f32[1280]{0:T(1024)S(1)}, u32[]{:S(2)}) copy-start(f32[1280]{0:T(1024)S(1)} %get-tuple-element.197) | copy-start | bytes 15364
  84.9 55.4 %copy-start.39 = (f32[512,64]{0,1:T(8,128)}, f32[512,64]{0,1:T(8,128)S(1)}, u32[]{:S(2)}) copy-start(f32[512,64]{0,1:T(8,128)S(1)} %get-tuple-element.256) | copy-start | bytes 393220
  133.8 4.5 copy-start.13
  133.8 4.5 copy-start.17
  133.8 4.5 copy-start.83
  150.5 4.6 copy-start.89
  157.0 18.8 %copy-start.80 = (pred[16,256]{1,0:T(8,128)(4,1)S(1)}, pred[16,256]{1,0:T(8,128)(4,1)}, u32[]{:S(2)}) copy-start(pred[16,256]{1,0:T(8,128)(4,1)} %broadcast_in_dim.89) | copy-start | bytes 12292
  185.5 5.4 copy-start.31
  185.5 121.8 %all-to-all-start = ((bf16[16,256,1280]{2,1,0:T(8,128)(2,1)}), bf16[16,256,1280]{2,1,0:T(8,128)(2,1)}, u32[]{:S(2)}, u32[]{:S(2)}) async-start(bf16[16,256,1280]{2,1,0:T(8,128)(2,1)} %broadcast_select_fusion.1), calls=%async_computation | async-start | bytes 20971520 | tf_op jit(solution)/shard_map/all_to_all | solution.py:176
  190.8 440.9 %all-gather.8.cloned.1.call-start = ((), (), s32[]{:S(2)}) async-start(), calls=%async_computation.10 | async-start | bytes 7096320 | tf_op jit(solution)/shard_map/all_gather | solution.py:103
  479.4 5.4 copy-start.10
  479.4 170.8 %all-to-all-start.1 = ((bf16[2,2048,1280]{2,0,1:T(2,128)(2,1)}), bf16[2,2048,1280]{2,0,1:T(2,128)(2,1)}, u32[]{:S(2)}, u32[]{:S(2)}) async-start(bf16[2,2048,1280]{2,0,1:T(2,128)(2,1)} %copy.167), calls=%async_computation.1 | async-start | bytes 20971520 | tf_op jit(solution)/shard_map/all_to_all | solution.py:187
  484.7 843.2 %all-reduce.7.cloned.1.call-start = ((), (), s32[]{:S(2)}) async-start(), calls=%async_computation.17 | async-start | bytes 163840
  484.8 161.7 %copy-start.77 = (f32[512]{0:T(512)}, f32[512]{0:T(512)S(1)}, u32[]{:S(2)}) copy-start(f32[512]{0:T(512)S(1)} %fusion.69) | copy-start | bytes 6148
  492.7 19.5 %copy-start.73 = (f32[40,16]{0,1:T(8,128)S(1)}, f32[40,16]{0,1:T(8,128)}, u32[]{:S(2)}) copy-start(f32[40,16]{0,1:T(8,128)} %param.28) | copy-start | bytes 7684
  492.7 138.3 %copy-start.55 = (s32[3584]{0:T(1024)S(1)}, s32[3584]{0:T(1024)}, u32[]{:S(2)}) copy-start(s32[3584]{0:T(1024)} %copy-done.54) | copy-start | bytes 43012
  492.7 138.3 %copy-start.57 = (s32[3584]{0:T(1024)S(1)}, s32[3584]{0:T(1024)}, u32[]{:S(2)}) copy-start(s32[3584]{0:T(1024)} %copy-done.56) | copy-start | bytes 43012
  492.7 138.3 %copy-start.4 = (bf16[512,1280]{1,0:T(8,128)(2,1)S(1)}, bf16[512,1280]{1,0:T(8,128)(2,1)}, u32[]{:S(2)}) copy-start(bf16[512,1280]{1,0:T(8,128)(2,1)} %copy-done.3) | copy-start | bytes 3932164
  492.7 138.8 %copy-start.53 = (s32[512,7]{0,1:T(8,128)S(1)}, s32[512,7]{0,1:T(8,128)}, u32[]{:S(2)}) copy-start(s32[512,7]{0,1:T(8,128)} %param.24) | copy-start | bytes 43012
  631.0 53.7 %copy-start.68 = (pred[3584]{0:T(1024)(128)(4,1)}, pred[3584]{0:T(1024)(128)(4,1)S(1)}, u32[]{:S(2)}) copy-start(pred[3584]{0:T(1024)(128)(4,1)S(1)} %get-tuple-element.224) | copy-start | bytes 10756
  631.0 29.0 %copy-start.58 = (s32[4096]{0:T(1024)}, s32[4096]{0:T(1024)S(1)}, u32[]{:S(2)}) copy-start(s32[4096]{0:T(1024)S(1)} %pad_clamp_fusion) | copy-start | bytes 49156
  639.0 7.4 copy-start.42
  697.2 633.3 %reduce-scatter.10.cloned.1.call-start = ((), (), s32[]{:S(2)}) async-start(), calls=%async_computation.13 | async-start | bytes 14192640 | tf_op jit(solution)/shard_map/reduce_scatter | solution.py:368
  708.2 735.8 %reduce-scatter.16.cloned.1.call-start = ((), (), s32[]{:S(2)}) async-start(), calls=%async_computation.16 | async-start | bytes 5734400 | tf_op jit(solution)/shard_map/reduce_scatter | solution.py:268
  709.0 11.8 copy-start.28
  720.8 7.7 copy-start.66
  966.7 477.3 %reduce-scatter.14.cloned.1.call-start = ((), (), s32[]{:S(2)}) async-start(), calls=%async_computation.15 | async-start | bytes 5734400 | tf_op jit(solution)/shard_map/reduce_scatter | solution.py:265
  993.8 18.8 %copy-start.93 = (bf16[2,2048,896]{2,1,0:T(8,128)(2,1)S(1)}, bf16[2,2048,896]{2,1,0:T(8,128)(2,1)}, u32[]{:S(2)}) copy-start(bf16[2,2048,896]{2,1,0:T(8,128)(2,1)} %get-tuple-element.226) | copy-start | bytes 22020100
  1066.8 5.4 copy-start.61
  1066.8 5.4 copy-start.63
  1066.8 5.4 copy-start.92
  1066.8 121.9 %all-to-all-start.3 = ((bf16[2,2048,1280]{2,0,1:T(2,128)(2,1)}), bf16[2,2048,1280]{2,0,1:T(2,128)(2,1)}, u32[]{:S(2)}, u32[]{:S(2)}) async-start(bf16[2,2048,1280]{2,0,1:T(2,128)(2,1)} %copy.171), calls=%async_computation.3 | async-start | bytes 20971520 | tf_op jit(solution)/shard_map/all_to_all | solution.py:249
  1072.1 372.0 %reduce-scatter.12.cloned.1.call-start = ((), (), s32[]{:S(2)}) async-start(), calls=%async_computation.14 | async-start | bytes 5734400 | tf_op jit(solution)/shard_map/reduce_scatter | solution.py:262
  1094.5 510.2 %reduce-scatter.8.cloned.1.call-start = ((), (), s32[]{:S(2)}) async-start(), calls=%async_computation.12 | async-start | bytes 27033600 | tf_op jit(solution)/shard_map/reduce_scatter | solution.py:367
  1188.7 9.8 copy-start.59
  1198.5 24.8 %copy-start.69 = (pred[3584]{0:T(1024)(128)(4,1)S(1)}, pred[3584]{0:T(1024)(128)(4,1)}, u32[]{:S(2)}) copy-start(pred[3584]{0:T(1024)(128)(4,1)} %copy-done.68) | copy-start | bytes 10756
  1273.4 5.3 copy-start.2
  1273.4 5.3 copy-start.48
  1273.4 5.3 copy-start.50
  1273.4 5.3 copy-start.65
  1273.4 5.3 copy-start.76
  1290.5 7.0 slice-start
  1290.5 7.2 slice-start.1
  1290.5 7.8 slice-start.2
  1308.2 6.5 copy-start.38
  1330.0 24.7 %copy-start.72 = (f32[40,16]{0,1:T(8,128)}, f32[40,16]{0,1:T(8,128)S(1)}, u32[]{:S(2)}) copy-start(f32[40,16]{0,1:T(8,128)S(1)} %get-tuple-element.215) | copy-start | bytes 7684
  1354.7 13.5 slice-start.3
  1354.7 13.5 slice-start.4
  1359.1 9.0 slice-start.5
  1359.1 9.0 slice-start.6
  1363.3 4.9 slice-start.7
  1363.3 4.9 copy-start.29
  1368.2 25.9 %copy-start.9 = (f32[512,1280]{1,0:T(8,128)S(1)}, f32[512,1280]{1,0:T(8,128)}, u32[]{:S(2)}) copy-start(f32[512,1280]{1,0:T(8,128)} %copy-done.7) | copy-start | bytes 7864324
  1368.2 25.9 %copy-start.43 = (bf16[512,896]{1,0:T(8,128)(2,1)S(1)}, bf16[512,896]{1,0:T(8,128)(2,1)}, u32[]{:S(2)}) copy-start(bf16[512,896]{1,0:T(8,128)(2,1)} %copy-done.42) | copy-start | bytes 2752516
  1444.1 6.0 slice-start.8
  1470.5 134.2 %copy-start.18 = (f32[4,40,1280]{2,1,0:T(8,128)S(1)}, f32[4,40,1280]{2,1,0:T(8,128)}, u32[]{:S(2)}) copy-start(f32[4,40,1280]{2,1,0:T(8,128)} %param.25) | copy-start | bytes 2457604
  1470.5 134.2 %copy-start.45 = (f32[4,40,1280]{2,1,0:T(8,128)S(1)}, f32[4,40,1280]{2,1,0:T(8,128)}, u32[]{:S(2)}) copy-start(f32[4,40,1280]{2,1,0:T(8,128)} %param.26) | copy-start | bytes 2457604
  1472.6 134.5 %copy-start.44 = (f32[4,40,1280]{2,1,0:T(8,128)S(1)}, f32[4,40,1280]{2,1,0:T(8,128)}, u32[]{:S(2)}) copy-start(f32[4,40,1280]{2,1,0:T(8,128)} %param.27) | copy-start | bytes 2457604
  (52 other events, 123.3 us)
Sparse Core Ops, SparseCore 0:
  11.5 100.8 all-gather.5
  114.5 235.7 all-gather.9
  353.8 69.8 all-gather.7
  697.4 116.3 all-reduce.6
  816.5 212.3 reduce-scatter.9
  1031.7 81.6 reduce-scatter.15
  1116.4 83.6 reduce-scatter.13
  1203.1 83.6 reduce-scatter.11
  1328.0 276.6 reduce-scatter.7
where the time goes:
time: 1630 us; the launch traced here: 1620 us
  waiting for transfers between devices  403 us (25%)
  blocking collectives  381 us (23%)
  local copies, waits for them, and re-layouts  374 us (23%)
  matrix products  264 us (16%)
  other arithmetic  158 us (10%)
  between operations  18.3 us (1%)
  starting transfers between devices  16.3 us (1%)
    all_to_all x1, blocking collectives, local(): lax.all_to_all(send_grads, 'expert', split_axis=0, concat_axis=1, tiled=T...  178 us
    reduce_scatter x1, waiting for transfers between devices, local(): lax.psum_scatter(attn_grads, ('dp', 'expert'), scatter_dimension=1, tiled...  131 us
    all_gather x1, blocking collectives, local(): lax.all_gather(router_weight.astype(jnp.bfloat16), ('dp', 'expert'), axis...  118 us
    all_to_all x1, waiting for transfers between devices, local(): lax.all_to_all(send_rows, 'expert', split_axis=0, concat_axis=1, tiled=True)  116 us
    all_to_all x1, waiting for transfers between devices, local(): lax.all_to_all(grad_rows, 'expert', split_axis=1, concat_axis=0, tiled=True)  94.1 us
    convert_element_type x1, local copies, waits for them, and re-layouts, local(): expert_out = jnp.einsum('erf,edf->erd', hidden16, expert16[:, 2], preferr...  74.6 us
    all_gather x1, blocking collectives, local(): lax.all_gather(norm_gains.astype(jnp.bfloat16), ('dp', 'expert'), axis=1,...  43.3 us
    psum x1, blocking collectives, local(): lax.psum((jnp.sum(valid_rows * block_value * block_value), jnp.sum(valid_...  41.4 us
  transfers between devices with their start and end apart: 12, of which 5 were waited for; matrix products, arithmetic and copies ran while one was open for 45% of the time, Pallas kernels for 0%

commit v1 on v0

v1 whole, which is shorter than its diff:
```python
import functools
import math

import jax
import jax.numpy as jnp
from jax import lax
from jax.experimental import pallas as pl
from jax.experimental.pallas import tpu as pltpu
from jax.sharding import PartitionSpec as P

HEADS = 10
STEP = 3
BF = jnp.bfloat16
F32 = jnp.float32
BOTH = ("dp", "expert")


eps_norm = 1e-06
momentum_rate = 0.9
decay_rate = 0.0001
rate_attention = 0.01
rate_router = 0.03
rate_shared = 0.01
rate_routed = 0.04
rate_gains = 0.2
masked_score = -1e30
block_limit = 512


def norm_forward(values, gain_row):
    inverse = lax.rsqrt(jnp.mean(values * values, axis=-1, keepdims=True) + eps_norm)
    normal_part = values * inverse
    return (normal_part * gain_row, normal_part, inverse)


def norm_backward(grad_out, normal_part, inverse, gain_row):
    grad_hat = grad_out * gain_row
    grad_in = inverse * (
        grad_hat - normal_part * jnp.mean(grad_hat * normal_part, axis=-1, keepdims=True)
    )
    return (grad_in, jnp.sum(grad_out * normal_part, axis=0))


def rotate(values, positions, direction):
    half_dim = values.shape[-1] // 2
    frequency = 10000.0 ** (-jnp.arange(half_dim, dtype=F32) / half_dim)
    angles = positions.astype(F32)[:, None] * frequency[None, :]
    cosine = jnp.cos(angles)[:, None, :]
    sine_part = direction * jnp.sin(angles)[:, None, :]
    first_half = values[..., :half_dim]
    second_half = values[..., half_dim:]
    return jnp.concatenate(
        [
            first_half * cosine - second_half * sine_part,
            second_half * cosine + first_half * sine_part,
        ],
        axis=-1,
    )


def silu_slope(pre_value):
    sigmoid_part = jax.nn.sigmoid(pre_value)
    return sigmoid_part * (1.0 + pre_value * (1.0 - sigmoid_part))


def update(weight, moment, average, gradient, step_rate):
    decayed = gradient + decay_rate * weight
    moment_new = momentum_rate * moment + decayed
    weight_new = weight - step_rate * (decayed + momentum_rate * moment_new)
    average_new = average + (weight_new - average) / (STEP + 1.0)
    return (gradient, weight_new, moment_new, average_new, weight_new.astype(BF))


def dot_nn(a,b): return lax.dot_general(a,b,(((1,),(0,)),((),())),preferred_element_type=F32)
def dot_nt(a,b): return lax.dot_general(a,b,(((1,),(1,)),((),())),preferred_element_type=F32)
def dot_tn(a,b): return lax.dot_general(a,b,(((0,),(0,)),((),())),preferred_element_type=F32)

def chunks(n,c): return [(s,min(c,n-s)) for s in range(0,n,c)]

def expert_kernel(first, n_seq, sps, *refs):
    it=iter(refs)
    eid_ref=next(it); choice_ref=next(it); slot_ref=next(it); router_ref=next(it); w_hbm=next(it)
    sec_hbm=[next(it) for _ in range(n_seq)]
    dout_hbm=[next(it) for _ in range(n_seq)]
    prev=None
    if not first: prev=[next(it) for _ in range(4)]
    outs=[next(it) for _ in range(4)]
    dg_ref=next(it); wg_hbm=next(it)
    w_v,tok,rows_v,dy_v,h_v,da_v,db_v,ob,wsem,tsem,osem,gsem=it
    n_dp=w_hbm.shape[0]; slab=w_hbm.shape[2]
    seq=slot_ref.shape[1]
    width=sec_hbm[0].shape[1]
    ff=w_v.shape[2]
    cap=rows_v.shape[0]//n_seq
    steps=n_seq//sps
    def wcopy(d,j): return pltpu.make_async_copy(w_hbm.at[d,j], w_v.at[j,pl.ds(d*slab,slab)], wsem.at[d,j])
    def tcopy(k,q,j,slot):
        src=(sec_hbm if j==0 else dout_hbm)[k*sps+q]
        return pltpu.make_async_copy(src.at[pl.ds(0,seq)], tok.at[slot,q,j], tsem.at[slot,q,j])
    def ocopy(p,q,j):
        return pltpu.make_async_copy(ob.at[q,j], outs[2*j+q].at[p], osem.at[q,j])
    def pcopy(p,q,j):
        return pltpu.make_async_copy(prev[2*j+q].at[p], ob.at[q,j], gsem.at[q,j])
    for q in range(sps):
        for j in range(2): tcopy(0,q,j,0).start()
    for j in range(3):
        for d in range(n_dp): wcopy(d,j).start()
    lane=lax.broadcasted_iota(jnp.int32,(seq,128),1)
    sub=lax.broadcasted_iota(jnp.int32,(cap,seq),0)
    eid=eid_ref[0]; loc=eid_ref[1]
    def step(p,carry):
        slot=lax.rem(p,2)
        for k in range(1,steps):
            @pl.when(p+1==k)
            def _():
                for q in range(sps):
                    for j in range(2): tcopy(k,q,j,lax.rem(k,2)).start()
        for q in range(sps):
            for j in range(2): tcopy(0,q,j,slot).wait()
        @pl.when(p>0)
        def _():
            for q in range(sps):
                for j in range(2): ocopy(p-1,q,j).wait()
        if not first:
            for q in range(sps):
                for j in range(2): pcopy(p,q,j).start()
        base=pl.multiple_of(p*sps*cap,sps*cap)
        gcols=[];onehots=[]
        for q in range(sps):
            sec=tok[slot,q,0]
            r=p*sps+q
            logits=dot_nt(sec,router_ref[...])
            ch=choice_ref[r]
            table=ch[:,0:1]==lane
            for k in range(1,ch.shape[1]): table=table|(ch[:,k:k+1]==lane)
            masked=jnp.where(table,logits,-1e30)
            ex=jnp.exp(masked-jnp.max(masked,axis=1,keepdims=True))
            ex=jnp.where(table,ex,0.0)
            gates=ex/jnp.sum(ex,axis=1,keepdims=True)
            gcol=jnp.sum(jnp.where(lane==eid,gates,0.0),axis=1,keepdims=True)
            onehot=(slot_ref[pl.ds(r,1),:]==sub).astype(F32).astype(BF)
            rows_v[pl.ds(base+q*cap,cap),:]=dot_nn(onehot,sec).astype(BF)
            gd=(gcol*tok[slot,q,1].astype(F32)).astype(BF)
            dy_v[pl.ds(base+q*cap,cap),:]=dot_nn(onehot,gd).astype(BF)
            gcols.append(gcol); onehots.append(onehot)
        @pl.when(p==0)
        def _():
            for j in range(3):
                for d in range(n_dp): wcopy(d,j).wait()
        win=pl.ds(base,sps*cap)
        for c0,cn in chunks(ff,256):
            cs=slice(c0,c0+cn)
            rows2=rows_v[win,:]
            a=dot_nn(rows2,w_v[0,:,cs]); b=dot_nn(rows2,w_v[1,:,cs]); dh=dot_nn(dy_v[win,:],w_v[2,:,cs])
            sig=1.0/(1.0+jnp.exp(-a))
            silu=a*sig
            h_v[win,cs]=(silu*b).astype(BF)
            da_v[win,cs]=(dh*b*(sig*(1.0+a*(1.0-sig)))).astype(BF)
            db_v[win,cs]=(dh*silu).astype(BF)
        if not first:
            for q in range(sps):
                for j in range(2): pcopy(p,q,j).wait()
        dgs=[jnp.zeros((seq,1),F32) for _ in range(sps)]
        for n0,nn in chunks(width,256):
            ns=slice(n0,n0+nn)
            y=dot_nt(h_v[win,:],w_v[2,ns,:]).astype(BF)
            dr=(dot_nt(da_v[win,:],w_v[0,ns,:])+dot_nt(db_v[win,:],w_v[1,ns,:])).astype(BF)
            for q in range(sps):
                yt=dot_tn(onehots[q],y[q*cap:(q+1)*cap])
                dt=dot_tn(onehots[q],dr[q*cap:(q+1)*cap])
                dgs[q]=dgs[q]+jnp.sum(tok[slot,q,1,:,ns].astype(F32)*yt,axis=1,keepdims=True)
                yt=yt*gcols[q]
                if not first:
                    yt=yt+ob[q,0,:,ns].astype(F32); dt=dt+ob[q,1,:,ns].astype(F32)
                ob[q,0,:,ns]=yt.astype(BF); ob[q,1,:,ns]=dt.astype(BF)
        for q in range(sps):
            r=p*sps+q
            dgt=jnp.transpose(jnp.where(lane==0,dgs[q],0.0))
            dg_ref[r]=dgt[0:8,:]
            for j in range(2): ocopy(p,q,j).start()
        return carry
    lax.fori_loop(0,steps,step,0)
    for q in range(sps):
        for j in range(2): ocopy(0,q,j).wait()
    def wg(i,carry):
        m=pl.ds(pl.multiple_of(i*256,256),256)
        rt=rows_v[:,m]
        w_v[0,m,:]=dot_tn(rt,da_v[...]).astype(BF)
        w_v[1,m,:]=dot_tn(rt,db_v[...]).astype(BF)
        w_v[2,m,:]=dot_tn(dy_v[:,m],h_v[...]).astype(BF)
        return carry
    lax.fori_loop(0,width//256,wg,0)
    def gcopy(d,j): return pltpu.make_async_copy(w_v.at[j,pl.ds(d*slab,slab)], wg_hbm.at[d,j], wsem.at[d,j])
    for j in range(3):
        for d in range(n_dp): gcopy(d,j).start()
    for j in range(3):
        for d in range(n_dp): gcopy(d,j).wait()

def expert_call(eid, choice_rel, slots, router_pad, w, secs, douts, prev, cap):
    n_seq=len(secs); sps=2
    seq=slots.shape[1]
    width=secs[0].shape[1]
    n_dp,_,slab,ff=w.shape
    first=prev is None
    ANY=pl.BlockSpec(memory_space=pl.ANY); VM=pl.BlockSpec(memory_space=pltpu.VMEM); SM=pl.BlockSpec(memory_space=pltpu.SMEM)
    args=[eid,choice_rel,slots,router_pad,w,*secs,*douts]+([] if first else list(prev))
    in_specs=[SM,VM,VM,VM]+[ANY]*(len(args)-4)
    half=jax.ShapeDtypeStruct((n_seq//2,seq,width),BF)
    out_shape=[half]*4+[jax.ShapeDtypeStruct((n_seq,8,seq),F32),jax.ShapeDtypeStruct(w.shape,BF)]
    out_specs=[ANY]*4+[VM,ANY]
    R=n_seq*cap
    scratch=[pltpu.VMEM((3,width,ff),BF),pltpu.VMEM((2,sps,2,seq,width),BF),pltpu.VMEM((R,width),BF),pltpu.VMEM((R,width),BF),
      pltpu.VMEM((R,ff),BF),pltpu.VMEM((R,ff),BF),pltpu.VMEM((R,ff),BF),pltpu.VMEM((sps,2,seq,width),BF),
      pltpu.SemaphoreType.DMA((n_dp,3)),pltpu.SemaphoreType.DMA((2,sps,2)),pltpu.SemaphoreType.DMA((sps,2)),pltpu.SemaphoreType.DMA((sps,2))]
    fl=2*R*width*ff*9+2*4*n_seq*cap*seq*width
    return pl.pallas_call(functools.partial(expert_kernel,first,n_seq,sps),out_shape=out_shape,in_specs=in_specs,out_specs=out_specs,
      scratch_shapes=scratch,compiler_params=pltpu.CompilerParams(vmem_limit_bytes=62*1024*1024),
      cost_estimate=pl.CostEstimate(flops=fl,bytes_accessed=60_000_000,transcendentals=R*ff),name="routed_expert")(*args)


def permute(values, pairs):
    return lax.ppermute(values, "expert", pairs)


def pairs_of(mask, count):
    return [(i, i ^ mask) for i in range(count)]


def mixed_pairs(even_mask, odd_mask, count):
    return [(i, i ^ (odd_mask if i % 2 else even_mask)) for i in range(count)]


def after(values, *others):
    return lax.optimization_barrier((values, others))[0]


def ring_pairs():
    count = lax.axis_size("dp")
    return [(i, (i + 1) % count) for i in range(count)]


def gather_ring(own):
    count = lax.axis_size("dp")
    here = lax.axis_index("dp")
    whole = jnp.zeros((count,) + own.shape, own.dtype)
    origin = (0,) * own.ndim
    for step in range(count):
        whole = lax.dynamic_update_slice(whole, own[None], (lax.rem(here - step + count, count),) + origin)
        if step < count - 1:
            own = lax.ppermute(own, "dp", ring_pairs())
    return whole


def scatter_ring(terms):
    count = lax.axis_size("dp")
    here = lax.axis_index("dp")
    take = lambda step: lax.dynamic_index_in_dim(terms, lax.rem(here - step + count, count), axis=0, keepdims=False)
    held = take(1)
    for step in range(1, count):
        arrived = lax.ppermute(held, "dp", ring_pairs())
        total = arrived.astype(F32) + take(step + 1 if step < count - 1 else 0).astype(F32)
        held = total.astype(terms.dtype)
    return total


def total_of(values):
    for axis in ("expert", "dp"):
        step = 1
        while step < lax.axis_size(axis):
            values = values + lax.ppermute(values, axis, [(i, i ^ step) for i in range(lax.axis_size(axis))])
            step *= 2
    return values


def gather_chips(own, is_core0):
    count = lax.axis_size("expert")
    from_x = permute(own, pairs_of(2, count))
    from_y = permute(own, pairs_of(4, count))
    onward = jnp.where(is_core0, from_x, from_y)
    from_far = permute(onward, mixed_pairs(4, 2, count))
    return [own, from_x, from_y, from_far]


def gather_plane(own, is_core0):
    count = lax.axis_size("expert")
    found = []
    for piece in gather_chips(own, is_core0):
        found += [piece, permute(piece, pairs_of(1, count))]
    return found


def reduce_plane(even, odd, is_core0):
    count = lax.axis_size("expert")
    kind = even.dtype
    other = permute(odd, pairs_of(1, count))
    both = even.astype(F32) + other.astype(F32)
    far = permute(both[3].astype(kind), mixed_pairs(4, 2, count)).astype(F32)
    to_x = (both[1] + jnp.where(is_core0, far, 0.0)).astype(kind)
    to_y = (both[2] + jnp.where(is_core0, 0.0, far)).astype(kind)
    return both[0] + permute(to_x, pairs_of(2, count)).astype(F32) + permute(to_y, pairs_of(4, count)).astype(F32)


def place_rows(pieces, me):
    parts, rows, width = pieces[0].shape
    whole = jnp.zeros((parts, len(pieces), rows, width), pieces[0].dtype)
    for r, piece in enumerate(pieces):
        whole = lax.dynamic_update_slice(whole, piece[:, None], (0, me ^ r, 0, 0))
    return whole.reshape(parts * len(pieces) * rows, width)


def scatter_rows(whole, me, is_core0, kind):
    parts, count = lax.axis_size("dp"), lax.axis_size("expert")
    rows = whole.shape[0] // (parts * count)
    cut = whole.reshape(parts, count, rows, whole.shape[1])
    take = lambda r: lax.dynamic_index_in_dim(cut, me ^ r, axis=1, keepdims=False).astype(kind)
    even = jnp.stack([take(r) for r in range(0, count, 2)])
    odd = jnp.stack([take(r) for r in range(1, count, 2)])
    return scatter_ring(reduce_plane(even, odd, is_core0).astype(kind))


def scatter_dp(values):
    return lax.psum_scatter(values, "dp", scatter_dimension=0, tiled=False).astype(F32)


def local(
    tokens,
    cotangent,
    lengths,
    choices,
    attn_weight,
    attn_moment,
    attn_average,
    router_weight,
    router_moment,
    router_average,
    shared_weight,
    shared_moment,
    shared_average,
    routed_weight,
    routed_moment,
    routed_average,
    norm_gains,
    gain_moment,
    gain_average,
):
    seq_len, model_width = tokens.shape
    topk_count = choices.shape[1]
    head_dim = model_width // HEADS
    groups = lax.axis_size("expert")
    routed_count = routed_weight.shape[0] * groups
    capacity = (seq_len * topk_count * 8 // (7 * routed_count) + 7) // 8 * 8
    total_tokens = seq_len * groups * lax.axis_size("dp")
    step_root = 1.0 / math.sqrt(total_tokens)
    score_scale = 1.0 / math.sqrt(head_dim)
    block_rows = min(seq_len, block_limit)
    block_count = seq_len // block_rows
    me = lax.axis_index("expert")
    is_core0 = lax.rem(me, 2) == 0
    relative = me ^ jnp.arange(groups, dtype=jnp.int32)
    per_device = routed_weight.shape[0]
    positions = jnp.arange(seq_len, dtype=jnp.int32)
    length_here = lengths[0]
    valid_rows = (positions < length_here).astype(F32)[:, None]
    grad_out = cotangent.astype(F32) * valid_rows
    grad_out16 = grad_out.astype(BF)

    routed16 = [lax.all_gather(routed_weight[e].astype(BF), "dp", axis=0, tiled=False) for e in range(per_device)]
    small = jnp.pad(jnp.concatenate([router_weight, norm_gains.T], axis=1).astype(BF), ((0, 0), (0, 110)))
    small_cut = gather_ring(small)
    small_all = place_rows(gather_plane(small_cut, is_core0), me)
    small_all = small_all.T
    router16t = small_all[:routed_count]
    gains16 = small_all[routed_count : routed_count + 2]
    attn16 = []
    pieces = gather_plane(gather_ring(attn_weight[:2].astype(BF)), is_core0)
    attn16 += [place_rows([p[:, j] for p in pieces], me) for j in range(2)]
    pieces = gather_plane(gather_ring(attn_weight[2:].astype(BF)), is_core0)
    attn16 += [place_rows([p[:, j] for p in pieces], me) for j in range(2)]

    choice_rows = jnp.pad(choices.T.astype(BF), ((0, 16 - topk_count), (0, model_width - seq_len)))
    marked = jnp.concatenate([grad_out16, choice_rows], axis=0)
    grads_all = gather_plane(after(marked, pieces[6]), is_core0)
    pieces = gather_plane(gather_ring(shared_weight.astype(BF)), is_core0)
    shared16 = [place_rows([p[:, j] for p in pieces], me) for j in range(3)]

    choice_all = jnp.stack([g[seq_len : seq_len + topk_count, :seq_len] for g in grads_all]).astype(jnp.int32)
    own_experts = me * per_device + jnp.arange(per_device, dtype=jnp.int32)
    hits = jnp.any(choice_all[:, None] == own_experts[None, :, None, None], axis=2)
    before = (positions[:, None] < positions[None, :]).astype(BF)
    ranks = jnp.einsum("set,tu->seu", hits.astype(BF), before, preferred_element_type=F32).astype(jnp.int32)
    slot_all = jnp.where(hits, ranks, -1)
    choice_all = jnp.transpose(choice_all, (0, 2, 1))
    gain_first = gains16[0].astype(F32)
    gain_second = gains16[1].astype(F32)
    key_positions = positions[None, :]
    residual_in = tokens.astype(F32)
    normed_first, hat_first, inverse_first = norm_forward(residual_in, gain_first)
    first16 = normed_first.astype(BF)
    query_linear = jnp.dot(first16, attn16[0], preferred_element_type=F32)
    key_linear = jnp.dot(first16, attn16[1], preferred_element_type=F32)
    value_linear = jnp.dot(first16, attn16[2], preferred_element_type=F32)
    query16 = rotate(query_linear.reshape(seq_len, HEADS, head_dim), positions, 1.0).astype(
        BF
    )
    key16 = rotate(key_linear.reshape(seq_len, HEADS, head_dim), positions, 1.0).astype(
        BF
    )
    value16 = value_linear.reshape(seq_len, HEADS, head_dim).astype(BF)

    def block_scores(start_row):
        scores = (
            jnp.einsum("qhd,khd->hqk", query16, key16, preferred_element_type=F32)
            * score_scale
        )
        query_positions = start_row + jnp.arange(block_rows, dtype=jnp.int32)[:, None]
        allowed = (key_positions <= query_positions) & (key_positions < length_here)
        return (query16, jnp.where(allowed[None], scores, masked_score))

    def forward_block(block_index):
        query_block, masked = block_scores(block_index * block_rows)
        row_peak = jnp.max(masked, axis=-1, keepdims=True)
        exp_part = jnp.exp(masked - row_peak)
        row_total = jnp.sum(exp_part, axis=-1, keepdims=True)
        probs16 = (exp_part / row_total).astype(BF)
        context = jnp.einsum("hqk,khd->qhd", probs16, value16, preferred_element_type=F32)
        return (context.astype(BF), (row_peak + jnp.log(row_total))[..., 0])

    contexts, log_totals = lax.map(forward_block, jnp.arange(block_count))
    context16 = contexts.reshape(seq_len, model_width)
    attn_out = jnp.dot(context16, attn16[3], preferred_element_type=F32)
    hidden_state = residual_in + attn_out
    normed_second, hat_second, inverse_second = norm_forward(hidden_state, gain_second)
    second16 = normed_second.astype(BF)
    seconds_all = gather_plane(second16, is_core0)
    router_pad = jnp.pad(router16t, ((0, 128 - routed_count), (0, 0)))
    partial = None
    gate_grads, routed_grads = [], []
    for e in range(per_device):
        ids = jnp.stack([own_experts[e], own_experts[e]])
        *partial, gate_part, weight_part = expert_call(
            ids, choice_all, slot_all[:, e], router_pad, routed16[e], seconds_all, grads_all, partial, capacity
        )
        gate_grads.append(gate_part[:, 0])
        routed_grads.append(scatter_dp(weight_part))
    routed_sum = reduce_plane(partial[0], partial[1], is_core0)
    routed_back = reduce_plane(partial[2], partial[3], is_core0)
    gate_sent = jnp.take(jnp.stack(gate_grads, axis=1), relative, axis=0)
    gate_back = lax.all_to_all(gate_sent, "expert", split_axis=0, concat_axis=0, tiled=True)
    grad_gate = gate_back.reshape(routed_count, seq_len).T

    logits = lax.dot_general(second16, router16t, (((1,), (1,)), ((), ())), preferred_element_type=F32)
    table = jnp.any(choices[:, :, None] == jnp.arange(routed_count, dtype=jnp.int32)[None, None, :], axis=1)
    chosen = jnp.where(table, logits, masked_score)
    chosen_exp = jnp.where(table, jnp.exp(chosen - jnp.max(chosen, axis=1, keepdims=True)), 0.0)
    gate_weights = chosen_exp / jnp.sum(chosen_exp, axis=1, keepdims=True)
    shared_gate = jnp.dot(second16, shared16[0], preferred_element_type=F32)
    shared_up = jnp.dot(second16, shared16[1], preferred_element_type=F32)
    shared_hidden = (jax.nn.silu(shared_gate) * shared_up).astype(BF)
    shared_out = jnp.einsum(
        "lf,df->ld", shared_hidden, shared16[2], preferred_element_type=F32
    )
    block_value = hidden_state + shared_out + routed_sum
    grad_shared_hidden = jnp.dot(grad_out16, shared16[2], preferred_element_type=F32)
    grad_shared_gate16 = (grad_shared_hidden * shared_up * silu_slope(shared_gate)).astype(
        BF
    )
    grad_shared_up16 = (grad_shared_hidden * jax.nn.silu(shared_gate)).astype(BF)
    shared_grads = (
        [
            jnp.einsum(
                "ld,lf->df", second16, grad_shared_gate16, preferred_element_type=F32
            ),
            jnp.einsum("ld,lf->df", second16, grad_shared_up16, preferred_element_type=F32),
            jnp.einsum("ld,lf->df", grad_out16, shared_hidden, preferred_element_type=F32),
        ]
    )
    grad_second = jnp.einsum(
        "lf,df->ld", grad_shared_gate16, shared16[0], preferred_element_type=F32
    )
    grad_second = grad_second + jnp.einsum(
        "lf,df->ld", grad_shared_up16, shared16[1], preferred_element_type=F32
    )
    routed_back, early = lax.optimization_barrier((routed_back, routed_grads[0]))
    routed_grad_shard = jnp.stack([early] + routed_grads[1:])
    grad_second = grad_second + routed_back
    gate_mean = jnp.sum(gate_weights * grad_gate, axis=1, keepdims=True)
    grad_logits = gate_weights * (grad_gate - gate_mean)
    router_float = router16t.astype(F32)
    grad_second = grad_second + jnp.dot(grad_logits, router_float, precision=lax.Precision.HIGHEST)
    router_grad_full = lax.dot_general(
        grad_logits, second16.astype(F32), (((0,), (0,)), ((), ())), precision=lax.Precision.HIGHEST
    )
    grad_norm_second, grad_gain_second = norm_backward(
        grad_second, hat_second, inverse_second, gain_second
    )
    grad_hidden_state = grad_out + grad_norm_second
    grad_attn16 = grad_hidden_state.astype(BF)
    grad_out_proj = jnp.einsum(
        "ld,le->de", context16, grad_attn16, preferred_element_type=F32
    )
    grad_context16 = (
        jnp.einsum("le,de->ld", grad_attn16, attn16[3], preferred_element_type=F32)
        .astype(BF)
        .reshape(seq_len, HEADS, head_dim)
    )

    def backward_block(carried, inputs):
        grad_keys, grad_values = carried
        block_index, log_block = inputs
        start_row = block_index * block_rows
        query_block, masked = block_scores(start_row)
        probability = jnp.exp(masked - log_block[..., None])
        grad_probs = jnp.einsum(
            "qhd,khd->hqk", grad_context16, value16, preferred_element_type=F32
        )
        row_delta = jnp.sum(probability * grad_probs, axis=-1, keepdims=True)
        grad_scores16 = (probability * (grad_probs - row_delta)).astype(BF)
        grad_query = (
            jnp.einsum("hqk,khd->qhd", grad_scores16, key16, preferred_element_type=F32)
            * score_scale
        )
        grad_keys = (
            grad_keys
            + jnp.einsum(
                "hqk,qhd->khd", grad_scores16, query_block, preferred_element_type=F32
            )
            * score_scale
        )
        grad_values = grad_values + jnp.einsum(
            "hqk,qhd->khd",
            probability.astype(BF),
            grad_context16,
            preferred_element_type=F32,
        )
        return ((grad_keys, grad_values), grad_query)

    zero_heads = jnp.zeros((seq_len, HEADS, head_dim), F32)
    (grad_keys, grad_values), grad_queries = lax.scan(
        backward_block, (zero_heads, zero_heads), (jnp.arange(block_count), log_totals)
    )
    grad_query16 = (
        rotate(grad_queries.reshape(seq_len, HEADS, head_dim), positions, -1.0)
        .reshape(seq_len, model_width)
        .astype(BF)
    )
    grad_key16 = (
        rotate(grad_keys, positions, -1.0).reshape(seq_len, model_width).astype(BF)
    )
    grad_value16 = grad_values.reshape(seq_len, model_width).astype(BF)
    attn_grads = (
        [
            jnp.einsum("ld,le->de", first16, grad_query16, preferred_element_type=F32),
            jnp.einsum("ld,le->de", first16, grad_key16, preferred_element_type=F32),
            jnp.einsum("ld,le->de", first16, grad_value16, preferred_element_type=F32),
            grad_out_proj,
        ]
    )
    grad_first = jnp.einsum(
        "le,de->ld", grad_query16, attn16[0], preferred_element_type=F32
    )
    grad_first = grad_first + jnp.einsum(
        "le,de->ld", grad_key16, attn16[1], preferred_element_type=F32
    )
    grad_first = grad_first + jnp.einsum(
        "le,de->ld", grad_value16, attn16[2], preferred_element_type=F32
    )
    grad_norm_first, grad_gain_first = norm_backward(
        grad_first, hat_first, inverse_first, gain_first
    )
    input_grad = grad_hidden_state + grad_norm_first
    scalars = jnp.stack(
        [
            jnp.sum(valid_rows * block_value * block_value),
            jnp.sum(valid_rows * input_grad * input_grad),
            length_here.astype(F32),
        ]
    )
    row_sums = total_of(scalars)
    small_grads = jnp.concatenate([router_grad_full, grad_gain_first[None], grad_gain_second[None]])
    small_grads = jnp.pad(small_grads, ((0, 128 - small_grads.shape[0]), (0, 0))).T
    small_grad = scatter_rows(small_grads, me, is_core0, F32)
    router_grad = small_grad[:, :routed_count]
    gain_grad = small_grad[:, routed_count : routed_count + 2].T
    shared_grad = jnp.stack([scatter_rows(g, me, is_core0, BF) for g in shared_grads])
    attn_grad = jnp.stack([scatter_rows(g, me, is_core0, BF) for g in attn_grads])
    denominator = model_width * row_sums[2]
    masked_rms = jnp.stack(
        [jnp.sqrt(row_sums[0] / denominator), jnp.sqrt(row_sums[1] / denominator)]
    )
    attn_parts = update(
        attn_weight, attn_moment, attn_average, attn_grad, rate_attention * step_root
    )
    router_parts = update(
        router_weight, router_moment, router_average, router_grad, rate_router * step_root
    )
    shared_parts = update(
        shared_weight, shared_moment, shared_average, shared_grad, rate_shared * step_root
    )
    routed_parts = update(
        routed_weight, routed_moment, routed_average, routed_grad_shard, rate_routed * step_root
    )
    gain_parts = update(norm_gains, gain_moment, gain_average, gain_grad, rate_gains * step_root)
    return (
        block_value.astype(BF),
        input_grad,
        masked_rms,
        attn_parts[0],
        attn_parts[1],
        attn_parts[2],
        attn_parts[3],
        attn_parts[4],
        router_parts[0],
        router_parts[1],
        router_parts[2],
        router_parts[3],
        router_parts[4],
        shared_parts[0],
        shared_parts[1],
        shared_parts[2],
        shared_parts[3],
        shared_parts[4],
        routed_parts[0],
        routed_parts[1],
        routed_parts[2],
        routed_parts[3],
        routed_parts[4],
        gain_parts[0],
        gain_parts[1],
        gain_parts[2],
        gain_parts[3],
    )


def solution(mesh):
    placed = (
        P(("dp", "expert"), None),
        P(("dp", "expert"), None),
        P(("dp", "expert")),
        P(("dp", "expert"), None),
        P(None, ("dp", "expert"), None),
        P(None, ("dp", "expert"), None),
        P(None, ("dp", "expert"), None),
        P(("dp", "expert"), None),
        P(("dp", "expert"), None),
        P(("dp", "expert"), None),
        P(None, ("dp", "expert"), None),
        P(None, ("dp", "expert"), None),
        P(None, ("dp", "expert"), None),
        P("expert", None, "dp", None),
        P("expert", None, "dp", None),
        P("expert", None, "dp", None),
        P(None, ("dp", "expert")),
        P(None, ("dp", "expert")),
        P(None, ("dp", "expert")),
    )
    return jax.shard_map(
        local,
        mesh=mesh,
        in_specs=placed,
        out_specs=(
            P(("dp", "expert"), None),
            P(("dp", "expert"), None),
            P(),
            P(None, ("dp", "expert"), None),
            P(None, ("dp", "expert"), None),
            P(None, ("dp", "expert"), None),
            P(None, ("dp", "expert"), None),
            P(None, ("dp", "expert"), None),
            P(("dp", "expert"), None),
            P(("dp", "expert"), None),
            P(("dp", "expert"), None),
            P(("dp", "expert"), None),
            P(("dp", "expert"), None),
            P(None, ("dp", "expert"), None),
            P(None, ("dp", "expert"), None),
            P(None, ("dp", "expert"), None),
            P(None, ("dp", "expert"), None),
            P(None, ("dp", "expert"), None),
            P("expert", None, "dp", None),
            P("expert", None, "dp", None),
            P("expert", None, "dp", None),
            P("expert", None, "dp", None),
            P("expert", None, "dp", None),
            P(None, ("dp", "expert")),
            P(None, ("dp", "expert")),
            P(None, ("dp", "expert")),
            P(None, ("dp", "expert")),
        ),
        check_vma=False,
    )
```

time: 1630 us -> 923 us (0.57)
  blocking collectives: 381 us -> 0 us
  local copies, waits for them, and re-layouts: 374 us -> 110 us
  waiting for transfers between devices: 403 us -> 212 us
  Pallas kernels: 0 us -> 184 us
  matrix products: 264 us -> 96.9 us
  starting transfers between devices: 16.3 us -> 170 us
  other arithmetic: 158 us -> 120 us
    ppermute x0 -> x123, waiting for transfers between devices: none -> 212 us  [the longest x82 142 us: permute(): return lax.ppermute(values, 'expert', pairs)]
    all_to_all x3 -> x1, waiting for transfers between devices: 210 us -> 0.01 us  [local(): lax.all_to_all(gate_sent, 'expert', split_axis=0, concat_axis=0, tiled=True)]
    pallas_call x0 -> x2, Pallas kernels: none -> 184 us  [expert_call(): pl.pallas_call(functools.partial(expert_kernel, first, n_seq, sps), out_s...]
    all_to_all x1 -> x0, blocking collectives: 178 us -> none  [local(): lax.all_to_all(send_grads, 'expert', split_axis=0, concat_axis=1, tiled=T...]
    ppermute x0 -> x123, starting transfers between devices: none -> 167 us  [the longest x82 78.2 us: permute(): return lax.ppermute(values, 'expert', pairs)]
    dot_general x31 -> x23, matrix products: 227 us -> 63.2 us  [the longest x1 6 us: local(): key_linear = jnp.dot(first16, attn16[1], preferred_element_type=F32)]
    all_gather x2 -> x0, blocking collectives: 162 us -> none  [the longest x1 118 us: local(): lax.all_gather(router_weight.astype(jnp.bfloat16), ('dp', 'expert'), axis...]
    reduce_scatter x5 -> x2, waiting for transfers between devices: 131 us -> 0.01 us  [scatter_dp(): lax.psum_scatter(values, 'dp', scatter_dimension=0, tiled=False).astype(F32)]
  transfers between devices with their start and end apart: 12 -> 128, of which waited for: 5 -> 58; matrix products, arithmetic and copies ran while one was open for 45% -> 33% of each run, Pallas kernels for 0% -> 20%
where the time goes in v1:
time: 923 us; the launch traced here: 913 us
  waiting for transfers between devices  212 us (23%)
  Pallas kernels  184 us (20%)
  starting transfers between devices  170 us (18%)
  other arithmetic  120 us (13%)
  local copies, waits for them, and re-layouts  110 us (12%)
  matrix products  96.9 us (10%)
  between operations  19.4 us (2%)
    pallas_call x2, Pallas kernels, expert_call(): pl.pallas_call(functools.partial(expert_kernel, first, n_seq, sps), out_s...  184 us
    ppermute x82, waiting for transfers between devices, permute(): return lax.ppermute(values, 'expert', pairs)  142 us
    ppermute x82, starting transfers between devices, permute(): return lax.ppermute(values, 'expert', pairs)  78.2 us
    ppermute x12, starting transfers between devices, gather_ring(): own = lax.ppermute(own, 'dp', ring_pairs())  45 us
    ppermute x24, waiting for transfers between devices, scatter_ring(): arrived = lax.ppermute(held, 'dp', ring_pairs())  41.6 us
    ppermute x24, starting transfers between devices, scatter_ring(): arrived = lax.ppermute(held, 'dp', ring_pairs())  39.3 us
    dynamic_update_slice x36, local copies, waits for them, and re-layouts, place_rows(): whole = lax.dynamic_update_slice(whole, piece[:, None], (0, me ^ r, 0, 0))  27.6 us
    add x10, other arithmetic, reduce_plane(): both = even.astype(F32) + other.astype(F32)  23.1 us
  transfers between devices with their start and end apart: 128, of which 58 were waited for; matrix products, arithmetic and copies ran while one was open for 33% of the time, Pallas kernels for 20%

profile of v1, /device:TPU:0, one launch (start us, length us, event | category | flops | bytes accessed | tf_op | source)
XLA Modules:
  0.0 912.6 jit_solution(17357786457702094285)
XLA Ops:
  7.2 3.4 convert.97
  39.3 4.9 collective-permute-done.1
  44.3 5.7 collective-permute-start.2
  64.7 5.8 collective-permute-start.21
  77.1 3.6 collective-permute-done.21
  80.7 4.4 collective-permute-start.22
  85.8 3.6 collective-permute-done.11
  89.4 9.0 collective-permute-start.12
  99.2 9.6 %collective-permute-start.32 = (bf16[3,40,896]{2,1,0:T(8,128)(2,1)S(1)}, bf16[3,40,896]{2,1,0:T(8,128)(2,1)S(1)}, u32[]{:S(2)}, u32[]{:S(2)}) collective-permute-start(bf16[3,40,896]{2,1,0:T(8,128)(2,1)S(1)} %collective-permute-done.31), channel_id=1, source_target_pairs={{0,8},{8,16},{16,24},{24,0},{1,9},{9,17},{17,25},{25,1},{2,10},{10... | collective-permute-start | bytes 645128 | tf_op jit(solution)/shard_map/ppermute | solution.py:250
  124.5 3.5 collective-permute-done.32
  136.4 12.2 %collective-permute-done.14 = bf16[4,2,40,1280]{3,2,1,0:T(8,128)(2,1)S(1)} collective-permute-done((bf16[4,2,40,1280]{3,2,1,0:T(8,128)(2,1)}, bf16[4,2,40,1280]{3,2,1,0:T(8,128)(2,1)S(1)}, u32[]{:S(2)}, u32[]{:S(2)}) %collective-permute-start.14) | collective-permute-done | bytes 819232 | tf_op jit(solution)/shard_map/ppermute | solution.py:222
  157.4 13.8 %collective-permute-done.34 = bf16[4,3,40,896]{3,2,1,0:T(8,128)(2,1)S(1)} collective-permute-done((bf16[4,3,40,896]{3,2,1,0:T(8,128)(2,1)S(1)}, bf16[4,3,40,896]{3,2,1,0:T(8,128)(2,1)S(1)}, u32[]{:S(2)}, u32[]{:S(2)}) %collective-permute-start.34) | collective-permute-done | bytes 860192 | tf_op jit(solution)/shard_map/ppermute | solution.py:222
  172.9 8.7 collective-permute-done.18
  204.1 5.8 copy.566
  209.9 5.7 copy.565
  215.6 6.0 fusion.46
  221.6 3.5 fusion.48
  227.1 5.9 copy.564
  233.0 4.4 convolution_convert_fusion.1
  258.3 3.3 fusion.243
  264.7 3.8 multiply_convert_fusion.3
  275.3 4.8 fusion.245
  288.3 13.6 %collective-permute-done.45.refs_19_ = bf16[528,1280]{1,0:T(8,128)(2,1)S(1)} collective-permute-done((bf16[528,1280]{1,0:T(8,128)(2,1)S(1)}, bf16[528,1280]{1,0:T(8,128)(2,1)S(1)}, u32[]{:S(2)}, u32[]{:S(2)}) %collective-permute-start.45) | collective-permute-done | bytes 1351712 | tf_op jit(solution)/shard_map/ppermute | solution.py:222
  306.1 9.8 %collective-permute-done.52.refs_11_ = bf16[512,1280]{1,0:T(8,128)(2,1)} collective-permute-done((bf16[512,1280]{1,0:T(8,128)(2,1)S(1)}, bf16[512,1280]{1,0:T(8,128)(2,1)}, u32[]{:S(2)}, u32[]{:S(2)}) %collective-permute-start.52) | collective-permute-done | bytes 1310752 | tf_op jit(solution)/shard_map/ppermute | solution.py:222
  320.6 91.7 %routed_expert.2 = (bf16[4,512,1280]{2,1,0:T(8,128)(2,1)}, bf16[4,512,1280]{2,1,0:T(8,128)(2,1)}, bf16[4,512,1280]{2,1,0:T(8,128)(2,1)}, bf16[4,512,1280]{2,1,0:...) custom-call(s32[2]{0:T(128)} %pad_add_fusion.1.refs_0_, s32[8,512,7]{2,1,0:T(8,128)} %copy.573.refs_1_, ...), custom_call_target="tpu_custom_call" | custom-call | flops 53016002560 | bytes 60000000 | tf_op jit(solution)/shard_map/routed_expert/pallas_call | solution.py:216
  412.4 92.4 %routed_expert.3 = (bf16[4,512,1280]{2,1,0:T(8,128)(2,1)}, bf16[4,512,1280]{2,1,0:T(8,128)(2,1)}, bf16[4,512,1280]{2,1,0:T(8,128)(2,1)}, bf16[4,512,1280]{2,1,0:...) custom-call(s32[2]{0:T(128)} %pad_add_fusion.refs_0_, s32[8,512,7]{2,1,0:T(8,128)} %copy.573.refs_1_, ...), custom_call_target="tpu_custom_call" | custom-call | flops 53016002560 | bytes 60000000 | tf_op jit(solution)/shard_map/routed_expert/pallas_call | solution.py:216
  514.7 4.0 collective-permute-done.117
  526.1 24.0 %collective-permute-start.106 = (bf16[40,896]{1,0:T(8,128)(2,1)S(1)}, bf16[40,896]{1,0:T(8,128)(2,1)S(1)}, u32[]{:S(2)}, u32[]{:S(2)}) collective-permute-start(bf16[40,896]{1,0:T(8,128)(2,1)S(1)} %dynamic-slice_bitcast_fusion.14), channel_id=1, source_target_pairs={{0,8},{8,16},{16,24},{24,0},{1,9},{9,17},{17,25},{25,1},{2,10},{10... | collective-permute-start | bytes 215048 | tf_op jit(solution)/shard_map/ppermute | solution.py:260
  553.1 3.2 collective-permute-start.113
  559.0 3.2 collective-permute-start.107
  573.2 3.2 collective-permute-done.115
  583.1 3.3 all-to-all-start
  586.6 5.2 convert_add_fusion
  595.7 5.2 convert_add_fusion.1
  604.1 5.6 collective-permute-done.59
  609.7 4.5 fusion.19
  621.0 8.6 collective-permute-done.55
  629.6 4.9 fusion.15
  634.6 3.5 collective-permute-start.56
  639.3 7.0 collective-permute-done.60
  646.3 11.5 %collective-permute-done.61 = bf16[512,1280]{1,0:T(8,128)(2,1)} collective-permute-done((bf16[512,1280]{1,0:T(8,128)(2,1)S(1)}, bf16[512,1280]{1,0:T(8,128)(2,1)}, u32[]{:S(2)}, u32[]{:S(2)}) %collective-permute-start.61) | collective-permute-done | bytes 1310752 | tf_op jit(solution)/shard_map/ppermute | solution.py:222
  657.7 4.3 fusion.32
  662.0 3.6 bitcast_convert_fusion
  665.7 4.2 fusion.10
  680.6 10.7 %multiply_reduce_fusion = (f32[10,512]{1,0:T(8,128)S(1)}, f32[10,512,512]{1,2,0:T(8,128)}) fusion(f32[10,512,512]{1,2,0:T(8,128)} %copy-done, f32[10,512]{1,0:T(8,128)S(1)} %copy-done.88, bf16[512,10,128]{2,0,1:T(8,128)(2,1)} %copy-done.67, bf16[512,10,128]{0,2,1:T(8,128)(2,1)} %bitcast.773), kind=kOutput, calls=%fused_computation.2 | convolution fusion | flops 678947840 | bytes 23633920 | tf_op jit(solution)/shard_map/while/body/eval_jaxpr/qhd,khd->hqk/dot_general | solution.py:513
  691.3 6.7 multiply_convert_fusion
  703.1 3.9 fusion.246
  711.0 4.0 fusion.12
  723.4 3.6 fusion.248
  740.6 7.6 fusion.29
  750.2 3.6 fusion.44
  753.8 3.6 convert_element_type.1717
  757.4 11.1 %fusion.231 = (bf16[2,3,320,896]{3,2,1,0:T(8,128)(2,1)}, f32[2,3,320,896]{3,2,1,0:T(8,128)S(1)}, f32[2,3,320,896]{3,2,1,0:T(8,128)}, f32[2,3,320,896]{3,2,1,0:T(8,128)}) fusion(f32[2,3,320,896]{3,2,1,0:T(8,128)} %param.32, f32[2,3,320,896]{3,2,1,0:T(8,128)} %param.33, f32[1,3,320,896]{3,2,1,0:T(8,128)} %convert_element_type.1717, ...), kind=kLoop, calls=%fused_computation.604 | loop fusion | flops 17203200 | bytes 44728320 | tf_op jit(solution)/shard_map/convert_element_type | solution.py:71
  768.5 9.4 %multiply_add_fusion = f32[2,3,320,896]{3,2,1,0:T(8,128)} fusion(f32[2,3,320,896]{3,2,1,0:T(8,128)} %param.34, f32[2,3,320,896]{3,2,1,0:T(8,128)S(1)} %get-tuple-element.208), kind=kLoop, calls=%fused_computation.12 | loop fusion | flops 5160960 | bytes 20643840 | tf_op jit(solution)/shard_map/add | solution.py:70
  799.1 3.5 collective-permute-done.65
  803.4 3.7 collective-permute-done.66
  810.0 3.6 collective-permute-done.100
  814.3 5.4 collective-permute-done.101
  839.5 5.4 collective-permute-done.82
  845.8 7.8 collective-permute-done.89
  861.3 5.1 collective-permute-done.77
  866.6 8.5 collective-permute-done.84
  875.4 4.5 collective-permute-done.91
  881.8 3.5 collective-permute-start.86
  (764 shorter events, 329.9 us)
Async XLA Ops:
  7.2 313.4 %all-gather.5.cloned.1.call-start = ((), (), s32[]{:S(2)}) async-start(), calls=%async_computation.4 | async-start | bytes 8601600 | tf_op jit(solution)/shard_map/all_gather | solution.py:367
  12.9 399.5 %all-gather.3.cloned.1.call-start = ((), (), s32[]{:S(2)}) async-start(), calls=%async_computation.3 | async-start | bytes 8601600 | tf_op jit(solution)/shard_map/all_gather | solution.py:367
  13.8 51.0 %collective-permute-start.20 = (bf16[2,40,1280]{2,1,0:T(8,128)(2,1)}, bf16[2,40,1280]{2,1,0:T(8,128)(2,1)}, u32[]{:S(2)}, u32[]{:S(2)}) collective-permute-start(bf16[2,40,1280]{2,1,0:T(8,128)(2,1)} %get-tuple-element.374), channel_id=1, source_target_pairs={{0,8},{8,16},{16,24},{24,0},{1,9},{9,17},{17,25},{25,1},{2,10},{10... | collective-permute-start | bytes 614408 | tf_op jit(solution)/shard_map/ppermute | solution.py:250
  17.4 19.3 %collective-permute-start = (bf16[40,128]{0,1:T(8,128)(2,1)}, bf16[40,128]{0,1:T(8,128)(2,1)}, u32[]{:S(2)}, u32[]{:S(2)}) collective-permute-start(bf16[40,128]{0,1:T(8,128)(2,1)} %get-tuple-element.388), channel_id=1, source_target_pairs={{0,8},{8,16},{16,24},{24,0},{1,9},{9,17},{17,25},{25,1},{2,10},{10... | collective-permute-start | bytes 30728 | tf_op jit(solution)/shard_map/ppermute | solution.py:250
  19.0 53.2 %collective-permute-start.10 = (bf16[2,40,1280]{2,1,0:T(8,128)(2,1)}, bf16[2,40,1280]{2,1,0:T(8,128)(2,1)}, u32[]{:S(2)}, u32[]{:S(2)}) collective-permute-start(bf16[2,40,1280]{2,1,0:T(8,128)(2,1)} %get-tuple-element.375), channel_id=1, source_target_pairs={{0,8},{8,16},{16,24},{24,0},{1,9},{9,17},{17,25},{25,1},{2,10},{10... | collective-permute-start | bytes 614408 | tf_op jit(solution)/shard_map/ppermute | solution.py:250
  21.4 55.0 %collective-permute-start.30 = (bf16[3,40,896]{2,1,0:T(8,128)(2,1)}, bf16[3,40,896]{2,1,0:T(8,128)(2,1)S(1)}, u32[]{:S(2)}, u32[]{:S(2)}) collective-permute-start(bf16[3,40,896]{2,1,0:T(8,128)(2,1)} %get-tuple-element.225), channel_id=1, source_target_pairs={{0,8},{8,16},{16,24},{24,0},{1,9},{9,17},{17,25},{25,1},{2,10},{10... | collective-permute-start | bytes 645128 | tf_op jit(solution)/shard_map/ppermute | solution.py:250
  21.4 640.6 %reduce-scatter.3.cloned.1.call-start = ((), (), s32[]{:S(2)}) async-start(), calls=%async_computation.5 | async-start | bytes 8601600 | tf_op jit(solution)/shard_map/reduce_scatter | solution.py:322
  76.3 22.8 %collective-permute-start.31 = (bf16[3,40,896]{2,1,0:T(8,128)(2,1)S(1)}, bf16[3,40,896]{2,1,0:T(8,128)(2,1)S(1)}, u32[]{:S(2)}, u32[]{:S(2)}) collective-permute-start(bf16[3,40,896]{2,1,0:T(8,128)(2,1)S(1)} %collective-permute-done.30), channel_id=1, source_target_pairs={{0,8},{8,16},{16,24},{24,0},{1,9},{9,17},{17,25},{25,1},{2,10},{10... | collective-permute-start | bytes 645128 | tf_op jit(solution)/shard_map/ppermute | solution.py:250
  80.7 28.8 %collective-permute-start.22 = (bf16[2,40,1280]{2,1,0:T(8,128)(2,1)S(1)}, bf16[2,40,1280]{2,1,0:T(8,128)(2,1)S(1)}, u32[]{:S(2)}, u32[]{:S(2)}) collective-permute-start(bf16[2,40,1280]{2,1,0:T(8,128)(2,1)S(1)} %collective-permute-done.21), channel_id=1, source_target_pairs={{0,8},{8,16},{16,24},{24,0},{1,9},{9,17},{17,25},{25,1},{2,10},{10... | collective-permute-start | bytes 614408 | tf_op jit(solution)/shard_map/ppermute | solution.py:250
  89.4 30.3 %collective-permute-start.12 = (bf16[2,40,1280]{2,1,0:T(8,128)(2,1)S(1)}, bf16[2,40,1280]{2,1,0:T(8,128)(2,1)S(1)}, u32[]{:S(2)}, u32[]{:S(2)}) collective-permute-start(bf16[2,40,1280]{2,1,0:T(8,128)(2,1)S(1)} %collective-permute-done.11), channel_id=1, source_target_pairs={{0,8},{8,16},{16,24},{24,0},{1,9},{9,17},{17,25},{25,1},{2,10},{10... | collective-permute-start | bytes 614408 | tf_op jit(solution)/shard_map/ppermute | solution.py:250
  99.2 28.8 %collective-permute-start.32 = (bf16[3,40,896]{2,1,0:T(8,128)(2,1)S(1)}, bf16[3,40,896]{2,1,0:T(8,128)(2,1)S(1)}, u32[]{:S(2)}, u32[]{:S(2)}) collective-permute-start(bf16[3,40,896]{2,1,0:T(8,128)(2,1)S(1)} %collective-permute-done.31), channel_id=1, source_target_pairs={{0,8},{8,16},{16,24},{24,0},{1,9},{9,17},{17,25},{25,1},{2,10},{10... | collective-permute-start | bytes 645128 | tf_op jit(solution)/shard_map/ppermute | solution.py:250
  110.2 39.0 %collective-permute-start.23 = (bf16[4,2,40,1280]{3,2,1,0:T(8,128)(2,1)}, bf16[4,2,40,1280]{3,2,1,0:T(8,128)(2,1)S(1)}, u32[]{:S(2)}, u32[]{:S(2)}) collective-permute-start(bf16[4,2,40,1280]{3,2,1,0:T(8,128)(2,1)} %bitcast_dynamic-update-slice_fusion.4), channel_id=1, source_target_pairs={{0,1},{1,0},{2,3},{3,2},{4,5},{5,4},{6,7},{7,6},{8,9},{9,8},{10,11... | collective-permute-start | bytes 2457608 | tf_op jit(solution)/shard_map/ppermute | solution.py:222
  110.2 41.3 %collective-permute-start.24 = (bf16[4,2,40,1280]{3,2,1,0:T(8,128)(2,1)}, bf16[4,2,40,1280]{3,2,1,0:T(8,128)(2,1)S(1)}, u32[]{:S(2)}, u32[]{:S(2)}) collective-permute-start(bf16[4,2,40,1280]{3,2,1,0:T(8,128)(2,1)} %bitcast_dynamic-update-slice_fusion.4), channel_id=1, source_target_pairs={{0,2},{1,3},{2,0},{3,1},{4,6},{5,7},{6,4},{7,5},{8,10},{9,11},{10,... | collective-permute-start | bytes 2457608 | tf_op jit(solution)/shard_map/ppermute | solution.py:222
  110.8 43.2 %collective-permute-start.26 = (bf16[4,2,40,1280]{3,2,1,0:T(8,128)(2,1)}, bf16[4,2,40,1280]{3,2,1,0:T(8,128)(2,1)S(1)}, u32[]{:S(2)}, u32[]{:S(2)}) collective-permute-start(bf16[4,2,40,1280]{3,2,1,0:T(8,128)(2,1)} %bitcast_dynamic-update-slice_fusion.4), channel_id=1, source_target_pairs={{0,4},{1,5},{2,6},{3,7},{4,0},{5,1},{6,2},{7,3},{8,12},{9,13},{10,... | collective-permute-start | bytes 2457608 | tf_op jit(solution)/shard_map/ppermute | solution.py:222
  120.4 28.2 %collective-permute-start.14 = (bf16[4,2,40,1280]{3,2,1,0:T(8,128)(2,1)}, bf16[4,2,40,1280]{3,2,1,0:T(8,128)(2,1)S(1)}, u32[]{:S(2)}, u32[]{:S(2)}) collective-permute-start(bf16[4,2,40,1280]{3,2,1,0:T(8,128)(2,1)} %bitcast_dynamic-update-slice_fusion.8), channel_id=1, source_target_pairs={{0,2},{1,3},{2,0},{3,1},{4,6},{5,7},{6,4},{7,5},{8,10},{9,11},{10,... | collective-permute-start | bytes 2457608 | tf_op jit(solution)/shard_map/ppermute | solution.py:222
  128.0 21.0 %collective-permute-start.16 = (bf16[4,2,40,1280]{3,2,1,0:T(8,128)(2,1)}, bf16[4,2,40,1280]{3,2,1,0:T(8,128)(2,1)S(1)}, u32[]{:S(2)}, u32[]{:S(2)}) collective-permute-start(bf16[4,2,40,1280]{3,2,1,0:T(8,128)(2,1)} %bitcast_dynamic-update-slice_fusion.8), channel_id=1, source_target_pairs={{0,4},{1,5},{2,6},{3,7},{4,0},{5,1},{6,2},{7,3},{8,12},{9,13},{10,... | collective-permute-start | bytes 2457608 | tf_op jit(solution)/shard_map/ppermute | solution.py:222
  149.2 22.0 %collective-permute-start.34 = (bf16[4,3,40,896]{3,2,1,0:T(8,128)(2,1)S(1)}, bf16[4,3,40,896]{3,2,1,0:T(8,128)(2,1)S(1)}, u32[]{:S(2)}, u32[]{:S(2)}) collective-permute-start(bf16[4,3,40,896]{3,2,1,0:T(8,128)(2,1)S(1)} %bitcast_dynamic-update-slice_fusion), channel_id=1, source_target_pairs={{0,2},{1,3},{2,0},{3,1},{4,6},{5,7},{6,4},{7,5},{8,10},{9,11},{10,... | collective-permute-start | bytes 2580488 | tf_op jit(solution)/shard_map/ppermute | solution.py:222
  151.5 21.2 %collective-permute-start.36 = (bf16[4,3,40,896]{3,2,1,0:T(8,128)(2,1)S(1)}, bf16[4,3,40,896]{3,2,1,0:T(8,128)(2,1)S(1)}, u32[]{:S(2)}, u32[]{:S(2)}) collective-permute-start(bf16[4,3,40,896]{3,2,1,0:T(8,128)(2,1)S(1)} %bitcast_dynamic-update-slice_fusion), channel_id=1, source_target_pairs={{0,4},{1,5},{2,6},{3,7},{4,0},{5,1},{6,2},{7,3},{8,12},{9,13},{10,... | collective-permute-start | bytes 2580488 | tf_op jit(solution)/shard_map/ppermute | solution.py:222
  154.0 27.6 %collective-permute-start.18 = (bf16[4,2,40,1280]{3,2,1,0:T(8,128)(2,1)S(1)}, bf16[4,2,40,1280]{3,2,1,0:T(8,128)(2,1)}, u32[]{:S(2)}, u32[]{:S(2)}) collective-permute-start(bf16[4,2,40,1280]{3,2,1,0:T(8,128)(2,1)S(1)} %broadcast_select_fusion.4), channel_id=1, source_target_pairs={{0,4},{1,3},{2,6},{3,1},{4,0},{5,7},{6,2},{7,5},{8,12},{9,11},{10,... | collective-permute-start | bytes 2457608 | tf_op jit(solution)/shard_map/ppermute | solution.py:222
  154.6 27.0 %collective-permute-start.25 = (bf16[4,2,40,1280]{3,2,1,0:T(8,128)(2,1)S(1)}, bf16[4,2,40,1280]{3,2,1,0:T(8,128)(2,1)S(1)}, u32[]{:S(2)}, u32[]{:S(2)}) collective-permute-start(bf16[4,2,40,1280]{3,2,1,0:T(8,128)(2,1)S(1)} %collective-permute-done.24), channel_id=1, source_target_pairs={{0,1},{1,0},{2,3},{3,2},{4,5},{5,4},{6,7},{7,6},{8,9},{9,8},{10,11... | collective-permute-start | bytes 2457608 | tf_op jit(solution)/shard_map/ppermute | solution.py:222
  154.8 35.4 %collective-permute-start.28 = (bf16[4,2,40,1280]{3,2,1,0:T(8,128)(2,1)S(1)}, bf16[4,2,40,1280]{3,2,1,0:T(8,128)(2,1)S(1)}, u32[]{:S(2)}, u32[]{:S(2)}) collective-permute-start(bf16[4,2,40,1280]{3,2,1,0:T(8,128)(2,1)S(1)} %broadcast_select_fusion.3), channel_id=1, source_target_pairs={{0,4},{1,3},{2,6},{3,1},{4,0},{5,7},{6,2},{7,5},{8,12},{9,11},{10,... | collective-permute-start | bytes 2457608 | tf_op jit(solution)/shard_map/ppermute | solution.py:222
  171.2 17.6 %collective-permute-start.27 = (bf16[4,2,40,1280]{3,2,1,0:T(8,128)(2,1)S(1)}, bf16[4,2,40,1280]{3,2,1,0:T(8,128)(2,1)S(1)}, u32[]{:S(2)}, u32[]{:S(2)}) collective-permute-start(bf16[4,2,40,1280]{3,2,1,0:T(8,128)(2,1)S(1)} %collective-permute-done.26), channel_id=1, source_target_pairs={{0,1},{1,0},{2,3},{3,2},{4,5},{5,4},{6,7},{7,6},{8,9},{9,8},{10,11... | collective-permute-start | bytes 2457608 | tf_op jit(solution)/shard_map/ppermute | solution.py:222
  181.6 18.9 %collective-permute-start.38 = (bf16[4,3,40,896]{3,2,1,0:T(8,128)(2,1)S(1)}, bf16[4,3,40,896]{3,2,1,0:T(8,128)(2,1)}, u32[]{:S(2)}, u32[]{:S(2)}) collective-permute-start(bf16[4,3,40,896]{3,2,1,0:T(8,128)(2,1)S(1)} %broadcast_select_fusion.2), channel_id=1, source_target_pairs={{0,4},{1,3},{2,6},{3,1},{4,0},{5,7},{6,2},{7,5},{8,12},{9,11},{10,... | collective-permute-start | bytes 2580488 | tf_op jit(solution)/shard_map/ppermute | solution.py:222
  188.9 94.9 %collective-permute-start.40 = (bf16[528,1280]{1,0:T(8,128)(2,1)}, bf16[528,1280]{1,0:T(8,128)(2,1)}, u32[]{:S(2)}, u32[]{:S(2)}) collective-permute-start(bf16[528,1280]{1,0:T(8,128)(2,1)} %fusion.41.refs_13_), channel_id=1, source_target_pairs={{0,1},{1,0},{2,3},{3,2},{4,5},{5,4},{6,7},{7,6},{8,9},{9,8},{10,11... | collective-permute-start | bytes 4055048 | tf_op jit(solution)/shard_map/ppermute | solution.py:222
  190.3 91.2 %collective-permute-start.41 = (bf16[528,1280]{1,0:T(8,128)(2,1)}, bf16[528,1280]{1,0:T(8,128)(2,1)}, u32[]{:S(2)}, u32[]{:S(2)}) collective-permute-start(bf16[528,1280]{1,0:T(8,128)(2,1)} %fusion.41.refs_13_), channel_id=1, source_target_pairs={{0,2},{1,3},{2,0},{3,1},{4,6},{5,7},{6,4},{7,5},{8,10},{9,11},{10,... | collective-permute-start | bytes 4055048 | tf_op jit(solution)/shard_map/ppermute | solution.py:222
  195.2 86.5 %collective-permute-start.43 = (bf16[528,1280]{1,0:T(8,128)(2,1)}, bf16[528,1280]{1,0:T(8,128)(2,1)}, u32[]{:S(2)}, u32[]{:S(2)}) collective-permute-start(bf16[528,1280]{1,0:T(8,128)(2,1)} %fusion.41.refs_13_), channel_id=1, source_target_pairs={{0,4},{1,5},{2,6},{3,7},{4,0},{5,1},{6,2},{7,3},{8,12},{9,13},{10,... | collective-permute-start | bytes 4055048 | tf_op jit(solution)/shard_map/ppermute | solution.py:222
  200.5 24.6 %collective-permute-start.19 = (bf16[4,2,40,1280]{3,2,1,0:T(8,128)(2,1)}, bf16[4,2,40,1280]{3,2,1,0:T(8,128)(2,1)}, u32[]{:S(2)}, u32[]{:S(2)}) collective-permute-start(bf16[4,2,40,1280]{3,2,1,0:T(8,128)(2,1)} %collective-permute-done.18), channel_id=1, source_target_pairs={{0,1},{1,0},{2,3},{3,2},{4,5},{5,4},{6,7},{7,6},{8,9},{9,8},{10,11... | collective-permute-start | bytes 2457608 | tf_op jit(solution)/shard_map/ppermute | solution.py:222
  203.1 51.5 %collective-permute-start.39 = (bf16[4,3,40,896]{3,2,1,0:T(8,128)(2,1)}, bf16[4,3,40,896]{3,2,1,0:T(8,128)(2,1)}, u32[]{:S(2)}, u32[]{:S(2)}) collective-permute-start(bf16[4,3,40,896]{3,2,1,0:T(8,128)(2,1)} %collective-permute-done.38), channel_id=1, source_target_pairs={{0,1},{1,0},{2,3},{3,2},{4,5},{5,4},{6,7},{7,6},{8,9},{9,8},{10,11... | collective-permute-start | bytes 2580488 | tf_op jit(solution)/shard_map/ppermute | solution.py:222
  249.9 35.8 %collective-permute-start.48 = (bf16[512,1280]{1,0:T(8,128)(2,1)S(1)}, bf16[512,1280]{1,0:T(8,128)(2,1)S(1)}, u32[]{:S(2)}, u32[]{:S(2)}) collective-permute-start(bf16[512,1280]{1,0:T(8,128)(2,1)S(1)} %multiply_convert_fusion.1.refs_5_), channel_id=1, source_target_pairs={{0,2},{1,3},{2,0},{3,1},{4,6},{5,7},{6,4},{7,5},{8,10},{9,11},{10,... | collective-permute-start | bytes 3932168 | tf_op jit(solution)/shard_map/ppermute | solution.py:222
  254.6 31.1 %collective-permute-start.50 = (bf16[512,1280]{1,0:T(8,128)(2,1)S(1)}, bf16[512,1280]{1,0:T(8,128)(2,1)}, u32[]{:S(2)}, u32[]{:S(2)}) collective-permute-start(bf16[512,1280]{1,0:T(8,128)(2,1)S(1)} %multiply_convert_fusion.1.refs_5_), channel_id=1, source_target_pairs={{0,4},{1,5},{2,6},{3,7},{4,0},{5,1},{6,2},{7,3},{8,12},{9,13},{10,... | collective-permute-start | bytes 3932168 | tf_op jit(solution)/shard_map/ppermute | solution.py:222
  281.7 21.0 %collective-permute-start.109 = (bf16[4,4,40,896]{3,2,1,0:T(8,128)(2,1)S(1)}, bf16[4,4,40,896]{3,2,1,0:T(8,128)(2,1)S(1)}, u32[]{:S(2)}, u32[]{:S(2)}) collective-permute-start(bf16[4,4,40,896]{3,2,1,0:T(8,128)(2,1)S(1)} %pad_maximum_fusion.10), channel_id=1, source_target_pairs={{0,1},{1,0},{2,3},{3,2},{4,5},{5,4},{6,7},{7,6},{8,9},{9,8},{10,11... | collective-permute-start | bytes 3440648 | tf_op jit(solution)/shard_map/ppermute | solution.py:222
  283.7 18.1 %collective-permute-start.45 = (bf16[528,1280]{1,0:T(8,128)(2,1)S(1)}, bf16[528,1280]{1,0:T(8,128)(2,1)S(1)}, u32[]{:S(2)}, u32[]{:S(2)}) collective-permute-start(bf16[528,1280]{1,0:T(8,128)(2,1)S(1)} %broadcast_select_fusion), channel_id=1, source_target_pairs={{0,4},{1,3},{2,6},{3,1},{4,0},{5,7},{6,2},{7,5},{8,12},{9,11},{10,... | collective-permute-start | bytes 4055048 | tf_op jit(solution)/shard_map/ppermute | solution.py:222
  285.7 19.1 %collective-permute-start.42 = (bf16[528,1280]{1,0:T(8,128)(2,1)}, bf16[528,1280]{1,0:T(8,128)(2,1)S(1)}, u32[]{:S(2)}, u32[]{:S(2)}) collective-permute-start(bf16[528,1280]{1,0:T(8,128)(2,1)} %collective-permute-done.41.refs_15_), channel_id=1, source_target_pairs={{0,1},{1,0},{2,3},{3,2},{4,5},{5,4},{6,7},{7,6},{8,9},{9,8},{10,11... | collective-permute-start | bytes 4055048 | tf_op jit(solution)/shard_map/ppermute | solution.py:222
  285.7 20.0 %collective-permute-start.44 = (bf16[528,1280]{1,0:T(8,128)(2,1)}, bf16[528,1280]{1,0:T(8,128)(2,1)S(1)}, u32[]{:S(2)}, u32[]{:S(2)}) collective-permute-start(bf16[528,1280]{1,0:T(8,128)(2,1)} %collective-permute-done.43.refs_17_), channel_id=1, source_target_pairs={{0,1},{1,0},{2,3},{3,2},{4,5},{5,4},{6,7},{7,6},{8,9},{9,8},{10,11... | collective-permute-start | bytes 4055048 | tf_op jit(solution)/shard_map/ppermute | solution.py:222
  286.4 29.6 %collective-permute-start.52 = (bf16[512,1280]{1,0:T(8,128)(2,1)S(1)}, bf16[512,1280]{1,0:T(8,128)(2,1)}, u32[]{:S(2)}, u32[]{:S(2)}) collective-permute-start(bf16[512,1280]{1,0:T(8,128)(2,1)S(1)} %broadcast_select_fusion.1), channel_id=1, source_target_pairs={{0,4},{1,3},{2,6},{3,1},{4,0},{5,7},{6,2},{7,5},{8,12},{9,11},{10,... | collective-permute-start | bytes 3932168 | tf_op jit(solution)/shard_map/ppermute | solution.py:222
  316.0 191.6 %collective-permute-start.116 = (bf16[4,4,40,896]{3,2,1,0:T(8,128)(2,1)}, bf16[4,4,40,896]{3,2,1,0:T(8,128)(2,1)}, u32[]{:S(2)}, u32[]{:S(2)}) collective-permute-start(bf16[4,4,40,896]{3,2,1,0:T(8,128)(2,1)} %pad_maximum_fusion.11), channel_id=1, source_target_pairs={{0,1},{1,0},{2,3},{3,2},{4,5},{5,4},{6,7},{7,6},{8,9},{9,8},{10,11... | collective-permute-start | bytes 3440648 | tf_op jit(solution)/shard_map/ppermute | solution.py:222
  320.0 190.0 %collective-permute-start.103 = (bf16[4,40,896]{2,1,0:T(8,128)(2,1)}, bf16[4,40,896]{2,1,0:T(8,128)(2,1)S(1)}, u32[]{:S(2)}, u32[]{:S(2)}) collective-permute-start(bf16[4,40,896]{2,1,0:T(8,128)(2,1)} %fusion.172), channel_id=1, source_target_pairs={{0,4},{1,3},{2,6},{3,1},{4,0},{5,7},{6,2},{7,5},{8,12},{9,11},{10,... | collective-permute-start | bytes 860168 | tf_op jit(solution)/shard_map/ppermute | solution.py:222
  504.9 81.7 %collective-permute-start.58 = (bf16[4,512,1280]{2,1,0:T(8,128)(2,1)}, bf16[4,512,1280]{2,1,0:T(8,128)(2,1)}, u32[]{:S(2)}, u32[]{:S(2)}) collective-permute-start(bf16[4,512,1280]{2,1,0:T(8,128)(2,1)} %get-tuple-element.107), channel_id=1, source_target_pairs={{0,1},{1,0},{2,3},{3,2},{4,5},{5,4},{6,7},{7,6},{8,9},{9,8},{10,11... | collective-permute-start | bytes 15728648 | tf_op jit(solution)/shard_map/ppermute | solution.py:222
  518.6 31.5 %collective-permute-start.112 = (bf16[4,40,896]{2,1,0:T(8,128)(2,1)S(1)}, bf16[4,40,896]{2,1,0:T(8,128)(2,1)S(1)}, u32[]{:S(2)}, u32[]{:S(2)}) collective-permute-start(bf16[4,40,896]{2,1,0:T(8,128)(2,1)S(1)} %get-tuple-element.287), channel_id=1, source_target_pairs={{0,4},{1,5},{2,6},{3,7},{4,0},{5,1},{6,2},{7,3},{8,12},{9,13},{10,... | collective-permute-start | bytes 860168 | tf_op jit(solution)/shard_map/ppermute | solution.py:222
  520.4 32.8 %collective-permute-start.118 = (bf16[4,40,896]{2,1,0:T(8,128)(2,1)S(1)}, bf16[4,40,896]{2,1,0:T(8,128)(2,1)S(1)}, u32[]{:S(2)}, u32[]{:S(2)}) collective-permute-start(bf16[4,40,896]{2,1,0:T(8,128)(2,1)S(1)} %get-tuple-element.288), channel_id=1, source_target_pairs={{0,2},{1,3},{2,0},{3,1},{4,6},{5,7},{6,4},{7,5},{8,10},{9,11},{10,... | collective-permute-start | bytes 860168 | tf_op jit(solution)/shard_map/ppermute | solution.py:222
  524.8 31.5 %collective-permute-start.119 = (bf16[4,40,896]{2,1,0:T(8,128)(2,1)S(1)}, bf16[4,40,896]{2,1,0:T(8,128)(2,1)S(1)}, u32[]{:S(2)}, u32[]{:S(2)}) collective-permute-start(bf16[4,40,896]{2,1,0:T(8,128)(2,1)S(1)} %get-tuple-element.289), channel_id=1, source_target_pairs={{0,4},{1,5},{2,6},{3,7},{4,0},{5,1},{6,2},{7,3},{8,12},{9,13},{10,... | collective-permute-start | bytes 860168 | tf_op jit(solution)/shard_map/ppermute | solution.py:222
  526.1 32.8 %collective-permute-start.106 = (bf16[40,896]{1,0:T(8,128)(2,1)S(1)}, bf16[40,896]{1,0:T(8,128)(2,1)S(1)}, u32[]{:S(2)}, u32[]{:S(2)}) collective-permute-start(bf16[40,896]{1,0:T(8,128)(2,1)S(1)} %dynamic-slice_bitcast_fusion.14), channel_id=1, source_target_pairs={{0,8},{8,16},{16,24},{24,0},{1,9},{9,17},{17,25},{25,1},{2,10},{10... | collective-permute-start | bytes 215048 | tf_op jit(solution)/shard_map/ppermute | solution.py:260
  550.1 43.7 %collective-permute-start.54 = (bf16[4,512,1280]{2,1,0:T(8,128)(2,1)}, bf16[4,512,1280]{2,1,0:T(8,128)(2,1)}, u32[]{:S(2)}, u32[]{:S(2)}) collective-permute-start(bf16[4,512,1280]{2,1,0:T(8,128)(2,1)} %get-tuple-element.105), channel_id=1, source_target_pairs={{0,1},{1,0},{2,3},{3,2},{4,5},{5,4},{6,7},{7,6},{8,9},{9,8},{10,11... | collective-permute-start | bytes 15728648 | tf_op jit(solution)/shard_map/ppermute | solution.py:222
  583.1 35.3 %all-to-all-start = ((f32[8,2,512]{2,1,0:T(2,128)}), f32[8,2,512]{2,1,0:T(2,128)S(1)}, u32[]{:S(2)}, u32[]{:S(2)}) async-start(f32[8,2,512]{2,1,0:T(2,128)} %broadcast_select_fusion.7), calls=%async_computation.1 | async-start | bytes 65536 | tf_op jit(solution)/shard_map/all_to_all | solution.py:448
  586.5 167.3 %reduce-scatter.5.cloned.1.call-start = ((), (), s32[]{:S(2)}) async-start(), calls=%async_computation.6 | async-start | bytes 8601600 | tf_op jit(solution)/shard_map/reduce_scatter | solution.py:322
  591.9 17.8 %collective-permute-start.59 = (bf16[512,1280]{1,0:T(8,128)(2,1)S(1)}, bf16[512,1280]{1,0:T(8,128)(2,1)}, u32[]{:S(2)}, u32[]{:S(2)}) collective-permute-start(bf16[512,1280]{1,0:T(8,128)(2,1)S(1)} %fusion.43), channel_id=1, source_target_pairs={{0,4},{1,3},{2,6},{3,1},{4,0},{5,7},{6,2},{7,5},{8,12},{9,11},{10,... | collective-permute-start | bytes 3932168 | tf_op jit(solution)/shard_map/ppermute | solution.py:222
  602.2 27.4 %collective-permute-start.55 = (bf16[512,1280]{1,0:T(8,128)(2,1)}, bf16[512,1280]{1,0:T(8,128)(2,1)}, u32[]{:S(2)}, u32[]{:S(2)}) collective-permute-start(bf16[512,1280]{1,0:T(8,128)(2,1)} %fusion.42), channel_id=1, source_target_pairs={{0,4},{1,3},{2,6},{3,1},{4,0},{5,7},{6,2},{7,5},{8,12},{9,11},{10,... | collective-permute-start | bytes 3932168 | tf_op jit(solution)/shard_map/ppermute | solution.py:222
  614.2 32.0 %collective-permute-start.60 = (bf16[512,1280]{1,0:T(8,128)(2,1)}, bf16[512,1280]{1,0:T(8,128)(2,1)}, u32[]{:S(2)}, u32[]{:S(2)}) collective-permute-start(bf16[512,1280]{1,0:T(8,128)(2,1)} %get-tuple-element.226), channel_id=1, source_target_pairs={{0,2},{1,3},{2,0},{3,1},{4,6},{5,7},{6,4},{7,5},{8,10},{9,11},{10,... | collective-permute-start | bytes 3932168 | tf_op jit(solution)/shard_map/ppermute | solution.py:222
  616.1 41.6 %collective-permute-start.61 = (bf16[512,1280]{1,0:T(8,128)(2,1)S(1)}, bf16[512,1280]{1,0:T(8,128)(2,1)}, u32[]{:S(2)}, u32[]{:S(2)}) collective-permute-start(bf16[512,1280]{1,0:T(8,128)(2,1)S(1)} %get-tuple-element.227), channel_id=1, source_target_pairs={{0,4},{1,5},{2,6},{3,7},{4,0},{5,1},{6,2},{7,3},{8,12},{9,13},{10,... | collective-permute-start | bytes 3932168 | tf_op jit(solution)/shard_map/ppermute | solution.py:222
  634.6 105.2 %collective-permute-start.56 = (bf16[512,1280]{1,0:T(8,128)(2,1)}, bf16[512,1280]{1,0:T(8,128)(2,1)}, u32[]{:S(2)}, u32[]{:S(2)}) collective-permute-start(bf16[512,1280]{1,0:T(8,128)(2,1)} %get-tuple-element.228), channel_id=1, source_target_pairs={{0,2},{1,3},{2,0},{3,1},{4,6},{5,7},{6,4},{7,5},{8,10},{9,11},{10,... | collective-permute-start | bytes 3932168 | tf_op jit(solution)/shard_map/ppermute | solution.py:222
  638.0 101.7 %collective-permute-start.57 = (bf16[512,1280]{1,0:T(8,128)(2,1)}, bf16[512,1280]{1,0:T(8,128)(2,1)}, u32[]{:S(2)}, u32[]{:S(2)}) collective-permute-start(bf16[512,1280]{1,0:T(8,128)(2,1)} %get-tuple-element.229), channel_id=1, source_target_pairs={{0,4},{1,5},{2,6},{3,7},{4,0},{5,1},{6,2},{7,3},{8,12},{9,13},{10,... | collective-permute-start | bytes 3932168 | tf_op jit(solution)/shard_map/ppermute | solution.py:222
  720.8 58.2 %collective-permute-start.95 = (f32[4,4,40,128]{3,2,1,0:T(8,128)}, f32[4,4,40,128]{3,2,1,0:T(8,128)}, u32[]{:S(2)}, u32[]{:S(2)}) collective-permute-start(f32[4,4,40,128]{3,2,1,0:T(8,128)} %pad_maximum_fusion.18), channel_id=1, source_target_pairs={{0,1},{1,0},{2,3},{3,2},{4,5},{5,4},{6,7},{7,6},{8,9},{9,8},{10,11... | collective-permute-start | bytes 983048 | tf_op jit(solution)/shard_map/ppermute | solution.py:222
  729.7 91.8 %collective-permute-start.67 = (bf16[4,4,40,1280]{3,2,1,0:T(8,128)(2,1)}, bf16[4,4,40,1280]{3,2,1,0:T(8,128)(2,1)}, u32[]{:S(2)}, u32[]{:S(2)}) collective-permute-start(bf16[4,4,40,1280]{3,2,1,0:T(8,128)(2,1)} %pad_maximum_fusion.1), channel_id=1, source_target_pairs={{0,1},{1,0},{2,3},{3,2},{4,5},{5,4},{6,7},{7,6},{8,9},{9,8},{10,11... | collective-permute-start | bytes 4915208 | tf_op jit(solution)/shard_map/ppermute | solution.py:222
  737.8 86.9 %collective-permute-start.74 = (bf16[4,4,40,1280]{3,2,1,0:T(8,128)(2,1)}, bf16[4,4,40,1280]{3,2,1,0:T(8,128)(2,1)}, u32[]{:S(2)}, u32[]{:S(2)}) collective-permute-start(bf16[4,4,40,1280]{3,2,1,0:T(8,128)(2,1)} %pad_maximum_fusion.2), channel_id=1, source_target_pairs={{0,1},{1,0},{2,3},{3,2},{4,5},{5,4},{6,7},{7,6},{8,9},{9,8},{10,11... | collective-permute-start | bytes 4915208 | tf_op jit(solution)/shard_map/ppermute | solution.py:222
  739.7 88.2 %collective-permute-start.81 = (bf16[4,4,40,1280]{3,2,1,0:T(8,128)(2,1)}, bf16[4,4,40,1280]{3,2,1,0:T(8,128)(2,1)}, u32[]{:S(2)}, u32[]{:S(2)}) collective-permute-start(bf16[4,4,40,1280]{3,2,1,0:T(8,128)(2,1)} %pad_maximum_fusion.3), channel_id=1, source_target_pairs={{0,1},{1,0},{2,3},{3,2},{4,5},{5,4},{6,7},{7,6},{8,9},{9,8},{10,11... | collective-permute-start | bytes 4915208 | tf_op jit(solution)/shard_map/ppermute | solution.py:222
  749.6 38.3 %collective-permute-start.62 = (f32[3]{0:T(128)S(1)}, f32[3]{0:T(128)S(1)}, u32[]{:S(2)}, u32[]{:S(2)}) collective-permute-start(f32[3]{0:T(128)S(1)} %pad_maximum_fusion.20), channel_id=1, source_target_pairs={{0,1},{1,0},{2,3},{3,2},{4,5},{5,4},{6,7},{7,6},{8,9},{9,8},{10,11... | collective-permute-start | bytes 44 | tf_op jit(solution)/shard_map/ppermute | solution.py:270
  807.0 24.1 %collective-permute-start.88 = (bf16[4,4,40,1280]{3,2,1,0:T(8,128)(2,1)}, bf16[4,4,40,1280]{3,2,1,0:T(8,128)(2,1)}, u32[]{:S(2)}, u32[]{:S(2)}) collective-permute-start(bf16[4,4,40,1280]{3,2,1,0:T(8,128)(2,1)} %pad_maximum_fusion.4), channel_id=1, source_target_pairs={{0,1},{1,0},{2,3},{3,2},{4,5},{5,4},{6,7},{7,6},{8,9},{9,8},{10,11... | collective-permute-start | bytes 4915208 | tf_op jit(solution)/shard_map/ppermute | solution.py:222
  833.1 20.5 %collective-permute-start.89 = (bf16[4,40,1280]{2,1,0:T(8,128)(2,1)S(1)}, bf16[4,40,1280]{2,1,0:T(8,128)(2,1)S(1)}, u32[]{:S(2)}, u32[]{:S(2)}) collective-permute-start(bf16[4,40,1280]{2,1,0:T(8,128)(2,1)S(1)} %fusion.147), channel_id=1, source_target_pairs={{0,4},{1,3},{2,6},{3,1},{4,0},{5,7},{6,2},{7,5},{8,12},{9,11},{10,... | collective-permute-start | bytes 1228808 | tf_op jit(solution)/shard_map/ppermute | solution.py:222
  834.3 21.2 %collective-permute-start.69 = (bf16[4,40,1280]{2,1,0:T(8,128)(2,1)S(1)}, bf16[4,40,1280]{2,1,0:T(8,128)(2,1)S(1)}, u32[]{:S(2)}, u32[]{:S(2)}) collective-permute-start(bf16[4,40,1280]{2,1,0:T(8,128)(2,1)S(1)} %get-tuple-element.230), channel_id=1, source_target_pairs={{0,2},{1,3},{2,0},{3,1},{4,6},{5,7},{6,4},{7,5},{8,10},{9,11},{10,... | collective-permute-start | bytes 1228808 | tf_op jit(solution)/shard_map/ppermute | solution.py:222
  836.2 21.8 %collective-permute-start.70 = (bf16[4,40,1280]{2,1,0:T(8,128)(2,1)S(1)}, bf16[4,40,1280]{2,1,0:T(8,128)(2,1)S(1)}, u32[]{:S(2)}, u32[]{:S(2)}) collective-permute-start(bf16[4,40,1280]{2,1,0:T(8,128)(2,1)S(1)} %get-tuple-element.231), channel_id=1, source_target_pairs={{0,4},{1,5},{2,6},{3,7},{4,0},{5,1},{6,2},{7,3},{8,12},{9,13},{10,... | collective-permute-start | bytes 1228808 | tf_op jit(solution)/shard_map/ppermute | solution.py:222
  837.6 22.3 %collective-permute-start.76 = (bf16[4,40,1280]{2,1,0:T(8,128)(2,1)S(1)}, bf16[4,40,1280]{2,1,0:T(8,128)(2,1)S(1)}, u32[]{:S(2)}, u32[]{:S(2)}) collective-permute-start(bf16[4,40,1280]{2,1,0:T(8,128)(2,1)S(1)} %get-tuple-element.232), channel_id=1, source_target_pairs={{0,2},{1,3},{2,0},{3,1},{4,6},{5,7},{6,4},{7,5},{8,10},{9,11},{10,... | collective-permute-start | bytes 1228808 | tf_op jit(solution)/shard_map/ppermute | solution.py:222
  844.9 21.5 %collective-permute-start.77 = (bf16[4,40,1280]{2,1,0:T(8,128)(2,1)S(1)}, bf16[4,40,1280]{2,1,0:T(8,128)(2,1)S(1)}, u32[]{:S(2)}, u32[]{:S(2)}) collective-permute-start(bf16[4,40,1280]{2,1,0:T(8,128)(2,1)S(1)} %get-tuple-element.233), channel_id=1, source_target_pairs={{0,4},{1,5},{2,6},{3,7},{4,0},{5,1},{6,2},{7,3},{8,12},{9,13},{10,... | collective-permute-start | bytes 1228808 | tf_op jit(solution)/shard_map/ppermute | solution.py:222
  855.5 19.6 %collective-permute-start.84 = (bf16[4,40,1280]{2,1,0:T(8,128)(2,1)S(1)}, bf16[4,40,1280]{2,1,0:T(8,128)(2,1)S(1)}, u32[]{:S(2)}, u32[]{:S(2)}) collective-permute-start(bf16[4,40,1280]{2,1,0:T(8,128)(2,1)S(1)} %get-tuple-element.235), channel_id=1, source_target_pairs={{0,4},{1,5},{2,6},{3,7},{4,0},{5,1},{6,2},{7,3},{8,12},{9,13},{10,... | collective-permute-start | bytes 1228808 | tf_op jit(solution)/shard_map/ppermute | solution.py:222
  859.9 20.0 %collective-permute-start.91 = (bf16[4,40,1280]{2,1,0:T(8,128)(2,1)S(1)}, bf16[4,40,1280]{2,1,0:T(8,128)(2,1)S(1)}, u32[]{:S(2)}, u32[]{:S(2)}) collective-permute-start(bf16[4,40,1280]{2,1,0:T(8,128)(2,1)S(1)} %get-tuple-element.237), channel_id=1, source_target_pairs={{0,4},{1,5},{2,6},{3,7},{4,0},{5,1},{6,2},{7,3},{8,12},{9,13},{10,... | collective-permute-start | bytes 1228808 | tf_op jit(solution)/shard_map/ppermute | solution.py:222
  (204 other events, 2594.0 us)
Sparse Core Ops, SparseCore 0:
  13.0 160.3 all-gather.4
  174.9 123.9 all-gather.2
  412.5 145.3 reduce-scatter.2
  618.6 116.6 reduce-scatter.4

commit v2 on v0

v2 whole, which is shorter than its diff:
```python
import functools
import math

import jax
import jax.numpy as jnp
from jax import lax
from jax.experimental import pallas as pl
from jax.experimental.layout import Layout, with_layout_constraint
from jax.experimental.pallas import tpu as pltpu
from jax.sharding import PartitionSpec as P

HEADS = 10
STEP = 3
BF = jnp.bfloat16
F32 = jnp.float32
BOTH = ("dp", "expert")


eps_norm = 1e-06
momentum_rate = 0.9
decay_rate = 0.0001
rate_attention = 0.01
rate_router = 0.03
rate_shared = 0.01
rate_routed = 0.04
rate_gains = 0.2
masked_score = -1e30
VMEM_LIMIT = 58 * 1024 * 1024


def silu_slope(pre_value):
    sigmoid_part = jax.nn.sigmoid(pre_value)
    return sigmoid_part * (1.0 + pre_value * (1.0 - sigmoid_part))


def update(weight, moment, average, gradient, step_rate):
    decayed = gradient + decay_rate * weight
    moment_new = momentum_rate * moment + decayed
    weight_new = weight - step_rate * (decayed + momentum_rate * moment_new)
    average_new = average + (weight_new - average) / (STEP + 1.0)
    return (gradient, weight_new, moment_new, average_new, weight_new.astype(BF))


def estimate(flops):
    return pl.CostEstimate(flops=flops, bytes_accessed=1, transcendentals=0)


def dot_nn(a,b): return lax.dot_general(a,b,(((1,),(0,)),((),())),preferred_element_type=F32)
def dot_nt(a,b): return lax.dot_general(a,b,(((1,),(1,)),((),())),preferred_element_type=F32)
def dot_tn(a,b): return lax.dot_general(a,b,(((0,),(0,)),((),())),preferred_element_type=F32)

def chunks(n,c): return [(s,min(c,n-s)) for s in range(0,n,c)]

def pair_columns(ff):
    return [(c0, cn, 2 * c0, 2 * c0 + cn) for c0, cn in chunks(ff, 256)]


def expert_pair_kernel(first, *refs):
    it = iter(refs)
    take = lambda count: [next(it) for _ in range(count)]
    eid_ref, choice_ref, slot_ref, router_ref, w_hbm = take(5)
    gate_ref = None if first else next(it)
    sources = [take(2), take(2)]
    prev = [] if first else [take(2), take(2)]
    outs = [take(2), take(2)]
    dg_ref, rows_out, dy_out, h_out, dab_out = take(5)
    gate_out = next(it) if first else None
    gu_v, down_v, tok, rows_v, dy_v, h_v, dab_v, ob, wsem, dsem, tsem, psem, osem, ssem = it
    n_dp = w_hbm.shape[0]
    width, ff = down_v.shape
    slab = width // n_dp
    seq = slot_ref.shape[1]
    cap = rows_v.shape[0] // 2
    tcopies = [[pltpu.make_async_copy(sources[j][q], tok.at[q, j], tsem.at[q, j]) for j in range(2)] for q in range(2)]
    wcopies = []
    for d in range(n_dp):
        own = pl.ds(d * slab, slab)
        for c, (c0, cn, g0, u0) in enumerate(pair_columns(ff)):
            for j, to in ((0, g0), (1, u0)):
                src = w_hbm.at[d, j, pl.ds(0, slab), pl.ds(c0, cn)]
                wcopies.append(pltpu.make_async_copy(src, gu_v.at[own, pl.ds(to, cn)], wsem.at[d, c, j]))
    dcopies = [
        pltpu.make_async_copy(w_hbm.at[d, 2, pl.ds(0, slab)], down_v.at[pl.ds(d * slab, slab)], dsem.at[d]) for d in range(n_dp)
    ]
    for copies in tcopies:
        for copy in copies:
            copy.start()
    lane = lax.broadcasted_iota(jnp.int32, (seq, 128), 1)
    sub = lax.broadcasted_iota(jnp.int32, (cap, seq), 0)
    eid = eid_ref[0]
    gcols, onehots = [], []
    for q in range(2):
        tcopies[q][0].wait()
        if q == 0:
            for copy in wcopies + dcopies:
                copy.start()
        sec = tok[q, 0]
        if first:
            logits = dot_nt(sec, router_ref[...])
            table = choice_ref[q, :, 0:1] == lane
            for k in range(1, choice_ref.shape[2]):
                table = table | (choice_ref[q, :, k : k + 1] == lane)
            masked = jnp.where(table, logits, masked_score)
            weight = jnp.where(table, jnp.exp(masked - jnp.max(masked, axis=1, keepdims=True)), 0.0)
            gates = weight / jnp.sum(weight, axis=1, keepdims=True)
            gate_out[q] = gates
        else:
            gates = gate_ref[q]
        gcol = jnp.sum(jnp.where(lane == eid, gates, 0.0), axis=1, keepdims=True)
        onehot = (slot_ref[q : q + 1, :] == sub).astype(F32).astype(BF)
        rows_v[q * cap : (q + 1) * cap, :] = dot_nn(onehot, sec).astype(BF)
        tcopies[q][1].wait()
        gated = (gcol * tok[q, 1].astype(F32)).astype(BF)
        dy_v[q * cap : (q + 1) * cap, :] = dot_nn(onehot, gated).astype(BF)
        gcols.append(gcol)
        onehots.append(onehot)
    pcopies = [pltpu.make_async_copy(prev[j][q], ob.at[q, j], psem.at[q, j]) for q in range(2) for j in range(2) if not first]
    for copy in pcopies:
        copy.start()
    saves = [pltpu.make_async_copy(rows_v, rows_out, ssem.at[0]), pltpu.make_async_copy(dy_v, dy_out, ssem.at[1])]
    for copy in saves:
        copy.start()
    for copy in wcopies + dcopies:
        copy.wait()
    gain_sum = jnp.zeros((2 * cap, 128), F32)
    for c0, cn, g0, u0 in pair_columns(ff):
        both = dot_nn(rows_v[...], gu_v[:, g0 : g0 + 2 * cn])
        a, b = both[:, :cn], both[:, cn:]
        dh = dot_nn(dy_v[...], down_v[:, c0 : c0 + cn])
        sigmoid = 0.5 * jnp.tanh(0.5 * a) + 0.5
        silu = a * sigmoid
        dsilu = dh * silu
        gain = dsilu * b
        for p0, pn in chunks(cn, 128):
            gain_sum = gain_sum + gain[:, p0 : p0 + pn]
        h_v[:, c0 : c0 + cn] = (silu * b).astype(BF)
        dab_v[:, g0 : g0 + cn] = (dh * b * (sigmoid + silu * (1.0 - sigmoid))).astype(BF)
        dab_v[:, u0 : u0 + cn] = dsilu.astype(BF)
    late = [pltpu.make_async_copy(h_v, h_out, ssem.at[2]), pltpu.make_async_copy(dab_v, dab_out, ssem.at[3])]
    for copy in late:
        copy.start()
    for copy in pcopies:
        copy.wait()
    sends = []
    gain_slot = jnp.sum(gain_sum, axis=1, keepdims=True)
    for q in range(2):
        spread = onehots[q].astype(F32) * gain_slot[q * cap : (q + 1) * cap]
        dg_ref[q] = jnp.broadcast_to(jnp.sum(spread, axis=0, keepdims=True), (8, seq))
    for n, (n0, nn) in enumerate(chunks(width, 512)):
        ns = slice(n0, n0 + nn)
        y = dot_nt(h_v[...], down_v[ns, :]).astype(BF)
        dr = dot_nt(dab_v[...], gu_v[ns, :]).astype(BF)
        for q in range(2):
            yt = dot_tn(onehots[q], y[q * cap : (q + 1) * cap])
            dt = dot_tn(onehots[q], dr[q * cap : (q + 1) * cap])
            yt = yt * gcols[q]
            if not first:
                yt = yt + ob[q, 0, :, ns].astype(F32)
                dt = dt + ob[q, 1, :, ns].astype(F32)
            ob[q, 0, :, ns] = yt.astype(BF)
            ob[q, 1, :, ns] = dt.astype(BF)
            for j in range(2):
                part = pl.ds(n0, nn)
                copy = pltpu.make_async_copy(ob.at[q, j, :, part], outs[j][q].at[:, part], osem.at[q, j, n])
                copy.start()
                sends.append(copy)
    for copy in saves + late + sends:
        copy.wait()


def expert_pair_call(eid, choice, slots, router_pad, w, secs, douts, prev, gates, cap):
    seq = slots.shape[1]
    width = secs[0].shape[1]
    n_dp, _, _, ff = w.shape
    parts = len(chunks(width, 512))
    flat = [] if prev is None else [v for pair in prev for v in pair]
    full = jax.ShapeDtypeStruct((seq, width), BF)
    shapes = [(2 * cap, width), (2 * cap, width), (2 * cap, ff), (2 * cap, 2 * ff)]
    dma = pltpu.SemaphoreType.DMA
    out = pl.pallas_call(
        functools.partial(expert_pair_kernel, prev is None),
        out_shape=[full] * 4
        + [jax.ShapeDtypeStruct((2, 8, seq), F32)]
        + [jax.ShapeDtypeStruct(shape, BF) for shape in shapes]
        + [jax.ShapeDtypeStruct((2, seq, 128), F32)] * (prev is None),
        in_specs=kernel_specs("svvva" + "v" * (prev is not None) + "a" * (4 + len(flat))),
        out_specs=kernel_specs("aaaavaaaa" + "v" * (prev is None)),
        scratch_shapes=[pltpu.VMEM((width, 2 * ff), BF), pltpu.VMEM((width, ff), BF), pltpu.VMEM((2, 2, seq, width), BF)]
        + [pltpu.VMEM(shape, BF) for shape in shapes]
        + [pltpu.VMEM((2, 2, seq, width), BF)]
        + [dma((n_dp, len(chunks(ff, 256)), 2)), dma((n_dp,)), dma((2, 2)), dma((2, 2)), dma((2, 2, parts)), dma((4,))],
        compiler_params=pltpu.CompilerParams(vmem_limit_bytes=VMEM_LIMIT),
        cost_estimate=estimate(18 * cap * width * ff),
        name="expert_pair",
    )(eid, choice, slots, router_pad, w, *([] if prev is None else [gates]), *secs, *douts, *flat)
    return (out[0:2], out[2:4]), out[4], out[5:9], out[9] if prev is None else gates


def weight_grad_kernel(count, *refs):
    saved = [refs[4 * i : 4 * i + 4] for i in range(count)]
    out_ref, rows_v, dy_v, h_v, dab_v, g_v, isem, osem = refs[4 * count :]
    width, ff = g_v.shape[1:]
    n_dp = out_ref.shape[0]
    slab = width // n_dp
    piece = rows_v.shape[0] // count
    loads = {}
    for j, to in ((1, dy_v), (2, h_v), (0, rows_v), (3, dab_v)):
        loads[j] = [
            pltpu.make_async_copy(saved[i][j], to.at[pl.ds(i * piece, piece)], isem.at[j, i]) for i in range(count)
        ]
        for copy in loads[j]:
            copy.start()
    stores = [
        [pltpu.make_async_copy(g_v.at[j, pl.ds(d * slab, slab)], out_ref.at[d, j], osem.at[j, d]) for d in range(n_dp)]
        for j in range(3)
    ]
    for copy in loads[1] + loads[2]:
        copy.wait()

    def down(i, carry):
        m = pl.ds(pl.multiple_of(i * 256, 256), 256)
        g_v[2, m, :] = dot_tn(dy_v[:, m], h_v[...]).astype(BF)
        return carry

    lax.fori_loop(0, width // 256, down, 0)
    for copy in stores[2]:
        copy.start()
    for copy in loads[0] + loads[3]:
        copy.wait()

    def front(i, carry):
        m = pl.ds(pl.multiple_of(i * 256, 256), 256)
        both = dot_tn(rows_v[:, m], dab_v[...])
        for c0, cn, g0, u0 in pair_columns(ff):
            g_v[0, m, c0 : c0 + cn] = both[:, g0 : g0 + cn].astype(BF)
            g_v[1, m, c0 : c0 + cn] = both[:, u0 : u0 + cn].astype(BF)
        return carry

    lax.fori_loop(0, width // 256, front, 0)
    for copy in stores[0] + stores[1]:
        copy.start()
    for copy in stores[0] + stores[1] + stores[2]:
        copy.wait()


def weight_grad_call(saved, n_dp):
    count = len(saved)
    width, ff = saved[0][0].shape[1], saved[0][2].shape[1]
    rows = count * saved[0][0].shape[0]
    dma = pltpu.SemaphoreType.DMA
    return pl.pallas_call(
        functools.partial(weight_grad_kernel, count),
        out_shape=jax.ShapeDtypeStruct((n_dp, 3, width // n_dp, ff), BF),
        in_specs=kernel_specs("a" * (4 * count)),
        out_specs=pl.BlockSpec(memory_space=pl.ANY),
        scratch_shapes=[pltpu.VMEM((rows, n), BF) for n in (width, width, ff, 2 * ff)]
        + [pltpu.VMEM((3, width, ff), BF), dma((4, count)), dma((3, n_dp))],
        compiler_params=pltpu.CompilerParams(vmem_limit_bytes=VMEM_LIMIT),
        cost_estimate=estimate(6 * rows * width * ff),
        name="expert_weights",
    )(*[v for part in saved for v in part])


def rotated(values, cosine, sine):
    return values * cosine + pltpu.roll(values, values.shape[1] // 2, 1) * sine


def head_block(h):
    return pl.ds(pl.multiple_of(h * 128, 128), 128)


def masked_scores(query, key, start, length, scale):
    scores = dot_nt(query, key) * scale
    at = lax.broadcasted_iota(jnp.int32, scores.shape, 0) + start
    to = lax.broadcasted_iota(jnp.int32, scores.shape, 1)
    return jnp.where((to <= at) & (to < length), scores, masked_score)


def attention_kernel(
    scale, tok_ref, gain_ref, cos_ref, sin_ref, len_ref, wq, wk, wv, wo,
    first_ref, q_ref, k_ref, v_ref, ctx_ref, lse_ref, hidden_ref, second_ref, w_v, sem,
):
    copies = [pltpu.make_async_copy(w, w_v.at[j], sem.at[j]) for j, w in enumerate((wq, wk, wv, wo))]
    for copy in copies:
        copy.start()
    seq, width = tok_ref.shape
    length = len_ref[0]
    x = tok_ref[...].astype(F32)
    inverse = lax.rsqrt(jnp.mean(x * x, axis=1, keepdims=True) + eps_norm)
    first_ref[...] = (x * inverse * gain_ref[0:1, :]).astype(BF)
    for j, out_ref in enumerate((q_ref, k_ref, v_ref)):
        copies[j].wait()
        for c0, cn in chunks(width, 256):
            lin = dot_nn(first_ref[...], w_v[j, :, c0 : c0 + cn])
            for h0, hn in chunks(cn, 128):
                part = lin[:, h0 : h0 + hn]
                if j < 2:
                    part = rotated(part, cos_ref[...], sin_ref[...])
                out_ref[:, c0 + h0 : c0 + h0 + hn] = part.astype(BF)
    lane = lax.broadcasted_iota(jnp.int32, (seq, 128), 1)
    block = 256

    def heads(g, carry):
        for u in range(2):
            h = g * 2 + u
            hs = head_block(h)
            logs = []
            for start in range(0, seq, block):
                end = start + block
                masked = masked_scores(q_ref[start:end, hs], k_ref[:end, hs], start, length, scale)
                peak = jnp.max(masked, axis=1, keepdims=True)
                weight = jnp.exp(masked - peak)
                total = jnp.sum(weight, axis=1, keepdims=True)
                probs = (weight / total).astype(BF)
                ctx_ref[start:end, hs] = dot_nn(probs, v_ref[:end, hs]).astype(BF)
                logs.append(peak + jnp.log(total))
            log = jnp.concatenate(logs, axis=0)
            lse_ref[...] = jnp.where(lane == h, log, lse_ref[...])
        return carry

    lse_ref[...] = jnp.zeros_like(lse_ref)
    lax.fori_loop(0, width // 256, heads, 0)
    copies[3].wait()
    squares = jnp.zeros((seq, 1), F32)
    for c0, cn in chunks(width, 256):
        cs = slice(c0, c0 + cn)
        hidden = tok_ref[:, cs].astype(F32) + dot_nn(ctx_ref[...], w_v[3, :, cs])
        hidden_ref[:, cs] = hidden
        squares = squares + jnp.sum(hidden * hidden, axis=1, keepdims=True)
    inverse = lax.rsqrt(squares / width + eps_norm)
    second_ref[...] = (hidden_ref[...] * inverse * gain_ref[1:2, :]).astype(BF)


def kernel_specs(places):
    kinds = {"v": pltpu.VMEM, "s": pltpu.SMEM, "a": pl.ANY}
    return [pl.BlockSpec(memory_space=kinds[p]) for p in places]


def attention_call(tokens, gains, cosine, sine, lengths, weights, scale):
    seq, width = tokens.shape
    half = jax.ShapeDtypeStruct((seq, width), BF)
    return pl.pallas_call(
        functools.partial(attention_kernel, scale),
        out_shape=[half] * 5
        + [jax.ShapeDtypeStruct((seq, 128), F32), jax.ShapeDtypeStruct((seq, width), F32), half],
        in_specs=kernel_specs("vvvvsaaaa"),
        out_specs=kernel_specs("vvvvvvvv"),
        scratch_shapes=[pltpu.VMEM((4, width, width), BF), pltpu.SemaphoreType.DMA((4,))],
        compiler_params=pltpu.CompilerParams(vmem_limit_bytes=VMEM_LIMIT),
        cost_estimate=estimate(0),
        name="attention_forward",
    )(tokens, gains, cosine, sine, lengths, *weights)


def store_pieces(even_ref, odd_ref, slot, rows_ref, grad_ref):
    count, _, piece, _ = even_ref.shape
    for part, out_ref in enumerate((even_ref, odd_ref)):
        for j in range(count):
            at = (part * count + j) * piece
            out_ref[j, slot] = dot_nn(rows_ref[at : at + piece, :], grad_ref[...]).astype(BF)


def piece_shape(number, width, out_width):
    count = lax.axis_size("expert") // 2
    return jax.ShapeDtypeStruct((count, number, width // (2 * count), out_width), BF)


def hidden_back_kernel(
    dn_ref, base_ref, side_x_ref, side_y_ref, hidden_ref, dout_ref, gain_ref, ctx_ref, wo, dhid_ref, dctx_ref, even_ref, odd_ref, gain_out, w_v, dattn_v, sem
):
    copy = pltpu.make_async_copy(wo, w_v, sem)
    copy.start()
    seq, width = hidden_ref.shape
    hidden = hidden_ref[...]
    inverse = lax.rsqrt(jnp.mean(hidden * hidden, axis=1, keepdims=True) + eps_norm)
    hat = hidden * inverse
    dn = dn_ref[...] + base_ref[...] + side_x_ref[...].astype(F32) + side_y_ref[...].astype(F32)
    gain_out[...] = jnp.sum(dn * hat, axis=0, keepdims=True)
    scaled = dn * gain_ref[1:2, :]
    mean = jnp.mean(scaled * hat, axis=1, keepdims=True)
    dhid = dout_ref[...].astype(F32) + inverse * (scaled - hat * mean)
    dhid_ref[...] = dhid
    dattn_v[...] = dhid.astype(BF)
    store_pieces(even_ref, odd_ref, 0, ctx_ref, dattn_v)
    copy.wait()
    for c0, cn in chunks(width, 256):
        dctx_ref[:, c0 : c0 + cn] = dot_nt(dattn_v[...], w_v[c0 : c0 + cn, :]).astype(BF)


def hidden_back_call(dn, base, sides, hidden, dout, gains, ctx_rel, wo):
    seq, width = hidden.shape
    half = jax.ShapeDtypeStruct((seq, width), BF)
    part = piece_shape(1, width, width)
    return pl.pallas_call(
        hidden_back_kernel,
        out_shape=[jax.ShapeDtypeStruct((seq, width), F32), half, part, part, jax.ShapeDtypeStruct((1, width), F32)],
        in_specs=kernel_specs("vvvvvvvva"),
        out_specs=kernel_specs("vvvvv"),
        scratch_shapes=[pltpu.VMEM((width, width), BF), pltpu.VMEM((seq, width), BF), pltpu.SemaphoreType.DMA],
        compiler_params=pltpu.CompilerParams(vmem_limit_bytes=VMEM_LIMIT),
        cost_estimate=estimate(0),
        name="hidden_backward",
    )(dn, base, *sides, hidden, dout, gains, ctx_rel, wo)


def heads_back_kernel(
    scale, q_ref, k_ref, v_ref, dctx_ref, lse_ref, cos_ref, sin_ref, first_ref, len_ref,
    dq_ref, dk_ref, dv_ref, even_ref, odd_ref,
):
    seq, width = q_ref.shape
    length = len_ref[0]
    lane = lax.broadcasted_iota(jnp.int32, (seq, 128), 1)
    block = 256

    def heads(g, carry):
        for u in range(2):
            h = g * 2 + u
            hs = head_block(h)
            log = jnp.sum(jnp.where(lane == h, lse_ref[...], 0.0), axis=1, keepdims=True)
            key_parts, value_parts = [], []
            for start in range(0, seq, block):
                end = start + block
                rows = slice(start, end)
                masked = masked_scores(q_ref[rows, hs], k_ref[:end, hs], start, length, scale)
                probs = jnp.exp(masked - log[rows])
                dprobs = dot_nt(dctx_ref[rows, hs], v_ref[:end, hs])
                delta = jnp.sum(probs * dprobs, axis=1, keepdims=True)
                dscores = (probs * (dprobs - delta)).astype(BF)
                dq = dot_nn(dscores, k_ref[:end, hs]) * scale
                dq_ref[rows, hs] = rotated(dq, cos_ref[rows, :], -sin_ref[rows, :]).astype(BF)
                key_parts.append(dot_tn(dscores, q_ref[rows, hs]))
                value_parts.append(dot_tn(probs.astype(BF), dctx_ref[rows, hs]))
            for start in range(0, seq, block):
                rows = slice(start, start + block)
                dk = sum(p[rows] for p in key_parts if p.shape[0] > start) * scale
                dv = sum(p[rows] for p in value_parts if p.shape[0] > start)
                dk_ref[rows, hs] = rotated(dk, cos_ref[rows, :], -sin_ref[rows, :]).astype(BF)
                dv_ref[rows, hs] = dv.astype(BF)
        return carry

    lax.fori_loop(0, width // 256, heads, 0)
    for j, grad_ref in ((2, dv_ref), (1, dk_ref), (0, dq_ref)):
        store_pieces(even_ref, odd_ref, j, first_ref, grad_ref)


def heads_back_call(q, k, v, dctx, lse, cosine, sine, first_rel, lengths, scale):
    seq, width = q.shape
    half = jax.ShapeDtypeStruct((seq, width), BF)
    part = piece_shape(3, width, width)
    return pl.pallas_call(
        functools.partial(heads_back_kernel, scale),
        out_shape=[half] * 3 + [part] * 2,
        in_specs=kernel_specs("vvvvvvvvs"),
        out_specs=kernel_specs("v" * 5),
        compiler_params=pltpu.CompilerParams(vmem_limit_bytes=VMEM_LIMIT),
        cost_estimate=estimate(0),
        name="heads_backward",
    )(q, k, v, dctx, lse, cosine, sine, first_rel, lengths)


def input_back_kernel(
    dq_ref, dk_ref, dv_ref, tok_ref, gain_ref, dhid_ref, len_ref, wq, wk, wv, out_ref, gain_out, sum_ref, w_v, dn_v, sem
):
    copies = [pltpu.make_async_copy(w, w_v.at[j], sem.at[j]) for j, w in enumerate((wq, wk, wv))]
    for copy in copies:
        copy.start()
    seq, width = tok_ref.shape
    x = tok_ref[...].astype(F32)
    inverse = lax.rsqrt(jnp.mean(x * x, axis=1, keepdims=True) + eps_norm)
    for copy in copies:
        copy.wait()
    for c0, cn in chunks(width, 256):
        cs = slice(c0, c0 + cn)
        dn_v[:, cs] = (
            dot_nt(dq_ref[...], w_v[0, cs, :]) + dot_nt(dk_ref[...], w_v[1, cs, :]) + dot_nt(dv_ref[...], w_v[2, cs, :])
        )
    hat = tok_ref[...].astype(F32) * inverse
    dn = dn_v[...]
    gain_out[...] = jnp.sum(dn * hat, axis=0, keepdims=True)
    scaled = dn * gain_ref[0:1, :]
    mean = jnp.mean(scaled * hat, axis=1, keepdims=True)
    result = dhid_ref[...] + inverse * (scaled - hat * mean)
    out_ref[...] = result
    valid = lax.broadcasted_iota(jnp.int32, result.shape, 0) < len_ref[0]
    sum_ref[0] = jnp.sum(jnp.where(valid, result * result, 0.0))


def input_back_call(dq, dk, dv, tokens, gains, dhidden, lengths, weights):
    seq, width = tokens.shape
    return pl.pallas_call(
        input_back_kernel,
        out_shape=[
            jax.ShapeDtypeStruct((seq, width), F32),
            jax.ShapeDtypeStruct((1, width), F32),
            jax.ShapeDtypeStruct((1,), F32),
        ],
        in_specs=kernel_specs("vvvvvvsaaa"),
        out_specs=kernel_specs("vvs"),
        scratch_shapes=[pltpu.VMEM((3, width, width), BF), pltpu.VMEM((seq, width), F32), pltpu.SemaphoreType.DMA((3,))],
        compiler_params=pltpu.CompilerParams(vmem_limit_bytes=VMEM_LIMIT),
        cost_estimate=estimate(0),
        name="input_backward",
    )(dq, dk, dv, tokens, gains, dhidden, lengths, *weights)


def shared_kernel(
    second_ref, second_rel_ref, dout_ref, dout_rel_ref, wg, wu, wd, out_ref, dn_ref, even_ref, odd_ref, w_v, h_v, da_v, db_v, sem
):
    copies = [pltpu.make_async_copy(w, w_v.at[j], sem.at[j]) for j, w in enumerate((wg, wu, wd))]
    for copy in copies:
        copy.start()
    for copy in copies:
        copy.wait()
    width, ff = w_v.shape[1:]
    for c0, cn in chunks(ff, 256):
        cs = slice(c0, c0 + cn)
        gate = dot_nn(second_ref[...], w_v[0, :, cs])
        up = dot_nn(second_ref[...], w_v[1, :, cs])
        back = dot_nn(dout_ref[...], w_v[2, :, cs])
        sigmoid = 1.0 / (1.0 + jnp.exp(-gate))
        silu = gate * sigmoid
        h_v[:, cs] = (silu * up).astype(BF)
        da_v[:, cs] = (back * up * (sigmoid * (1.0 + gate * (1.0 - sigmoid)))).astype(BF)
        db_v[:, cs] = (back * silu).astype(BF)
    for c0, cn in chunks(width, 256):
        cs = slice(c0, c0 + cn)
        out_ref[:, cs] = dot_nt(h_v[...], w_v[2, cs, :])
        dn_ref[:, cs] = dot_nt(da_v[...], w_v[0, cs, :]) + dot_nt(db_v[...], w_v[1, cs, :])
    store_pieces(even_ref, odd_ref, 0, second_rel_ref, da_v)
    store_pieces(even_ref, odd_ref, 1, second_rel_ref, db_v)
    store_pieces(even_ref, odd_ref, 2, dout_rel_ref, h_v)


def shared_call(second, second_rel, dout, dout_rel, weights):
    seq, width = second.shape
    ff = weights[0].shape[1]
    full = jax.ShapeDtypeStruct((seq, width), F32)
    part = piece_shape(3, width, ff)
    return pl.pallas_call(
        shared_kernel,
        out_shape=[full, full, part, part],
        in_specs=kernel_specs("vvvvaaa"),
        out_specs=kernel_specs("vvvv"),
        scratch_shapes=[pltpu.VMEM((3, width, ff), BF)]
        + [pltpu.VMEM((seq, ff), BF)] * 3
        + [pltpu.SemaphoreType.DMA((3,))],
        compiler_params=pltpu.CompilerParams(vmem_limit_bytes=VMEM_LIMIT),
        cost_estimate=estimate(0),
        name="shared_expert",
    )(second, second_rel, dout, dout_rel, *weights)


def update_kernel(rate, grad_ref, w_ref, m_ref, a_ref, *refs):
    grad_out, new_out, moment_out, average_out, copy_out = refs[-5:]
    parts = update(w_ref[0, 0], m_ref[0, 0], a_ref[0, 0], grad_ref[0].astype(F32), rate)
    for target, part in zip((grad_out, new_out, moment_out, average_out, copy_out), parts):
        target[0, 0] = part


def update_call(e, grad, weight, moment, average, done, rate):
    experts, kinds, rows, ff = weight.shape
    cuts = 2 if rows % 32 == 0 else 1
    full = pl.BlockSpec((1, 1, rows // cuts, ff), lambda j, i: (e, j, i, 0))
    return pl.pallas_call(
        functools.partial(update_kernel, rate),
        grid=(kinds, cuts),
        out_shape=[jax.ShapeDtypeStruct(weight.shape, F32)] * 4 + [jax.ShapeDtypeStruct(weight.shape, BF)],
        in_specs=[pl.BlockSpec((1, rows // cuts, ff), lambda j, i: (j, i, 0))]
        + [full] * 3
        + [pl.BlockSpec(memory_space=pl.ANY)] * len(done),
        out_specs=[full] * 5,
        input_output_aliases={4 + i: i for i in range(len(done))},
        compiler_params=pltpu.CompilerParams(vmem_limit_bytes=VMEM_LIMIT),
        cost_estimate=estimate(0),
        name="routed_update",
    )(grad, weight, moment, average, *done)


def permute(values, pairs):
    return lax.ppermute(values, "expert", pairs)


def pairs_of(mask, count):
    return [(i, i ^ mask) for i in range(count)]


def mixed_pairs(even_mask, odd_mask, count):
    return [(i, i ^ (odd_mask if i % 2 else even_mask)) for i in range(count)]


def after(values, *others):
    return lax.optimization_barrier((values, others))[0] if others else values


class Order:
    def __init__(self):
        self.last = ()

    def now(self, values):
        return after(values, *self.last)

    def close(self, *values):
        self.last = values


def send_dp(values, k):
    return lax.ppermute(values, "dp", [(i, i ^ k) for i in range(lax.axis_size("dp"))])


def stack_dp(pieces):
    whole = jnp.zeros((len(pieces),) + pieces[0].shape, pieces[0].dtype)
    for k, piece in enumerate(pieces):
        whole = lax.dynamic_update_slice(whole, piece[None], (lax.axis_index("dp") ^ k,) + (0,) * piece.ndim)
    return whole


def sum_dp(terms, axis, order):
    here = lax.axis_index("dp")
    found = []
    for k in range(lax.axis_size("dp")):
        term = lax.dynamic_index_in_dim(terms, here ^ k, axis=axis, keepdims=False)
        found.append((send_dp(order.now(term), k) if k else term).astype(F32))
    return tree_sum(found)


def tree_sum(terms):
    while len(terms) > 1:
        terms = [a + b for a, b in zip(terms[::2], terms[1::2])]
    return terms[0]


def permute_near(values):
    count = lax.axis_size("expert")
    return permute(values, pairs_of(2, count)), permute(values, pairs_of(4, count))


def permute_far(values):
    return permute(values, mixed_pairs(4, 2, lax.axis_size("expert")))


def permute_core(values):
    return permute(values, pairs_of(1, lax.axis_size("expert")))


def row_major(values):
    return with_layout_constraint(values, Layout(tuple(range(values.ndim))))


class PlaneSum:
    def __init__(self, even, odd, is_core0):
        self.even, self.odd, self.is_core0, self.kind = even, odd, is_core0, getattr(even, "dtype", BF)
        self.other = [None] * len(even)

    def take(self, j):
        return self.even[j].astype(F32) + self.other[j].astype(F32)

    def core(self, order):
        self.other = row_major(permute_core(row_major(order.now(self.odd))))
        return self.other

    def core_of(self, j, order):
        self.other[j] = permute_core(order.now(self.odd[j]))
        return self.other[j]

    def far(self, order):
        self.third = permute_far(order.now(self.take(3).astype(self.kind)))
        return self.third

    def near(self, order):
        count = lax.axis_size("expert")
        if not isinstance(self.other, list):
            self.other = order.now(self.other)
        third = self.third.astype(F32)
        to_x = (self.take(1) + jnp.where(self.is_core0, third, 0.0)).astype(self.kind)
        to_y = (self.take(2) + jnp.where(self.is_core0, 0.0, third)).astype(self.kind)
        to_x, to_y = order.now((to_x, to_y))
        self.sides = (permute(to_x, pairs_of(2, count)), permute(to_y, pairs_of(4, count)))
        return self.sides

    def total(self):
        return self.take(0) + self.sides[0].astype(F32) + self.sides[1].astype(F32)


def place_rows(pieces, me):
    parts, rows, width = pieces[0].shape
    whole = jnp.zeros((parts, len(pieces), rows, width), pieces[0].dtype)
    for r, piece in enumerate(pieces):
        whole = lax.dynamic_update_slice(whole, piece[:, None], (0, me ^ r, 0, 0))
    return whole.reshape(parts * len(pieces) * rows, width)


def piece_sum(even, odd, is_core0):
    parts = lax.axis_size("dp")
    cut = even.shape[:2] + (parts, even.shape[2] // parts, even.shape[3])
    return PlaneSum(even.reshape(cut), odd.reshape(cut), is_core0)


def relative_rows(me, width):
    parts, count = lax.axis_size("dp"), lax.axis_size("expert")
    rows = width // (parts * count)
    far = jnp.concatenate([jnp.arange(0, count, 2, dtype=jnp.int32), jnp.arange(1, count, 2, dtype=jnp.int32)])
    owner = jnp.arange(parts, dtype=jnp.int32)[None, :] * count + (me ^ far)[:, None]
    return (owner[:, :, None] * rows + jnp.arange(rows, dtype=jnp.int32)).reshape(width)


def local(
    tokens,
    cotangent,
    lengths,
    choices,
    attn_weight,
    attn_moment,
    attn_average,
    router_weight,
    router_moment,
    router_average,
    shared_weight,
    shared_moment,
    shared_average,
    routed_weight,
    routed_moment,
    routed_average,
    norm_gains,
    gain_moment,
    gain_average,
):
    seq_len, model_width = tokens.shape
    topk_count = choices.shape[1]
    head_dim = model_width // HEADS
    groups = lax.axis_size("expert")
    routed_count = routed_weight.shape[0] * groups
    capacity = (seq_len * topk_count * 8 // (7 * routed_count) + 7) // 8 * 8
    total_tokens = seq_len * groups * lax.axis_size("dp")
    step_root = 1.0 / math.sqrt(total_tokens)
    score_scale = 1.0 / math.sqrt(head_dim)
    me = lax.axis_index("expert")
    is_core0 = lax.rem(me, 2) == 0
    relative = me ^ jnp.arange(groups, dtype=jnp.int32)
    per_device = routed_weight.shape[0]
    positions = jnp.arange(seq_len, dtype=jnp.int32)
    length_here = lengths[0]
    valid_rows = (positions < length_here).astype(F32)[:, None]
    grad_out = cotangent.astype(F32) * valid_rows
    grad_out16 = grad_out.astype(BF)

    order = Order()
    select = lambda pair: jnp.where(is_core0, *pair)
    small = jnp.concatenate([router_weight, norm_gains.T], axis=1)
    small = jnp.pad(small[None], ((0, 1), (0, 0), (0, 128 - small.shape[1])))
    parts = lax.axis_size("dp")
    front_own = jnp.concatenate([attn_weight[:2], small], axis=2).astype(BF)
    back_own = attn_weight[2:].astype(BF)
    front_parts = [front_own] + [send_dp(front_own, k) for k in range(1, parts)]
    grad_near = permute_near(grad_out16)
    back_parts = [back_own] + [send_dp(back_own, k) for k in range(1, parts)]
    order.close(front_parts, grad_near)
    slab = routed_weight.shape[2]
    routed_low = [routed_weight[e].astype(BF) for e in range(per_device)]
    routed_low[0] = jnp.concatenate([routed_low[0], shared_weight.astype(BF)], axis=1)
    routed16 = [lax.all_gather(low, "dp", axis=0, tiled=False) for low in order.now(routed_low)]
    front = stack_dp(front_parts)

    choice_own = jnp.pad(choices.T.astype(BF), ((0, 16 - topk_count), (0, 0)))
    front_near = permute_near(order.now(front))
    choice_near = permute_near(order.now(choice_own))
    order.close(front_near, choice_near)
    back = stack_dp(order.now(back_parts))

    back_near = permute_near(order.now(back))
    front_far = permute_far(order.now(select(front_near)))
    choice_far = permute_far(order.now(select(choice_near)))
    front_core = [permute_core(order.now(p)) for p in (front, *front_near)]
    choice_core = [permute_core(order.now(p)) for p in (choice_own, *choice_near)]
    order.close(back_near, front_far, choice_far, front_core, choice_core)

    back_far = permute_far(order.now(select(back_near)))
    back_core = [permute_core(order.now(p)) for p in (back, *back_near)]
    front_core.append(permute_core(order.now(front_far)))
    choice_core.append(permute_core(order.now(choice_far)))
    order.close(back_far, back_core, front_core, choice_core)
    back_core.append(permute_core(order.now(back_far)))
    grad_far = permute_far(order.now(select(grad_near)))
    grad_core = [permute_core(order.now(p)) for p in (grad_out16, *grad_near)]
    front = [p for pair in zip((front, *front_near, front_far), front_core) for p in pair]
    back = [p for pair in zip((back, *back_near, back_far), back_core) for p in pair]
    choice_all = [p for pair in zip((choice_own, *choice_near, choice_far), choice_core) for p in pair]
    attn16 = [place_rows([p[:, j, :, :model_width] for p in front], me) for j in range(2)]
    attn16 += [place_rows([p[:, j] for p in back], me) for j in range(2)]
    small_all = place_rows([p[:, 0, :, model_width:] for p in front], me).T
    router16t = small_all[:routed_count]
    gains16 = small_all[routed_count : routed_count + 2]
    choice_all = jnp.stack([p[:topk_count] for p in choice_all]).astype(jnp.int32)
    own_experts = me * per_device + jnp.arange(per_device, dtype=jnp.int32)
    hits = jnp.any(choice_all[:, None] == own_experts[None, :, None, None], axis=2)
    before = (positions[:, None] < positions[None, :]).astype(BF)
    ranks = jnp.einsum("set,tu->seu", hits.astype(BF), before, preferred_element_type=F32).astype(jnp.int32)
    slot_all = jnp.where(hits, ranks, -1)
    choice_all = jnp.transpose(choice_all, (0, 2, 1))
    gain_first = gains16[0].astype(F32)
    gain_second = gains16[1].astype(F32)
    half_dim = head_dim // 2
    frequency = 10000.0 ** (-jnp.arange(half_dim, dtype=F32) / half_dim)
    angles = positions.astype(F32)[:, None] * frequency[None, :]
    cosine = jnp.concatenate([jnp.cos(angles), jnp.cos(angles)], axis=1)
    sine = jnp.concatenate([-jnp.sin(angles), jnp.sin(angles)], axis=1)
    gains = jnp.stack([gain_first, gain_second])
    first16, query16, key16, value16, context16, log_totals, hidden_state, second16 = attention_call(
        tokens, gains, cosine, sine, lengths, attn16, score_scale
    )
    order.close(second16, grad_far, grad_core)

    router_pad = jnp.pad(router16t, ((0, 128 - routed_count), (0, 0)))
    second_near = permute_near(second16)
    second_core = [permute_core(second16)]
    grad_core.append(permute_core(order.now(grad_far)))
    grads_even = (grad_out16, *grad_near, grad_far)
    seconds_even = [second16, *second_near]

    def pair(e, j, prev, gates):
        return expert_pair_call(
            own_experts[e][None],
            choice_all[2 * j : 2 * j + 2],
            slot_all[2 * j : 2 * j + 2, e],
            router_pad,
            routed16[e],
            order.now((seconds_even[j], second_core[j])),
            (grads_even[j], grad_core[j]),
            prev,
            gates,
            capacity,
        )

    order.close(second_core, grad_core)
    results = [[None] * 4 for _ in range(per_device)]
    results[0][0] = pair(0, 0, None, None)
    sort_rows = (jnp.arange(model_width, dtype=jnp.int32)[None, :] == relative_rows(me, model_width)[:, None]).astype(BF)
    sort = lambda values: lax.dot_general(
        sort_rows, values, (((1,), (1,)), ((), ())), preferred_element_type=F32
    ).astype(BF)
    sorted_rows = [sort(after(v, results[0][0][1])) for v in (first16, second16, context16, grad_out16)]
    order.close(second_near, results[0][0][1], sorted_rows)
    first_rel, second_rel, context_rel, out_rel = order.now(sorted_rows)

    second_far = permute_far(order.now(select(second_near)))
    second_core += [permute_core(order.now(p)) for p in second_near]
    order.close(second_core)
    shared_cut = order.now(routed16[0][:, :, slab:])
    shared_near = permute_near(shared_cut)
    results[0][1] = pair(0, 1, None, None)
    order.close(second_far, results[0][1][1], shared_near)
    seconds_even.append(second_far)
    second_core.append(permute_core(order.now(second_far)))
    shared_far = permute_far(order.now(select(shared_near)))
    shared_core = [permute_core(order.now(p)) for p in (shared_cut, *shared_near)]
    results[0][2] = pair(0, 2, None, None)
    order.close(second_core[3], results[0][2][1], shared_far, shared_core)
    shared_core.append(permute_core(order.now(shared_far)))
    results[0][3] = pair(0, 3, None, None)
    order.close(results[0][3][1], shared_core)
    shared_all = [p for both in zip((shared_cut, *shared_near, shared_far), order.now(shared_core)) for p in both]
    shared16 = [place_rows([p[:, j] for p in shared_all], me) for j in range(3)]
    shared_out, shared_back, shared_even, shared_odd = shared_call(
        order.now(second16), second_rel, grad_out16, out_rel, shared16
    )
    order.close(shared_back)
    routed_grads = []

    def finish_expert(e):
        grads = weight_grad_call(order.now([result[2] for result in results[e]]), parts)
        routed_grads.append(lax.psum_scatter(grads, "dp", scatter_dimension=0, tiled=False))
        return grads

    order.close(finish_expert(0))

    shared_sum = piece_sum(shared_even, shared_odd, is_core0)
    shared_core = shared_sum.core(order)
    for e in range(1, per_device):
        back_sum = PlaneSum([None] * 4, [None] * 4, is_core0) if e == per_device - 1 else None
        out_sum = PlaneSum([None] * 4, [None] * 4, is_core0) if e == per_device - 1 else None

        def step(j):
            results[e][j] = pair(e, j, results[e - 1][j][0], results[e - 1][j][3])
            if back_sum is not None:
                for total, found in zip((out_sum, back_sum), results[e][j][0]):
                    total.even[j], total.odd[j] = found

        step(3)
        order.close(results[e][3][1], shared_core)
        waits = []
        if back_sum is not None:
            waits += [back_sum.core_of(3, order), out_sum.core_of(3, order), shared_sum.far(order)]
        step(1)
        order.close(results[e][1][1], waits)
        if back_sum is not None:
            waits = [back_sum.far(order), back_sum.core_of(1, order), out_sum.core_of(1, order)]
        step(2)
        order.close(results[e][2][1], waits)
        if back_sum is not None:
            order.close(back_sum.core_of(2, order))
            sides = back_sum.near(order)
            waits = [out_sum.core_of(2, order)]
        step(0)
        if back_sum is not None:
            waits += [sides]
        order.close(results[e][0][1], waits)
        if back_sum is not None:
            waits = [back_sum.core_of(0, order), out_sum.far(order), out_sum.core_of(0, order)]
        order.close(finish_expert(e), waits)
    gate_grads = [jnp.concatenate([result[1][:, 0] for result in results[e]]) for e in range(per_device)]
    gate_sent = jnp.take(jnp.stack(gate_grads, axis=1), relative, axis=0)
    gate_back = lax.all_to_all(gate_sent, "expert", split_axis=0, concat_axis=0, tiled=True)
    grad_gate = gate_back.reshape(routed_count, seq_len).T
    logits = lax.dot_general(second16, router16t, (((1,), (1,)), ((), ())), preferred_element_type=F32)
    table = jnp.any(choices[:, :, None] == jnp.arange(routed_count, dtype=jnp.int32)[None, None, :], axis=1)
    chosen = jnp.where(table, logits, masked_score)
    chosen_exp = jnp.where(table, jnp.exp(chosen - jnp.max(chosen, axis=1, keepdims=True)), 0.0)
    gate_weights = chosen_exp / jnp.sum(chosen_exp, axis=1, keepdims=True)
    grad_second = shared_back
    grad_logits = grad_gate - gate_weights * jnp.sum(grad_gate, axis=1, keepdims=True)
    router_float = router16t.astype(F32)
    grad_second = grad_second + jnp.dot(grad_logits, router_float, precision=lax.Precision.HIGHEST)
    router_grad_full = lax.dot_general(
        grad_logits, second16.astype(F32), (((0,), (0,)), ((), ())), precision=lax.Precision.HIGHEST
    )
    order.close(order.now(grad_second))

    out_near = out_sum.near(order)
    grad_hidden_state, grad_context16, out_even, out_odd, grad_gain_second = hidden_back_call(
        order.now(grad_second), back_sum.take(0), sides, hidden_state, grad_out16, gains, context_rel, attn16[3]
    )
    order.close(grad_context16)

    shared_near = shared_sum.near(order)
    proj_sum = piece_sum(out_even, out_odd, is_core0)
    proj_core = proj_sum.core(order)
    grad_query16, grad_key16, grad_value16, head_even, head_odd = heads_back_call(
        query16, key16, value16, order.now(grad_context16), log_totals, cosine, sine, first_rel, lengths, score_scale
    )
    order.close(proj_core, grad_query16, out_near)

    head_sum = piece_sum(head_even, head_odd, is_core0)
    order.close(head_sum.core(order), proj_sum.far(order), shared_near)

    head_far = head_sum.far(order)
    proj_near = proj_sum.near(order)
    input_grad, grad_gain_first, input_square = input_back_call(
        order.now(grad_query16), grad_key16, grad_value16, tokens, gains, grad_hidden_state, lengths, attn16[:3]
    )
    block_value = hidden_state + shared_out + out_sum.total()
    order.close(head_far, input_grad, block_value)

    scalars = jnp.stack(
        [
            jnp.sum(valid_rows * block_value * block_value),
            input_square[0],
            length_here.astype(F32),
        ]
    )
    small_grads = jnp.concatenate([router_grad_full, grad_gain_first, grad_gain_second])
    scalars = jnp.broadcast_to(scalars[:, None], (3, model_width))
    small_grads = jnp.concatenate([small_grads, scalars])
    small_grads = jnp.pad(small_grads, ((0, 128 - small_grads.shape[0]), (0, 0)))
    small_grads = jnp.take(small_grads.T.reshape(parts, groups, -1, 128), relative, axis=1)
    head_near = head_sum.near(order)
    early_parts = update_call(
        0, order.now(routed_grads[0]), routed_weight, routed_moment, routed_average, [], rate_routed * step_root
    )
    order.close(head_near, proj_near, early_parts[-1])

    small_total = tree_sum(
        [small_grads[:, 0]] + [permute(order.now(small_grads[:, r]), pairs_of(r, groups)) for r in range(1, groups)]
    )
    attn_total = jnp.concatenate([head_sum.total(), proj_sum.total()]).astype(BF)
    attn_grad = sum_dp(attn_total, 1, order)
    shared_grad = sum_dp(shared_sum.total().astype(BF), 1, order)
    order.close(small_total)
    small_grad = sum_dp(small_total, 0, order)
    router_grad = small_grad[:, :routed_count]
    gain_grad = small_grad[:, routed_count : routed_count + 2].T
    row_sums = small_grad[0, routed_count + 2 : routed_count + 5]
    denominator = model_width * row_sums[2]
    masked_rms = jnp.stack(
        [jnp.sqrt(row_sums[0] / denominator), jnp.sqrt(row_sums[1] / denominator)]
    )
    attn_parts = update(
        attn_weight, attn_moment, attn_average, attn_grad, rate_attention * step_root
    )
    router_parts = update(
        router_weight, router_moment, router_average, router_grad, rate_router * step_root
    )
    shared_parts = update(
        shared_weight, shared_moment, shared_average, shared_grad, rate_shared * step_root
    )
    routed_parts = early_parts
    for e in range(1, per_device):
        routed_parts = update_call(
            e, routed_grads[e], routed_weight, routed_moment, routed_average, routed_parts, rate_routed * step_root
        )
    gain_parts = update(norm_gains, gain_moment, gain_average, gain_grad, rate_gains * step_root)
    return (
        block_value.astype(BF),
        input_grad,
        masked_rms,
        attn_parts[0],
        attn_parts[1],
        attn_parts[2],
        attn_parts[3],
        attn_parts[4],
        router_parts[0],
        router_parts[1],
        router_parts[2],
        router_parts[3],
        router_parts[4],
        shared_parts[0],
        shared_parts[1],
        shared_parts[2],
        shared_parts[3],
        shared_parts[4],
        routed_parts[0],
        routed_parts[1],
        routed_parts[2],
        routed_parts[3],
        routed_parts[4],
        gain_parts[0],
        gain_parts[1],
        gain_parts[2],
        gain_parts[3],
    )


def solution(mesh):
    placed = (
        P(("dp", "expert"), None),
        P(("dp", "expert"), None),
        P(("dp", "expert")),
        P(("dp", "expert"), None),
        P(None, ("dp", "expert"), None),
        P(None, ("dp", "expert"), None),
        P(None, ("dp", "expert"), None),
        P(("dp", "expert"), None),
        P(("dp", "expert"), None),
        P(("dp", "expert"), None),
        P(None, ("dp", "expert"), None),
        P(None, ("dp", "expert"), None),
        P(None, ("dp", "expert"), None),
        P("expert", None, "dp", None),
        P("expert", None, "dp", None),
        P("expert", None, "dp", None),
        P(None, ("dp", "expert")),
        P(None, ("dp", "expert")),
        P(None, ("dp", "expert")),
    )
    return jax.shard_map(
        local,
        mesh=mesh,
        in_specs=placed,
        out_specs=(
            P(("dp", "expert"), None),
            P(("dp", "expert"), None),
            P(),
            P(None, ("dp", "expert"), None),
            P(None, ("dp", "expert"), None),
            P(None, ("dp", "expert"), None),
            P(None, ("dp", "expert"), None),
            P(None, ("dp", "expert"), None),
            P(("dp", "expert"), None),
            P(("dp", "expert"), None),
            P(("dp", "expert"), None),
            P(("dp", "expert"), None),
            P(("dp", "expert"), None),
            P(None, ("dp", "expert"), None),
            P(None, ("dp", "expert"), None),
            P(None, ("dp", "expert"), None),
            P(None, ("dp", "expert"), None),
            P(None, ("dp", "expert"), None),
            P("expert", None, "dp", None),
            P("expert", None, "dp", None),
            P("expert", None, "dp", None),
            P("expert", None, "dp", None),
            P("expert", None, "dp", None),
            P(None, ("dp", "expert")),
            P(None, ("dp", "expert")),
            P(None, ("dp", "expert")),
            P(None, ("dp", "expert")),
        ),
        check_vma=False,
    )
```

time: 1630 us -> 768 us (0.47)
  blocking collectives: 381 us -> 0 us
  Pallas kernels: 0 us -> 320 us
  local copies, waits for them, and re-layouts: 374 us -> 71 us
  matrix products: 264 us -> 21.9 us
  waiting for transfers between devices: 403 us -> 166 us
  other arithmetic: 158 us -> 75.7 us
  starting transfers between devices: 16.3 us -> 83.5 us
    pallas_call x0 -> x17, Pallas kernels: none -> 320 us  [the longest x8 158 us: expert_pair_call(): pl.pallas_call(functools.partial(expert_pair_kernel, prev is None), out_s...]
    dot_general x39 -> x8, matrix products: 264 us -> 21.9 us  [the longest x4 13.4 us: local(): lax.dot_general(sort_rows, values, (((1,), (1,)), ((), ())), preferred_el...]
    all_to_all x3 -> x1, waiting for transfers between devices: 210 us -> 1.74 us  [local(): lax.all_to_all(gate_sent, 'expert', split_axis=0, concat_axis=0, tiled=True)]
    all_to_all x1 -> x0, blocking collectives: 178 us -> none  [local(): lax.all_to_all(send_grads, 'expert', split_axis=0, concat_axis=1, tiled=T...]
    ppermute x0 -> x90, waiting for transfers between devices: none -> 165 us  [the longest x75 111 us: permute(): return lax.ppermute(values, 'expert', pairs)]
    all_gather x2 -> x0, blocking collectives: 162 us -> none  [the longest x1 118 us: local(): lax.all_gather(router_weight.astype(jnp.bfloat16), ('dp', 'expert'), axis...]
    convert_element_type x5 -> x2, local copies, waits for them, and re-layouts: 136 us -> 2.16 us  [the longest x1 1.49 us: local(): routed_low = [routed_weight[e].astype(BF) for e in range(per_device)]]
    reduce_scatter x5 -> x2, waiting for transfers between devices: 131 us -> 0.01 us  [finish_expert(): lax.psum_scatter(grads, 'dp', scatter_dimension=0, tiled=False)]
  transfers between devices with their start and end apart: 12 -> 95, of which waited for: 5 -> 32; matrix products, arithmetic and copies ran while one was open for 45% -> 21% of each run, Pallas kernels for 0% -> 41%
where the time goes in v2:
time: 768 us; the launch traced here: 757 us
  Pallas kernels  320 us (42%)
  waiting for transfers between devices  166 us (22%)
  starting transfers between devices  83.5 us (11%)
  other arithmetic  75.7 us (10%)
  local copies, waits for them, and re-layouts  71 us (9%)
  matrix products  21.9 us (3%)
  between operations  18.4 us (2%)
    pallas_call x8, Pallas kernels, expert_pair_call(): pl.pallas_call(functools.partial(expert_pair_kernel, prev is None), out_s...  158 us
    ppermute x75, waiting for transfers between devices, permute(): return lax.ppermute(values, 'expert', pairs)  111 us
    ppermute x15, waiting for transfers between devices, send_dp(): lax.ppermute(values, 'dp', [(i, i ^ k) for i in range(lax.axis_size('dp'))])  53.9 us
    ppermute x75, starting transfers between devices, permute(): return lax.ppermute(values, 'expert', pairs)  48.2 us
    pallas_call x2, Pallas kernels, weight_grad_call(): pl.pallas_call(functools.partial(weight_grad_kernel, count), out_shape=ja...  46.3 us
    dynamic_update_slice x35, local copies, waits for them, and re-layouts, place_rows(): whole = lax.dynamic_update_slice(whole, piece[:, None], (0, me ^ r, 0, 0))  34 us
    ppermute x15, starting transfers between devices, send_dp(): lax.ppermute(values, 'dp', [(i, i ^ k) for i in range(lax.axis_size('dp'))])  31.2 us
    pallas_call x1, Pallas kernels, attention_call(): pl.pallas_call(functools.partial(attention_kernel, scale), out_shape=[hal...  23.6 us
  transfers between devices with their start and end apart: 95, of which 32 were waited for; matrix products, arithmetic and copies ran while one was open for 21% of the time, Pallas kernels for 41%

profile of v2, /device:TPU:0, one launch (start us, length us, event | category | flops | bytes accessed | tf_op | source)
XLA Modules:
  0.0 757.1 jit_solution(2955904251766409776)
XLA Ops:
  9.6 3.0 collective-permute-start.3
  16.2 2.6 collective-permute-start.1
  19.0 3.4 convert.53
  25.4 9.8 %collective-permute-done.1 = bf16[2,40,1408]{2,1,0:T(8,128)(2,1)S(1)} collective-permute-done((bf16[2,40,1408]{2,1,0:T(8,128)(2,1)S(1)}, bf16[2,40,1408]{2,1,0:T(8,128)(2,1)S(1)}, u32[]{:S(2)}, u32[]{:S(2)}) %collective-permute-start.1) | collective-permute-done | bytes 225312 | tf_op jit(solution)/shard_map/ppermute | solution.py:607
  35.2 6.3 collective-permute-done.3.refs_7_.refs_8_
  44.7 2.6 collective-permute-start.14
  65.6 2.5 broadcast_select_fusion
  68.1 13.9 %collective-permute-done.7 = bf16[16,512]{1,0:T(8,128)(2,1)S(1)} collective-permute-done((bf16[16,512]{1,0:T(8,128)(2,1)S(1)}, bf16[16,512]{1,0:T(8,128)(2,1)S(1)}, u32[]{:S(2)}, u32[]{:S(2)}) %collective-permute-start.7) | collective-permute-done | bytes 16416 | tf_op jit(solution)/shard_map/ppermute | solution.py:580
  83.6 2.2 collective-permute-done.8
  86.8 11.6 %collective-permute-done.15 = bf16[2,40,1280]{2,1,0:T(8,128)(2,1)S(1)} collective-permute-done((bf16[2,40,1280]{2,1,0:T(8,128)(2,1)S(1)}, bf16[2,40,1280]{2,1,0:T(8,128)(2,1)S(1)}, u32[]{:S(2)}, u32[]{:S(2)}) %collective-permute-start.15) | collective-permute-done | bytes 204832 | tf_op jit(solution)/shard_map/ppermute | solution.py:607
  106.6 20.3 %collective-permute-done.18 = bf16[16,512]{1,0:T(8,128)(2,1)S(1)} collective-permute-done((bf16[16,512]{1,0:T(8,128)(2,1)S(1)}, bf16[16,512]{1,0:T(8,128)(2,1)S(1)}, u32[]{:S(2)}, u32[]{:S(2)}) %collective-permute-start.18) | collective-permute-done | bytes 16416 | tf_op jit(solution)/shard_map/ppermute | solution.py:580
  159.0 2.7 slice_dynamic-update-slice_fusion
  161.7 23.6 %attention_forward.1 = (bf16[512,1280]{1,0:T(8,128)(2,1)}, bf16[512,1280]{1,0:T(8,128)(2,1)}, bf16[512,1280]{1,0:T(8,128)(2,1)}, bf16[512,1280]{1,0:T(8,128)(2,1...) custom-call(bf16[512,1280]{1,0:T(8,128)(2,1)} %tok_ref.3, ...), custom_call_target="tpu_custom_call" | custom-call | bytes 1 | tf_op jit(solution)/shard_map/attention_forward/pallas_call | solution.py:342
  192.3 20.6 %expert_pair.8 = (bf16[512,1280]{1,0:T(8,128)(2,1)}, bf16[512,1280]{1,0:T(8,128)(2,1)}, bf16[512,1280]{1,0:T(8,128)(2,1)}, bf16[512,1280]{1,0:T(8,128)(2,1)}, f3...) custom-call(s32[1]{0:T(128)} %get-tuple-element.789.refs_0_, ...), custom_call_target="tpu_custom_call" | custom-call | flops 5284823040 | bytes 1 | tf_op jit(solution)/shard_map/expert_pair/pallas_call | solution.py:180
  213.0 3.0 fusion.10.ctx_ref
  215.9 3.0 fusion.11.dout_rel_ref
  218.9 4.5 fusion.9.second_rel_ref
  223.4 3.0 fusion.8.first_ref
  232.7 18.9 %expert_pair.9 = (bf16[512,1280]{1,0:T(8,128)(2,1)}, bf16[512,1280]{1,0:T(8,128)(2,1)}, bf16[512,1280]{1,0:T(8,128)(2,1)}, bf16[512,1280]{1,0:T(8,128)(2,1)}, f3...) custom-call(s32[1]{0:T(128)} %get-tuple-element.789.refs_0_, ...), custom_call_target="tpu_custom_call" | custom-call | flops 5284823040 | bytes 1 | tf_op jit(solution)/shard_map/expert_pair/pallas_call | solution.py:180
  251.6 2.5 collective-permute-done.37.refs_5_.refs_6_
  254.1 9.1 %collective-permute-done.41 = bf16[4,3,40,896]{3,2,1,0:T(8,128)(2,1)S(1)} collective-permute-done((bf16[4,3,40,896]{3,2,1,0:T(8,128)(2,1)S(1)}, bf16[4,3,40,896]{3,2,1,0:T(8,128)(2,1)S(1)}, u32[]{:S(2)}, u32[]{:S(2)}) %collective-permute-start.41) | collective-permute-done | bytes 860192 | tf_op jit(solution)/shard_map/ppermute | solution.py:580
  265.3 18.7 %expert_pair.10 = (bf16[512,1280]{1,0:T(8,128)(2,1)}, bf16[512,1280]{1,0:T(8,128)(2,1)}, bf16[512,1280]{1,0:T(8,128)(2,1)}, bf16[512,1280]{1,0:T(8,128)(2,1)}, f...) custom-call(s32[1]{0:T(128)} %get-tuple-element.789.refs_0_, ...), custom_call_target="tpu_custom_call" | custom-call | flops 5284823040 | bytes 1 | tf_op jit(solution)/shard_map/expert_pair/pallas_call | solution.py:180
  288.5 18.6 %expert_pair.11 = (bf16[512,1280]{1,0:T(8,128)(2,1)}, bf16[512,1280]{1,0:T(8,128)(2,1)}, bf16[512,1280]{1,0:T(8,128)(2,1)}, bf16[512,1280]{1,0:T(8,128)(2,1)}, f...) custom-call(s32[1]{0:T(128)} %get-tuple-element.789.refs_0_, ...), custom_call_target="tpu_custom_call" | custom-call | flops 5284823040 | bytes 1 | tf_op jit(solution)/shard_map/expert_pair/pallas_call | solution.py:180
  317.3 20.6 %shared_expert.1 = (f32[512,1280]{1,0:T(8,128)}, f32[512,1280]{1,0:T(8,128)}, bf16[4,3,160,896]{3,2,1,0:T(8,128)(2,1)}, bf16[4,3,160,896]{3,2,1,0:T(8,128)(2,1)}) custom-call(bf16[512,1280]{1,0:T(8,128)(2,1)} %get-tuple-element.429.refs_5_.second_ref.refs_6_, bf16[1280,512]{1,0:T(8,128)(2,1)} %fusion.9.second_rel_ref, bf16[512,1280]{1,0:T(8,128)(2,1)} %copy-done.3, ...), custom_call_target="tpu_custom_call" | custom-call | bytes 1 | tf_op jit(solution)/shard_map/shared_expert/pallas_call | solution.py:539
  337.9 23.1 %expert_weights.2 = bf16[4,3,320,896]{3,2,1,0:T(8,128)(2,1)} custom-call(bf16[512,1280]{1,0:T(8,128)(2,1)} %get-tuple-element.376.refs_0_, bf16[512,1280]{1,0:T(8,128)(2,1)} %get-tuple-element.377.refs_1_, bf16[512,896]{1,0:T(8,128)(2,1)} %get-tuple-element.378.refs_2_, bf16[512,1792]{1,0:T(8,128)(2,1)} %get-tuple-element.379.refs_3_, ...), custom_call_target="tpu_custom_call" | custom-call | flops 14092861440 | bytes 1 | tf_op jit(solution)/shard_map/expert_weights/pallas_call | solution.py:251
  361.3 20.3 %expert_pair.12 = (bf16[512,1280]{1,0:T(8,128)(2,1)}, bf16[512,1280]{1,0:T(8,128)(2,1)}, bf16[512,1280]{1,0:T(8,128)(2,1)}, bf16[512,1280]{1,0:T(8,128)(2,1)}, f...) custom-call(s32[1]{0:T(128)} %get-tuple-element.790.refs_0_, ...), custom_call_target="tpu_custom_call" | custom-call | flops 5284823040 | bytes 1 | tf_op jit(solution)/shard_map/expert_pair/pallas_call | solution.py:180
  383.3 2.2 fusion.80
  385.5 2.3 fusion.36
  389.9 20.2 %expert_pair.13 = (bf16[512,1280]{1,0:T(8,128)(2,1)}, bf16[512,1280]{1,0:T(8,128)(2,1)}, bf16[512,1280]{1,0:T(8,128)(2,1)}, bf16[512,1280]{1,0:T(8,128)(2,1)}, f...) custom-call(s32[1]{0:T(128)} %get-tuple-element.790.refs_0_, ...), custom_call_target="tpu_custom_call" | custom-call | flops 5284823040 | bytes 1 | tf_op jit(solution)/shard_map/expert_pair/pallas_call | solution.py:180
  411.7 2.7 add_convert_fusion.1
  416.5 20.0 %expert_pair.14 = (bf16[512,1280]{1,0:T(8,128)(2,1)}, bf16[512,1280]{1,0:T(8,128)(2,1)}, bf16[512,1280]{1,0:T(8,128)(2,1)}, bf16[512,1280]{1,0:T(8,128)(2,1)}, f...) custom-call(s32[1]{0:T(128)} %get-tuple-element.790.refs_0_, ...), custom_call_target="tpu_custom_call" | custom-call | flops 5284823040 | bytes 1 | tf_op jit(solution)/shard_map/expert_pair/pallas_call | solution.py:180
  437.7 2.1 collective-permute-done.55
  439.9 4.8 fusion.15
  446.5 20.3 %expert_pair.15 = (bf16[512,1280]{1,0:T(8,128)(2,1)}, bf16[512,1280]{1,0:T(8,128)(2,1)}, bf16[512,1280]{1,0:T(8,128)(2,1)}, bf16[512,1280]{1,0:T(8,128)(2,1)}, f...) custom-call(s32[1]{0:T(128)} %get-tuple-element.790.refs_0_, ...), custom_call_target="tpu_custom_call" | custom-call | flops 5284823040 | bytes 1 | tf_op jit(solution)/shard_map/expert_pair/pallas_call | solution.py:180
  469.0 3.4 all-to-all-start
  472.5 3.1 add_convert_fusion
  477.4 4.5 convolution_add_fusion.dn_ref
  483.1 23.1 %expert_weights.3 = bf16[4,3,320,896]{3,2,1,0:T(8,128)(2,1)} custom-call(bf16[512,1280]{1,0:T(8,128)(2,1)} %get-tuple-element.465.refs_0_, bf16[512,1280]{1,0:T(8,128)(2,1)} %get-tuple-element.466.refs_1_, bf16[512,896]{1,0:T(8,128)(2,1)} %get-tuple-element.467.refs_2_, bf16[512,1792]{1,0:T(8,128)(2,1)} %get-tuple-element.468.refs_3_, ...), custom_call_target="tpu_custom_call" | custom-call | flops 14092861440 | bytes 1 | tf_op jit(solution)/shard_map/expert_weights/pallas_call | solution.py:251
  506.2 3.5 convert_add_fusion.base_ref
  509.7 11.9 %hidden_backward.1 = (f32[512,1280]{1,0:T(8,128)}, bf16[512,1280]{1,0:T(8,128)(2,1)}, bf16[4,1,160,1280]{3,2,1,0:T(8,128)(2,1)}, bf16[4,1,160,1280]{3,2,1,0:T(8,128)(2,1)}, f32[1,1280]{1,0:T(1,128)}) custom-call(f32[512,1280]{1,0:T(8,128)} %convolution_add_fusion.dn_ref, f32[512,1280]{1,0:T(8,128)} %convert_add_fusion.base_ref, ...), custom_call_target="tpu_custom_call" | custom-call | bytes 1 | tf_op jit(solution)/shard_map/hidden_backward/pallas_call | solution.py:394
  521.7 4.7 fusion.19
  528.4 23.2 %heads_backward.1 = (bf16[512,1280]{1,0:T(8,128)(2,1)}, bf16[512,1280]{1,0:T(8,128)(2,1)}, bf16[512,1280]{1,0:T(8,128)(2,1)}, bf16[4,3,160,1280]{3,2,1,0:T(8,128)(2,1)}, bf16[4,3,160,1280]{3,2,1,0:T(8,128)(2,1)}) custom-call(bf16[512,1280]{1,0:T(8,128)(2,1)} %get-tuple-element.486.q_ref, bf16[512,1280]{1,0:T(8,128)(2,1)} %get-tuple-element.487.k_ref, ...), custom_call_target="tpu_custom_call" | custom-call | bytes 1 | tf_op jit(solution)/shard_map/heads_backward/pallas_call | solution.py:450
  551.6 6.2 collective-permute-done.62
  561.4 2.5 fusion.32
  567.0 18.6 %collective-permute-done.67 = bf16[3,4,40,896]{3,2,1,0:T(8,128)(2,1)S(1)} collective-permute-done((bf16[3,4,40,896]{3,2,1,0:T(8,128)(2,1)S(1)}, bf16[3,4,40,896]{3,2,1,0:T(8,128)(2,1)S(1)}, u32[]{:S(2)}, u32[]{:S(2)}) %collective-permute-start.67) | collective-permute-done | bytes 860192 | tf_op jit(solution)/shard_map/ppermute | solution.py:580
  590.3 2.8 fusion.28
  593.1 3.8 collective-permute-done.66
  599.1 5.1 fusion.20
  604.2 2.3 fusion.43
  608.8 15.1 %input_backward.1 = (f32[512,1280]{1,0:T(8,128)}, f32[1,1280]{1,0:T(1,128)}, f32[1]{0:T(128)}) custom-call(bf16[512,1280]{1,0:T(8,128)(2,1)} %get-tuple-element.506.dq_ref, bf16[512,1280]{1,0:T(8,128)(2,1)} %get-tuple-element.507.dk_ref, bf16[512,1280]{1,0:T(8,128)(2,1)} %get-tuple-element.508.dv_ref, bf16[512,1280]{1,0:T(8,128)(2,1)} %tok_ref.3, ...), custom_call_target="tpu_custom_call" | custom-call | bytes 1 | tf_op jit(solution)/shard_map/input_backward/pallas_call | solution.py:490
  623.9 4.4 fusion.24
  633.2 11.0 %routed_update.2 = (f32[2,3,320,896]{3,2,1,0:T(8,128)}, f32[2,3,320,896]{3,2,1,0:T(8,128)}, f32[2,3,320,896]{3,2,1,0:T(8,128)}, f32[2,3,320,896]{3,2,1,0:T(8,128)}, bf16[2,3,320,896]{3,2,1,0:T(8,128)(2,1)}) custom-call(bf16[3,320,896]{2,1,0:T(8,128)(2,1)} %bitcast.269, f32[2,3,320,896]{3,2,1,0:T(8,128)} %w_ref.3, f32[2,3,320,896]{3,2,1,0:T(8,128)} %m_ref.3, ...), custom_call_target="tpu_custom_call" | custom-call | bytes 1 | tf_op jit(solution)/shard_map/routed_update/pallas_call | solution.py:564
  644.2 10.9 %collective-permute-done.70 = bf16[3,4,40,1280]{3,2,1,0:T(8,128)(2,1)} collective-permute-done((bf16[3,4,40,1280]{3,2,1,0:T(8,128)(2,1)}, bf16[3,4,40,1280]{3,2,1,0:T(8,128)(2,1)}, u32[]{:S(2)}, u32[]{:S(2)}) %collective-permute-start.70) | collective-permute-done | bytes 1228832 | tf_op jit(solution)/shard_map/ppermute | solution.py:580
  663.2 2.6 fusion.27
  666.0 2.7 collective-permute-done.77
  669.5 9.2 %collective-permute-start.81 = (f32[40,128]{0,1:T(8,128)}, f32[40,128]{0,1:T(8,128)S(1)}, u32[]{:S(2)}, u32[]{:S(2)}) collective-permute-start(f32[40,128]{0,1:T(8,128)} %copy.279), channel_id=1, source_target_pairs={{0,8},{8,0},{16,24},{24,16},{1,9},{9,1},{17,25},{25,17},{2,10},{10... | collective-permute-start | bytes 61448 | tf_op jit(solution)/shard_map/ppermute | solution.py:607
  679.3 5.5 collective-permute-start.83
  687.2 2.4 collective-permute-start.88
  691.8 2.3 collective-permute-start.85
  700.7 4.1 collective-permute-done.88
  706.7 2.2 fusion.74
  710.8 5.6 collective-permute-done.84
  716.4 20.3 %collective-permute-done.85 = bf16[4,40,1280]{2,1,0:T(8,128)(2,1)S(1)} collective-permute-done((bf16[4,40,1280]{2,1,0:T(8,128)(2,1)}, bf16[4,40,1280]{2,1,0:T(8,128)(2,1)S(1)}, u32[]{:S(2)}, u32[]{:S(2)}) %collective-permute-start.85) | collective-permute-done | bytes 409632 | tf_op jit(solution)/shard_map/ppermute | solution.py:607
  739.5 10.9 %routed_update.3 = (f32[2,3,320,896]{3,2,1,0:T(8,128)}, f32[2,3,320,896]{3,2,1,0:T(8,128)}, f32[2,3,320,896]{3,2,1,0:T(8,128)}, f32[2,3,320,896]{3,2,1,0:T(8,128)}, bf16[2,3,320,896]{3,2,1,0:T(8,128)(2,1)}) custom-call(bf16[3,320,896]{2,1,0:T(8,128)(2,1)} %bitcast.270, ...), custom_call_target="tpu_custom_call", output_to_operand_aliasing={{0}: (4, {}), {1}: (5, {}), {2}: (6, {}), {3}: (7, {}), {4}... | custom-call | bytes 1 | tf_op jit(solution)/shard_map/routed_update/pallas_call | solution.py:564
  (496 shorter events, 165.8 us)
Async XLA Ops:
  7.2 185.1 %all-gather.5.cloned.1.call-start = ((), (), s32[]{:S(2)}) async-start(), calls=%async_computation.5 | async-start | bytes 9676800 | tf_op jit(solution)/shard_map/all_gather | solution.py:760
  9.6 31.9 %collective-permute-start.3 = (bf16[512,1280]{1,0:T(8,128)(2,1)S(1)}, bf16[512,1280]{1,0:T(8,128)(2,1)}, u32[]{:S(2)}, u32[]{:S(2)}) collective-permute-start(bf16[512,1280]{1,0:T(8,128)(2,1)S(1)} %multiply_convert_fusion.refs_7_.dout_ref.refs_8_), channel_id=1, source_target_pairs={{0,2},{1,3},{2,0},{3,1},{4,6},{5,7},{6,4},{7,5},{8,10},{9,11},{10,... | collective-permute-start | bytes 3932168 | tf_op jit(solution)/shard_map/ppermute | solution.py:580
  12.6 30.3 %collective-permute-start.4 = (bf16[512,1280]{1,0:T(8,128)(2,1)S(1)}, bf16[512,1280]{1,0:T(8,128)(2,1)}, u32[]{:S(2)}, u32[]{:S(2)}) collective-permute-start(bf16[512,1280]{1,0:T(8,128)(2,1)S(1)} %multiply_convert_fusion.refs_7_.dout_ref.refs_8_), channel_id=1, source_target_pairs={{0,4},{1,5},{2,6},{3,7},{4,0},{5,1},{6,2},{7,3},{8,12},{9,13},{10,... | collective-permute-start | bytes 3932168 | tf_op jit(solution)/shard_map/ppermute | solution.py:580
  16.2 19.0 %collective-permute-start.1 = (bf16[2,40,1408]{2,1,0:T(8,128)(2,1)S(1)}, bf16[2,40,1408]{2,1,0:T(8,128)(2,1)S(1)}, u32[]{:S(2)}, u32[]{:S(2)}) collective-permute-start(bf16[2,40,1408]{2,1,0:T(8,128)(2,1)S(1)} %pad_maximum_fusion.3), channel_id=1, source_target_pairs={{0,16},{8,24},{16,0},{24,8},{1,17},{9,25},{17,1},{25,9},{2,18},{10... | collective-permute-start | bytes 675848 | tf_op jit(solution)/shard_map/ppermute | solution.py:607
  18.8 16.4 %collective-permute-start.2 = (bf16[2,40,1408]{2,1,0:T(8,128)(2,1)S(1)}, bf16[2,40,1408]{2,1,0:T(8,128)(2,1)S(1)}, u32[]{:S(2)}, u32[]{:S(2)}) collective-permute-start(bf16[2,40,1408]{2,1,0:T(8,128)(2,1)S(1)} %pad_maximum_fusion.3), channel_id=1, source_target_pairs={{0,24},{8,16},{16,8},{24,0},{1,25},{9,17},{17,9},{25,1},{2,26},{10... | collective-permute-start | bytes 675848 | tf_op jit(solution)/shard_map/ppermute | solution.py:607
  43.0 318.3 %all-gather.7.cloned.1.call-start = ((), (), s32[]{:S(2)}) async-start(), calls=%async_computation.6 | async-start | bytes 8601600 | tf_op jit(solution)/shard_map/all_gather | solution.py:760
  43.1 43.8 %collective-permute-start.13 = (bf16[2,40,1280]{2,1,0:T(8,128)(2,1)S(1)}, bf16[2,40,1280]{2,1,0:T(8,128)(2,1)}, u32[]{:S(2)}, u32[]{:S(2)}) collective-permute-start(bf16[2,40,1280]{2,1,0:T(8,128)(2,1)S(1)} %get-tuple-element.294), channel_id=1, source_target_pairs={{0,8},{8,0},{16,24},{24,16},{1,9},{9,1},{17,25},{25,17},{2,10},{10... | collective-permute-start | bytes 614408 | tf_op jit(solution)/shard_map/ppermute | solution.py:607
  44.7 42.1 %collective-permute-start.14 = (bf16[2,40,1280]{2,1,0:T(8,128)(2,1)S(1)}, bf16[2,40,1280]{2,1,0:T(8,128)(2,1)}, u32[]{:S(2)}, u32[]{:S(2)}) collective-permute-start(bf16[2,40,1280]{2,1,0:T(8,128)(2,1)S(1)} %get-tuple-element.294), channel_id=1, source_target_pairs={{0,16},{8,24},{16,0},{24,8},{1,17},{9,25},{17,1},{25,9},{2,18},{10... | collective-permute-start | bytes 614408 | tf_op jit(solution)/shard_map/ppermute | solution.py:607
  61.5 37.0 %collective-permute-start.5 = (bf16[4,2,40,1408]{3,2,1,0:T(8,128)(2,1)}, bf16[4,2,40,1408]{3,2,1,0:T(8,128)(2,1)}, u32[]{:S(2)}, u32[]{:S(2)}) collective-permute-start(bf16[4,2,40,1408]{3,2,1,0:T(8,128)(2,1)} %bitcast_dynamic-update-slice_fusion), channel_id=1, source_target_pairs={{0,2},{1,3},{2,0},{3,1},{4,6},{5,7},{6,4},{7,5},{8,10},{9,11},{10,... | collective-permute-start | bytes 2703368 | tf_op jit(solution)/shard_map/ppermute | solution.py:580
  62.0 36.4 %collective-permute-start.6 = (bf16[4,2,40,1408]{3,2,1,0:T(8,128)(2,1)}, bf16[4,2,40,1408]{3,2,1,0:T(8,128)(2,1)}, u32[]{:S(2)}, u32[]{:S(2)}) collective-permute-start(bf16[4,2,40,1408]{3,2,1,0:T(8,128)(2,1)} %bitcast_dynamic-update-slice_fusion), channel_id=1, source_target_pairs={{0,4},{1,5},{2,6},{3,7},{4,0},{5,1},{6,2},{7,3},{8,12},{9,13},{10,... | collective-permute-start | bytes 2703368 | tf_op jit(solution)/shard_map/ppermute | solution.py:580
  63.5 18.5 %collective-permute-start.7 = (bf16[16,512]{1,0:T(8,128)(2,1)S(1)}, bf16[16,512]{1,0:T(8,128)(2,1)S(1)}, u32[]{:S(2)}, u32[]{:S(2)}) collective-permute-start(bf16[16,512]{1,0:T(8,128)(2,1)S(1)} %pad.17), channel_id=1, source_target_pairs={{0,2},{1,3},{2,0},{3,1},{4,6},{5,7},{6,4},{7,5},{8,10},{9,11},{10,... | collective-permute-start | bytes 49160 | tf_op jit(solution)/shard_map/ppermute | solution.py:580
  65.0 568.2 %reduce-scatter.3.cloned.1.call-start = ((), (), s32[]{:S(2)}) async-start(), calls=%async_computation.3 | async-start | bytes 8601600 | tf_op jit(solution)/shard_map/reduce_scatter | solution.py:870
  100.5 28.2 %collective-permute-start.16 = (bf16[4,2,40,1280]{3,2,1,0:T(8,128)(2,1)S(1)}, bf16[4,2,40,1280]{3,2,1,0:T(8,128)(2,1)S(1)}, u32[]{:S(2)}, u32[]{:S(2)}) collective-permute-start(bf16[4,2,40,1280]{3,2,1,0:T(8,128)(2,1)S(1)} %bitcast_dynamic-update-slice_fusion.3), channel_id=1, source_target_pairs={{0,2},{1,3},{2,0},{3,1},{4,6},{5,7},{6,4},{7,5},{8,10},{9,11},{10,... | collective-permute-start | bytes 2457608 | tf_op jit(solution)/shard_map/ppermute | solution.py:580
  101.2 27.7 %collective-permute-start.17 = (bf16[4,2,40,1280]{3,2,1,0:T(8,128)(2,1)S(1)}, bf16[4,2,40,1280]{3,2,1,0:T(8,128)(2,1)S(1)}, u32[]{:S(2)}, u32[]{:S(2)}) collective-permute-start(bf16[4,2,40,1280]{3,2,1,0:T(8,128)(2,1)S(1)} %bitcast_dynamic-update-slice_fusion.3), channel_id=1, source_target_pairs={{0,4},{1,5},{2,6},{3,7},{4,0},{5,1},{6,2},{7,3},{8,12},{9,13},{10,... | collective-permute-start | bytes 2457608 | tf_op jit(solution)/shard_map/ppermute | solution.py:580
  104.0 25.0 %collective-permute-start.12 = (bf16[4,2,40,1408]{3,2,1,0:T(8,128)(2,1)S(1)}, bf16[4,2,40,1408]{3,2,1,0:T(8,128)(2,1)S(1)}, u32[]{:S(2)}, u32[]{:S(2)}) collective-permute-start(bf16[4,2,40,1408]{3,2,1,0:T(8,128)(2,1)S(1)} %broadcast_select_fusion.2), channel_id=1, source_target_pairs={{0,4},{1,3},{2,6},{3,1},{4,0},{5,7},{6,2},{7,5},{8,12},{9,11},{10,... | collective-permute-start | bytes 2703368 | tf_op jit(solution)/shard_map/ppermute | solution.py:580
  104.6 22.3 %collective-permute-start.18 = (bf16[16,512]{1,0:T(8,128)(2,1)S(1)}, bf16[16,512]{1,0:T(8,128)(2,1)S(1)}, u32[]{:S(2)}, u32[]{:S(2)}) collective-permute-start(bf16[16,512]{1,0:T(8,128)(2,1)S(1)} %broadcast_select_fusion.7), channel_id=1, source_target_pairs={{0,4},{1,3},{2,6},{3,1},{4,0},{5,7},{6,2},{7,5},{8,12},{9,11},{10,... | collective-permute-start | bytes 49160 | tf_op jit(solution)/shard_map/ppermute | solution.py:580
  106.1 20.8 %collective-permute-start.19 = (bf16[16,512]{1,0:T(8,128)(2,1)S(1)}, bf16[16,512]{1,0:T(8,128)(2,1)S(1)}, u32[]{:S(2)}, u32[]{:S(2)}) collective-permute-start(bf16[16,512]{1,0:T(8,128)(2,1)S(1)} %copy-done.60), channel_id=1, source_target_pairs={{0,1},{1,0},{2,3},{3,2},{4,5},{5,4},{6,7},{7,6},{8,9},{9,8},{10,11... | collective-permute-start | bytes 49160 | tf_op jit(solution)/shard_map/ppermute | solution.py:580
  133.4 13.9 %collective-permute-start.26 = (bf16[4,2,40,1280]{3,2,1,0:T(8,128)(2,1)S(1)}, bf16[4,2,40,1280]{3,2,1,0:T(8,128)(2,1)}, u32[]{:S(2)}, u32[]{:S(2)}) collective-permute-start(bf16[4,2,40,1280]{3,2,1,0:T(8,128)(2,1)S(1)} %broadcast_select_fusion.4), channel_id=1, source_target_pairs={{0,4},{1,3},{2,6},{3,1},{4,0},{5,7},{6,2},{7,5},{8,12},{9,11},{10,... | collective-permute-start | bytes 2457608 | tf_op jit(solution)/shard_map/ppermute | solution.py:580
  154.0 31.6 %collective-permute-start.35 = (bf16[512,1280]{1,0:T(8,128)(2,1)}, bf16[512,1280]{1,0:T(8,128)(2,1)}, u32[]{:S(2)}, u32[]{:S(2)}) collective-permute-start(bf16[512,1280]{1,0:T(8,128)(2,1)} %broadcast_select_fusion), channel_id=1, source_target_pairs={{0,4},{1,3},{2,6},{3,1},{4,0},{5,7},{6,2},{7,5},{8,12},{9,11},{10,... | collective-permute-start | bytes 3932168 | tf_op jit(solution)/shard_map/ppermute | solution.py:580
  155.0 30.6 %collective-permute-start.34 = (bf16[512,1280]{1,0:T(8,128)(2,1)}, bf16[512,1280]{1,0:T(8,128)(2,1)}, u32[]{:S(2)}, u32[]{:S(2)}) collective-permute-start(bf16[512,1280]{1,0:T(8,128)(2,1)} %collective-permute-done.4.refs_7_.refs_8_), channel_id=1, source_target_pairs={{0,1},{1,0},{2,3},{3,2},{4,5},{5,4},{6,7},{7,6},{8,9},{9,8},{10,11... | collective-permute-start | bytes 3932168 | tf_op jit(solution)/shard_map/ppermute | solution.py:580
  155.2 30.4 %collective-permute-start.33 = (bf16[512,1280]{1,0:T(8,128)(2,1)}, bf16[512,1280]{1,0:T(8,128)(2,1)}, u32[]{:S(2)}, u32[]{:S(2)}) collective-permute-start(bf16[512,1280]{1,0:T(8,128)(2,1)} %collective-permute-done.3.refs_7_.refs_8_), channel_id=1, source_target_pairs={{0,1},{1,0},{2,3},{3,2},{4,5},{5,4},{6,7},{7,6},{8,9},{9,8},{10,11... | collective-permute-start | bytes 3932168 | tf_op jit(solution)/shard_map/ppermute | solution.py:580
  155.5 30.1 %collective-permute-start.32 = (bf16[512,1280]{1,0:T(8,128)(2,1)}, bf16[512,1280]{1,0:T(8,128)(2,1)S(1)}, u32[]{:S(2)}, u32[]{:S(2)}) collective-permute-start(bf16[512,1280]{1,0:T(8,128)(2,1)} %copy-done.3), channel_id=1, source_target_pairs={{0,1},{1,0},{2,3},{3,2},{4,5},{5,4},{6,7},{7,6},{8,9},{9,8},{10,11... | collective-permute-start | bytes 3932168 | tf_op jit(solution)/shard_map/ppermute | solution.py:580
  190.0 36.4 %collective-permute-start.29 = (bf16[512,1280]{1,0:T(8,128)(2,1)}, bf16[512,1280]{1,0:T(8,128)(2,1)S(1)}, u32[]{:S(2)}, u32[]{:S(2)}) collective-permute-start(bf16[512,1280]{1,0:T(8,128)(2,1)} %get-tuple-element.429.refs_5_.second_ref.refs_6_), channel_id=1, source_target_pairs={{0,2},{1,3},{2,0},{3,1},{4,6},{5,7},{6,4},{7,5},{8,10},{9,11},{10,... | collective-permute-start | bytes 3932168 | tf_op jit(solution)/shard_map/ppermute | solution.py:580
  190.8 35.6 %collective-permute-start.30 = (bf16[512,1280]{1,0:T(8,128)(2,1)}, bf16[512,1280]{1,0:T(8,128)(2,1)S(1)}, u32[]{:S(2)}, u32[]{:S(2)}) collective-permute-start(bf16[512,1280]{1,0:T(8,128)(2,1)} %get-tuple-element.429.refs_5_.second_ref.refs_6_), channel_id=1, source_target_pairs={{0,4},{1,5},{2,6},{3,7},{4,0},{5,1},{6,2},{7,3},{8,12},{9,13},{10,... | collective-permute-start | bytes 3932168 | tf_op jit(solution)/shard_map/ppermute | solution.py:580
  227.1 27.0 %collective-permute-start.37 = (bf16[512,1280]{1,0:T(8,128)(2,1)S(1)}, bf16[512,1280]{1,0:T(8,128)(2,1)}, u32[]{:S(2)}, u32[]{:S(2)}) collective-permute-start(bf16[512,1280]{1,0:T(8,128)(2,1)S(1)} %broadcast_select_fusion.1), channel_id=1, source_target_pairs={{0,4},{1,3},{2,6},{3,1},{4,0},{5,7},{6,2},{7,5},{8,12},{9,11},{10,... | collective-permute-start | bytes 3932168 | tf_op jit(solution)/shard_map/ppermute | solution.py:580
  231.4 22.7 %collective-permute-start.40 = (bf16[4,3,40,896]{3,2,1,0:T(8,128)(2,1)S(1)}, bf16[4,3,40,896]{3,2,1,0:T(8,128)(2,1)S(1)}, u32[]{:S(2)}, u32[]{:S(2)}) collective-permute-start(bf16[4,3,40,896]{3,2,1,0:T(8,128)(2,1)S(1)} %slice.644), channel_id=1, source_target_pairs={{0,2},{1,3},{2,0},{3,1},{4,6},{5,7},{6,4},{7,5},{8,10},{9,11},{10,... | collective-permute-start | bytes 2580488 | tf_op jit(solution)/shard_map/ppermute | solution.py:580
  232.4 30.8 %collective-permute-start.41 = (bf16[4,3,40,896]{3,2,1,0:T(8,128)(2,1)S(1)}, bf16[4,3,40,896]{3,2,1,0:T(8,128)(2,1)S(1)}, u32[]{:S(2)}, u32[]{:S(2)}) collective-permute-start(bf16[4,3,40,896]{3,2,1,0:T(8,128)(2,1)S(1)} %slice.644), channel_id=1, source_target_pairs={{0,4},{1,5},{2,6},{3,7},{4,0},{5,1},{6,2},{7,3},{8,12},{9,13},{10,... | collective-permute-start | bytes 2580488 | tf_op jit(solution)/shard_map/ppermute | solution.py:580
  263.2 20.8 %collective-permute-start.42 = (bf16[512,1280]{1,0:T(8,128)(2,1)}, bf16[512,1280]{1,0:T(8,128)(2,1)}, u32[]{:S(2)}, u32[]{:S(2)}) collective-permute-start(bf16[512,1280]{1,0:T(8,128)(2,1)} %collective-permute-done.37.refs_5_.refs_6_), channel_id=1, source_target_pairs={{0,1},{1,0},{2,3},{3,2},{4,5},{5,4},{6,7},{7,6},{8,9},{9,8},{10,11... | collective-permute-start | bytes 3932168 | tf_op jit(solution)/shard_map/ppermute | solution.py:580
  263.2 20.8 %collective-permute-start.46 = (bf16[4,3,40,896]{3,2,1,0:T(8,128)(2,1)S(1)}, bf16[4,3,40,896]{3,2,1,0:T(8,128)(2,1)S(1)}, u32[]{:S(2)}, u32[]{:S(2)}) collective-permute-start(bf16[4,3,40,896]{3,2,1,0:T(8,128)(2,1)S(1)} %collective-permute-done.41), channel_id=1, source_target_pairs={{0,1},{1,0},{2,3},{3,2},{4,5},{5,4},{6,7},{7,6},{8,9},{9,8},{10,11... | collective-permute-start | bytes 2580488 | tf_op jit(solution)/shard_map/ppermute | solution.py:580
  263.7 20.3 %collective-permute-start.45 = (bf16[4,3,40,896]{3,2,1,0:T(8,128)(2,1)S(1)}, bf16[4,3,40,896]{3,2,1,0:T(8,128)(2,1)S(1)}, u32[]{:S(2)}, u32[]{:S(2)}) collective-permute-start(bf16[4,3,40,896]{3,2,1,0:T(8,128)(2,1)S(1)} %collective-permute-done.40), channel_id=1, source_target_pairs={{0,1},{1,0},{2,3},{3,2},{4,5},{5,4},{6,7},{7,6},{8,9},{9,8},{10,11... | collective-permute-start | bytes 2580488 | tf_op jit(solution)/shard_map/ppermute | solution.py:580
  263.7 20.3 %collective-permute-start.44 = (bf16[4,3,40,896]{3,2,1,0:T(8,128)(2,1)S(1)}, bf16[4,3,40,896]{3,2,1,0:T(8,128)(2,1)}, u32[]{:S(2)}, u32[]{:S(2)}) collective-permute-start(bf16[4,3,40,896]{3,2,1,0:T(8,128)(2,1)S(1)} %slice.644), channel_id=1, source_target_pairs={{0,1},{1,0},{2,3},{3,2},{4,5},{5,4},{6,7},{7,6},{8,9},{9,8},{10,11... | collective-permute-start | bytes 2580488 | tf_op jit(solution)/shard_map/ppermute | solution.py:580
  265.3 18.8 %collective-permute-start.43 = (bf16[4,3,40,896]{3,2,1,0:T(8,128)(2,1)}, bf16[4,3,40,896]{3,2,1,0:T(8,128)(2,1)}, u32[]{:S(2)}, u32[]{:S(2)}) collective-permute-start(bf16[4,3,40,896]{3,2,1,0:T(8,128)(2,1)} %broadcast_select_fusion.3), channel_id=1, source_target_pairs={{0,4},{1,3},{2,6},{3,1},{4,0},{5,7},{6,2},{7,5},{8,12},{9,11},{10,... | collective-permute-start | bytes 2580488 | tf_op jit(solution)/shard_map/ppermute | solution.py:580
  361.1 20.5 %collective-permute-start.48 = (bf16[4,3,4,40,896]{4,3,2,1,0:T(8,128)(2,1)}, bf16[4,3,4,40,896]{4,3,2,1,0:T(8,128)(2,1)S(1)}, u32[]{:S(2)}, u32[]{:S(2)}) collective-permute-start(bf16[4,3,4,40,896]{4,3,2,1,0:T(8,128)(2,1)} %bitcast.290), channel_id=1, source_target_pairs={{0,1},{1,0},{2,3},{3,2},{4,5},{5,4},{6,7},{7,6},{8,9},{9,8},{10,11... | collective-permute-start | bytes 10321928 | tf_op jit(solution)/shard_map/ppermute | solution.py:580
  381.6 28.6 %collective-permute-start.49 = (bf16[512,1280]{1,0:T(8,128)(2,1)}, bf16[512,1280]{1,0:T(8,128)(2,1)}, u32[]{:S(2)}, u32[]{:S(2)}) collective-permute-start(bf16[512,1280]{1,0:T(8,128)(2,1)} %get-tuple-element.409), channel_id=1, source_target_pairs={{0,1},{1,0},{2,3},{3,2},{4,5},{5,4},{6,7},{7,6},{8,9},{9,8},{10,11... | collective-permute-start | bytes 3932168 | tf_op jit(solution)/shard_map/ppermute | solution.py:580
  382.0 28.1 %collective-permute-start.50 = (bf16[512,1280]{1,0:T(8,128)(2,1)}, bf16[512,1280]{1,0:T(8,128)(2,1)S(1)}, u32[]{:S(2)}, u32[]{:S(2)}) collective-permute-start(bf16[512,1280]{1,0:T(8,128)(2,1)} %get-tuple-element.411), channel_id=1, source_target_pairs={{0,1},{1,0},{2,3},{3,2},{4,5},{5,4},{6,7},{7,6},{8,9},{9,8},{10,11... | collective-permute-start | bytes 3932168 | tf_op jit(solution)/shard_map/ppermute | solution.py:580
  387.8 22.3 %collective-permute-start.51 = (bf16[3,4,40,896]{3,2,1,0:T(8,128)(2,1)}, bf16[3,4,40,896]{3,2,1,0:T(8,128)(2,1)}, u32[]{:S(2)}, u32[]{:S(2)}) collective-permute-start(bf16[3,4,40,896]{3,2,1,0:T(8,128)(2,1)} %fusion.36), channel_id=1, source_target_pairs={{0,4},{1,3},{2,6},{3,1},{4,0},{5,7},{6,2},{7,5},{8,12},{9,11},{10,... | collective-permute-start | bytes 2580488 | tf_op jit(solution)/shard_map/ppermute | solution.py:580
  411.2 25.3 %collective-permute-start.54 = (bf16[512,1280]{1,0:T(8,128)(2,1)}, bf16[512,1280]{1,0:T(8,128)(2,1)S(1)}, u32[]{:S(2)}, u32[]{:S(2)}) collective-permute-start(bf16[512,1280]{1,0:T(8,128)(2,1)} %get-tuple-element.427), channel_id=1, source_target_pairs={{0,1},{1,0},{2,3},{3,2},{4,5},{5,4},{6,7},{7,6},{8,9},{9,8},{10,11... | collective-permute-start | bytes 3932168 | tf_op jit(solution)/shard_map/ppermute | solution.py:580
  411.2 25.3 %collective-permute-start.53 = (bf16[512,1280]{1,0:T(8,128)(2,1)}, bf16[512,1280]{1,0:T(8,128)(2,1)}, u32[]{:S(2)}, u32[]{:S(2)}) collective-permute-start(bf16[512,1280]{1,0:T(8,128)(2,1)} %get-tuple-element.425), channel_id=1, source_target_pairs={{0,1},{1,0},{2,3},{3,2},{4,5},{5,4},{6,7},{7,6},{8,9},{9,8},{10,11... | collective-permute-start | bytes 3932168 | tf_op jit(solution)/shard_map/ppermute | solution.py:580
  414.4 22.1 %collective-permute-start.52 = (bf16[512,1280]{1,0:T(8,128)(2,1)}, bf16[512,1280]{1,0:T(8,128)(2,1)}, u32[]{:S(2)}, u32[]{:S(2)}) collective-permute-start(bf16[512,1280]{1,0:T(8,128)(2,1)} %add_convert_fusion.1), channel_id=1, source_target_pairs={{0,4},{1,3},{2,6},{3,1},{4,0},{5,7},{6,2},{7,5},{8,12},{9,11},{10,... | collective-permute-start | bytes 3932168 | tf_op jit(solution)/shard_map/ppermute | solution.py:580
  444.6 37.3 %collective-permute-start.57 = (bf16[512,1280]{1,0:T(8,128)(2,1)}, bf16[512,1280]{1,0:T(8,128)(2,1)}, u32[]{:S(2)}, u32[]{:S(2)}) collective-permute-start(bf16[512,1280]{1,0:T(8,128)(2,1)} %get-tuple-element.442), channel_id=1, source_target_pairs={{0,2},{1,3},{2,0},{3,1},{4,6},{5,7},{6,4},{7,5},{8,10},{9,11},{10,... | collective-permute-start | bytes 3932168 | tf_op jit(solution)/shard_map/ppermute | solution.py:580
  446.2 35.7 %collective-permute-start.58 = (bf16[512,1280]{1,0:T(8,128)(2,1)}, bf16[512,1280]{1,0:T(8,128)(2,1)}, u32[]{:S(2)}, u32[]{:S(2)}) collective-permute-start(bf16[512,1280]{1,0:T(8,128)(2,1)} %get-tuple-element.443), channel_id=1, source_target_pairs={{0,4},{1,5},{2,6},{3,7},{4,0},{5,1},{6,2},{7,3},{8,12},{9,13},{10,... | collective-permute-start | bytes 3932168 | tf_op jit(solution)/shard_map/ppermute | solution.py:580
  446.5 35.4 %collective-permute-start.56 = (bf16[512,1280]{1,0:T(8,128)(2,1)}, bf16[512,1280]{1,0:T(8,128)(2,1)}, u32[]{:S(2)}, u32[]{:S(2)}) collective-permute-start(bf16[512,1280]{1,0:T(8,128)(2,1)} %get-tuple-element.439), channel_id=1, source_target_pairs={{0,1},{1,0},{2,3},{3,2},{4,5},{5,4},{6,7},{7,6},{8,9},{9,8},{10,11... | collective-permute-start | bytes 3932168 | tf_op jit(solution)/shard_map/ppermute | solution.py:580
  472.5 267.0 %reduce-scatter.5.cloned.1.call-start = ((), (), s32[]{:S(2)}) async-start(), calls=%async_computation.4 | async-start | bytes 8601600 | tf_op jit(solution)/shard_map/reduce_scatter | solution.py:870
  481.9 24.3 %collective-permute-start.61 = (bf16[512,1280]{1,0:T(8,128)(2,1)}, bf16[512,1280]{1,0:T(8,128)(2,1)}, u32[]{:S(2)}, u32[]{:S(2)}) collective-permute-start(bf16[512,1280]{1,0:T(8,128)(2,1)} %get-tuple-element.482), channel_id=1, source_target_pairs={{0,1},{1,0},{2,3},{3,2},{4,5},{5,4},{6,7},{7,6},{8,9},{9,8},{10,11... | collective-permute-start | bytes 3932168 | tf_op jit(solution)/shard_map/ppermute | solution.py:580
  482.1 24.1 %collective-permute-start.59 = (bf16[512,1280]{1,0:T(8,128)(2,1)}, bf16[512,1280]{1,0:T(8,128)(2,1)}, u32[]{:S(2)}, u32[]{:S(2)}) collective-permute-start(bf16[512,1280]{1,0:T(8,128)(2,1)} %get-tuple-element.444), channel_id=1, source_target_pairs={{0,1},{1,0},{2,3},{3,2},{4,5},{5,4},{6,7},{7,6},{8,9},{9,8},{10,11... | collective-permute-start | bytes 3932168 | tf_op jit(solution)/shard_map/ppermute | solution.py:580
  482.5 23.7 %collective-permute-start.60 = (bf16[512,1280]{1,0:T(8,128)(2,1)}, bf16[512,1280]{1,0:T(8,128)(2,1)}, u32[]{:S(2)}, u32[]{:S(2)}) collective-permute-start(bf16[512,1280]{1,0:T(8,128)(2,1)} %add_convert_fusion), channel_id=1, source_target_pairs={{0,4},{1,3},{2,6},{3,1},{4,0},{5,7},{6,2},{7,5},{8,12},{9,11},{10,... | collective-permute-start | bytes 3932168 | tf_op jit(solution)/shard_map/ppermute | solution.py:580
  521.6 37.7 %collective-permute-start.64 = (bf16[4,1,4,40,1280]{4,3,2,1,0:T(8,128)(2,1)}, bf16[4,1,4,40,1280]{4,3,2,1,0:T(8,128)(2,1)}, u32[]{:S(2)}, u32[]{:S(2)}) collective-permute-start(bf16[4,1,4,40,1280]{4,3,2,1,0:T(8,128)(2,1)} %bitcast.291), channel_id=1, source_target_pairs={{0,1},{1,0},{2,3},{3,2},{4,5},{5,4},{6,7},{7,6},{8,9},{9,8},{10,11... | collective-permute-start | bytes 4915208 | tf_op jit(solution)/shard_map/ppermute | solution.py:580
  526.4 31.5 %collective-permute-start.62 = (bf16[512,1280]{1,0:T(8,128)(2,1)}, bf16[512,1280]{1,0:T(8,128)(2,1)}, u32[]{:S(2)}, u32[]{:S(2)}) collective-permute-start(bf16[512,1280]{1,0:T(8,128)(2,1)} %get-tuple-element.484), channel_id=1, source_target_pairs={{0,2},{1,3},{2,0},{3,1},{4,6},{5,7},{6,4},{7,5},{8,10},{9,11},{10,... | collective-permute-start | bytes 3932168 | tf_op jit(solution)/shard_map/ppermute | solution.py:580
  528.1 31.2 %collective-permute-start.63 = (bf16[512,1280]{1,0:T(8,128)(2,1)}, bf16[512,1280]{1,0:T(8,128)(2,1)}, u32[]{:S(2)}, u32[]{:S(2)}) collective-permute-start(bf16[512,1280]{1,0:T(8,128)(2,1)} %get-tuple-element.485), channel_id=1, source_target_pairs={{0,4},{1,5},{2,6},{3,7},{4,0},{5,1},{6,2},{7,3},{8,12},{9,13},{10,... | collective-permute-start | bytes 3932168 | tf_op jit(solution)/shard_map/ppermute | solution.py:580
  559.3 31.0 %collective-permute-start.65 = (bf16[4,3,4,40,1280]{4,3,2,1,0:T(8,128)(2,1)}, bf16[4,3,4,40,1280]{4,3,2,1,0:T(8,128)(2,1)}, u32[]{:S(2)}, u32[]{:S(2)}) collective-permute-start(bf16[4,3,4,40,1280]{4,3,2,1,0:T(8,128)(2,1)} %bitcast.289), channel_id=1, source_target_pairs={{0,1},{1,0},{2,3},{3,2},{4,5},{5,4},{6,7},{7,6},{8,9},{9,8},{10,11... | collective-permute-start | bytes 14745608 | tf_op jit(solution)/shard_map/ppermute | solution.py:580
  563.9 21.6 %collective-permute-start.67 = (bf16[3,4,40,896]{3,2,1,0:T(8,128)(2,1)S(1)}, bf16[3,4,40,896]{3,2,1,0:T(8,128)(2,1)S(1)}, u32[]{:S(2)}, u32[]{:S(2)}) collective-permute-start(bf16[3,4,40,896]{3,2,1,0:T(8,128)(2,1)S(1)} %get-tuple-element.504), channel_id=1, source_target_pairs={{0,2},{1,3},{2,0},{3,1},{4,6},{5,7},{6,4},{7,5},{8,10},{9,11},{10,... | collective-permute-start | bytes 2580488 | tf_op jit(solution)/shard_map/ppermute | solution.py:580
  564.3 21.3 %collective-permute-start.68 = (bf16[3,4,40,896]{3,2,1,0:T(8,128)(2,1)S(1)}, bf16[3,4,40,896]{3,2,1,0:T(8,128)(2,1)S(1)}, u32[]{:S(2)}, u32[]{:S(2)}) collective-permute-start(bf16[3,4,40,896]{3,2,1,0:T(8,128)(2,1)S(1)} %get-tuple-element.505), channel_id=1, source_target_pairs={{0,4},{1,5},{2,6},{3,7},{4,0},{5,1},{6,2},{7,3},{8,12},{9,13},{10,... | collective-permute-start | bytes 2580488 | tf_op jit(solution)/shard_map/ppermute | solution.py:580
  596.8 27.0 %collective-permute-start.69 = (bf16[3,4,40,1280]{3,2,1,0:T(8,128)(2,1)}, bf16[3,4,40,1280]{3,2,1,0:T(8,128)(2,1)}, u32[]{:S(2)}, u32[]{:S(2)}) collective-permute-start(bf16[3,4,40,1280]{3,2,1,0:T(8,128)(2,1)} %fusion.28), channel_id=1, source_target_pairs={{0,4},{1,3},{2,6},{3,1},{4,0},{5,7},{6,2},{7,5},{8,12},{9,11},{10,... | collective-permute-start | bytes 3686408 | tf_op jit(solution)/shard_map/ppermute | solution.py:580
  606.5 37.7 %collective-permute-start.72 = (bf16[1,4,40,1280]{3,2,1,0:T(8,128)(2,1)}, bf16[1,4,40,1280]{3,2,1,0:T(8,128)(2,1)S(1)}, u32[]{:S(2)}, u32[]{:S(2)}) collective-permute-start(bf16[1,4,40,1280]{3,2,1,0:T(8,128)(2,1)} %get-tuple-element.520), channel_id=1, source_target_pairs={{0,2},{1,3},{2,0},{3,1},{4,6},{5,7},{6,4},{7,5},{8,10},{9,11},{10,... | collective-permute-start | bytes 1228808 | tf_op jit(solution)/shard_map/ppermute | solution.py:580
  607.1 37.2 %collective-permute-start.73 = (bf16[1,4,40,1280]{3,2,1,0:T(8,128)(2,1)}, bf16[1,4,40,1280]{3,2,1,0:T(8,128)(2,1)}, u32[]{:S(2)}, u32[]{:S(2)}) collective-permute-start(bf16[1,4,40,1280]{3,2,1,0:T(8,128)(2,1)} %get-tuple-element.521), channel_id=1, source_target_pairs={{0,4},{1,5},{2,6},{3,7},{4,0},{5,1},{6,2},{7,3},{8,12},{9,13},{10,... | collective-permute-start | bytes 1228808 | tf_op jit(solution)/shard_map/ppermute | solution.py:580
  628.3 26.8 %collective-permute-start.70 = (bf16[3,4,40,1280]{3,2,1,0:T(8,128)(2,1)}, bf16[3,4,40,1280]{3,2,1,0:T(8,128)(2,1)}, u32[]{:S(2)}, u32[]{:S(2)}) collective-permute-start(bf16[3,4,40,1280]{3,2,1,0:T(8,128)(2,1)} %get-tuple-element.517), channel_id=1, source_target_pairs={{0,2},{1,3},{2,0},{3,1},{4,6},{5,7},{6,4},{7,5},{8,10},{9,11},{10,... | collective-permute-start | bytes 3686408 | tf_op jit(solution)/shard_map/ppermute | solution.py:580
  628.6 26.9 %collective-permute-start.71 = (bf16[3,4,40,1280]{3,2,1,0:T(8,128)(2,1)}, bf16[3,4,40,1280]{3,2,1,0:T(8,128)(2,1)}, u32[]{:S(2)}, u32[]{:S(2)}) collective-permute-start(bf16[3,4,40,1280]{3,2,1,0:T(8,128)(2,1)} %get-tuple-element.518), channel_id=1, source_target_pairs={{0,4},{1,5},{2,6},{3,7},{4,0},{5,1},{6,2},{7,3},{8,12},{9,13},{10,... | collective-permute-start | bytes 3686408 | tf_op jit(solution)/shard_map/ppermute | solution.py:580
  669.5 20.2 %collective-permute-start.81 = (f32[40,128]{0,1:T(8,128)}, f32[40,128]{0,1:T(8,128)S(1)}, u32[]{:S(2)}, u32[]{:S(2)}) collective-permute-start(f32[40,128]{0,1:T(8,128)} %copy.279), channel_id=1, source_target_pairs={{0,8},{8,0},{16,24},{24,16},{1,9},{9,1},{17,25},{25,17},{2,10},{10... | collective-permute-start | bytes 61448 | tf_op jit(solution)/shard_map/ppermute | solution.py:607
  686.6 13.9 %collective-permute-start.87 = (bf16[3,40,896]{2,1,0:T(8,128)(2,1)}, bf16[3,40,896]{2,1,0:T(8,128)(2,1)S(1)}, u32[]{:S(2)}, u32[]{:S(2)}) collective-permute-start(bf16[3,40,896]{2,1,0:T(8,128)(2,1)} %get-tuple-element.537), channel_id=1, source_target_pairs={{0,8},{8,0},{16,24},{24,16},{1,9},{9,1},{17,25},{25,17},{2,10},{10... | collective-permute-start | bytes 645128 | tf_op jit(solution)/shard_map/ppermute | solution.py:607
  687.2 17.7 %collective-permute-start.88 = (bf16[3,40,896]{2,1,0:T(8,128)(2,1)}, bf16[3,40,896]{2,1,0:T(8,128)(2,1)S(1)}, u32[]{:S(2)}, u32[]{:S(2)}) collective-permute-start(bf16[3,40,896]{2,1,0:T(8,128)(2,1)} %get-tuple-element.538), channel_id=1, source_target_pairs={{0,16},{8,24},{16,0},{24,8},{1,17},{9,25},{17,1},{25,9},{2,18},{10... | collective-permute-start | bytes 645128 | tf_op jit(solution)/shard_map/ppermute | solution.py:607
  689.7 17.0 %collective-permute-start.89 = (bf16[3,40,896]{2,1,0:T(8,128)(2,1)S(1)}, bf16[3,40,896]{2,1,0:T(8,128)(2,1)S(1)}, u32[]{:S(2)}, u32[]{:S(2)}) collective-permute-start(bf16[3,40,896]{2,1,0:T(8,128)(2,1)S(1)} %copy-done.43), channel_id=1, source_target_pairs={{0,24},{8,16},{16,8},{24,0},{1,25},{9,17},{17,9},{25,1},{2,26},{10... | collective-permute-start | bytes 645128 | tf_op jit(solution)/shard_map/ppermute | solution.py:607
  691.2 25.2 %collective-permute-start.84 = (bf16[4,40,1280]{2,1,0:T(8,128)(2,1)}, bf16[4,40,1280]{2,1,0:T(8,128)(2,1)S(1)}, u32[]{:S(2)}, u32[]{:S(2)}) collective-permute-start(bf16[4,40,1280]{2,1,0:T(8,128)(2,1)} %get-tuple-element.534), channel_id=1, source_target_pairs={{0,8},{8,0},{16,24},{24,16},{1,9},{9,1},{17,25},{25,17},{2,10},{10... | collective-permute-start | bytes 1228808 | tf_op jit(solution)/shard_map/ppermute | solution.py:607
  691.8 44.8 %collective-permute-start.85 = (bf16[4,40,1280]{2,1,0:T(8,128)(2,1)}, bf16[4,40,1280]{2,1,0:T(8,128)(2,1)S(1)}, u32[]{:S(2)}, u32[]{:S(2)}) collective-permute-start(bf16[4,40,1280]{2,1,0:T(8,128)(2,1)} %get-tuple-element.535), channel_id=1, source_target_pairs={{0,16},{8,24},{16,0},{24,8},{1,17},{9,25},{17,1},{25,9},{2,18},{10... | collective-permute-start | bytes 1228808 | tf_op jit(solution)/shard_map/ppermute | solution.py:607
  700.5 36.2 %collective-permute-start.86 = (bf16[4,40,1280]{2,1,0:T(8,128)(2,1)}, bf16[4,40,1280]{2,1,0:T(8,128)(2,1)S(1)}, u32[]{:S(2)}, u32[]{:S(2)}) collective-permute-start(bf16[4,40,1280]{2,1,0:T(8,128)(2,1)} %get-tuple-element.536), channel_id=1, source_target_pairs={{0,24},{8,16},{16,8},{24,0},{1,25},{9,17},{17,9},{25,1},{2,26},{10... | collective-permute-start | bytes 1228808 | tf_op jit(solution)/shard_map/ppermute | solution.py:607
  (110 other events, 1304.9 us)
Sparse Core Ops, SparseCore 0:
  43.1 148.0 all-gather.4
  192.8 123.1 all-gather.6
  361.4 129.7 reduce-scatter.2
  528.6 130.3 reduce-scatter.4

commit v3 on v2

--- a/solution.py
+++ b/solution.py
@@ -366,7 +366,7 @@
 
 
 def hidden_back_kernel(
-    dn_ref, base_ref, side_x_ref, side_y_ref, hidden_ref, dout_ref, gain_ref, ctx_ref, wo, dhid_ref, dctx_ref, even_ref, odd_ref, gain_out, w_v, dattn_v, sem
+    dn_ref, logit_ref, router_ref, base_ref, side_x_ref, side_y_ref, hidden_ref, dout_ref, gain_ref, ctx_ref, wo, dhid_ref, dctx_ref, even_ref, odd_ref, gain_out, w_v, dattn_v, sem
 ):
     copy = pltpu.make_async_copy(wo, w_v, sem)
     copy.start()
@@ -374,7 +374,13 @@
     hidden = hidden_ref[...]
     inverse = lax.rsqrt(jnp.mean(hidden * hidden, axis=1, keepdims=True) + eps_norm)
     hat = hidden * inverse
-    dn = dn_ref[...] + base_ref[...] + side_x_ref[...].astype(F32) + side_y_ref[...].astype(F32)
+    logits = logit_ref[...]
+    high = logits.astype(BF)
+    rest = logits - high.astype(F32)
+    low = rest.astype(BF)
+    least = (rest - low.astype(F32)).astype(BF)
+    routers = sum(dot_nn(part, router_ref[...]) for part in (least, low, high))
+    dn = dn_ref[...] + routers + base_ref[...] + side_x_ref[...].astype(F32) + side_y_ref[...].astype(F32)
     gain_out[...] = jnp.sum(dn * hat, axis=0, keepdims=True)
     scaled = dn * gain_ref[1:2, :]
     mean = jnp.mean(scaled * hat, axis=1, keepdims=True)
@@ -387,20 +393,20 @@
         dctx_ref[:, c0 : c0 + cn] = dot_nt(dattn_v[...], w_v[c0 : c0 + cn, :]).astype(BF)
 
 
-def hidden_back_call(dn, base, sides, hidden, dout, gains, ctx_rel, wo):
+def hidden_back_call(dn, logits, router, base, sides, hidden, dout, gains, ctx_rel, wo):
     seq, width = hidden.shape
     half = jax.ShapeDtypeStruct((seq, width), BF)
     part = piece_shape(1, width, width)
     return pl.pallas_call(
         hidden_back_kernel,
         out_shape=[jax.ShapeDtypeStruct((seq, width), F32), half, part, part, jax.ShapeDtypeStruct((1, width), F32)],
-        in_specs=kernel_specs("vvvvvvvva"),
+        in_specs=kernel_specs("vvvvvvvvvva"),
         out_specs=kernel_specs("vvvvv"),
         scratch_shapes=[pltpu.VMEM((width, width), BF), pltpu.VMEM((seq, width), BF), pltpu.SemaphoreType.DMA],
         compiler_params=pltpu.CompilerParams(vmem_limit_bytes=VMEM_LIMIT),
-        cost_estimate=estimate(0),
+        cost_estimate=estimate(15 * seq * width * width),
         name="hidden_backward",
-    )(dn, base, *sides, hidden, dout, gains, ctx_rel, wo)
+    )(dn, logits, router, base, *sides, hidden, dout, gains, ctx_rel, wo)
 
 
 def heads_back_kernel(
@@ -439,21 +445,22 @@
         return carry
 
     lax.fori_loop(0, width // 256, heads, 0)
-    for j, grad_ref in ((2, dv_ref), (1, dk_ref), (0, dq_ref)):
-        store_pieces(even_ref, odd_ref, j, first_ref, grad_ref)
+    store_pieces(even_ref, odd_ref, 2, first_ref, dv_ref)
+    store_pieces(even_ref, odd_ref, 0, first_ref, dq_ref)
+    store_pieces(even_ref, odd_ref, 1, first_ref, dk_ref)
 
 
 def heads_back_call(q, k, v, dctx, lse, cosine, sine, first_rel, lengths, scale):
     seq, width = q.shape
     half = jax.ShapeDtypeStruct((seq, width), BF)
-    part = piece_shape(3, width, width)
+    wide = piece_shape(3, width, width)
     return pl.pallas_call(
         functools.partial(heads_back_kernel, scale),
-        out_shape=[half] * 3 + [part] * 2,
+        out_shape=[half] * 3 + [wide] * 2,
         in_specs=kernel_specs("vvvvvvvvs"),
         out_specs=kernel_specs("v" * 5),
         compiler_params=pltpu.CompilerParams(vmem_limit_bytes=VMEM_LIMIT),
-        cost_estimate=estimate(0),
+        cost_estimate=estimate(26 * seq * width * width),
         name="heads_backward",
     )(q, k, v, dctx, lse, cosine, sine, first_rel, lengths)
 
@@ -498,7 +505,7 @@
         out_specs=kernel_specs("vvs"),
         scratch_shapes=[pltpu.VMEM((3, width, width), BF), pltpu.VMEM((seq, width), F32), pltpu.SemaphoreType.DMA((3,))],
         compiler_params=pltpu.CompilerParams(vmem_limit_bytes=VMEM_LIMIT),
-        cost_estimate=estimate(0),
+        cost_estimate=estimate(18 * seq * width * width),
         name="input_backward",
     )(dq, dk, dv, tokens, gains, dhidden, lengths, *weights)
 
@@ -571,7 +578,7 @@
         out_specs=[full] * 5,
         input_output_aliases={4 + i: i for i in range(len(done))},
         compiler_params=pltpu.CompilerParams(vmem_limit_bytes=VMEM_LIMIT),
-        cost_estimate=estimate(0),
+        cost_estimate=estimate(10_000_000_000),
         name="routed_update",
     )(grad, weight, moment, average, *done)
 
@@ -607,20 +614,42 @@
     return lax.ppermute(values, "dp", [(i, i ^ k) for i in range(lax.axis_size("dp"))])
 
 
+def stack_kernel(at_ref, *refs):
+    count = (len(refs) - 2)
+    copies = [
+        pltpu.make_async_copy(refs[k], refs[count].at[at_ref[0] ^ k], refs[-1].at[k]) for k in range(count)
+    ]
+    for copy in copies:
+        copy.start()
+    for copy in copies:
+        copy.wait()
+
+
 def stack_dp(pieces):
-    whole = jnp.zeros((len(pieces),) + pieces[0].shape, pieces[0].dtype)
-    for k, piece in enumerate(pieces):
-        whole = lax.dynamic_update_slice(whole, piece[None], (lax.axis_index("dp") ^ k,) + (0,) * piece.ndim)
-    return whole
-
-
-def sum_dp(terms, axis, order):
+    count = len(pieces)
+    return pl.pallas_call(
+        stack_kernel,
+        out_shape=jax.ShapeDtypeStruct((count,) + pieces[0].shape, BF),
+        in_specs=kernel_specs("s" + "a" * count),
+        out_specs=pl.BlockSpec(memory_space=pltpu.VMEM),
+        scratch_shapes=[pltpu.SemaphoreType.DMA((count,))],
+        compiler_params=pltpu.CompilerParams(vmem_limit_bytes=VMEM_LIMIT),
+        cost_estimate=estimate(0),
+        name="stack_dp",
+    )(lax.axis_index("dp")[None], *pieces)
+
+
+def send_terms(terms, axis, order):
     here = lax.axis_index("dp")
     found = []
     for k in range(lax.axis_size("dp")):
         term = lax.dynamic_index_in_dim(terms, here ^ k, axis=axis, keepdims=False)
-        found.append((send_dp(order.now(term), k) if k else term).astype(F32))
-    return tree_sum(found)
+        found.append(send_dp(order.now(term), k) if k else order.now(term))
+    return found
+
+
+def sum_terms(found):
+    return tree_sum([term.astype(F32) for term in found])
 
 
 def tree_sum(terms):
@@ -673,7 +702,7 @@
         third = self.third.astype(F32)
         to_x = (self.take(1) + jnp.where(self.is_core0, third, 0.0)).astype(self.kind)
         to_y = (self.take(2) + jnp.where(self.is_core0, 0.0, third)).astype(self.kind)
-        to_x, to_y = order.now((to_x, to_y))
+        to_x, to_y = self.sent = order.now((to_x, to_y))
         self.sides = (permute(to_x, pairs_of(2, count)), permute(to_y, pairs_of(4, count)))
         return self.sides
 
@@ -681,12 +710,36 @@
         return self.take(0) + self.sides[0].astype(F32) + self.sides[1].astype(F32)
 
 
-def place_rows(pieces, me):
-    parts, rows, width = pieces[0].shape
-    whole = jnp.zeros((parts, len(pieces), rows, width), pieces[0].dtype)
-    for r, piece in enumerate(pieces):
-        whole = lax.dynamic_update_slice(whole, piece[:, None], (0, me ^ r, 0, 0))
-    return whole.reshape(parts * len(pieces) * rows, width)
+def place_kernel(cuts, at_ref, *refs):
+    sem = refs[-1]
+    outs = refs[-1 - len(cuts) : -1]
+    count = sem.shape[0]
+    copies = []
+    for i, (group, kind, column) in enumerate(cuts):
+        for r in range(count):
+            source = refs[group * count + r].at[:, kind, :, pl.ds(column, outs[i].shape[3])]
+            copies.append(pltpu.make_async_copy(source, outs[i].at[:, at_ref[0] ^ r], sem.at[r, i]))
+    for copy in copies:
+        copy.start()
+    for copy in copies:
+        copy.wait()
+
+
+def place_rows(groups, me, cuts):
+    count = len(groups[0])
+    parts, _, rows, _ = groups[0][0].shape
+    shapes = [(parts, count, rows, cut[3]) for cut in cuts]
+    out = pl.pallas_call(
+        functools.partial(place_kernel, [cut[:3] for cut in cuts]),
+        out_shape=[jax.ShapeDtypeStruct(shape, BF) for shape in shapes],
+        in_specs=kernel_specs("s" + "a" * (count * len(groups))),
+        out_specs=kernel_specs("v" * len(cuts)),
+        scratch_shapes=[pltpu.SemaphoreType.DMA((count, len(cuts)))],
+        compiler_params=pltpu.CompilerParams(vmem_limit_bytes=VMEM_LIMIT),
+        cost_estimate=estimate(0),
+        name="place_rows",
+    )(me[None], *[piece for group in groups for piece in group])
+    return [v.reshape(parts * count * rows, v.shape[3]) for v in out]
 
 
 def piece_sum(even, odd, is_core0):
@@ -750,46 +803,48 @@
     parts = lax.axis_size("dp")
     front_own = jnp.concatenate([attn_weight[:2], small], axis=2).astype(BF)
     back_own = attn_weight[2:].astype(BF)
+    shared_own = shared_weight.astype(BF)
     front_parts = [front_own] + [send_dp(front_own, k) for k in range(1, parts)]
     grad_near = permute_near(grad_out16)
-    back_parts = [back_own] + [send_dp(back_own, k) for k in range(1, parts)]
     order.close(front_parts, grad_near)
-    slab = routed_weight.shape[2]
-    routed_low = [routed_weight[e].astype(BF) for e in range(per_device)]
-    routed_low[0] = jnp.concatenate([routed_low[0], shared_weight.astype(BF)], axis=1)
-    routed16 = [lax.all_gather(low, "dp", axis=0, tiled=False) for low in order.now(routed_low)]
+    back_parts = [back_own] + [send_dp(order.now(back_own), k) for k in range(1, parts)]
     front = stack_dp(front_parts)
 
     choice_own = jnp.pad(choices.T.astype(BF), ((0, 16 - topk_count), (0, 0)))
+    choice_all = lax.all_to_all(
+        jnp.broadcast_to(choice_own, (groups,) + choice_own.shape), "expert", split_axis=0, concat_axis=0, tiled=True
+    )
     front_near = permute_near(order.now(front))
-    choice_near = permute_near(order.now(choice_own))
-    order.close(front_near, choice_near)
-    back = stack_dp(order.now(back_parts))
-
+    order.close(front_near, back_parts)
+    back = stack_dp(back_parts)
+    shared_cut = lax.all_to_all(
+        order.now(jnp.broadcast_to(shared_own, (parts,) + shared_own.shape)), "dp", split_axis=0, concat_axis=0, tiled=True
+    )
+
+    front_held = list(order.now((front, *front_near)))
     back_near = permute_near(order.now(back))
     front_far = permute_far(order.now(select(front_near)))
-    choice_far = permute_far(order.now(select(choice_near)))
     front_core = [permute_core(order.now(p)) for p in (front, *front_near)]
-    choice_core = [permute_core(order.now(p)) for p in (choice_own, *choice_near)]
-    order.close(back_near, front_far, choice_far, front_core, choice_core)
-
+    order.close(back_near, front_far, front_core, shared_cut)
+    routed_low = [routed_weight[e].astype(BF) for e in range(per_device)]
+    routed16 = [lax.all_gather(low, "dp", axis=0, tiled=False) for low in order.now(routed_low)]
+
+    back_held = list(order.now((back, *back_near)))
     back_far = permute_far(order.now(select(back_near)))
     back_core = [permute_core(order.now(p)) for p in (back, *back_near)]
     front_core.append(permute_core(order.now(front_far)))
-    choice_core.append(permute_core(order.now(choice_far)))
-    order.close(back_far, back_core, front_core, choice_core)
+    order.close(back_far, back_core, front_core)
     back_core.append(permute_core(order.now(back_far)))
-    grad_far = permute_far(order.now(select(grad_near)))
+    shared_near = permute_near(order.now(shared_cut))
     grad_core = [permute_core(order.now(p)) for p in (grad_out16, *grad_near)]
-    front = [p for pair in zip((front, *front_near, front_far), front_core) for p in pair]
-    back = [p for pair in zip((back, *back_near, back_far), back_core) for p in pair]
-    choice_all = [p for pair in zip((choice_own, *choice_near, choice_far), choice_core) for p in pair]
-    attn16 = [place_rows([p[:, j, :, :model_width] for p in front], me) for j in range(2)]
-    attn16 += [place_rows([p[:, j] for p in back], me) for j in range(2)]
-    small_all = place_rows([p[:, 0, :, model_width:] for p in front], me).T
+    front = [p for pair in zip((*front_held, front_far), front_core) for p in pair]
+    back = [p for pair in zip((*back_held, back_far), back_core) for p in pair]
+    cuts = [(group, kind, 0, model_width) for group in range(2) for kind in range(2)]
+    *attn16, small_all = place_rows([front, back], me, cuts + [(0, 0, model_width, 128)])
+    small_all = small_all.T
     router16t = small_all[:routed_count]
     gains16 = small_all[routed_count : routed_count + 2]
-    choice_all = jnp.stack([p[:topk_count] for p in choice_all]).astype(jnp.int32)
+    choice_all = jnp.take(choice_all[:, :topk_count], relative, axis=0).astype(jnp.int32)
     own_experts = me * per_device + jnp.arange(per_device, dtype=jnp.int32)
     hits = jnp.any(choice_all[:, None] == own_experts[None, :, None, None], axis=2)
     before = (positions[:, None] < positions[None, :]).astype(BF)
@@ -807,13 +862,14 @@
     first16, query16, key16, value16, context16, log_totals, hidden_state, second16 = attention_call(
         tokens, gains, cosine, sine, lengths, attn16, score_scale
     )
-    order.close(second16, grad_far, grad_core)
+    order.close(second16, shared_near, grad_core)
 
     router_pad = jnp.pad(router16t, ((0, 128 - routed_count), (0, 0)))
-    second_near = permute_near(second16)
+    shared_sent = order.now(select(shared_near))
+    shared_far = permute_far(shared_sent)
+    second_near = permute_near(after(second16, shared_sent))
     second_core = [permute_core(second16)]
-    grad_core.append(permute_core(order.now(grad_far)))
-    grads_even = (grad_out16, *grad_near, grad_far)
+    grads_even = [grad_out16, *grad_near]
     seconds_even = [second16, *second_near]
 
     def pair(e, j, prev, gates):
@@ -830,39 +886,42 @@
             capacity,
         )
 
-    order.close(second_core, grad_core)
-    results = [[None] * 4 for _ in range(per_device)]
-    results[0][0] = pair(0, 0, None, None)
+    shared_core = [permute_core(order.now(p)) for p in (shared_cut, *shared_near)]
     sort_rows = (jnp.arange(model_width, dtype=jnp.int32)[None, :] == relative_rows(me, model_width)[:, None]).astype(BF)
     sort = lambda values: lax.dot_general(
         sort_rows, values, (((1,), (1,)), ((), ())), preferred_element_type=F32
     ).astype(BF)
-    sorted_rows = [sort(after(v, results[0][0][1])) for v in (first16, second16, context16, grad_out16)]
-    order.close(second_near, results[0][0][1], sorted_rows)
-    first_rel, second_rel, context_rel, out_rel = order.now(sorted_rows)
-
+    out_rel, second_rel = [sort(order.now(v)) for v in (grad_out16, second16)]
+    order.close(second_core, shared_far, shared_core, out_rel, second_rel)
+    shared_core.append(permute_core(order.now(shared_far)))
+    shared_all = [p for both in zip((shared_cut, *shared_near, shared_far), shared_core) for p in both]
+    shared16 = place_rows([shared_all], me, [(0, j, 0, shared_weight.shape[2]) for j in range(3)])
+    shared_out, shared_back, shared_even, shared_odd = shared_call(
+        order.now(second16), second_rel, grad_out16, out_rel, shared16
+    )
+    order.close(shared_back, second_near)
+
+    results = [[None] * 4 for _ in range(per_device)]
     second_far = permute_far(order.now(select(second_near)))
     second_core += [permute_core(order.now(p)) for p in second_near]
-    order.close(second_core)
-    shared_cut = order.now(routed16[0][:, :, slab:])
-    shared_near = permute_near(shared_cut)
-    results[0][1] = pair(0, 1, None, None)
-    order.close(second_far, results[0][1][1], shared_near)
+    grad_far = permute_far(order.now(select(grad_near)))
+    grads_even.append(grad_far)
+    shared_sum = piece_sum(shared_even, shared_odd, is_core0)
+    shared_core = shared_sum.core(order)
+    results[0][0] = pair(0, 0, None, None)
+    first_rel, context_rel = [sort(after(v, results[0][0][1])) for v in (first16, context16)]
+    order.close(second_core, results[0][0][1], second_far, shared_core, grad_far, first_rel, context_rel)
+    grad_core.append(permute_core(order.now(grad_far)))
     seconds_even.append(second_far)
     second_core.append(permute_core(order.now(second_far)))
-    shared_far = permute_far(order.now(select(shared_near)))
-    shared_core = [permute_core(order.now(p)) for p in (shared_cut, *shared_near)]
+    shared_far = shared_sum.far(order)
+    results[0][1] = pair(0, 1, None, None)
+    order.close(second_core[3], grad_core[3], results[0][1][1], shared_far)
+    shared_near = shared_sum.near(order)
     results[0][2] = pair(0, 2, None, None)
-    order.close(second_core[3], results[0][2][1], shared_far, shared_core)
-    shared_core.append(permute_core(order.now(shared_far)))
+    order.close(results[0][2][1])
     results[0][3] = pair(0, 3, None, None)
-    order.close(results[0][3][1], shared_core)
-    shared_all = [p for both in zip((shared_cut, *shared_near, shared_far), order.now(shared_core)) for p in both]
-    shared16 = [place_rows([p[:, j] for p in shared_all], me) for j in range(3)]
-    shared_out, shared_back, shared_even, shared_odd = shared_call(
-        order.now(second16), second_rel, grad_out16, out_rel, shared16
-    )
-    order.close(shared_back)
+    order.close(results[0][3][1], shared_near)
     routed_grads = []
 
     def finish_expert(e):
@@ -871,9 +930,6 @@
         return grads
 
     order.close(finish_expert(0))
-
-    shared_sum = piece_sum(shared_even, shared_odd, is_core0)
-    shared_core = shared_sum.core(order)
     for e in range(1, per_device):
         back_sum = PlaneSum([None] * 4, [None] * 4, is_core0) if e == per_device - 1 else None
         out_sum = PlaneSum([None] * 4, [None] * 4, is_core0) if e == per_device - 1 else None
@@ -885,10 +941,10 @@
                     total.even[j], total.odd[j] = found
 
         step(3)
-        order.close(results[e][3][1], shared_core)
+        order.close(results[e][3][1])
         waits = []
         if back_sum is not None:
-            waits += [back_sum.core_of(3, order), out_sum.core_of(3, order), shared_sum.far(order)]
+            waits += [back_sum.core_of(3, order), out_sum.core_of(3, order)]
         step(1)
         order.close(results[e][1][1], waits)
         if back_sum is not None:
@@ -901,36 +957,33 @@
             waits = [out_sum.core_of(2, order)]
         step(0)
         if back_sum is not None:
-            waits += [sides]
+            gate_grads = [jnp.concatenate([result[1][:, 0] for result in row]) for row in results]
+            gate_sent = jnp.take(jnp.stack(gate_grads, axis=1), relative, axis=0)
+            gate_back = lax.all_to_all(gate_sent, "expert", split_axis=0, concat_axis=0, tiled=True)
+            waits += [sides, gate_back]
         order.close(results[e][0][1], waits)
         if back_sum is not None:
             waits = [back_sum.core_of(0, order), out_sum.far(order), out_sum.core_of(0, order)]
         order.close(finish_expert(e), waits)
-    gate_grads = [jnp.concatenate([result[1][:, 0] for result in results[e]]) for e in range(per_device)]
-    gate_sent = jnp.take(jnp.stack(gate_grads, axis=1), relative, axis=0)
-    gate_back = lax.all_to_all(gate_sent, "expert", split_axis=0, concat_axis=0, tiled=True)
-    grad_gate = gate_back.reshape(routed_count, seq_len).T
+    grad_gate = order.now(gate_back).reshape(routed_count, seq_len).T
     logits = lax.dot_general(second16, router16t, (((1,), (1,)), ((), ())), preferred_element_type=F32)
     table = jnp.any(choices[:, :, None] == jnp.arange(routed_count, dtype=jnp.int32)[None, None, :], axis=1)
     chosen = jnp.where(table, logits, masked_score)
     chosen_exp = jnp.where(table, jnp.exp(chosen - jnp.max(chosen, axis=1, keepdims=True)), 0.0)
     gate_weights = chosen_exp / jnp.sum(chosen_exp, axis=1, keepdims=True)
-    grad_second = shared_back
     grad_logits = grad_gate - gate_weights * jnp.sum(grad_gate, axis=1, keepdims=True)
-    router_float = router16t.astype(F32)
-    grad_second = grad_second + jnp.dot(grad_logits, router_float, precision=lax.Precision.HIGHEST)
+    wide_logits = jnp.pad(grad_logits, ((0, 0), (0, 128 - routed_count)))
     router_grad_full = lax.dot_general(
         grad_logits, second16.astype(F32), (((0,), (0,)), ((), ())), precision=lax.Precision.HIGHEST
     )
-    order.close(order.now(grad_second))
+    order.close(order.now(wide_logits))
 
     out_near = out_sum.near(order)
     grad_hidden_state, grad_context16, out_even, out_odd, grad_gain_second = hidden_back_call(
-        order.now(grad_second), back_sum.take(0), sides, hidden_state, grad_out16, gains, context_rel, attn16[3]
+        shared_back, order.now(wide_logits), router_pad, back_sum.take(0), sides, hidden_state, grad_out16, gains, context_rel, attn16[3]
     )
     order.close(grad_context16)
 
-    shared_near = shared_sum.near(order)
     proj_sum = piece_sum(out_even, out_odd, is_core0)
     proj_core = proj_sum.core(order)
     grad_query16, grad_key16, grad_value16, head_even, head_odd = heads_back_call(
@@ -939,16 +992,27 @@
     order.close(proj_core, grad_query16, out_near)
 
     head_sum = piece_sum(head_even, head_odd, is_core0)
-    order.close(head_sum.core(order), proj_sum.far(order), shared_near)
+    proj_far = proj_sum.far(order)
+    head_core = head_sum.core(order)
+    input_grad, grad_gain_first, input_square = input_back_call(
+        order.now(grad_query16), grad_key16, grad_value16, tokens, gains, grad_hidden_state, lengths, attn16[:3]
+    )
+    order.close(head_core, proj_far, input_grad)
 
     head_far = head_sum.far(order)
     proj_near = proj_sum.near(order)
-    input_grad, grad_gain_first, input_square = input_back_call(
-        order.now(grad_query16), grad_key16, grad_value16, tokens, gains, grad_hidden_state, lengths, attn16[:3]
-    )
-    block_value = hidden_state + shared_out + out_sum.total()
-    order.close(head_far, input_grad, block_value)
-
+    shared_grad = lax.all_to_all(
+        jnp.swapaxes(shared_sum.total().astype(BF), 0, 1), "dp", split_axis=0, concat_axis=0, tiled=True
+    )
+    early_parts = update_call(
+        0, order.now(routed_grads[0]), routed_weight, routed_moment, routed_average, [], rate_routed * step_root
+    )
+    order.close(head_far, proj_near, early_parts[-1])
+
+    head_near = head_sum.near(order)
+    proj_found = send_terms(after(proj_sum.total().astype(BF), head_sum.sent), 1, order)
+    held = head_sum.sent
+    block_value = after(hidden_state, held) + shared_out + out_sum.total()
     scalars = jnp.stack(
         [
             jnp.sum(valid_rows * block_value * block_value),
@@ -960,21 +1024,23 @@
     scalars = jnp.broadcast_to(scalars[:, None], (3, model_width))
     small_grads = jnp.concatenate([small_grads, scalars])
     small_grads = jnp.pad(small_grads, ((0, 128 - small_grads.shape[0]), (0, 0)))
-    small_grads = jnp.take(small_grads.T.reshape(parts, groups, -1, 128), relative, axis=1)
-    head_near = head_sum.near(order)
-    early_parts = update_call(
-        0, order.now(routed_grads[0]), routed_weight, routed_moment, routed_average, [], rate_routed * step_root
-    )
-    order.close(head_near, proj_near, early_parts[-1])
-
-    small_total = tree_sum(
-        [small_grads[:, 0]] + [permute(order.now(small_grads[:, r]), pairs_of(r, groups)) for r in range(1, groups)]
-    )
-    attn_total = jnp.concatenate([head_sum.total(), proj_sum.total()]).astype(BF)
-    attn_grad = sum_dp(attn_total, 1, order)
-    shared_grad = sum_dp(shared_sum.total().astype(BF), 1, order)
-    order.close(small_total)
-    small_grad = sum_dp(small_total, 0, order)
+    small_grads = jnp.swapaxes(small_grads.T.reshape(parts, groups, -1, 128), 0, 1)
+    small_found = lax.all_to_all(small_grads, "expert", split_axis=0, concat_axis=0, tiled=True)
+    routed_parts = early_parts
+    for e in range(1, per_device):
+        routed_parts = update_call(
+            e, order.now(routed_grads[e]), routed_weight, routed_moment, routed_average, routed_parts, rate_routed * step_root
+        )
+    order.close(head_near, routed_parts[-1])
+
+    head_total = order.now(head_sum.total().astype(BF))
+    head_found = send_terms(head_total, 1, order)
+    proj_found, shared_grad, small_found = after((proj_found, shared_grad, small_found), head_total)
+    small_total = tree_sum([small_found[r] for r in range(groups)])
+    small_found = lax.all_to_all(small_total, "dp", split_axis=0, concat_axis=0, tiled=True)
+    small_grad = tree_sum([small_found[d] for d in range(parts)])
+    shared_grad = sum_terms([shared_grad[d] for d in range(parts)])
+    attn_grad = jnp.concatenate([sum_terms(head_found), sum_terms(proj_found)])
     router_grad = small_grad[:, :routed_count]
     gain_grad = small_grad[:, routed_count : routed_count + 2].T
     row_sums = small_grad[0, routed_count + 2 : routed_count + 5]
@@ -991,11 +1057,6 @@
     shared_parts = update(
         shared_weight, shared_moment, shared_average, shared_grad, rate_shared * step_root
     )
-    routed_parts = early_parts
-    for e in range(1, per_device):
-        routed_parts = update_call(
-            e, routed_grads[e], routed_weight, routed_moment, routed_average, routed_parts, rate_routed * step_root
-        )
     gain_parts = update(norm_gains, gain_moment, gain_average, gain_grad, rate_gains * step_root)
     return (
         block_value.astype(BF),

time: 768 us -> 718 us (0.935)
  local copies, waits for them, and re-layouts: 71 us -> 43 us
  waiting for transfers between devices: 166 us -> 140 us
  Pallas kernels: 320 us -> 343 us
  matrix products: 21.9 us -> 13.4 us
    dynamic_update_slice x42 -> x0, local copies, waits for them, and re-layouts: 38.1 us -> none  [the longest x35 34 us: place_rows(): whole = lax.dynamic_update_slice(whole, piece[:, None], (0, me ^ r, 0, 0))]
    ppermute x75 -> x61, waiting for transfers between devices: 111 us -> 84.3 us  [permute(): return lax.ppermute(values, 'expert', pairs)]
    ppermute x15 -> x12, waiting for transfers between devices: 53.9 us -> 30.1 us  [send_dp(): lax.ppermute(values, 'dp', [(i, i ^ k) for i in range(lax.axis_size('dp'))])]
    pallas_call x0 -> x4, Pallas kernels: none -> 20.4 us  [the longest x2 16 us: place_rows(): pl.pallas_call(functools.partial(place_kernel, [cut[:3] for cut in cuts])...]
    all_to_all x0 -> x5, starting transfers between devices: none -> 19.8 us  [the longest x1 4.78 us: local(): lax.all_to_all(small_total, 'dp', split_axis=0, concat_axis=0, tiled=True)]
    all_to_all x0 -> x5, waiting for transfers between devices: none -> 19.7 us  [the longest x1 19.7 us: local(): lax.all_to_all(small_total, 'dp', split_axis=0, concat_axis=0, tiled=True)]
    ppermute x15 -> x12, starting transfers between devices: 31.2 us -> 17.6 us  [send_dp(): lax.ppermute(values, 'dp', [(i, i ^ k) for i in range(lax.axis_size('dp'))])]
    ppermute x75 -> x61, starting transfers between devices: 48.2 us -> 37.4 us  [permute(): return lax.ppermute(values, 'expert', pairs)]
  transfers between devices with their start and end apart: 95 -> 83, of which waited for: 32 -> 22; matrix products, arithmetic and copies ran while one was open for 21% -> 16% of each run, Pallas kernels for 41% -> 48%
where the time goes in v3:
time: 718 us; the launch traced here: 713 us
  Pallas kernels  343 us (48%)
  waiting for transfers between devices  140 us (19%)
  starting transfers between devices  79.6 us (11%)
  other arithmetic  75.3 us (10%)
  local copies, waits for them, and re-layouts  43 us (6%)
  between operations  18.2 us (3%)
  matrix products  13.4 us (2%)
    pallas_call x8, Pallas kernels, expert_pair_call(): pl.pallas_call(functools.partial(expert_pair_kernel, prev is None), out_s...  159 us
    ppermute x61, waiting for transfers between devices, permute(): return lax.ppermute(values, 'expert', pairs)  84.3 us
    pallas_call x2, Pallas kernels, weight_grad_call(): pl.pallas_call(functools.partial(weight_grad_kernel, count), out_shape=ja...  46.2 us
    ppermute x61, starting transfers between devices, permute(): return lax.ppermute(values, 'expert', pairs)  37.4 us
    ppermute x12, waiting for transfers between devices, send_dp(): lax.ppermute(values, 'dp', [(i, i ^ k) for i in range(lax.axis_size('dp'))])  30.1 us
    pallas_call x1, Pallas kernels, attention_call(): pl.pallas_call(functools.partial(attention_kernel, scale), out_shape=[hal...  23.4 us
    pallas_call x1, Pallas kernels, heads_back_call(): pl.pallas_call(functools.partial(heads_back_kernel, scale), out_shape=[ha...  23.2 us
    pallas_call x2, Pallas kernels, update_call(): pl.pallas_call(functools.partial(update_kernel, rate), grid=(kinds, cuts)...  22 us
  transfers between devices with their start and end apart: 83, of which 22 were waited for; matrix products, arithmetic and copies ran while one was open for 16% of the time, Pallas kernels for 48%

profile of v3, /device:TPU:0, one launch (start us, length us, event | category | flops | bytes accessed | tf_op | source)
XLA Modules:
  0.0 712.5 jit_solution(9478023555993744007)
XLA Ops:
  9.6 3.0 collective-permute-start.3
  16.9 2.6 collective-permute-start.1
  19.7 6.0 collective-permute-done.refs_1_
  25.7 10.2 %collective-permute-done.1.refs_2_ = bf16[2,40,1408]{2,1,0:T(8,128)(2,1)S(1)} collective-permute-done((bf16[2,40,1408]{2,1,0:T(8,128)(2,1)S(1)}, bf16[2,40,1408]{2,1,0:T(8,128)(2,1)S(1)}, u32[]{:S(2)}, u32[]{:S(2)}) %collective-permute-start.1) | collective-permute-done | bytes 225312 | tf_op jit(solution)/shard_map/ppermute | solution.py:614
  36.6 2.3 stack_dp.2.refs_0_
  38.9 2.6 collective-permute-done.3.refs_7_.refs_8_
  46.6 2.6 collective-permute-start.8
  49.4 3.3 collective-permute-done.7.refs_1_
  52.7 10.6 %collective-permute-done.8.refs_2_ = bf16[2,40,1280]{2,1,0:T(8,128)(2,1)S(1)} collective-permute-done((bf16[2,40,1280]{2,1,0:T(8,128)(2,1)S(1)}, bf16[2,40,1280]{2,1,0:T(8,128)(2,1)S(1)}, u32[]{:S(2)}, u32[]{:S(2)}) %collective-permute-start.8) | collective-permute-done | bytes 204832 | tf_op jit(solution)/shard_map/ppermute | solution.py:614
  69.4 4.4 all-to-all-start
  75.5 12.9 %collective-permute-done.14.refs_10_ = bf16[4,2,40,1280]{3,2,1,0:T(8,128)(2,1)} collective-permute-done((bf16[4,2,40,1280]{3,2,1,0:T(8,128)(2,1)}, bf16[4,2,40,1280]{3,2,1,0:T(8,128)(2,1)}, u32[]{:S(2)}, u32[]{:S(2)}) %collective-permute-start.14) | collective-permute-done | bytes 819232 | tf_op jit(solution)/shard_map/ppermute | solution.py:587
  89.0 3.4 convert.49
  94.4 10.3 %collective-permute-done.15.refs_12_ = bf16[4,2,40,1280]{3,2,1,0:T(8,128)(2,1)S(1)} collective-permute-done((bf16[4,2,40,1280]{3,2,1,0:T(8,128)(2,1)S(1)}, bf16[4,2,40,1280]{3,2,1,0:T(8,128)(2,1)S(1)}, u32[]{:S(2)}, u32[]{:S(2)}) %collective-permute-start.15) | collective-permute-done | bytes 819232 | tf_op jit(solution)/shard_map/ppermute | solution.py:587
  110.9 11.4 %collective-permute-done.20.refs_14_ = bf16[4,2,40,1280]{3,2,1,0:T(8,128)(2,1)} collective-permute-done((bf16[4,2,40,1280]{3,2,1,0:T(8,128)(2,1)S(1)}, bf16[4,2,40,1280]{3,2,1,0:T(8,128)(2,1)}, u32[]{:S(2)}, u32[]{:S(2)}) %collective-permute-start.20) | collective-permute-done | bytes 819232 | tf_op jit(solution)/shard_map/ppermute | solution.py:587
  125.4 3.4 all-to-all-start.1
  135.6 10.0 %place_rows.2 = (bf16[4,8,40,1280]{3,2,1,0:T(8,128)(2,1)}, bf16[4,8,40,1280]{3,2,1,0:T(8,128)(2,1)}, bf16[4,8,40,1280]{3,2,1,0:T(8,128)(2,1)}, bf16[4,8,40,1280]{3,2,1,0:T(8,128)(2,1)}, bf16[4,8,40,128]{3,2,1,0:T(8,128)(2,1)}) custom-call(s32[1]{0:T(128)} %bitcast.at_ref, bf16[4,2,40,1408]{3,2,1,0:T(8,128)(2,1)} %stack_dp.2.refs_0_, ...), custom_call_target="tpu_custom_call" | custom-call | bytes 1 | tf_op jit(solution)/shard_map/place_rows/pallas_call | solution.py:732
  147.4 23.4 %attention_forward.1 = (bf16[512,1280]{1,0:T(8,128)(2,1)}, bf16[512,1280]{1,0:T(8,128)(2,1)}, bf16[512,1280]{1,0:T(8,128)(2,1)}, bf16[512,1280]{1,0:T(8,128)(2,1...) custom-call(bf16[512,1280]{1,0:T(8,128)(2,1)} %tok_ref.3, ...), custom_call_target="tpu_custom_call" | custom-call | bytes 1 | tf_op jit(solution)/shard_map/attention_forward/pallas_call | solution.py:342
  171.9 2.3 broadcast_select_fusion.3
  175.3 3.0 fusion.9.second_rel_ref
  180.4 3.0 fusion.8.dout_rel_ref
  183.4 10.2 %collective-permute-done.28.refs_6_ = bf16[4,3,40,896]{3,2,1,0:T(8,128)(2,1)} collective-permute-done((bf16[4,3,40,896]{3,2,1,0:T(8,128)(2,1)}, bf16[4,3,40,896]{3,2,1,0:T(8,128)(2,1)}, u32[]{:S(2)}, u32[]{:S(2)}) %collective-permute-start.28) | collective-permute-done | bytes 860192 | tf_op jit(solution)/shard_map/ppermute | solution.py:587
  197.0 6.0 place_rows.3
  203.0 20.5 %shared_expert.1 = (f32[512,1280]{1,0:T(8,128)}, f32[512,1280]{1,0:T(8,128)}, bf16[4,3,160,896]{3,2,1,0:T(8,128)(2,1)}, bf16[4,3,160,896]{3,2,1,0:T(8,128)(2,1)}) custom-call(bf16[512,1280]{1,0:T(8,128)(2,1)} %get-tuple-element.437.second_ref.refs_5_.refs_6_, bf16[1280,512]{1,0:T(8,128)(2,1)} %fusion.9.second_rel_ref, bf16[512,1280]{1,0:T(8,128)(2,1)} %copy-done.3, ...), custom_call_target="tpu_custom_call" | custom-call | bytes 1 | tf_op jit(solution)/shard_map/shared_expert/pallas_call | solution.py:546
  232.7 20.6 %expert_pair.8 = (bf16[512,1280]{1,0:T(8,128)(2,1)}, bf16[512,1280]{1,0:T(8,128)(2,1)}, bf16[512,1280]{1,0:T(8,128)(2,1)}, bf16[512,1280]{1,0:T(8,128)(2,1)}, f3...) custom-call(s32[1]{0:T(128)} %get-tuple-element.708.refs_0_, ...), custom_call_target="tpu_custom_call" | custom-call | flops 5284823040 | bytes 1 | tf_op jit(solution)/shard_map/expert_pair/pallas_call | solution.py:180
  253.4 3.0 fusion.11.ctx_ref
  256.4 3.0 fusion.10.first_ref
  259.4 2.6 collective-permute-done.37.refs_5_.refs_6_
  264.2 2.9 collective-permute-done.40.refs_6_.refs_7_
  268.1 18.9 %expert_pair.9 = (bf16[512,1280]{1,0:T(8,128)(2,1)}, bf16[512,1280]{1,0:T(8,128)(2,1)}, bf16[512,1280]{1,0:T(8,128)(2,1)}, bf16[512,1280]{1,0:T(8,128)(2,1)}, f3...) custom-call(s32[1]{0:T(128)} %get-tuple-element.708.refs_0_, ...), custom_call_target="tpu_custom_call" | custom-call | flops 5284823040 | bytes 1 | tf_op jit(solution)/shard_map/expert_pair/pallas_call | solution.py:180
  290.8 19.0 %expert_pair.10 = (bf16[512,1280]{1,0:T(8,128)(2,1)}, bf16[512,1280]{1,0:T(8,128)(2,1)}, bf16[512,1280]{1,0:T(8,128)(2,1)}, bf16[512,1280]{1,0:T(8,128)(2,1)}, f...) custom-call(s32[1]{0:T(128)} %get-tuple-element.708.refs_0_, ...), custom_call_target="tpu_custom_call" | custom-call | flops 5284823040 | bytes 1 | tf_op jit(solution)/shard_map/expert_pair/pallas_call | solution.py:180
  309.9 19.1 %expert_pair.11 = (bf16[512,1280]{1,0:T(8,128)(2,1)}, bf16[512,1280]{1,0:T(8,128)(2,1)}, bf16[512,1280]{1,0:T(8,128)(2,1)}, bf16[512,1280]{1,0:T(8,128)(2,1)}, f...) custom-call(s32[1]{0:T(128)} %get-tuple-element.708.refs_0_, ...), custom_call_target="tpu_custom_call" | custom-call | flops 5284823040 | bytes 1 | tf_op jit(solution)/shard_map/expert_pair/pallas_call | solution.py:180
  330.0 23.1 %expert_weights.2 = bf16[4,3,320,896]{3,2,1,0:T(8,128)(2,1)} custom-call(bf16[512,1280]{1,0:T(8,128)(2,1)} %get-tuple-element.388.refs_0_, bf16[512,1280]{1,0:T(8,128)(2,1)} %get-tuple-element.389.refs_1_, bf16[512,896]{1,0:T(8,128)(2,1)} %get-tuple-element.390.refs_2_, bf16[512,1792]{1,0:T(8,128)(2,1)} %get-tuple-element.391.refs_3_, ...), custom_call_target="tpu_custom_call" | custom-call | flops 14092861440 | bytes 1 | tf_op jit(solution)/shard_map/expert_weights/pallas_call | solution.py:251
  353.1 3.7 all-gather.7.cloned.1.call-done
  356.8 20.5 %expert_pair.12 = (bf16[512,1280]{1,0:T(8,128)(2,1)}, bf16[512,1280]{1,0:T(8,128)(2,1)}, bf16[512,1280]{1,0:T(8,128)(2,1)}, bf16[512,1280]{1,0:T(8,128)(2,1)}, f...) custom-call(s32[1]{0:T(128)} %get-tuple-element.709.refs_0_, ...), custom_call_target="tpu_custom_call" | custom-call | flops 5284823040 | bytes 1 | tf_op jit(solution)/shard_map/expert_pair/pallas_call | solution.py:180
  377.8 20.3 %expert_pair.13 = (bf16[512,1280]{1,0:T(8,128)(2,1)}, bf16[512,1280]{1,0:T(8,128)(2,1)}, bf16[512,1280]{1,0:T(8,128)(2,1)}, bf16[512,1280]{1,0:T(8,128)(2,1)}, f...) custom-call(s32[1]{0:T(128)} %get-tuple-element.709.refs_0_, ...), custom_call_target="tpu_custom_call" | custom-call | flops 5284823040 | bytes 1 | tf_op jit(solution)/shard_map/expert_pair/pallas_call | solution.py:180
  399.8 2.8 add_convert_fusion.1
  406.2 20.5 %expert_pair.14 = (bf16[512,1280]{1,0:T(8,128)(2,1)}, bf16[512,1280]{1,0:T(8,128)(2,1)}, bf16[512,1280]{1,0:T(8,128)(2,1)}, bf16[512,1280]{1,0:T(8,128)(2,1)}, f...) custom-call(s32[1]{0:T(128)} %get-tuple-element.709.refs_0_, ...), custom_call_target="tpu_custom_call" | custom-call | flops 5284823040 | bytes 1 | tf_op jit(solution)/shard_map/expert_pair/pallas_call | solution.py:180
  430.1 3.9 fusion.15
  435.7 20.4 %expert_pair.15 = (bf16[512,1280]{1,0:T(8,128)(2,1)}, bf16[512,1280]{1,0:T(8,128)(2,1)}, bf16[512,1280]{1,0:T(8,128)(2,1)}, bf16[512,1280]{1,0:T(8,128)(2,1)}, f...) custom-call(s32[1]{0:T(128)} %get-tuple-element.709.refs_0_, ...), custom_call_target="tpu_custom_call" | custom-call | flops 5284823040 | bytes 1 | tf_op jit(solution)/shard_map/expert_pair/pallas_call | solution.py:180
  461.1 4.0 all-to-all-start.2
  465.1 3.1 add_convert_fusion
  471.6 23.1 %expert_weights.3 = bf16[4,3,320,896]{3,2,1,0:T(8,128)(2,1)} custom-call(bf16[512,1280]{1,0:T(8,128)(2,1)} %get-tuple-element.466.refs_0_, bf16[512,1280]{1,0:T(8,128)(2,1)} %get-tuple-element.467.refs_1_, bf16[512,896]{1,0:T(8,128)(2,1)} %get-tuple-element.468.refs_2_, bf16[512,1792]{1,0:T(8,128)(2,1)} %get-tuple-element.469.refs_3_, ...), custom_call_target="tpu_custom_call" | custom-call | flops 14092861440 | bytes 1 | tf_op jit(solution)/shard_map/expert_weights/pallas_call | solution.py:251
  500.8 3.5 convert_add_fusion.base_ref
  504.3 13.5 %hidden_backward.1 = (f32[512,1280]{1,0:T(8,128)}, bf16[512,1280]{1,0:T(8,128)(2,1)}, bf16[4,1,160,1280]{3,2,1,0:T(8,128)(2,1)}, bf16[4,1,160,1280]{3,2,1,0:T(8,128)(2,1)}, f32[1,1280]{1,0:T(1,128)}) custom-call(f32[512,1280]{1,0:T(8,128)} %get-tuple-element.335.dn_ref, f32[512,128]{1,0:T(8,128)} %pad.24.logit_ref, ...), custom_call_target="tpu_custom_call" | custom-call | flops 12582912000 | bytes 1 | tf_op jit(solution)/shard_map/hidden_backward/pallas_call | solution.py:400
  518.1 4.3 fusion.19
  524.4 23.2 %heads_backward.1 = (bf16[512,1280]{1,0:T(8,128)(2,1)}, bf16[512,1280]{1,0:T(8,128)(2,1)}, bf16[512,1280]{1,0:T(8,128)(2,1)}, bf16[4,3,160,1280]{3,2,1,0:T(8,128)(2,1)}, bf16[4,3,160,1280]{3,2,1,0:T(8,128)(2,1)}) custom-call(bf16[512,1280]{1,0:T(8,128)(2,1)} %get-tuple-element.316.q_ref, bf16[512,1280]{1,0:T(8,128)(2,1)} %get-tuple-element.317.k_ref, ...), custom_call_target="tpu_custom_call" | custom-call | flops 21810380800 | bytes 1 | tf_op jit(solution)/shard_map/heads_backward/pallas_call | solution.py:457
  547.6 6.0 collective-permute-done.58
  558.4 3.7 all-to-all-start.3
  562.8 2.7 fusion.64
  569.4 14.8 %input_backward.1 = (f32[512,1280]{1,0:T(8,128)}, f32[1,1280]{1,0:T(1,128)}, f32[1]{0:T(128)}) custom-call(bf16[512,1280]{1,0:T(8,128)(2,1)} %get-tuple-element.507.dq_ref, bf16[512,1280]{1,0:T(8,128)(2,1)} %get-tuple-element.508.dk_ref, bf16[512,1280]{1,0:T(8,128)(2,1)} %get-tuple-element.509.dv_ref, bf16[512,1280]{1,0:T(8,128)(2,1)} %tok_ref.3, ...), custom_call_target="tpu_custom_call" | custom-call | flops 15099494400 | bytes 1 | tf_op jit(solution)/shard_map/input_backward/pallas_call | solution.py:497
  587.7 2.7 fusion.28
  591.8 6.3 collective-permute-done.63
  600.1 11.1 %routed_update.2 = (f32[2,3,320,896]{3,2,1,0:T(8,128)}, f32[2,3,320,896]{3,2,1,0:T(8,128)}, f32[2,3,320,896]{3,2,1,0:T(8,128)}, f32[2,3,320,896]{3,2,1,0:T(8,128)}, bf16[2,3,320,896]{3,2,1,0:T(8,128)(2,1)}) custom-call(bf16[3,320,896]{2,1,0:T(8,128)(2,1)} %bitcast.228, f32[2,3,320,896]{3,2,1,0:T(8,128)} %w_ref.3, f32[2,3,320,896]{3,2,1,0:T(8,128)} %m_ref.3, ...), custom_call_target="tpu_custom_call" | custom-call | flops 10000000000 | bytes 1 | tf_op jit(solution)/shard_map/routed_update/pallas_call | solution.py:571
  611.3 4.6 fusion.24
  618.6 4.6 fusion.20
  625.8 3.8 collective-permute-start.67
  630.2 13.3 %collective-permute-done.68 = bf16[3,4,40,1280]{3,2,1,0:T(8,128)(2,1)} collective-permute-done((bf16[3,4,40,1280]{3,2,1,0:T(8,128)(2,1)}, bf16[3,4,40,1280]{3,2,1,0:T(8,128)(2,1)}, u32[]{:S(2)}, u32[]{:S(2)}) %collective-permute-start.68) | collective-permute-done | bytes 1228832 | tf_op jit(solution)/shard_map/ppermute | solution.py:587
  644.5 2.7 fusion.27
  647.2 3.6 all-to-all-start.4
  650.7 10.9 %routed_update.3 = (f32[2,3,320,896]{3,2,1,0:T(8,128)}, f32[2,3,320,896]{3,2,1,0:T(8,128)}, f32[2,3,320,896]{3,2,1,0:T(8,128)}, f32[2,3,320,896]{3,2,1,0:T(8,128)}, bf16[2,3,320,896]{3,2,1,0:T(8,128)(2,1)}) custom-call(bf16[3,320,896]{2,1,0:T(8,128)(2,1)} %bitcast.208, ...), custom_call_target="tpu_custom_call", output_to_operand_aliasing={{0}: (4, {}), {1}: (5, {}), {2}: (6, {}), {3}: (7, {}), {4}... | custom-call | flops 10000000000 | bytes 1 | tf_op jit(solution)/shard_map/routed_update/pallas_call | solution.py:571
  664.5 2.3 collective-permute-start.71
  667.8 4.8 all-to-all-start.5
  672.6 2.2 fusion.58
  676.7 19.7 %all-to-all-done.5 = f32[4,40,128]{2,1,0:T(8,128)S(1)} async-done(((f32[4,40,128]{2,1,0:T(8,128)}), f32[4,40,128]{2,1,0:T(8,128)S(1)}, u32[]{:S(2)}, u32[]{:S(2)}) %all-to-all-start.5) | async-done | bytes 81952 | tf_op jit(solution)/shard_map/all_to_all | solution.py:1040
  (441 shorter events, 128.8 us)
Async XLA Ops:
  9.6 31.9 %collective-permute-start.3 = (bf16[512,1280]{1,0:T(8,128)(2,1)S(1)}, bf16[512,1280]{1,0:T(8,128)(2,1)}, u32[]{:S(2)}, u32[]{:S(2)}) collective-permute-start(bf16[512,1280]{1,0:T(8,128)(2,1)S(1)} %multiply_convert_fusion.dout_ref.refs_7_.refs_8_), channel_id=1, source_target_pairs={{0,2},{1,3},{2,0},{3,1},{4,6},{5,7},{6,4},{7,5},{8,10},{9,11},{10,... | collective-permute-start | bytes 3932168 | tf_op jit(solution)/shard_map/ppermute | solution.py:587
  12.6 30.3 %collective-permute-start.4 = (bf16[512,1280]{1,0:T(8,128)(2,1)S(1)}, bf16[512,1280]{1,0:T(8,128)(2,1)}, u32[]{:S(2)}, u32[]{:S(2)}) collective-permute-start(bf16[512,1280]{1,0:T(8,128)(2,1)S(1)} %multiply_convert_fusion.dout_ref.refs_7_.refs_8_), channel_id=1, source_target_pairs={{0,4},{1,5},{2,6},{3,7},{4,0},{5,1},{6,2},{7,3},{8,12},{9,13},{10,... | collective-permute-start | bytes 3932168 | tf_op jit(solution)/shard_map/ppermute | solution.py:587
  16.9 19.0 %collective-permute-start.1 = (bf16[2,40,1408]{2,1,0:T(8,128)(2,1)S(1)}, bf16[2,40,1408]{2,1,0:T(8,128)(2,1)S(1)}, u32[]{:S(2)}, u32[]{:S(2)}) collective-permute-start(bf16[2,40,1408]{2,1,0:T(8,128)(2,1)S(1)} %fusion.51.refs_0_), channel_id=1, source_target_pairs={{0,16},{8,24},{16,0},{24,8},{1,17},{9,25},{17,1},{25,9},{2,18},{10... | collective-permute-start | bytes 675848 | tf_op jit(solution)/shard_map/ppermute | solution.py:614
  19.5 16.4 %collective-permute-start.2 = (bf16[2,40,1408]{2,1,0:T(8,128)(2,1)S(1)}, bf16[2,40,1408]{2,1,0:T(8,128)(2,1)S(1)}, u32[]{:S(2)}, u32[]{:S(2)}) collective-permute-start(bf16[2,40,1408]{2,1,0:T(8,128)(2,1)S(1)} %fusion.51.refs_0_), channel_id=1, source_target_pairs={{0,24},{8,16},{16,8},{24,0},{1,25},{9,17},{17,9},{25,1},{2,26},{10... | collective-permute-start | bytes 675848 | tf_op jit(solution)/shard_map/ppermute | solution.py:614
  42.9 23.9 %collective-permute-start.5 = (bf16[4,2,40,1408]{3,2,1,0:T(8,128)(2,1)}, bf16[4,2,40,1408]{3,2,1,0:T(8,128)(2,1)S(1)}, u32[]{:S(2)}, u32[]{:S(2)}) collective-permute-start(bf16[4,2,40,1408]{3,2,1,0:T(8,128)(2,1)} %stack_dp.2.refs_0_), channel_id=1, source_target_pairs={{0,2},{1,3},{2,0},{3,1},{4,6},{5,7},{6,4},{7,5},{8,10},{9,11},{10,... | collective-permute-start | bytes 2703368 | tf_op jit(solution)/shard_map/ppermute | solution.py:587
  43.3 23.6 %collective-permute-start.6 = (bf16[4,2,40,1408]{3,2,1,0:T(8,128)(2,1)}, bf16[4,2,40,1408]{3,2,1,0:T(8,128)(2,1)S(1)}, u32[]{:S(2)}, u32[]{:S(2)}) collective-permute-start(bf16[4,2,40,1408]{3,2,1,0:T(8,128)(2,1)} %stack_dp.2.refs_0_), channel_id=1, source_target_pairs={{0,4},{1,5},{2,6},{3,7},{4,0},{5,1},{6,2},{7,3},{8,12},{9,13},{10,... | collective-permute-start | bytes 2703368 | tf_op jit(solution)/shard_map/ppermute | solution.py:587
  46.6 16.7 %collective-permute-start.8 = (bf16[2,40,1280]{2,1,0:T(8,128)(2,1)S(1)}, bf16[2,40,1280]{2,1,0:T(8,128)(2,1)S(1)}, u32[]{:S(2)}, u32[]{:S(2)}) collective-permute-start(bf16[2,40,1280]{2,1,0:T(8,128)(2,1)S(1)} %copy-done.50), channel_id=1, source_target_pairs={{0,16},{8,24},{16,0},{24,8},{1,17},{9,25},{17,1},{25,9},{2,18},{10... | collective-permute-start | bytes 614408 | tf_op jit(solution)/shard_map/ppermute | solution.py:614
  66.9 21.6 %collective-permute-start.14 = (bf16[4,2,40,1280]{3,2,1,0:T(8,128)(2,1)}, bf16[4,2,40,1280]{3,2,1,0:T(8,128)(2,1)}, u32[]{:S(2)}, u32[]{:S(2)}) collective-permute-start(bf16[4,2,40,1280]{3,2,1,0:T(8,128)(2,1)} %stack_dp.3.refs_8_), channel_id=1, source_target_pairs={{0,2},{1,3},{2,0},{3,1},{4,6},{5,7},{6,4},{7,5},{8,10},{9,11},{10,... | collective-permute-start | bytes 2457608 | tf_op jit(solution)/shard_map/ppermute | solution.py:587
  69.4 37.8 %all-to-all-start = ((bf16[4,3,40,896]{3,2,1,0:T(8,128)(2,1)}), bf16[4,3,40,896]{3,2,1,0:T(8,128)(2,1)}, u32[]{:S(2)}, u32[]{:S(2)}) async-start(bf16[4,3,40,896]{3,2,1,0:T(8,128)(2,1)} %broadcast_in_dim.101), calls=%async_computation | async-start | bytes 1720320 | tf_op jit(solution)/shard_map/all_to_all | solution.py:820
  73.8 159.0 %all-gather.5.cloned.1.call-start = ((), (), s32[]{:S(2)}) async-start(), calls=%async_computation.10 | async-start | bytes 8601600 | tf_op jit(solution)/shard_map/all_gather | solution.py:830
  73.9 30.8 %collective-permute-start.13 = (bf16[4,2,40,1408]{3,2,1,0:T(8,128)(2,1)S(1)}, bf16[4,2,40,1408]{3,2,1,0:T(8,128)(2,1)S(1)}, u32[]{:S(2)}, u32[]{:S(2)}) collective-permute-start(bf16[4,2,40,1408]{3,2,1,0:T(8,128)(2,1)S(1)} %broadcast_select_fusion.2), channel_id=1, source_target_pairs={{0,4},{1,3},{2,6},{3,1},{4,0},{5,7},{6,2},{7,5},{8,12},{9,11},{10,... | collective-permute-start | bytes 2703368 | tf_op jit(solution)/shard_map/ppermute | solution.py:587
  75.0 29.8 %collective-permute-start.10 = (bf16[4,2,40,1408]{3,2,1,0:T(8,128)(2,1)S(1)}, bf16[4,2,40,1408]{3,2,1,0:T(8,128)(2,1)S(1)}, u32[]{:S(2)}, u32[]{:S(2)}) collective-permute-start(bf16[4,2,40,1408]{3,2,1,0:T(8,128)(2,1)S(1)} %copy-done.8), channel_id=1, source_target_pairs={{0,1},{1,0},{2,3},{3,2},{4,5},{5,4},{6,7},{7,6},{8,9},{9,8},{10,11... | collective-permute-start | bytes 2703368 | tf_op jit(solution)/shard_map/ppermute | solution.py:587
  75.0 29.8 %collective-permute-start.12 = (bf16[4,2,40,1408]{3,2,1,0:T(8,128)(2,1)S(1)}, bf16[4,2,40,1408]{3,2,1,0:T(8,128)(2,1)S(1)}, u32[]{:S(2)}, u32[]{:S(2)}) collective-permute-start(bf16[4,2,40,1408]{3,2,1,0:T(8,128)(2,1)S(1)} %collective-permute-done.6.refs_4_), channel_id=1, source_target_pairs={{0,1},{1,0},{2,3},{3,2},{4,5},{5,4},{6,7},{7,6},{8,9},{9,8},{10,11... | collective-permute-start | bytes 2703368 | tf_op jit(solution)/shard_map/ppermute | solution.py:587
  75.5 31.7 %collective-permute-start.11 = (bf16[4,2,40,1408]{3,2,1,0:T(8,128)(2,1)S(1)}, bf16[4,2,40,1408]{3,2,1,0:T(8,128)(2,1)}, u32[]{:S(2)}, u32[]{:S(2)}) collective-permute-start(bf16[4,2,40,1408]{3,2,1,0:T(8,128)(2,1)S(1)} %collective-permute-done.5.refs_2_), channel_id=1, source_target_pairs={{0,1},{1,0},{2,3},{3,2},{4,5},{5,4},{6,7},{7,6},{8,9},{9,8},{10,11... | collective-permute-start | bytes 2703368 | tf_op jit(solution)/shard_map/ppermute | solution.py:587
  88.4 16.3 %collective-permute-start.15 = (bf16[4,2,40,1280]{3,2,1,0:T(8,128)(2,1)S(1)}, bf16[4,2,40,1280]{3,2,1,0:T(8,128)(2,1)S(1)}, u32[]{:S(2)}, u32[]{:S(2)}) collective-permute-start(bf16[4,2,40,1280]{3,2,1,0:T(8,128)(2,1)S(1)} %copy-done.13), channel_id=1, source_target_pairs={{0,4},{1,5},{2,6},{3,7},{4,0},{5,1},{6,2},{7,3},{8,12},{9,13},{10,... | collective-permute-start | bytes 2457608 | tf_op jit(solution)/shard_map/ppermute | solution.py:587
  125.4 68.7 %all-to-all-start.1 = ((bf16[8,16,512]{2,1,0:T(8,128)(2,1)}), bf16[8,16,512]{2,1,0:T(8,128)(2,1)S(1)}, u32[]{:S(2)}, u32[]{:S(2)}) async-start(bf16[8,16,512]{2,1,0:T(8,128)(2,1)} %broadcast_in_dim.104), calls=%async_computation.1 | async-start | bytes 262144 | tf_op jit(solution)/shard_map/all_to_all | solution.py:814
  128.8 228.0 %all-gather.7.cloned.1.call-start = ((), (), s32[]{:S(2)}) async-start(), calls=%async_computation.11 | async-start | bytes 8601600 | tf_op jit(solution)/shard_map/all_gather | solution.py:830
  129.4 41.6 %collective-permute-start.27 = (bf16[512,1280]{1,0:T(8,128)(2,1)}, bf16[512,1280]{1,0:T(8,128)(2,1)}, u32[]{:S(2)}, u32[]{:S(2)}) collective-permute-start(bf16[512,1280]{1,0:T(8,128)(2,1)} %collective-permute-done.4.refs_7_.refs_8_), channel_id=1, source_target_pairs={{0,1},{1,0},{2,3},{3,2},{4,5},{5,4},{6,7},{7,6},{8,9},{9,8},{10,11... | collective-permute-start | bytes 3932168 | tf_op jit(solution)/shard_map/ppermute | solution.py:587
  130.0 41.1 %collective-permute-start.26 = (bf16[512,1280]{1,0:T(8,128)(2,1)}, bf16[512,1280]{1,0:T(8,128)(2,1)}, u32[]{:S(2)}, u32[]{:S(2)}) collective-permute-start(bf16[512,1280]{1,0:T(8,128)(2,1)} %collective-permute-done.3.refs_7_.refs_8_), channel_id=1, source_target_pairs={{0,1},{1,0},{2,3},{3,2},{4,5},{5,4},{6,7},{7,6},{8,9},{9,8},{10,11... | collective-permute-start | bytes 3932168 | tf_op jit(solution)/shard_map/ppermute | solution.py:587
  130.0 41.0 %collective-permute-start.25 = (bf16[512,1280]{1,0:T(8,128)(2,1)S(1)}, bf16[512,1280]{1,0:T(8,128)(2,1)}, u32[]{:S(2)}, u32[]{:S(2)}) collective-permute-start(bf16[512,1280]{1,0:T(8,128)(2,1)S(1)} %multiply_convert_fusion.dout_ref.refs_7_.refs_8_), channel_id=1, source_target_pairs={{0,1},{1,0},{2,3},{3,2},{4,5},{5,4},{6,7},{7,6},{8,9},{9,8},{10,11... | collective-permute-start | bytes 3932168 | tf_op jit(solution)/shard_map/ppermute | solution.py:587
  130.5 40.3 %collective-permute-start.23 = (bf16[4,3,40,896]{3,2,1,0:T(8,128)(2,1)}, bf16[4,3,40,896]{3,2,1,0:T(8,128)(2,1)}, u32[]{:S(2)}, u32[]{:S(2)}) collective-permute-start(bf16[4,3,40,896]{3,2,1,0:T(8,128)(2,1)} %all-to-all-done.refs_0_), channel_id=1, source_target_pairs={{0,2},{1,3},{2,0},{3,1},{4,6},{5,7},{6,4},{7,5},{8,10},{9,11},{10,... | collective-permute-start | bytes 2580488 | tf_op jit(solution)/shard_map/ppermute | solution.py:587
  134.1 36.9 %collective-permute-start.24 = (bf16[4,3,40,896]{3,2,1,0:T(8,128)(2,1)}, bf16[4,3,40,896]{3,2,1,0:T(8,128)(2,1)}, u32[]{:S(2)}, u32[]{:S(2)}) collective-permute-start(bf16[4,3,40,896]{3,2,1,0:T(8,128)(2,1)} %all-to-all-done.refs_0_), channel_id=1, source_target_pairs={{0,4},{1,5},{2,6},{3,7},{4,0},{5,1},{6,2},{7,3},{8,12},{9,13},{10,... | collective-permute-start | bytes 2580488 | tf_op jit(solution)/shard_map/ppermute | solution.py:587
  171.6 428.5 %reduce-scatter.3.cloned.1.call-start = ((), (), s32[]{:S(2)}) async-start(), calls=%async_computation.8 | async-start | bytes 8601600 | tf_op jit(solution)/shard_map/reduce_scatter | solution.py:929
  174.7 18.8 %collective-permute-start.28 = (bf16[4,3,40,896]{3,2,1,0:T(8,128)(2,1)}, bf16[4,3,40,896]{3,2,1,0:T(8,128)(2,1)}, u32[]{:S(2)}, u32[]{:S(2)}) collective-permute-start(bf16[4,3,40,896]{3,2,1,0:T(8,128)(2,1)} %broadcast_select_fusion.3), channel_id=1, source_target_pairs={{0,4},{1,3},{2,6},{3,1},{4,0},{5,7},{6,2},{7,5},{8,12},{9,11},{10,... | collective-permute-start | bytes 2580488 | tf_op jit(solution)/shard_map/ppermute | solution.py:587
  178.3 45.2 %collective-permute-start.33 = (bf16[512,1280]{1,0:T(8,128)(2,1)S(1)}, bf16[512,1280]{1,0:T(8,128)(2,1)}, u32[]{:S(2)}, u32[]{:S(2)}) collective-permute-start(bf16[512,1280]{1,0:T(8,128)(2,1)S(1)} %copy-done), channel_id=1, source_target_pairs={{0,2},{1,3},{2,0},{3,1},{4,6},{5,7},{6,4},{7,5},{8,10},{9,11},{10,... | collective-permute-start | bytes 3932168 | tf_op jit(solution)/shard_map/ppermute | solution.py:587
  178.8 44.7 %collective-permute-start.34 = (bf16[512,1280]{1,0:T(8,128)(2,1)S(1)}, bf16[512,1280]{1,0:T(8,128)(2,1)}, u32[]{:S(2)}, u32[]{:S(2)}) collective-permute-start(bf16[512,1280]{1,0:T(8,128)(2,1)S(1)} %copy-done), channel_id=1, source_target_pairs={{0,4},{1,5},{2,6},{3,7},{4,0},{5,1},{6,2},{7,3},{8,12},{9,13},{10,... | collective-permute-start | bytes 3932168 | tf_op jit(solution)/shard_map/ppermute | solution.py:587
  223.5 38.4 %collective-permute-start.38 = (bf16[4,3,4,40,896]{4,3,2,1,0:T(8,128)(2,1)}, bf16[4,3,4,40,896]{4,3,2,1,0:T(8,128)(2,1)}, u32[]{:S(2)}, u32[]{:S(2)}) collective-permute-start(bf16[4,3,4,40,896]{4,3,2,1,0:T(8,128)(2,1)} %bitcast.227), channel_id=1, source_target_pairs={{0,1},{1,0},{2,3},{3,2},{4,5},{5,4},{6,7},{7,6},{8,9},{9,8},{10,11... | collective-permute-start | bytes 10321928 | tf_op jit(solution)/shard_map/ppermute | solution.py:587
  230.1 29.2 %collective-permute-start.39 = (bf16[512,1280]{1,0:T(8,128)(2,1)S(1)}, bf16[512,1280]{1,0:T(8,128)(2,1)}, u32[]{:S(2)}, u32[]{:S(2)}) collective-permute-start(bf16[512,1280]{1,0:T(8,128)(2,1)S(1)} %broadcast_select_fusion), channel_id=1, source_target_pairs={{0,4},{1,3},{2,6},{3,1},{4,0},{5,7},{6,2},{7,5},{8,12},{9,11},{10,... | collective-permute-start | bytes 3932168 | tf_op jit(solution)/shard_map/ppermute | solution.py:587
  230.7 28.6 %collective-permute-start.36 = (bf16[512,1280]{1,0:T(8,128)(2,1)}, bf16[512,1280]{1,0:T(8,128)(2,1)}, u32[]{:S(2)}, u32[]{:S(2)}) collective-permute-start(bf16[512,1280]{1,0:T(8,128)(2,1)} %collective-permute-done.34.refs_5_.refs_6_), channel_id=1, source_target_pairs={{0,1},{1,0},{2,3},{3,2},{4,5},{5,4},{6,7},{7,6},{8,9},{9,8},{10,11... | collective-permute-start | bytes 3932168 | tf_op jit(solution)/shard_map/ppermute | solution.py:587
  230.8 28.5 %collective-permute-start.35 = (bf16[512,1280]{1,0:T(8,128)(2,1)}, bf16[512,1280]{1,0:T(8,128)(2,1)}, u32[]{:S(2)}, u32[]{:S(2)}) collective-permute-start(bf16[512,1280]{1,0:T(8,128)(2,1)} %collective-permute-done.33.refs_5_.refs_6_), channel_id=1, source_target_pairs={{0,1},{1,0},{2,3},{3,2},{4,5},{5,4},{6,7},{7,6},{8,9},{9,8},{10,11... | collective-permute-start | bytes 3932168 | tf_op jit(solution)/shard_map/ppermute | solution.py:587
  231.3 30.7 %collective-permute-start.37 = (bf16[512,1280]{1,0:T(8,128)(2,1)S(1)}, bf16[512,1280]{1,0:T(8,128)(2,1)}, u32[]{:S(2)}, u32[]{:S(2)}) collective-permute-start(bf16[512,1280]{1,0:T(8,128)(2,1)S(1)} %broadcast_select_fusion.1), channel_id=1, source_target_pairs={{0,4},{1,3},{2,6},{3,1},{4,0},{5,7},{6,2},{7,5},{8,12},{9,11},{10,... | collective-permute-start | bytes 3932168 | tf_op jit(solution)/shard_map/ppermute | solution.py:587
  262.0 25.0 %collective-permute-start.41 = (bf16[512,1280]{1,0:T(8,128)(2,1)}, bf16[512,1280]{1,0:T(8,128)(2,1)}, u32[]{:S(2)}, u32[]{:S(2)}) collective-permute-start(bf16[512,1280]{1,0:T(8,128)(2,1)} %collective-permute-done.39.refs_7_.refs_8_), channel_id=1, source_target_pairs={{0,1},{1,0},{2,3},{3,2},{4,5},{5,4},{6,7},{7,6},{8,9},{9,8},{10,11... | collective-permute-start | bytes 3932168 | tf_op jit(solution)/shard_map/ppermute | solution.py:587
  267.0 20.0 %collective-permute-start.42 = (bf16[3,4,40,896]{3,2,1,0:T(8,128)(2,1)S(1)}, bf16[3,4,40,896]{3,2,1,0:T(8,128)(2,1)S(1)}, u32[]{:S(2)}, u32[]{:S(2)}) collective-permute-start(bf16[3,4,40,896]{3,2,1,0:T(8,128)(2,1)S(1)} %fusion.36), channel_id=1, source_target_pairs={{0,4},{1,3},{2,6},{3,1},{4,0},{5,7},{6,2},{7,5},{8,12},{9,11},{10,... | collective-permute-start | bytes 2580488 | tf_op jit(solution)/shard_map/ppermute | solution.py:587
  289.2 39.8 %collective-permute-start.43 = (bf16[3,4,40,896]{3,2,1,0:T(8,128)(2,1)S(1)}, bf16[3,4,40,896]{3,2,1,0:T(8,128)(2,1)S(1)}, u32[]{:S(2)}, u32[]{:S(2)}) collective-permute-start(bf16[3,4,40,896]{3,2,1,0:T(8,128)(2,1)S(1)} %get-tuple-element.386), channel_id=1, source_target_pairs={{0,2},{1,3},{2,0},{3,1},{4,6},{5,7},{6,4},{7,5},{8,10},{9,11},{10,... | collective-permute-start | bytes 2580488 | tf_op jit(solution)/shard_map/ppermute | solution.py:587
  289.8 39.2 %collective-permute-start.44 = (bf16[3,4,40,896]{3,2,1,0:T(8,128)(2,1)S(1)}, bf16[3,4,40,896]{3,2,1,0:T(8,128)(2,1)S(1)}, u32[]{:S(2)}, u32[]{:S(2)}) collective-permute-start(bf16[3,4,40,896]{3,2,1,0:T(8,128)(2,1)S(1)} %get-tuple-element.387), channel_id=1, source_target_pairs={{0,4},{1,5},{2,6},{3,7},{4,0},{5,1},{6,2},{7,3},{8,12},{9,13},{10,... | collective-permute-start | bytes 2580488 | tf_op jit(solution)/shard_map/ppermute | solution.py:587
  377.2 20.9 %collective-permute-start.45 = (bf16[512,1280]{1,0:T(8,128)(2,1)}, bf16[512,1280]{1,0:T(8,128)(2,1)S(1)}, u32[]{:S(2)}, u32[]{:S(2)}) collective-permute-start(bf16[512,1280]{1,0:T(8,128)(2,1)} %get-tuple-element.419), channel_id=1, source_target_pairs={{0,1},{1,0},{2,3},{3,2},{4,5},{5,4},{6,7},{7,6},{8,9},{9,8},{10,11... | collective-permute-start | bytes 3932168 | tf_op jit(solution)/shard_map/ppermute | solution.py:587
  377.3 20.8 %collective-permute-start.46 = (bf16[512,1280]{1,0:T(8,128)(2,1)}, bf16[512,1280]{1,0:T(8,128)(2,1)S(1)}, u32[]{:S(2)}, u32[]{:S(2)}) collective-permute-start(bf16[512,1280]{1,0:T(8,128)(2,1)} %get-tuple-element.421), channel_id=1, source_target_pairs={{0,1},{1,0},{2,3},{3,2},{4,5},{5,4},{6,7},{7,6},{8,9},{9,8},{10,11... | collective-permute-start | bytes 3932168 | tf_op jit(solution)/shard_map/ppermute | solution.py:587
  399.2 27.5 %collective-permute-start.49 = (bf16[512,1280]{1,0:T(8,128)(2,1)}, bf16[512,1280]{1,0:T(8,128)(2,1)S(1)}, u32[]{:S(2)}, u32[]{:S(2)}) collective-permute-start(bf16[512,1280]{1,0:T(8,128)(2,1)} %get-tuple-element.435), channel_id=1, source_target_pairs={{0,1},{1,0},{2,3},{3,2},{4,5},{5,4},{6,7},{7,6},{8,9},{9,8},{10,11... | collective-permute-start | bytes 3932168 | tf_op jit(solution)/shard_map/ppermute | solution.py:587
  399.6 27.1 %collective-permute-start.48 = (bf16[512,1280]{1,0:T(8,128)(2,1)}, bf16[512,1280]{1,0:T(8,128)(2,1)S(1)}, u32[]{:S(2)}, u32[]{:S(2)}) collective-permute-start(bf16[512,1280]{1,0:T(8,128)(2,1)} %get-tuple-element.433), channel_id=1, source_target_pairs={{0,1},{1,0},{2,3},{3,2},{4,5},{5,4},{6,7},{7,6},{8,9},{9,8},{10,11... | collective-permute-start | bytes 3932168 | tf_op jit(solution)/shard_map/ppermute | solution.py:587
  402.5 24.2 %collective-permute-start.47 = (bf16[512,1280]{1,0:T(8,128)(2,1)}, bf16[512,1280]{1,0:T(8,128)(2,1)}, u32[]{:S(2)}, u32[]{:S(2)}) collective-permute-start(bf16[512,1280]{1,0:T(8,128)(2,1)} %add_convert_fusion.1), channel_id=1, source_target_pairs={{0,4},{1,3},{2,6},{3,1},{4,0},{5,7},{6,2},{7,5},{8,12},{9,11},{10,... | collective-permute-start | bytes 3932168 | tf_op jit(solution)/shard_map/ppermute | solution.py:587
  433.9 36.0 %collective-permute-start.52 = (bf16[512,1280]{1,0:T(8,128)(2,1)}, bf16[512,1280]{1,0:T(8,128)(2,1)}, u32[]{:S(2)}, u32[]{:S(2)}) collective-permute-start(bf16[512,1280]{1,0:T(8,128)(2,1)} %get-tuple-element.464), channel_id=1, source_target_pairs={{0,2},{1,3},{2,0},{3,1},{4,6},{5,7},{6,4},{7,5},{8,10},{9,11},{10,... | collective-permute-start | bytes 3932168 | tf_op jit(solution)/shard_map/ppermute | solution.py:587
  435.4 34.6 %collective-permute-start.53 = (bf16[512,1280]{1,0:T(8,128)(2,1)S(1)}, bf16[512,1280]{1,0:T(8,128)(2,1)}, u32[]{:S(2)}, u32[]{:S(2)}) collective-permute-start(bf16[512,1280]{1,0:T(8,128)(2,1)S(1)} %get-tuple-element.465), channel_id=1, source_target_pairs={{0,4},{1,5},{2,6},{3,7},{4,0},{5,1},{6,2},{7,3},{8,12},{9,13},{10,... | collective-permute-start | bytes 3932168 | tf_op jit(solution)/shard_map/ppermute | solution.py:587
  435.7 34.2 %collective-permute-start.51 = (bf16[512,1280]{1,0:T(8,128)(2,1)}, bf16[512,1280]{1,0:T(8,128)(2,1)S(1)}, u32[]{:S(2)}, u32[]{:S(2)}) collective-permute-start(bf16[512,1280]{1,0:T(8,128)(2,1)} %get-tuple-element.461), channel_id=1, source_target_pairs={{0,1},{1,0},{2,3},{3,2},{4,5},{5,4},{6,7},{7,6},{8,9},{9,8},{10,11... | collective-permute-start | bytes 3932168 | tf_op jit(solution)/shard_map/ppermute | solution.py:587
  465.1 182.0 %reduce-scatter.5.cloned.1.call-start = ((), (), s32[]{:S(2)}) async-start(), calls=%async_computation.9 | async-start | bytes 8601600 | tf_op jit(solution)/shard_map/reduce_scatter | solution.py:929
  470.0 24.8 %collective-permute-start.54 = (bf16[512,1280]{1,0:T(8,128)(2,1)}, bf16[512,1280]{1,0:T(8,128)(2,1)}, u32[]{:S(2)}, u32[]{:S(2)}) collective-permute-start(bf16[512,1280]{1,0:T(8,128)(2,1)} %get-tuple-element.483), channel_id=1, source_target_pairs={{0,1},{1,0},{2,3},{3,2},{4,5},{5,4},{6,7},{7,6},{8,9},{9,8},{10,11... | collective-permute-start | bytes 3932168 | tf_op jit(solution)/shard_map/ppermute | solution.py:587
  471.0 23.7 %collective-permute-start.56 = (bf16[512,1280]{1,0:T(8,128)(2,1)}, bf16[512,1280]{1,0:T(8,128)(2,1)S(1)}, u32[]{:S(2)}, u32[]{:S(2)}) collective-permute-start(bf16[512,1280]{1,0:T(8,128)(2,1)} %get-tuple-element.487), channel_id=1, source_target_pairs={{0,1},{1,0},{2,3},{3,2},{4,5},{5,4},{6,7},{7,6},{8,9},{9,8},{10,11... | collective-permute-start | bytes 3932168 | tf_op jit(solution)/shard_map/ppermute | solution.py:587
  471.0 23.8 %collective-permute-start.55 = (bf16[512,1280]{1,0:T(8,128)(2,1)}, bf16[512,1280]{1,0:T(8,128)(2,1)S(1)}, u32[]{:S(2)}, u32[]{:S(2)}) collective-permute-start(bf16[512,1280]{1,0:T(8,128)(2,1)} %add_convert_fusion), channel_id=1, source_target_pairs={{0,4},{1,3},{2,6},{3,1},{4,0},{5,7},{6,2},{7,5},{8,12},{9,11},{10,... | collective-permute-start | bytes 3932168 | tf_op jit(solution)/shard_map/ppermute | solution.py:587
  517.8 36.7 %collective-permute-start.57 = (bf16[4,1,4,40,1280]{4,3,2,1,0:T(8,128)(2,1)}, bf16[4,1,4,40,1280]{4,3,2,1,0:T(8,128)(2,1)}, u32[]{:S(2)}, u32[]{:S(2)}) collective-permute-start(bf16[4,1,4,40,1280]{4,3,2,1,0:T(8,128)(2,1)} %bitcast.229), channel_id=1, source_target_pairs={{0,1},{1,0},{2,3},{3,2},{4,5},{5,4},{6,7},{7,6},{8,9},{9,8},{10,11... | collective-permute-start | bytes 4915208 | tf_op jit(solution)/shard_map/ppermute | solution.py:587
  522.4 31.3 %collective-permute-start.58 = (bf16[512,1280]{1,0:T(8,128)(2,1)}, bf16[512,1280]{1,0:T(8,128)(2,1)}, u32[]{:S(2)}, u32[]{:S(2)}) collective-permute-start(bf16[512,1280]{1,0:T(8,128)(2,1)} %get-tuple-element.502), channel_id=1, source_target_pairs={{0,2},{1,3},{2,0},{3,1},{4,6},{5,7},{6,4},{7,5},{8,10},{9,11},{10,... | collective-permute-start | bytes 3932168 | tf_op jit(solution)/shard_map/ppermute | solution.py:587
  523.9 30.7 %collective-permute-start.59 = (bf16[512,1280]{1,0:T(8,128)(2,1)}, bf16[512,1280]{1,0:T(8,128)(2,1)S(1)}, u32[]{:S(2)}, u32[]{:S(2)}) collective-permute-start(bf16[512,1280]{1,0:T(8,128)(2,1)} %get-tuple-element.503), channel_id=1, source_target_pairs={{0,4},{1,5},{2,6},{3,7},{4,0},{5,1},{6,2},{7,3},{8,12},{9,13},{10,... | collective-permute-start | bytes 3932168 | tf_op jit(solution)/shard_map/ppermute | solution.py:587
  554.5 29.7 %collective-permute-start.60 = (bf16[4,3,4,40,1280]{4,3,2,1,0:T(8,128)(2,1)}, bf16[4,3,4,40,1280]{4,3,2,1,0:T(8,128)(2,1)}, u32[]{:S(2)}, u32[]{:S(2)}) collective-permute-start(bf16[4,3,4,40,1280]{4,3,2,1,0:T(8,128)(2,1)} %bitcast.226), channel_id=1, source_target_pairs={{0,1},{1,0},{2,3},{3,2},{4,5},{5,4},{6,7},{7,6},{8,9},{9,8},{10,11... | collective-permute-start | bytes 14745608 | tf_op jit(solution)/shard_map/ppermute | solution.py:587
  558.4 88.7 %all-to-all-start.3 = ((bf16[4,3,40,896]{3,2,1,0:T(8,128)(2,1)}), bf16[4,3,40,896]{3,2,1,0:T(8,128)(2,1)S(1)}, u32[]{:S(2)}, u32[]{:S(2)}) async-start(bf16[4,3,40,896]{3,2,1,0:T(8,128)(2,1)} %copy.234), calls=%async_computation.4 | async-start | bytes 1720320 | tf_op jit(solution)/shard_map/all_to_all | solution.py:1004
  568.7 15.5 %collective-permute-start.61 = (bf16[1,4,40,1280]{3,2,1,0:T(8,128)(2,1)}, bf16[1,4,40,1280]{3,2,1,0:T(8,128)(2,1)S(1)}, u32[]{:S(2)}, u32[]{:S(2)}) collective-permute-start(bf16[1,4,40,1280]{3,2,1,0:T(8,128)(2,1)} %fusion.48), channel_id=1, source_target_pairs={{0,4},{1,3},{2,6},{3,1},{4,0},{5,7},{6,2},{7,5},{8,12},{9,11},{10,... | collective-permute-start | bytes 1228808 | tf_op jit(solution)/shard_map/ppermute | solution.py:587
  590.4 20.8 %collective-permute-start.62 = (bf16[3,4,40,1280]{3,2,1,0:T(8,128)(2,1)}, bf16[3,4,40,1280]{3,2,1,0:T(8,128)(2,1)}, u32[]{:S(2)}, u32[]{:S(2)}) collective-permute-start(bf16[3,4,40,1280]{3,2,1,0:T(8,128)(2,1)} %fusion.28), channel_id=1, source_target_pairs={{0,4},{1,3},{2,6},{3,1},{4,0},{5,7},{6,2},{7,5},{8,12},{9,11},{10,... | collective-permute-start | bytes 3686408 | tf_op jit(solution)/shard_map/ppermute | solution.py:587
  615.9 27.6 %collective-permute-start.68 = (bf16[3,4,40,1280]{3,2,1,0:T(8,128)(2,1)}, bf16[3,4,40,1280]{3,2,1,0:T(8,128)(2,1)}, u32[]{:S(2)}, u32[]{:S(2)}) collective-permute-start(bf16[3,4,40,1280]{3,2,1,0:T(8,128)(2,1)} %get-tuple-element.519), channel_id=1, source_target_pairs={{0,2},{1,3},{2,0},{3,1},{4,6},{5,7},{6,4},{7,5},{8,10},{9,11},{10,... | collective-permute-start | bytes 3686408 | tf_op jit(solution)/shard_map/ppermute | solution.py:587
  617.3 27.2 %collective-permute-start.69 = (bf16[3,4,40,1280]{3,2,1,0:T(8,128)(2,1)}, bf16[3,4,40,1280]{3,2,1,0:T(8,128)(2,1)}, u32[]{:S(2)}, u32[]{:S(2)}) collective-permute-start(bf16[3,4,40,1280]{3,2,1,0:T(8,128)(2,1)} %get-tuple-element.520), channel_id=1, source_target_pairs={{0,4},{1,5},{2,6},{3,7},{4,0},{5,1},{6,2},{7,3},{8,12},{9,13},{10,... | collective-permute-start | bytes 3686408 | tf_op jit(solution)/shard_map/ppermute | solution.py:587
  625.8 41.0 %collective-permute-start.67 = (bf16[1,40,1280]{2,1,0:T(8,128)(2,1)}, bf16[1,40,1280]{2,1,0:T(8,128)(2,1)}, u32[]{:S(2)}, u32[]{:S(2)}) collective-permute-start(bf16[1,40,1280]{2,1,0:T(8,128)(2,1)} %get-tuple-element.528), channel_id=1, source_target_pairs={{0,24},{8,16},{16,8},{24,0},{1,25},{9,17},{17,9},{25,1},{2,26},{10... | collective-permute-start | bytes 307208 | tf_op jit(solution)/shard_map/ppermute | solution.py:614
  629.6 37.5 %collective-permute-start.66 = (bf16[1,40,1280]{2,1,0:T(8,128)(2,1)}, bf16[1,40,1280]{2,1,0:T(8,128)(2,1)}, u32[]{:S(2)}, u32[]{:S(2)}) collective-permute-start(bf16[1,40,1280]{2,1,0:T(8,128)(2,1)} %get-tuple-element.527), channel_id=1, source_target_pairs={{0,16},{8,24},{16,0},{24,8},{1,17},{9,25},{17,1},{25,9},{2,18},{10... | collective-permute-start | bytes 307208 | tf_op jit(solution)/shard_map/ppermute | solution.py:614
  629.6 37.5 %collective-permute-start.65 = (bf16[1,40,1280]{2,1,0:T(8,128)(2,1)}, bf16[1,40,1280]{2,1,0:T(8,128)(2,1)}, u32[]{:S(2)}, u32[]{:S(2)}) collective-permute-start(bf16[1,40,1280]{2,1,0:T(8,128)(2,1)} %get-tuple-element.526), channel_id=1, source_target_pairs={{0,8},{8,0},{16,24},{24,16},{1,9},{9,1},{17,25},{25,17},{2,10},{10... | collective-permute-start | bytes 307208 | tf_op jit(solution)/shard_map/ppermute | solution.py:614
  647.2 20.0 %all-to-all-start.4 = ((f32[8,4,40,128]{3,2,1,0:T(8,128)}), f32[8,4,40,128]{3,2,1,0:T(8,128)S(1)}, u32[]{:S(2)}, u32[]{:S(2)}) async-start(f32[8,4,40,128]{3,2,1,0:T(8,128)} %copy.236), calls=%async_computation.5 | async-start | bytes 1310720 | tf_op jit(solution)/shard_map/all_to_all | solution.py:1028
  662.7 39.2 %collective-permute-start.70 = (bf16[3,40,1280]{2,1,0:T(8,128)(2,1)}, bf16[3,40,1280]{2,1,0:T(8,128)(2,1)S(1)}, u32[]{:S(2)}, u32[]{:S(2)}) collective-permute-start(bf16[3,40,1280]{2,1,0:T(8,128)(2,1)} %get-tuple-element.541), channel_id=1, source_target_pairs={{0,8},{8,0},{16,24},{24,16},{1,9},{9,1},{17,25},{25,17},{2,10},{10... | collective-permute-start | bytes 921608 | tf_op jit(solution)/shard_map/ppermute | solution.py:614
  664.5 37.4 %collective-permute-start.71 = (bf16[3,40,1280]{2,1,0:T(8,128)(2,1)}, bf16[3,40,1280]{2,1,0:T(8,128)(2,1)S(1)}, u32[]{:S(2)}, u32[]{:S(2)}) collective-permute-start(bf16[3,40,1280]{2,1,0:T(8,128)(2,1)} %get-tuple-element.542), channel_id=1, source_target_pairs={{0,16},{8,24},{16,0},{24,8},{1,17},{9,25},{17,1},{25,9},{2,18},{10... | collective-permute-start | bytes 921608 | tf_op jit(solution)/shard_map/ppermute | solution.py:614
  666.8 35.1 %collective-permute-start.72 = (bf16[3,40,1280]{2,1,0:T(8,128)(2,1)}, bf16[3,40,1280]{2,1,0:T(8,128)(2,1)}, u32[]{:S(2)}, u32[]{:S(2)}) collective-permute-start(bf16[3,40,1280]{2,1,0:T(8,128)(2,1)} %get-tuple-element.543), channel_id=1, source_target_pairs={{0,24},{8,16},{16,8},{24,0},{1,25},{9,17},{17,9},{25,1},{2,26},{10... | collective-permute-start | bytes 921608 | tf_op jit(solution)/shard_map/ppermute | solution.py:614
  667.8 28.6 %all-to-all-start.5 = ((f32[4,40,128]{2,1,0:T(8,128)}), f32[4,40,128]{2,1,0:T(8,128)S(1)}, u32[]{:S(2)}, u32[]{:S(2)}) async-start(f32[4,40,128]{2,1,0:T(8,128)} %add_bitcast_fusion.1), calls=%async_computation.7 | async-start | bytes 163840 | tf_op jit(solution)/shard_map/all_to_all | solution.py:1040
  (112 other events, 1222.4 us)
Sparse Core Ops, SparseCore 0:
  107.3 124.6 all-gather.4
  233.5 123.2 all-gather.6
  359.7 118.5 reduce-scatter.2
  494.9 131.4 reduce-scatter.4

commit v4 on v3

--- a/solution.py
+++ b/solution.py
@@ -366,7 +366,7 @@
 
 
 def hidden_back_kernel(
-    dn_ref, logit_ref, router_ref, base_ref, side_x_ref, side_y_ref, hidden_ref, dout_ref, gain_ref, ctx_ref, wo, dhid_ref, dctx_ref, even_ref, odd_ref, gain_out, w_v, dattn_v, sem
+    dn_ref, logit_ref, router_ref, base_ref, core_ref, side_x_ref, side_y_ref, hidden_ref, dout_ref, gain_ref, ctx_ref, wo, dhid_ref, dctx_ref, even_ref, odd_ref, gain_out, w_v, dattn_v, sem
 ):
     copy = pltpu.make_async_copy(wo, w_v, sem)
     copy.start()
@@ -380,7 +380,7 @@
     low = rest.astype(BF)
     least = (rest - low.astype(F32)).astype(BF)
     routers = sum(dot_nn(part, router_ref[...]) for part in (least, low, high))
-    dn = dn_ref[...] + routers + base_ref[...] + side_x_ref[...].astype(F32) + side_y_ref[...].astype(F32)
+    dn = dn_ref[...] + routers + base_ref[...].astype(F32) + core_ref[...].astype(F32) + side_x_ref[...].astype(F32) + side_y_ref[...].astype(F32)
     gain_out[...] = jnp.sum(dn * hat, axis=0, keepdims=True)
     scaled = dn * gain_ref[1:2, :]
     mean = jnp.mean(scaled * hat, axis=1, keepdims=True)
@@ -393,20 +393,20 @@
         dctx_ref[:, c0 : c0 + cn] = dot_nt(dattn_v[...], w_v[c0 : c0 + cn, :]).astype(BF)
 
 
-def hidden_back_call(dn, logits, router, base, sides, hidden, dout, gains, ctx_rel, wo):
+def hidden_back_call(dn, logits, router, base, core, sides, hidden, dout, gains, ctx_rel, wo):
     seq, width = hidden.shape
     half = jax.ShapeDtypeStruct((seq, width), BF)
     part = piece_shape(1, width, width)
     return pl.pallas_call(
         hidden_back_kernel,
         out_shape=[jax.ShapeDtypeStruct((seq, width), F32), half, part, part, jax.ShapeDtypeStruct((1, width), F32)],
-        in_specs=kernel_specs("vvvvvvvvvva"),
+        in_specs=kernel_specs("vvvvvvvvvvva"),
         out_specs=kernel_specs("vvvvv"),
         scratch_shapes=[pltpu.VMEM((width, width), BF), pltpu.VMEM((seq, width), BF), pltpu.SemaphoreType.DMA],
         compiler_params=pltpu.CompilerParams(vmem_limit_bytes=VMEM_LIMIT),
         cost_estimate=estimate(15 * seq * width * width),
         name="hidden_backward",
-    )(dn, logits, router, base, *sides, hidden, dout, gains, ctx_rel, wo)
+    )(dn, logits, router, base, core, *sides, hidden, dout, gains, ctx_rel, wo)
 
 
 def heads_back_kernel(
@@ -980,7 +980,7 @@
 
     out_near = out_sum.near(order)
     grad_hidden_state, grad_context16, out_even, out_odd, grad_gain_second = hidden_back_call(
-        shared_back, order.now(wide_logits), router_pad, back_sum.take(0), sides, hidden_state, grad_out16, gains, context_rel, attn16[3]
+        shared_back, order.now(wide_logits), router_pad, back_sum.even[0], back_sum.other[0], sides, hidden_state, grad_out16, gains, context_rel, attn16[3]
     )
     order.close(grad_context16)
 
@@ -1002,7 +1002,7 @@
     head_far = head_sum.far(order)
     proj_near = proj_sum.near(order)
     shared_grad = lax.all_to_all(
-        jnp.swapaxes(shared_sum.total().astype(BF), 0, 1), "dp", split_axis=0, concat_axis=0, tiled=True
+        order.now(jnp.swapaxes(shared_sum.total().astype(BF), 0, 1)), "dp", split_axis=0, concat_axis=0, tiled=True
     )
     early_parts = update_call(
         0, order.now(routed_grads[0]), routed_weight, routed_moment, routed_average, [], rate_routed * step_root
@@ -1026,20 +1026,21 @@
     small_grads = jnp.pad(small_grads, ((0, 128 - small_grads.shape[0]), (0, 0)))
     small_grads = jnp.swapaxes(small_grads.T.reshape(parts, groups, -1, 128), 0, 1)
     small_found = lax.all_to_all(small_grads, "expert", split_axis=0, concat_axis=0, tiled=True)
+    order.close(head_near, routed_grads[1:])
+
+    head_total = order.now(head_sum.total().astype(BF))
+    head_found = send_terms(head_total, 1, order)
     routed_parts = early_parts
     for e in range(1, per_device):
         routed_parts = update_call(
-            e, order.now(routed_grads[e]), routed_weight, routed_moment, routed_average, routed_parts, rate_routed * step_root
+            e, after(order.now(routed_grads[e]), head_total), routed_weight, routed_moment, routed_average, routed_parts, rate_routed * step_root
         )
-    order.close(head_near, routed_parts[-1])
-
-    head_total = order.now(head_sum.total().astype(BF))
-    head_found = send_terms(head_total, 1, order)
     proj_found, shared_grad, small_found = after((proj_found, shared_grad, small_found), head_total)
     small_total = tree_sum([small_found[r] for r in range(groups)])
     small_found = lax.all_to_all(small_total, "dp", split_axis=0, concat_axis=0, tiled=True)
     small_grad = tree_sum([small_found[d] for d in range(parts)])
     shared_grad = sum_terms([shared_grad[d] for d in range(parts)])
+    head_found = after(head_found, routed_parts[-1])
     attn_grad = jnp.concatenate([sum_terms(head_found), sum_terms(proj_found)])
     router_grad = small_grad[:, :routed_count]
     gain_grad = small_grad[:, routed_count : routed_count + 2].T

time: 718 us -> 693 us (0.965)
  waiting for transfers between devices: 140 us -> 118 us
    ppermute x61, waiting for transfers between devices: 84.3 us -> 65.9 us  [permute(): return lax.ppermute(values, 'expert', pairs)]
    all_to_all x1, waiting for transfers between devices: 19.7 us -> 2.17 us  [local(): lax.all_to_all(small_total, 'dp', split_axis=0, concat_axis=0, tiled=True)]
    all_to_all x1, waiting for transfers between devices: 0.01 us -> 11.1 us  [local(): lax.all_to_all(order.now(jnp.swapaxes(shared_sum.total().astype(BF), 0, 1...]
    unnamed x191 -> x187, local copies, waits for them, and re-layouts: 15.7 us -> 15.9 us
  transfers between devices with their start and end apart: 83 -> 83, of which waited for: 22 -> 23; matrix products, arithmetic and copies ran while one was open for 16% -> 16% of each run, Pallas kernels for 48% -> 50%
where the time goes in v4:
time: 693 us; the launch traced here: 688 us
  Pallas kernels  343 us (49%)
  waiting for transfers between devices  118 us (17%)
  starting transfers between devices  79.8 us (12%)
  other arithmetic  73.5 us (11%)
  local copies, waits for them, and re-layouts  41.3 us (6%)
  between operations  18.3 us (3%)
  matrix products  13.4 us (2%)
    pallas_call x8, Pallas kernels, expert_pair_call(): pl.pallas_call(functools.partial(expert_pair_kernel, prev is None), out_s...  159 us
    ppermute x61, waiting for transfers between devices, permute(): return lax.ppermute(values, 'expert', pairs)  65.9 us
    pallas_call x2, Pallas kernels, weight_grad_call(): pl.pallas_call(functools.partial(weight_grad_kernel, count), out_shape=ja...  46.3 us
    ppermute x61, starting transfers between devices, permute(): return lax.ppermute(values, 'expert', pairs)  38.3 us
    ppermute x12, waiting for transfers between devices, send_dp(): lax.ppermute(values, 'dp', [(i, i ^ k) for i in range(lax.axis_size('dp'))])  30.1 us
    pallas_call x1, Pallas kernels, attention_call(): pl.pallas_call(functools.partial(attention_kernel, scale), out_shape=[hal...  23.3 us
    pallas_call x1, Pallas kernels, heads_back_call(): pl.pallas_call(functools.partial(heads_back_kernel, scale), out_shape=[ha...  23.2 us
    pallas_call x2, Pallas kernels, update_call(): pl.pallas_call(functools.partial(update_kernel, rate), grid=(kinds, cuts)...  22 us
  transfers between devices with their start and end apart: 83, of which 23 were waited for; matrix products, arithmetic and copies ran while one was open for 16% of the time, Pallas kernels for 50%

profile of v4, /device:TPU:0, one launch (start us, length us, event | category | flops | bytes accessed | tf_op | source)
XLA Modules:
  0.0 687.5 jit_solution(1281081893189316291)
XLA Ops:
  9.6 3.0 collective-permute-start.3
  16.9 2.6 collective-permute-start.1
  19.7 6.0 collective-permute-done.refs_1_
  25.7 10.2 %collective-permute-done.1.refs_2_ = bf16[2,40,1408]{2,1,0:T(8,128)(2,1)S(1)} collective-permute-done((bf16[2,40,1408]{2,1,0:T(8,128)(2,1)S(1)}, bf16[2,40,1408]{2,1,0:T(8,128)(2,1)S(1)}, u32[]{:S(2)}, u32[]{:S(2)}) %collective-permute-start.1) | collective-permute-done | bytes 225312 | tf_op jit(solution)/shard_map/ppermute | solution.py:614
  36.6 2.3 stack_dp.2.refs_0_
  38.9 2.6 collective-permute-done.3.refs_7_.refs_8_
  46.6 2.6 collective-permute-start.8
  49.4 3.3 collective-permute-done.7.refs_1_
  52.7 10.6 %collective-permute-done.8.refs_2_ = bf16[2,40,1280]{2,1,0:T(8,128)(2,1)S(1)} collective-permute-done((bf16[2,40,1280]{2,1,0:T(8,128)(2,1)S(1)}, bf16[2,40,1280]{2,1,0:T(8,128)(2,1)S(1)}, u32[]{:S(2)}, u32[]{:S(2)}) %collective-permute-start.8) | collective-permute-done | bytes 204832 | tf_op jit(solution)/shard_map/ppermute | solution.py:614
  69.4 4.4 all-to-all-start
  75.5 12.9 %collective-permute-done.14.refs_10_ = bf16[4,2,40,1280]{3,2,1,0:T(8,128)(2,1)} collective-permute-done((bf16[4,2,40,1280]{3,2,1,0:T(8,128)(2,1)}, bf16[4,2,40,1280]{3,2,1,0:T(8,128)(2,1)}, u32[]{:S(2)}, u32[]{:S(2)}) %collective-permute-start.14) | collective-permute-done | bytes 819232 | tf_op jit(solution)/shard_map/ppermute | solution.py:587
  89.0 3.4 convert.49
  94.4 10.3 %collective-permute-done.15.refs_12_ = bf16[4,2,40,1280]{3,2,1,0:T(8,128)(2,1)S(1)} collective-permute-done((bf16[4,2,40,1280]{3,2,1,0:T(8,128)(2,1)S(1)}, bf16[4,2,40,1280]{3,2,1,0:T(8,128)(2,1)S(1)}, u32[]{:S(2)}, u32[]{:S(2)}) %collective-permute-start.15) | collective-permute-done | bytes 819232 | tf_op jit(solution)/shard_map/ppermute | solution.py:587
  110.9 11.4 %collective-permute-done.20.refs_14_ = bf16[4,2,40,1280]{3,2,1,0:T(8,128)(2,1)} collective-permute-done((bf16[4,2,40,1280]{3,2,1,0:T(8,128)(2,1)S(1)}, bf16[4,2,40,1280]{3,2,1,0:T(8,128)(2,1)}, u32[]{:S(2)}, u32[]{:S(2)}) %collective-permute-start.20) | collective-permute-done | bytes 819232 | tf_op jit(solution)/shard_map/ppermute | solution.py:587
  125.4 3.4 all-to-all-start.1
  135.6 10.0 %place_rows.2 = (bf16[4,8,40,1280]{3,2,1,0:T(8,128)(2,1)}, bf16[4,8,40,1280]{3,2,1,0:T(8,128)(2,1)}, bf16[4,8,40,1280]{3,2,1,0:T(8,128)(2,1)}, bf16[4,8,40,1280]{3,2,1,0:T(8,128)(2,1)}, bf16[4,8,40,128]{3,2,1,0:T(8,128)(2,1)}) custom-call(s32[1]{0:T(128)} %bitcast.at_ref, bf16[4,2,40,1408]{3,2,1,0:T(8,128)(2,1)} %stack_dp.2.refs_0_, ...), custom_call_target="tpu_custom_call" | custom-call | bytes 1 | tf_op jit(solution)/shard_map/place_rows/pallas_call | solution.py:732
  147.3 23.3 %attention_forward.1 = (bf16[512,1280]{1,0:T(8,128)(2,1)}, bf16[512,1280]{1,0:T(8,128)(2,1)}, bf16[512,1280]{1,0:T(8,128)(2,1)}, bf16[512,1280]{1,0:T(8,128)(2,1...) custom-call(bf16[512,1280]{1,0:T(8,128)(2,1)} %tok_ref.3, ...), custom_call_target="tpu_custom_call" | custom-call | bytes 1 | tf_op jit(solution)/shard_map/attention_forward/pallas_call | solution.py:342
  171.8 2.3 broadcast_select_fusion.3
  175.3 3.0 fusion.9.second_rel_ref
  180.3 3.0 fusion.8.dout_rel_ref
  183.3 10.2 %collective-permute-done.28.refs_6_ = bf16[4,3,40,896]{3,2,1,0:T(8,128)(2,1)} collective-permute-done((bf16[4,3,40,896]{3,2,1,0:T(8,128)(2,1)}, bf16[4,3,40,896]{3,2,1,0:T(8,128)(2,1)}, u32[]{:S(2)}, u32[]{:S(2)}) %collective-permute-start.28) | collective-permute-done | bytes 860192 | tf_op jit(solution)/shard_map/ppermute | solution.py:587
  197.0 6.0 place_rows.3
  203.0 20.5 %shared_expert.1 = (f32[512,1280]{1,0:T(8,128)}, f32[512,1280]{1,0:T(8,128)}, bf16[4,3,160,896]{3,2,1,0:T(8,128)(2,1)}, bf16[4,3,160,896]{3,2,1,0:T(8,128)(2,1)}) custom-call(bf16[512,1280]{1,0:T(8,128)(2,1)} %get-tuple-element.443.second_ref.refs_5_.refs_6_, bf16[1280,512]{1,0:T(8,128)(2,1)} %fusion.9.second_rel_ref, bf16[512,1280]{1,0:T(8,128)(2,1)} %copy-done.3, ...), custom_call_target="tpu_custom_call" | custom-call | bytes 1 | tf_op jit(solution)/shard_map/shared_expert/pallas_call | solution.py:546
  232.7 20.5 %expert_pair.8 = (bf16[512,1280]{1,0:T(8,128)(2,1)}, bf16[512,1280]{1,0:T(8,128)(2,1)}, bf16[512,1280]{1,0:T(8,128)(2,1)}, bf16[512,1280]{1,0:T(8,128)(2,1)}, f3...) custom-call(s32[1]{0:T(128)} %get-tuple-element.720.refs_0_, ...), custom_call_target="tpu_custom_call" | custom-call | flops 5284823040 | bytes 1 | tf_op jit(solution)/shard_map/expert_pair/pallas_call | solution.py:180
  253.2 3.0 fusion.11.ctx_ref
  256.2 3.0 fusion.10.first_ref
  259.3 2.6 collective-permute-done.37.refs_5_.refs_6_
  264.1 2.9 collective-permute-done.40.refs_6_.refs_7_
  268.0 18.9 %expert_pair.9 = (bf16[512,1280]{1,0:T(8,128)(2,1)}, bf16[512,1280]{1,0:T(8,128)(2,1)}, bf16[512,1280]{1,0:T(8,128)(2,1)}, bf16[512,1280]{1,0:T(8,128)(2,1)}, f3...) custom-call(s32[1]{0:T(128)} %get-tuple-element.720.refs_0_, ...), custom_call_target="tpu_custom_call" | custom-call | flops 5284823040 | bytes 1 | tf_op jit(solution)/shard_map/expert_pair/pallas_call | solution.py:180
  287.0 2.2 fusion.32
  290.8 19.0 %expert_pair.10 = (bf16[512,1280]{1,0:T(8,128)(2,1)}, bf16[512,1280]{1,0:T(8,128)(2,1)}, bf16[512,1280]{1,0:T(8,128)(2,1)}, bf16[512,1280]{1,0:T(8,128)(2,1)}, f...) custom-call(s32[1]{0:T(128)} %get-tuple-element.720.refs_0_, ...), custom_call_target="tpu_custom_call" | custom-call | flops 5284823040 | bytes 1 | tf_op jit(solution)/shard_map/expert_pair/pallas_call | solution.py:180
  309.7 19.2 %expert_pair.11 = (bf16[512,1280]{1,0:T(8,128)(2,1)}, bf16[512,1280]{1,0:T(8,128)(2,1)}, bf16[512,1280]{1,0:T(8,128)(2,1)}, bf16[512,1280]{1,0:T(8,128)(2,1)}, f...) custom-call(s32[1]{0:T(128)} %get-tuple-element.720.refs_0_, ...), custom_call_target="tpu_custom_call" | custom-call | flops 5284823040 | bytes 1 | tf_op jit(solution)/shard_map/expert_pair/pallas_call | solution.py:180
  329.9 23.1 %expert_weights.2 = bf16[4,3,320,896]{3,2,1,0:T(8,128)(2,1)} custom-call(bf16[512,1280]{1,0:T(8,128)(2,1)} %get-tuple-element.394.refs_0_, bf16[512,1280]{1,0:T(8,128)(2,1)} %get-tuple-element.395.refs_1_, bf16[512,896]{1,0:T(8,128)(2,1)} %get-tuple-element.396.refs_2_, bf16[512,1792]{1,0:T(8,128)(2,1)} %get-tuple-element.397.refs_3_, ...), custom_call_target="tpu_custom_call" | custom-call | flops 14092861440 | bytes 1 | tf_op jit(solution)/shard_map/expert_weights/pallas_call | solution.py:251
  353.1 3.7 all-gather.7.cloned.1.call-done
  356.8 20.4 %expert_pair.12 = (bf16[512,1280]{1,0:T(8,128)(2,1)}, bf16[512,1280]{1,0:T(8,128)(2,1)}, bf16[512,1280]{1,0:T(8,128)(2,1)}, bf16[512,1280]{1,0:T(8,128)(2,1)}, f...) custom-call(s32[1]{0:T(128)} %get-tuple-element.721.refs_0_, ...), custom_call_target="tpu_custom_call" | custom-call | flops 5284823040 | bytes 1 | tf_op jit(solution)/shard_map/expert_pair/pallas_call | solution.py:180
  377.8 20.3 %expert_pair.13 = (bf16[512,1280]{1,0:T(8,128)(2,1)}, bf16[512,1280]{1,0:T(8,128)(2,1)}, bf16[512,1280]{1,0:T(8,128)(2,1)}, bf16[512,1280]{1,0:T(8,128)(2,1)}, f...) custom-call(s32[1]{0:T(128)} %get-tuple-element.721.refs_0_, ...), custom_call_target="tpu_custom_call" | custom-call | flops 5284823040 | bytes 1 | tf_op jit(solution)/shard_map/expert_pair/pallas_call | solution.py:180
  399.7 2.8 add_convert_fusion.1
  406.1 20.5 %expert_pair.14 = (bf16[512,1280]{1,0:T(8,128)(2,1)}, bf16[512,1280]{1,0:T(8,128)(2,1)}, bf16[512,1280]{1,0:T(8,128)(2,1)}, bf16[512,1280]{1,0:T(8,128)(2,1)}, f...) custom-call(s32[1]{0:T(128)} %get-tuple-element.721.refs_0_, ...), custom_call_target="tpu_custom_call" | custom-call | flops 5284823040 | bytes 1 | tf_op jit(solution)/shard_map/expert_pair/pallas_call | solution.py:180
  430.0 3.9 fusion.15
  435.7 20.5 %expert_pair.15 = (bf16[512,1280]{1,0:T(8,128)(2,1)}, bf16[512,1280]{1,0:T(8,128)(2,1)}, bf16[512,1280]{1,0:T(8,128)(2,1)}, bf16[512,1280]{1,0:T(8,128)(2,1)}, f...) custom-call(s32[1]{0:T(128)} %get-tuple-element.721.refs_0_, ...), custom_call_target="tpu_custom_call" | custom-call | flops 5284823040 | bytes 1 | tf_op jit(solution)/shard_map/expert_pair/pallas_call | solution.py:180
  461.1 4.0 all-to-all-start.2
  465.1 3.1 add_convert_fusion
  472.1 23.2 %expert_weights.3 = bf16[4,3,320,896]{3,2,1,0:T(8,128)(2,1)} custom-call(bf16[512,1280]{1,0:T(8,128)(2,1)} %get-tuple-element.472.refs_0_, bf16[512,1280]{1,0:T(8,128)(2,1)} %get-tuple-element.473.refs_1_, bf16[512,896]{1,0:T(8,128)(2,1)} %get-tuple-element.474.refs_2_, bf16[512,1792]{1,0:T(8,128)(2,1)} %get-tuple-element.475.refs_3_, ...), custom_call_target="tpu_custom_call" | custom-call | flops 14092861440 | bytes 1 | tf_op jit(solution)/shard_map/expert_weights/pallas_call | solution.py:251
  501.4 13.6 %hidden_backward.1 = (f32[512,1280]{1,0:T(8,128)}, bf16[512,1280]{1,0:T(8,128)(2,1)}, bf16[4,1,160,1280]{3,2,1,0:T(8,128)(2,1)}, bf16[4,1,160,1280]{3,2,1,0:T(8,128)(2,1)}, f32[1,1280]{1,0:T(1,128)}) custom-call(f32[512,1280]{1,0:T(8,128)} %get-tuple-element.341.dn_ref, f32[512,128]{1,0:T(8,128)} %pad.24.logit_ref, ...), custom_call_target="tpu_custom_call" | custom-call | flops 12582912000 | bytes 1 | tf_op jit(solution)/shard_map/hidden_backward/pallas_call | solution.py:400
  515.1 4.3 fusion.19
  521.5 23.2 %heads_backward.1 = (bf16[512,1280]{1,0:T(8,128)(2,1)}, bf16[512,1280]{1,0:T(8,128)(2,1)}, bf16[512,1280]{1,0:T(8,128)(2,1)}, bf16[4,3,160,1280]{3,2,1,0:T(8,128)(2,1)}, bf16[4,3,160,1280]{3,2,1,0:T(8,128)(2,1)}) custom-call(bf16[512,1280]{1,0:T(8,128)(2,1)} %get-tuple-element.322.q_ref, bf16[512,1280]{1,0:T(8,128)(2,1)} %get-tuple-element.323.k_ref, ...), custom_call_target="tpu_custom_call" | custom-call | flops 21810380800 | bytes 1 | tf_op jit(solution)/shard_map/heads_backward/pallas_call | solution.py:457
  544.8 6.2 collective-permute-done.58
  560.6 14.8 %input_backward.1 = (f32[512,1280]{1,0:T(8,128)}, f32[1,1280]{1,0:T(1,128)}, f32[1]{0:T(128)}) custom-call(bf16[512,1280]{1,0:T(8,128)(2,1)} %get-tuple-element.513.dq_ref, bf16[512,1280]{1,0:T(8,128)(2,1)} %get-tuple-element.514.dk_ref, bf16[512,1280]{1,0:T(8,128)(2,1)} %get-tuple-element.515.dv_ref, bf16[512,1280]{1,0:T(8,128)(2,1)} %tok_ref.3, ...), custom_call_target="tpu_custom_call" | custom-call | flops 15099494400 | bytes 1 | tf_op jit(solution)/shard_map/input_backward/pallas_call | solution.py:497
  575.5 2.3 fusion.44
  579.9 2.6 fusion.28
  584.9 3.7 all-to-all-start.3
  590.6 2.3 fusion.47
  592.9 11.0 %routed_update.2 = (f32[2,3,320,896]{3,2,1,0:T(8,128)}, f32[2,3,320,896]{3,2,1,0:T(8,128)}, f32[2,3,320,896]{3,2,1,0:T(8,128)}, f32[2,3,320,896]{3,2,1,0:T(8,128)}, bf16[2,3,320,896]{3,2,1,0:T(8,128)(2,1)}) custom-call(bf16[3,320,896]{2,1,0:T(8,128)(2,1)} %bitcast.228, f32[2,3,320,896]{3,2,1,0:T(8,128)} %w_ref.3, f32[2,3,320,896]{3,2,1,0:T(8,128)} %m_ref.3, ...), custom_call_target="tpu_custom_call" | custom-call | flops 10000000000 | bytes 1 | tf_op jit(solution)/shard_map/routed_update/pallas_call | solution.py:571
  604.0 4.6 fusion.24
  611.8 4.6 fusion.20
  620.3 3.1 collective-permute-start.65
  623.4 11.1 %all-to-all-done.3 = bf16[4,3,40,896]{3,2,1,0:T(8,128)(2,1)S(1)} async-done(((bf16[4,3,40,896]{3,2,1,0:T(8,128)(2,1)}), bf16[4,3,40,896]{3,2,1,0:T(8,128)(2,1)S(1)}, u32[]{:S(2)}, u32[]{:S(2)}) %all-to-all-start.3) | async-done | bytes 860192 | tf_op jit(solution)/shard_map/all_to_all | solution.py:1004
  634.5 4.2 all-to-all-start.4
  638.7 2.6 fusion.27
  644.5 2.3 collective-permute-start.70
  646.8 3.1 all-to-all-done.4
  651.7 3.4 all-to-all-start.5
  658.5 11.0 %routed_update.3 = (f32[2,3,320,896]{3,2,1,0:T(8,128)}, f32[2,3,320,896]{3,2,1,0:T(8,128)}, f32[2,3,320,896]{3,2,1,0:T(8,128)}, f32[2,3,320,896]{3,2,1,0:T(8,128)}, bf16[2,3,320,896]{3,2,1,0:T(8,128)(2,1)}) custom-call(bf16[3,320,896]{2,1,0:T(8,128)(2,1)} %bitcast.208, ...), custom_call_target="tpu_custom_call", output_to_operand_aliasing={{0}: (4, {}), {1}: (5, {}), {2}: (6, {}), {3}: (7, {}), {4}... | custom-call | flops 10000000000 | bytes 1 | tf_op jit(solution)/shard_map/routed_update/pallas_call | solution.py:571
  670.3 2.2 all-to-all-done.5
  (436 shorter events, 129.2 us)
Async XLA Ops:
  9.6 31.9 %collective-permute-start.3 = (bf16[512,1280]{1,0:T(8,128)(2,1)S(1)}, bf16[512,1280]{1,0:T(8,128)(2,1)}, u32[]{:S(2)}, u32[]{:S(2)}) collective-permute-start(bf16[512,1280]{1,0:T(8,128)(2,1)S(1)} %multiply_convert_fusion.dout_ref.refs_7_.refs_8_), channel_id=1, source_target_pairs={{0,2},{1,3},{2,0},{3,1},{4,6},{5,7},{6,4},{7,5},{8,10},{9,11},{10,... | collective-permute-start | bytes 3932168 | tf_op jit(solution)/shard_map/ppermute | solution.py:587
  12.6 30.3 %collective-permute-start.4 = (bf16[512,1280]{1,0:T(8,128)(2,1)S(1)}, bf16[512,1280]{1,0:T(8,128)(2,1)}, u32[]{:S(2)}, u32[]{:S(2)}) collective-permute-start(bf16[512,1280]{1,0:T(8,128)(2,1)S(1)} %multiply_convert_fusion.dout_ref.refs_7_.refs_8_), channel_id=1, source_target_pairs={{0,4},{1,5},{2,6},{3,7},{4,0},{5,1},{6,2},{7,3},{8,12},{9,13},{10,... | collective-permute-start | bytes 3932168 | tf_op jit(solution)/shard_map/ppermute | solution.py:587
  16.9 19.0 %collective-permute-start.1 = (bf16[2,40,1408]{2,1,0:T(8,128)(2,1)S(1)}, bf16[2,40,1408]{2,1,0:T(8,128)(2,1)S(1)}, u32[]{:S(2)}, u32[]{:S(2)}) collective-permute-start(bf16[2,40,1408]{2,1,0:T(8,128)(2,1)S(1)} %fusion.51.refs_0_), channel_id=1, source_target_pairs={{0,16},{8,24},{16,0},{24,8},{1,17},{9,25},{17,1},{25,9},{2,18},{10... | collective-permute-start | bytes 675848 | tf_op jit(solution)/shard_map/ppermute | solution.py:614
  19.5 16.4 %collective-permute-start.2 = (bf16[2,40,1408]{2,1,0:T(8,128)(2,1)S(1)}, bf16[2,40,1408]{2,1,0:T(8,128)(2,1)S(1)}, u32[]{:S(2)}, u32[]{:S(2)}) collective-permute-start(bf16[2,40,1408]{2,1,0:T(8,128)(2,1)S(1)} %fusion.51.refs_0_), channel_id=1, source_target_pairs={{0,24},{8,16},{16,8},{24,0},{1,25},{9,17},{17,9},{25,1},{2,26},{10... | collective-permute-start | bytes 675848 | tf_op jit(solution)/shard_map/ppermute | solution.py:614
  42.9 23.9 %collective-permute-start.5 = (bf16[4,2,40,1408]{3,2,1,0:T(8,128)(2,1)}, bf16[4,2,40,1408]{3,2,1,0:T(8,128)(2,1)S(1)}, u32[]{:S(2)}, u32[]{:S(2)}) collective-permute-start(bf16[4,2,40,1408]{3,2,1,0:T(8,128)(2,1)} %stack_dp.2.refs_0_), channel_id=1, source_target_pairs={{0,2},{1,3},{2,0},{3,1},{4,6},{5,7},{6,4},{7,5},{8,10},{9,11},{10,... | collective-permute-start | bytes 2703368 | tf_op jit(solution)/shard_map/ppermute | solution.py:587
  43.3 23.6 %collective-permute-start.6 = (bf16[4,2,40,1408]{3,2,1,0:T(8,128)(2,1)}, bf16[4,2,40,1408]{3,2,1,0:T(8,128)(2,1)S(1)}, u32[]{:S(2)}, u32[]{:S(2)}) collective-permute-start(bf16[4,2,40,1408]{3,2,1,0:T(8,128)(2,1)} %stack_dp.2.refs_0_), channel_id=1, source_target_pairs={{0,4},{1,5},{2,6},{3,7},{4,0},{5,1},{6,2},{7,3},{8,12},{9,13},{10,... | collective-permute-start | bytes 2703368 | tf_op jit(solution)/shard_map/ppermute | solution.py:587
  46.6 16.7 %collective-permute-start.8 = (bf16[2,40,1280]{2,1,0:T(8,128)(2,1)S(1)}, bf16[2,40,1280]{2,1,0:T(8,128)(2,1)S(1)}, u32[]{:S(2)}, u32[]{:S(2)}) collective-permute-start(bf16[2,40,1280]{2,1,0:T(8,128)(2,1)S(1)} %copy-done.48), channel_id=1, source_target_pairs={{0,16},{8,24},{16,0},{24,8},{1,17},{9,25},{17,1},{25,9},{2,18},{10... | collective-permute-start | bytes 614408 | tf_op jit(solution)/shard_map/ppermute | solution.py:614
  66.9 21.6 %collective-permute-start.14 = (bf16[4,2,40,1280]{3,2,1,0:T(8,128)(2,1)}, bf16[4,2,40,1280]{3,2,1,0:T(8,128)(2,1)}, u32[]{:S(2)}, u32[]{:S(2)}) collective-permute-start(bf16[4,2,40,1280]{3,2,1,0:T(8,128)(2,1)} %stack_dp.3.refs_8_), channel_id=1, source_target_pairs={{0,2},{1,3},{2,0},{3,1},{4,6},{5,7},{6,4},{7,5},{8,10},{9,11},{10,... | collective-permute-start | bytes 2457608 | tf_op jit(solution)/shard_map/ppermute | solution.py:587
  69.4 37.8 %all-to-all-start = ((bf16[4,3,40,896]{3,2,1,0:T(8,128)(2,1)}), bf16[4,3,40,896]{3,2,1,0:T(8,128)(2,1)}, u32[]{:S(2)}, u32[]{:S(2)}) async-start(bf16[4,3,40,896]{3,2,1,0:T(8,128)(2,1)} %broadcast_in_dim.101), calls=%async_computation | async-start | bytes 1720320 | tf_op jit(solution)/shard_map/all_to_all | solution.py:820
  73.8 158.9 %all-gather.5.cloned.1.call-start = ((), (), s32[]{:S(2)}) async-start(), calls=%async_computation.10 | async-start | bytes 8601600 | tf_op jit(solution)/shard_map/all_gather | solution.py:830
  73.9 30.8 %collective-permute-start.13 = (bf16[4,2,40,1408]{3,2,1,0:T(8,128)(2,1)S(1)}, bf16[4,2,40,1408]{3,2,1,0:T(8,128)(2,1)S(1)}, u32[]{:S(2)}, u32[]{:S(2)}) collective-permute-start(bf16[4,2,40,1408]{3,2,1,0:T(8,128)(2,1)S(1)} %broadcast_select_fusion.2), channel_id=1, source_target_pairs={{0,4},{1,3},{2,6},{3,1},{4,0},{5,7},{6,2},{7,5},{8,12},{9,11},{10,... | collective-permute-start | bytes 2703368 | tf_op jit(solution)/shard_map/ppermute | solution.py:587
  75.0 29.8 %collective-permute-start.10 = (bf16[4,2,40,1408]{3,2,1,0:T(8,128)(2,1)S(1)}, bf16[4,2,40,1408]{3,2,1,0:T(8,128)(2,1)S(1)}, u32[]{:S(2)}, u32[]{:S(2)}) collective-permute-start(bf16[4,2,40,1408]{3,2,1,0:T(8,128)(2,1)S(1)} %copy-done.8), channel_id=1, source_target_pairs={{0,1},{1,0},{2,3},{3,2},{4,5},{5,4},{6,7},{7,6},{8,9},{9,8},{10,11... | collective-permute-start | bytes 2703368 | tf_op jit(solution)/shard_map/ppermute | solution.py:587
  75.0 29.8 %collective-permute-start.12 = (bf16[4,2,40,1408]{3,2,1,0:T(8,128)(2,1)S(1)}, bf16[4,2,40,1408]{3,2,1,0:T(8,128)(2,1)S(1)}, u32[]{:S(2)}, u32[]{:S(2)}) collective-permute-start(bf16[4,2,40,1408]{3,2,1,0:T(8,128)(2,1)S(1)} %collective-permute-done.6.refs_4_), channel_id=1, source_target_pairs={{0,1},{1,0},{2,3},{3,2},{4,5},{5,4},{6,7},{7,6},{8,9},{9,8},{10,11... | collective-permute-start | bytes 2703368 | tf_op jit(solution)/shard_map/ppermute | solution.py:587
  75.5 31.7 %collective-permute-start.11 = (bf16[4,2,40,1408]{3,2,1,0:T(8,128)(2,1)S(1)}, bf16[4,2,40,1408]{3,2,1,0:T(8,128)(2,1)}, u32[]{:S(2)}, u32[]{:S(2)}) collective-permute-start(bf16[4,2,40,1408]{3,2,1,0:T(8,128)(2,1)S(1)} %collective-permute-done.5.refs_2_), channel_id=1, source_target_pairs={{0,1},{1,0},{2,3},{3,2},{4,5},{5,4},{6,7},{7,6},{8,9},{9,8},{10,11... | collective-permute-start | bytes 2703368 | tf_op jit(solution)/shard_map/ppermute | solution.py:587
  88.4 16.3 %collective-permute-start.15 = (bf16[4,2,40,1280]{3,2,1,0:T(8,128)(2,1)S(1)}, bf16[4,2,40,1280]{3,2,1,0:T(8,128)(2,1)S(1)}, u32[]{:S(2)}, u32[]{:S(2)}) collective-permute-start(bf16[4,2,40,1280]{3,2,1,0:T(8,128)(2,1)S(1)} %copy-done.13), channel_id=1, source_target_pairs={{0,4},{1,5},{2,6},{3,7},{4,0},{5,1},{6,2},{7,3},{8,12},{9,13},{10,... | collective-permute-start | bytes 2457608 | tf_op jit(solution)/shard_map/ppermute | solution.py:587
  125.4 68.7 %all-to-all-start.1 = ((bf16[8,16,512]{2,1,0:T(8,128)(2,1)}), bf16[8,16,512]{2,1,0:T(8,128)(2,1)S(1)}, u32[]{:S(2)}, u32[]{:S(2)}) async-start(bf16[8,16,512]{2,1,0:T(8,128)(2,1)} %broadcast_in_dim.104), calls=%async_computation.1 | async-start | bytes 262144 | tf_op jit(solution)/shard_map/all_to_all | solution.py:814
  128.8 228.0 %all-gather.7.cloned.1.call-start = ((), (), s32[]{:S(2)}) async-start(), calls=%async_computation.11 | async-start | bytes 8601600 | tf_op jit(solution)/shard_map/all_gather | solution.py:830
  129.4 41.5 %collective-permute-start.27 = (bf16[512,1280]{1,0:T(8,128)(2,1)}, bf16[512,1280]{1,0:T(8,128)(2,1)}, u32[]{:S(2)}, u32[]{:S(2)}) collective-permute-start(bf16[512,1280]{1,0:T(8,128)(2,1)} %collective-permute-done.4.refs_7_.refs_8_), channel_id=1, source_target_pairs={{0,1},{1,0},{2,3},{3,2},{4,5},{5,4},{6,7},{7,6},{8,9},{9,8},{10,11... | collective-permute-start | bytes 3932168 | tf_op jit(solution)/shard_map/ppermute | solution.py:587
  129.9 41.0 %collective-permute-start.26 = (bf16[512,1280]{1,0:T(8,128)(2,1)}, bf16[512,1280]{1,0:T(8,128)(2,1)}, u32[]{:S(2)}, u32[]{:S(2)}) collective-permute-start(bf16[512,1280]{1,0:T(8,128)(2,1)} %collective-permute-done.3.refs_7_.refs_8_), channel_id=1, source_target_pairs={{0,1},{1,0},{2,3},{3,2},{4,5},{5,4},{6,7},{7,6},{8,9},{9,8},{10,11... | collective-permute-start | bytes 3932168 | tf_op jit(solution)/shard_map/ppermute | solution.py:587
  130.0 40.9 %collective-permute-start.25 = (bf16[512,1280]{1,0:T(8,128)(2,1)S(1)}, bf16[512,1280]{1,0:T(8,128)(2,1)}, u32[]{:S(2)}, u32[]{:S(2)}) collective-permute-start(bf16[512,1280]{1,0:T(8,128)(2,1)S(1)} %multiply_convert_fusion.dout_ref.refs_7_.refs_8_), channel_id=1, source_target_pairs={{0,1},{1,0},{2,3},{3,2},{4,5},{5,4},{6,7},{7,6},{8,9},{9,8},{10,11... | collective-permute-start | bytes 3932168 | tf_op jit(solution)/shard_map/ppermute | solution.py:587
  130.4 40.2 %collective-permute-start.23 = (bf16[4,3,40,896]{3,2,1,0:T(8,128)(2,1)}, bf16[4,3,40,896]{3,2,1,0:T(8,128)(2,1)}, u32[]{:S(2)}, u32[]{:S(2)}) collective-permute-start(bf16[4,3,40,896]{3,2,1,0:T(8,128)(2,1)} %all-to-all-done.refs_0_), channel_id=1, source_target_pairs={{0,2},{1,3},{2,0},{3,1},{4,6},{5,7},{6,4},{7,5},{8,10},{9,11},{10,... | collective-permute-start | bytes 2580488 | tf_op jit(solution)/shard_map/ppermute | solution.py:587
  134.1 36.8 %collective-permute-start.24 = (bf16[4,3,40,896]{3,2,1,0:T(8,128)(2,1)}, bf16[4,3,40,896]{3,2,1,0:T(8,128)(2,1)}, u32[]{:S(2)}, u32[]{:S(2)}) collective-permute-start(bf16[4,3,40,896]{3,2,1,0:T(8,128)(2,1)} %all-to-all-done.refs_0_), channel_id=1, source_target_pairs={{0,4},{1,5},{2,6},{3,7},{4,0},{5,1},{6,2},{7,3},{8,12},{9,13},{10,... | collective-permute-start | bytes 2580488 | tf_op jit(solution)/shard_map/ppermute | solution.py:587
  171.6 421.3 %reduce-scatter.3.cloned.1.call-start = ((), (), s32[]{:S(2)}) async-start(), calls=%async_computation.8 | async-start | bytes 8601600 | tf_op jit(solution)/shard_map/reduce_scatter | solution.py:929
  174.6 18.8 %collective-permute-start.28 = (bf16[4,3,40,896]{3,2,1,0:T(8,128)(2,1)}, bf16[4,3,40,896]{3,2,1,0:T(8,128)(2,1)}, u32[]{:S(2)}, u32[]{:S(2)}) collective-permute-start(bf16[4,3,40,896]{3,2,1,0:T(8,128)(2,1)} %broadcast_select_fusion.3), channel_id=1, source_target_pairs={{0,4},{1,3},{2,6},{3,1},{4,0},{5,7},{6,2},{7,5},{8,12},{9,11},{10,... | collective-permute-start | bytes 2580488 | tf_op jit(solution)/shard_map/ppermute | solution.py:587
  178.2 45.2 %collective-permute-start.33 = (bf16[512,1280]{1,0:T(8,128)(2,1)S(1)}, bf16[512,1280]{1,0:T(8,128)(2,1)}, u32[]{:S(2)}, u32[]{:S(2)}) collective-permute-start(bf16[512,1280]{1,0:T(8,128)(2,1)S(1)} %copy-done), channel_id=1, source_target_pairs={{0,2},{1,3},{2,0},{3,1},{4,6},{5,7},{6,4},{7,5},{8,10},{9,11},{10,... | collective-permute-start | bytes 3932168 | tf_op jit(solution)/shard_map/ppermute | solution.py:587
  178.7 44.7 %collective-permute-start.34 = (bf16[512,1280]{1,0:T(8,128)(2,1)S(1)}, bf16[512,1280]{1,0:T(8,128)(2,1)}, u32[]{:S(2)}, u32[]{:S(2)}) collective-permute-start(bf16[512,1280]{1,0:T(8,128)(2,1)S(1)} %copy-done), channel_id=1, source_target_pairs={{0,4},{1,5},{2,6},{3,7},{4,0},{5,1},{6,2},{7,3},{8,12},{9,13},{10,... | collective-permute-start | bytes 3932168 | tf_op jit(solution)/shard_map/ppermute | solution.py:587
  223.5 38.4 %collective-permute-start.38 = (bf16[4,3,4,40,896]{4,3,2,1,0:T(8,128)(2,1)}, bf16[4,3,4,40,896]{4,3,2,1,0:T(8,128)(2,1)}, u32[]{:S(2)}, u32[]{:S(2)}) collective-permute-start(bf16[4,3,4,40,896]{4,3,2,1,0:T(8,128)(2,1)} %bitcast.227), channel_id=1, source_target_pairs={{0,1},{1,0},{2,3},{3,2},{4,5},{5,4},{6,7},{7,6},{8,9},{9,8},{10,11... | collective-permute-start | bytes 10321928 | tf_op jit(solution)/shard_map/ppermute | solution.py:587
  230.1 29.2 %collective-permute-start.39 = (bf16[512,1280]{1,0:T(8,128)(2,1)S(1)}, bf16[512,1280]{1,0:T(8,128)(2,1)}, u32[]{:S(2)}, u32[]{:S(2)}) collective-permute-start(bf16[512,1280]{1,0:T(8,128)(2,1)S(1)} %broadcast_select_fusion), channel_id=1, source_target_pairs={{0,4},{1,3},{2,6},{3,1},{4,0},{5,7},{6,2},{7,5},{8,12},{9,11},{10,... | collective-permute-start | bytes 3932168 | tf_op jit(solution)/shard_map/ppermute | solution.py:587
  230.7 28.6 %collective-permute-start.36 = (bf16[512,1280]{1,0:T(8,128)(2,1)}, bf16[512,1280]{1,0:T(8,128)(2,1)}, u32[]{:S(2)}, u32[]{:S(2)}) collective-permute-start(bf16[512,1280]{1,0:T(8,128)(2,1)} %collective-permute-done.34.refs_5_.refs_6_), channel_id=1, source_target_pairs={{0,1},{1,0},{2,3},{3,2},{4,5},{5,4},{6,7},{7,6},{8,9},{9,8},{10,11... | collective-permute-start | bytes 3932168 | tf_op jit(solution)/shard_map/ppermute | solution.py:587
  230.8 28.5 %collective-permute-start.35 = (bf16[512,1280]{1,0:T(8,128)(2,1)}, bf16[512,1280]{1,0:T(8,128)(2,1)}, u32[]{:S(2)}, u32[]{:S(2)}) collective-permute-start(bf16[512,1280]{1,0:T(8,128)(2,1)} %collective-permute-done.33.refs_5_.refs_6_), channel_id=1, source_target_pairs={{0,1},{1,0},{2,3},{3,2},{4,5},{5,4},{6,7},{7,6},{8,9},{9,8},{10,11... | collective-permute-start | bytes 3932168 | tf_op jit(solution)/shard_map/ppermute | solution.py:587
  231.2 30.7 %collective-permute-start.37 = (bf16[512,1280]{1,0:T(8,128)(2,1)S(1)}, bf16[512,1280]{1,0:T(8,128)(2,1)}, u32[]{:S(2)}, u32[]{:S(2)}) collective-permute-start(bf16[512,1280]{1,0:T(8,128)(2,1)S(1)} %broadcast_select_fusion.1), channel_id=1, source_target_pairs={{0,4},{1,3},{2,6},{3,1},{4,0},{5,7},{6,2},{7,5},{8,12},{9,11},{10,... | collective-permute-start | bytes 3932168 | tf_op jit(solution)/shard_map/ppermute | solution.py:587
  261.9 25.1 %collective-permute-start.41 = (bf16[512,1280]{1,0:T(8,128)(2,1)}, bf16[512,1280]{1,0:T(8,128)(2,1)}, u32[]{:S(2)}, u32[]{:S(2)}) collective-permute-start(bf16[512,1280]{1,0:T(8,128)(2,1)} %collective-permute-done.39.refs_7_.refs_8_), channel_id=1, source_target_pairs={{0,1},{1,0},{2,3},{3,2},{4,5},{5,4},{6,7},{7,6},{8,9},{9,8},{10,11... | collective-permute-start | bytes 3932168 | tf_op jit(solution)/shard_map/ppermute | solution.py:587
  267.0 20.0 %collective-permute-start.42 = (bf16[3,4,40,896]{3,2,1,0:T(8,128)(2,1)S(1)}, bf16[3,4,40,896]{3,2,1,0:T(8,128)(2,1)S(1)}, u32[]{:S(2)}, u32[]{:S(2)}) collective-permute-start(bf16[3,4,40,896]{3,2,1,0:T(8,128)(2,1)S(1)} %fusion.36), channel_id=1, source_target_pairs={{0,4},{1,3},{2,6},{3,1},{4,0},{5,7},{6,2},{7,5},{8,12},{9,11},{10,... | collective-permute-start | bytes 2580488 | tf_op jit(solution)/shard_map/ppermute | solution.py:587
  289.1 39.8 %collective-permute-start.43 = (bf16[3,4,40,896]{3,2,1,0:T(8,128)(2,1)S(1)}, bf16[3,4,40,896]{3,2,1,0:T(8,128)(2,1)S(1)}, u32[]{:S(2)}, u32[]{:S(2)}) collective-permute-start(bf16[3,4,40,896]{3,2,1,0:T(8,128)(2,1)S(1)} %get-tuple-element.392), channel_id=1, source_target_pairs={{0,2},{1,3},{2,0},{3,1},{4,6},{5,7},{6,4},{7,5},{8,10},{9,11},{10,... | collective-permute-start | bytes 2580488 | tf_op jit(solution)/shard_map/ppermute | solution.py:587
  289.8 39.2 %collective-permute-start.44 = (bf16[3,4,40,896]{3,2,1,0:T(8,128)(2,1)S(1)}, bf16[3,4,40,896]{3,2,1,0:T(8,128)(2,1)S(1)}, u32[]{:S(2)}, u32[]{:S(2)}) collective-permute-start(bf16[3,4,40,896]{3,2,1,0:T(8,128)(2,1)S(1)} %get-tuple-element.393), channel_id=1, source_target_pairs={{0,4},{1,5},{2,6},{3,7},{4,0},{5,1},{6,2},{7,3},{8,12},{9,13},{10,... | collective-permute-start | bytes 2580488 | tf_op jit(solution)/shard_map/ppermute | solution.py:587
  377.2 20.9 %collective-permute-start.45 = (bf16[512,1280]{1,0:T(8,128)(2,1)}, bf16[512,1280]{1,0:T(8,128)(2,1)S(1)}, u32[]{:S(2)}, u32[]{:S(2)}) collective-permute-start(bf16[512,1280]{1,0:T(8,128)(2,1)} %get-tuple-element.425), channel_id=1, source_target_pairs={{0,1},{1,0},{2,3},{3,2},{4,5},{5,4},{6,7},{7,6},{8,9},{9,8},{10,11... | collective-permute-start | bytes 3932168 | tf_op jit(solution)/shard_map/ppermute | solution.py:587
  377.3 20.8 %collective-permute-start.46 = (bf16[512,1280]{1,0:T(8,128)(2,1)}, bf16[512,1280]{1,0:T(8,128)(2,1)S(1)}, u32[]{:S(2)}, u32[]{:S(2)}) collective-permute-start(bf16[512,1280]{1,0:T(8,128)(2,1)} %get-tuple-element.427), channel_id=1, source_target_pairs={{0,1},{1,0},{2,3},{3,2},{4,5},{5,4},{6,7},{7,6},{8,9},{9,8},{10,11... | collective-permute-start | bytes 3932168 | tf_op jit(solution)/shard_map/ppermute | solution.py:587
  399.2 27.4 %collective-permute-start.49 = (bf16[512,1280]{1,0:T(8,128)(2,1)}, bf16[512,1280]{1,0:T(8,128)(2,1)S(1)}, u32[]{:S(2)}, u32[]{:S(2)}) collective-permute-start(bf16[512,1280]{1,0:T(8,128)(2,1)} %get-tuple-element.441), channel_id=1, source_target_pairs={{0,1},{1,0},{2,3},{3,2},{4,5},{5,4},{6,7},{7,6},{8,9},{9,8},{10,11... | collective-permute-start | bytes 3932168 | tf_op jit(solution)/shard_map/ppermute | solution.py:587
  399.6 27.1 %collective-permute-start.48 = (bf16[512,1280]{1,0:T(8,128)(2,1)}, bf16[512,1280]{1,0:T(8,128)(2,1)S(1)}, u32[]{:S(2)}, u32[]{:S(2)}) collective-permute-start(bf16[512,1280]{1,0:T(8,128)(2,1)} %get-tuple-element.439), channel_id=1, source_target_pairs={{0,1},{1,0},{2,3},{3,2},{4,5},{5,4},{6,7},{7,6},{8,9},{9,8},{10,11... | collective-permute-start | bytes 3932168 | tf_op jit(solution)/shard_map/ppermute | solution.py:587
  402.5 24.2 %collective-permute-start.47 = (bf16[512,1280]{1,0:T(8,128)(2,1)}, bf16[512,1280]{1,0:T(8,128)(2,1)}, u32[]{:S(2)}, u32[]{:S(2)}) collective-permute-start(bf16[512,1280]{1,0:T(8,128)(2,1)} %add_convert_fusion.1), channel_id=1, source_target_pairs={{0,4},{1,3},{2,6},{3,1},{4,0},{5,7},{6,2},{7,5},{8,12},{9,11},{10,... | collective-permute-start | bytes 3932168 | tf_op jit(solution)/shard_map/ppermute | solution.py:587
  433.9 36.1 %collective-permute-start.52 = (bf16[512,1280]{1,0:T(8,128)(2,1)}, bf16[512,1280]{1,0:T(8,128)(2,1)}, u32[]{:S(2)}, u32[]{:S(2)}) collective-permute-start(bf16[512,1280]{1,0:T(8,128)(2,1)} %get-tuple-element.470), channel_id=1, source_target_pairs={{0,2},{1,3},{2,0},{3,1},{4,6},{5,7},{6,4},{7,5},{8,10},{9,11},{10,... | collective-permute-start | bytes 3932168 | tf_op jit(solution)/shard_map/ppermute | solution.py:587
  435.3 34.7 %collective-permute-start.53 = (bf16[512,1280]{1,0:T(8,128)(2,1)S(1)}, bf16[512,1280]{1,0:T(8,128)(2,1)}, u32[]{:S(2)}, u32[]{:S(2)}) collective-permute-start(bf16[512,1280]{1,0:T(8,128)(2,1)S(1)} %get-tuple-element.471), channel_id=1, source_target_pairs={{0,4},{1,5},{2,6},{3,7},{4,0},{5,1},{6,2},{7,3},{8,12},{9,13},{10,... | collective-permute-start | bytes 3932168 | tf_op jit(solution)/shard_map/ppermute | solution.py:587
  435.7 34.3 %collective-permute-start.51 = (bf16[512,1280]{1,0:T(8,128)(2,1)}, bf16[512,1280]{1,0:T(8,128)(2,1)S(1)}, u32[]{:S(2)}, u32[]{:S(2)}) collective-permute-start(bf16[512,1280]{1,0:T(8,128)(2,1)} %get-tuple-element.467), channel_id=1, source_target_pairs={{0,1},{1,0},{2,3},{3,2},{4,5},{5,4},{6,7},{7,6},{8,9},{9,8},{10,11... | collective-permute-start | bytes 3932168 | tf_op jit(solution)/shard_map/ppermute | solution.py:587
  465.1 176.3 %reduce-scatter.5.cloned.1.call-start = ((), (), s32[]{:S(2)}) async-start(), calls=%async_computation.9 | async-start | bytes 8601600 | tf_op jit(solution)/shard_map/reduce_scatter | solution.py:929
  471.0 24.3 %collective-permute-start.56 = (bf16[512,1280]{1,0:T(8,128)(2,1)}, bf16[512,1280]{1,0:T(8,128)(2,1)S(1)}, u32[]{:S(2)}, u32[]{:S(2)}) collective-permute-start(bf16[512,1280]{1,0:T(8,128)(2,1)} %get-tuple-element.493), channel_id=1, source_target_pairs={{0,1},{1,0},{2,3},{3,2},{4,5},{5,4},{6,7},{7,6},{8,9},{9,8},{10,11... | collective-permute-start | bytes 3932168 | tf_op jit(solution)/shard_map/ppermute | solution.py:587
  471.0 24.3 %collective-permute-start.54 = (bf16[512,1280]{1,0:T(8,128)(2,1)}, bf16[512,1280]{1,0:T(8,128)(2,1)}, u32[]{:S(2)}, u32[]{:S(2)}) collective-permute-start(bf16[512,1280]{1,0:T(8,128)(2,1)} %get-tuple-element.489), channel_id=1, source_target_pairs={{0,1},{1,0},{2,3},{3,2},{4,5},{5,4},{6,7},{7,6},{8,9},{9,8},{10,11... | collective-permute-start | bytes 3932168 | tf_op jit(solution)/shard_map/ppermute | solution.py:587
  471.5 23.8 %collective-permute-start.55 = (bf16[512,1280]{1,0:T(8,128)(2,1)}, bf16[512,1280]{1,0:T(8,128)(2,1)S(1)}, u32[]{:S(2)}, u32[]{:S(2)}) collective-permute-start(bf16[512,1280]{1,0:T(8,128)(2,1)} %add_convert_fusion), channel_id=1, source_target_pairs={{0,4},{1,3},{2,6},{3,1},{4,0},{5,7},{6,2},{7,5},{8,12},{9,11},{10,... | collective-permute-start | bytes 3932168 | tf_op jit(solution)/shard_map/ppermute | solution.py:587
  515.0 36.7 %collective-permute-start.57 = (bf16[4,1,4,40,1280]{4,3,2,1,0:T(8,128)(2,1)}, bf16[4,1,4,40,1280]{4,3,2,1,0:T(8,128)(2,1)}, u32[]{:S(2)}, u32[]{:S(2)}) collective-permute-start(bf16[4,1,4,40,1280]{4,3,2,1,0:T(8,128)(2,1)} %bitcast.229), channel_id=1, source_target_pairs={{0,1},{1,0},{2,3},{3,2},{4,5},{5,4},{6,7},{7,6},{8,9},{9,8},{10,11... | collective-permute-start | bytes 4915208 | tf_op jit(solution)/shard_map/ppermute | solution.py:587
  519.5 31.5 %collective-permute-start.58 = (bf16[512,1280]{1,0:T(8,128)(2,1)}, bf16[512,1280]{1,0:T(8,128)(2,1)}, u32[]{:S(2)}, u32[]{:S(2)}) collective-permute-start(bf16[512,1280]{1,0:T(8,128)(2,1)} %get-tuple-element.508), channel_id=1, source_target_pairs={{0,2},{1,3},{2,0},{3,1},{4,6},{5,7},{6,4},{7,5},{8,10},{9,11},{10,... | collective-permute-start | bytes 3932168 | tf_op jit(solution)/shard_map/ppermute | solution.py:587
  520.7 31.1 %collective-permute-start.59 = (bf16[512,1280]{1,0:T(8,128)(2,1)}, bf16[512,1280]{1,0:T(8,128)(2,1)}, u32[]{:S(2)}, u32[]{:S(2)}) collective-permute-start(bf16[512,1280]{1,0:T(8,128)(2,1)} %get-tuple-element.509), channel_id=1, source_target_pairs={{0,4},{1,5},{2,6},{3,7},{4,0},{5,1},{6,2},{7,3},{8,12},{9,13},{10,... | collective-permute-start | bytes 3932168 | tf_op jit(solution)/shard_map/ppermute | solution.py:587
  551.8 23.7 %collective-permute-start.60 = (bf16[4,3,4,40,1280]{4,3,2,1,0:T(8,128)(2,1)}, bf16[4,3,4,40,1280]{4,3,2,1,0:T(8,128)(2,1)}, u32[]{:S(2)}, u32[]{:S(2)}) collective-permute-start(bf16[4,3,4,40,1280]{4,3,2,1,0:T(8,128)(2,1)} %bitcast.226), channel_id=1, source_target_pairs={{0,1},{1,0},{2,3},{3,2},{4,5},{5,4},{6,7},{7,6},{8,9},{9,8},{10,11... | collective-permute-start | bytes 14745608 | tf_op jit(solution)/shard_map/ppermute | solution.py:587
  559.7 15.7 %collective-permute-start.61 = (bf16[1,4,40,1280]{3,2,1,0:T(8,128)(2,1)}, bf16[1,4,40,1280]{3,2,1,0:T(8,128)(2,1)S(1)}, u32[]{:S(2)}, u32[]{:S(2)}) collective-permute-start(bf16[1,4,40,1280]{3,2,1,0:T(8,128)(2,1)} %fusion.48), channel_id=1, source_target_pairs={{0,4},{1,3},{2,6},{3,1},{4,0},{5,7},{6,2},{7,5},{8,12},{9,11},{10,... | collective-permute-start | bytes 1228808 | tf_op jit(solution)/shard_map/ppermute | solution.py:587
  582.5 21.5 %collective-permute-start.62 = (bf16[3,4,40,1280]{3,2,1,0:T(8,128)(2,1)}, bf16[3,4,40,1280]{3,2,1,0:T(8,128)(2,1)}, u32[]{:S(2)}, u32[]{:S(2)}) collective-permute-start(bf16[3,4,40,1280]{3,2,1,0:T(8,128)(2,1)} %fusion.28), channel_id=1, source_target_pairs={{0,4},{1,3},{2,6},{3,1},{4,0},{5,7},{6,2},{7,5},{8,12},{9,11},{10,... | collective-permute-start | bytes 3686408 | tf_op jit(solution)/shard_map/ppermute | solution.py:587
  584.9 49.6 %all-to-all-start.3 = ((bf16[4,3,40,896]{3,2,1,0:T(8,128)(2,1)}), bf16[4,3,40,896]{3,2,1,0:T(8,128)(2,1)S(1)}, u32[]{:S(2)}, u32[]{:S(2)}) async-start(bf16[4,3,40,896]{3,2,1,0:T(8,128)(2,1)} %copy.234), calls=%async_computation.4 | async-start | bytes 1720320 | tf_op jit(solution)/shard_map/all_to_all | solution.py:1004
  608.6 30.1 %collective-permute-start.68 = (bf16[3,4,40,1280]{3,2,1,0:T(8,128)(2,1)}, bf16[3,4,40,1280]{3,2,1,0:T(8,128)(2,1)}, u32[]{:S(2)}, u32[]{:S(2)}) collective-permute-start(bf16[3,4,40,1280]{3,2,1,0:T(8,128)(2,1)} %get-tuple-element.525), channel_id=1, source_target_pairs={{0,2},{1,3},{2,0},{3,1},{4,6},{5,7},{6,4},{7,5},{8,10},{9,11},{10,... | collective-permute-start | bytes 3686408 | tf_op jit(solution)/shard_map/ppermute | solution.py:587
  610.1 28.6 %collective-permute-start.69 = (bf16[3,4,40,1280]{3,2,1,0:T(8,128)(2,1)}, bf16[3,4,40,1280]{3,2,1,0:T(8,128)(2,1)}, u32[]{:S(2)}, u32[]{:S(2)}) collective-permute-start(bf16[3,4,40,1280]{3,2,1,0:T(8,128)(2,1)} %get-tuple-element.526), channel_id=1, source_target_pairs={{0,4},{1,5},{2,6},{3,7},{4,0},{5,1},{6,2},{7,3},{8,12},{9,13},{10,... | collective-permute-start | bytes 3686408 | tf_op jit(solution)/shard_map/ppermute | solution.py:587
  619.0 25.5 %collective-permute-start.67 = (bf16[1,40,1280]{2,1,0:T(8,128)(2,1)}, bf16[1,40,1280]{2,1,0:T(8,128)(2,1)}, u32[]{:S(2)}, u32[]{:S(2)}) collective-permute-start(bf16[1,40,1280]{2,1,0:T(8,128)(2,1)} %get-tuple-element.534), channel_id=1, source_target_pairs={{0,24},{8,16},{16,8},{24,0},{1,25},{9,17},{17,9},{25,1},{2,26},{10... | collective-permute-start | bytes 307208 | tf_op jit(solution)/shard_map/ppermute | solution.py:614
  620.3 26.5 %collective-permute-start.66 = (bf16[1,40,1280]{2,1,0:T(8,128)(2,1)}, bf16[1,40,1280]{2,1,0:T(8,128)(2,1)}, u32[]{:S(2)}, u32[]{:S(2)}) collective-permute-start(bf16[1,40,1280]{2,1,0:T(8,128)(2,1)} %get-tuple-element.533), channel_id=1, source_target_pairs={{0,16},{8,24},{16,0},{24,8},{1,17},{9,25},{17,1},{25,9},{2,18},{10... | collective-permute-start | bytes 307208 | tf_op jit(solution)/shard_map/ppermute | solution.py:614
  620.3 26.5 %collective-permute-start.65 = (bf16[1,40,1280]{2,1,0:T(8,128)(2,1)}, bf16[1,40,1280]{2,1,0:T(8,128)(2,1)}, u32[]{:S(2)}, u32[]{:S(2)}) collective-permute-start(bf16[1,40,1280]{2,1,0:T(8,128)(2,1)} %get-tuple-element.532), channel_id=1, source_target_pairs={{0,8},{8,0},{16,24},{24,16},{1,9},{9,1},{17,25},{25,17},{2,10},{10... | collective-permute-start | bytes 307208 | tf_op jit(solution)/shard_map/ppermute | solution.py:614
  634.5 15.4 %all-to-all-start.4 = ((f32[8,4,40,128]{3,2,1,0:T(8,128)}), f32[8,4,40,128]{3,2,1,0:T(8,128)}, u32[]{:S(2)}, u32[]{:S(2)}) async-start(f32[8,4,40,128]{3,2,1,0:T(8,128)} %copy.236), calls=%async_computation.5 | async-start | bytes 1310720 | tf_op jit(solution)/shard_map/all_to_all | solution.py:1028
  642.4 35.6 %collective-permute-start.72 = (bf16[3,40,1280]{2,1,0:T(8,128)(2,1)}, bf16[3,40,1280]{2,1,0:T(8,128)(2,1)S(1)}, u32[]{:S(2)}, u32[]{:S(2)}) collective-permute-start(bf16[3,40,1280]{2,1,0:T(8,128)(2,1)} %get-tuple-element.544), channel_id=1, source_target_pairs={{0,24},{8,16},{16,8},{24,0},{1,25},{9,17},{17,9},{25,1},{2,26},{10... | collective-permute-start | bytes 921608 | tf_op jit(solution)/shard_map/ppermute | solution.py:614
  644.5 33.4 %collective-permute-start.71 = (bf16[3,40,1280]{2,1,0:T(8,128)(2,1)}, bf16[3,40,1280]{2,1,0:T(8,128)(2,1)S(1)}, u32[]{:S(2)}, u32[]{:S(2)}) collective-permute-start(bf16[3,40,1280]{2,1,0:T(8,128)(2,1)} %get-tuple-element.543), channel_id=1, source_target_pairs={{0,16},{8,24},{16,0},{24,8},{1,17},{9,25},{17,1},{25,9},{2,18},{10... | collective-permute-start | bytes 921608 | tf_op jit(solution)/shard_map/ppermute | solution.py:614
  644.5 33.4 %collective-permute-start.70 = (bf16[3,40,1280]{2,1,0:T(8,128)(2,1)}, bf16[3,40,1280]{2,1,0:T(8,128)(2,1)S(1)}, u32[]{:S(2)}, u32[]{:S(2)}) collective-permute-start(bf16[3,40,1280]{2,1,0:T(8,128)(2,1)} %get-tuple-element.542), channel_id=1, source_target_pairs={{0,8},{8,0},{16,24},{24,16},{1,9},{9,1},{17,25},{25,17},{2,10},{10... | collective-permute-start | bytes 921608 | tf_op jit(solution)/shard_map/ppermute | solution.py:614
  651.7 20.8 %all-to-all-start.5 = ((f32[4,40,128]{2,1,0:T(8,128)}), f32[4,40,128]{2,1,0:T(8,128)S(1)}, u32[]{:S(2)}, u32[]{:S(2)}) async-start(f32[4,40,128]{2,1,0:T(8,128)} %add_bitcast_fusion.1), calls=%async_computation.7 | async-start | bytes 163840 | tf_op jit(solution)/shard_map/all_to_all | solution.py:1040
  (110 other events, 1068.6 us)
Sparse Core Ops, SparseCore 0:
  107.3 124.6 all-gather.4
  233.5 123.2 all-gather.6
  359.7 118.5 reduce-scatter.2
  495.4 132.8 reduce-scatter.4

commit v5 on v4

--- a/solution.py
+++ b/solution.py
@@ -203,42 +203,47 @@
     n_dp = out_ref.shape[0]
     slab = width // n_dp
     piece = rows_v.shape[0] // count
-    loads = {}
-    for j, to in ((1, dy_v), (2, h_v), (0, rows_v), (3, dab_v)):
-        loads[j] = [
-            pltpu.make_async_copy(saved[i][j], to.at[pl.ds(i * piece, piece)], isem.at[j, i]) for i in range(count)
-        ]
-        for copy in loads[j]:
-            copy.start()
+    cuts = chunks(width, 256)
+    loads = {2: [], 3: [], 1: [[] for _ in cuts], 0: [[] for _ in cuts]}
+    for i in range(count):
+        own = pl.ds(i * piece, piece)
+        for j, to in ((2, h_v), (3, dab_v)):
+            loads[j].append(pltpu.make_async_copy(saved[i][j], to.at[own], isem.at[j, i, 0]))
+        for j, to in ((1, dy_v), (0, rows_v)):
+            for c, (c0, cn) in enumerate(cuts):
+                source = saved[i][j].at[:, pl.ds(c0, cn)]
+                loads[j][c].append(pltpu.make_async_copy(source, to.at[own, pl.ds(c0, cn)], isem.at[j, i, c]))
+    for copy in loads[2] + sum(loads[1], []) + loads[3] + sum(loads[0], []):
+        copy.start()
     stores = [
         [pltpu.make_async_copy(g_v.at[j, pl.ds(d * slab, slab)], out_ref.at[d, j], osem.at[j, d]) for d in range(n_dp)]
         for j in range(3)
     ]
-    for copy in loads[1] + loads[2]:
+
+    def send(j, c):
+        done, before = sum(cuts[c]), cuts[c][0]
+        for d in range(n_dp):
+            if before < (d + 1) * slab <= done:
+                stores[j][d].start()
+
+    for copy in loads[2]:
         copy.wait()
-
-    def down(i, carry):
-        m = pl.ds(pl.multiple_of(i * 256, 256), 256)
-        g_v[2, m, :] = dot_tn(dy_v[:, m], h_v[...]).astype(BF)
-        return carry
-
-    lax.fori_loop(0, width // 256, down, 0)
-    for copy in stores[2]:
-        copy.start()
-    for copy in loads[0] + loads[3]:
+    for c, (c0, cn) in enumerate(cuts):
+        for copy in loads[1][c]:
+            copy.wait()
+        g_v[2, c0 : c0 + cn, :] = dot_tn(dy_v[:, c0 : c0 + cn], h_v[...]).astype(BF)
+        send(2, c)
+    for copy in loads[3]:
         copy.wait()
-
-    def front(i, carry):
-        m = pl.ds(pl.multiple_of(i * 256, 256), 256)
-        both = dot_tn(rows_v[:, m], dab_v[...])
-        for c0, cn, g0, u0 in pair_columns(ff):
-            g_v[0, m, c0 : c0 + cn] = both[:, g0 : g0 + cn].astype(BF)
-            g_v[1, m, c0 : c0 + cn] = both[:, u0 : u0 + cn].astype(BF)
-        return carry
-
-    lax.fori_loop(0, width // 256, front, 0)
-    for copy in stores[0] + stores[1]:
-        copy.start()
+    for c, (c0, cn) in enumerate(cuts):
+        for copy in loads[0][c]:
+            copy.wait()
+        both = dot_tn(rows_v[:, c0 : c0 + cn], dab_v[...])
+        for f0, fn, g0, u0 in pair_columns(ff):
+            g_v[0, c0 : c0 + cn, f0 : f0 + fn] = both[:, g0 : g0 + fn].astype(BF)
+            g_v[1, c0 : c0 + cn, f0 : f0 + fn] = both[:, u0 : u0 + fn].astype(BF)
+        send(0, c)
+        send(1, c)
     for copy in stores[0] + stores[1] + stores[2]:
         copy.wait()
 
@@ -254,7 +259,7 @@
         in_specs=kernel_specs("a" * (4 * count)),
         out_specs=pl.BlockSpec(memory_space=pl.ANY),
         scratch_shapes=[pltpu.VMEM((rows, n), BF) for n in (width, width, ff, 2 * ff)]
-        + [pltpu.VMEM((3, width, ff), BF), dma((4, count)), dma((3, n_dp))],
+        + [pltpu.VMEM((3, width, ff), BF), dma((4, count, len(chunks(width, 256)))), dma((3, n_dp))],
         compiler_params=pltpu.CompilerParams(vmem_limit_bytes=VMEM_LIMIT),
         cost_estimate=estimate(6 * rows * width * ff),
         name="expert_weights",
@@ -411,7 +416,7 @@
 
 def heads_back_kernel(
     scale, q_ref, k_ref, v_ref, dctx_ref, lse_ref, cos_ref, sin_ref, first_ref, len_ref,
-    dq_ref, dk_ref, dv_ref, even_ref, odd_ref,
+    dq_ref, dk_ref, dv_ref, even_ref, odd_ref, even_v, odd_v, sem,
 ):
     seq, width = q_ref.shape
     length = len_ref[0]
@@ -445,9 +450,14 @@
         return carry
 
     lax.fori_loop(0, width // 256, heads, 0)
-    store_pieces(even_ref, odd_ref, 2, first_ref, dv_ref)
-    store_pieces(even_ref, odd_ref, 0, first_ref, dq_ref)
-    store_pieces(even_ref, odd_ref, 1, first_ref, dk_ref)
+    copies = []
+    for j, grad_ref in ((2, dv_ref), (0, dq_ref), (1, dk_ref)):
+        store_pieces(even_v, odd_v, j, first_ref, grad_ref)
+        for part, (held, out_ref) in enumerate(((even_v, even_ref), (odd_v, odd_ref))):
+            copies.append(pltpu.make_async_copy(held.at[:, j], out_ref.at[:, j], sem.at[j, part]))
+            copies[-1].start()
+    for copy in copies:
+        copy.wait()
 
 
 def heads_back_call(q, k, v, dctx, lse, cosine, sine, first_rel, lengths, scale):
@@ -458,7 +468,8 @@
         functools.partial(heads_back_kernel, scale),
         out_shape=[half] * 3 + [wide] * 2,
         in_specs=kernel_specs("vvvvvvvvs"),
-        out_specs=kernel_specs("v" * 5),
+        out_specs=kernel_specs("vvvaa"),
+        scratch_shapes=[pltpu.VMEM(wide.shape, BF)] * 2 + [pltpu.SemaphoreType.DMA((3, 2))],
         compiler_params=pltpu.CompilerParams(vmem_limit_bytes=VMEM_LIMIT),
         cost_estimate=estimate(26 * seq * width * width),
         name="heads_backward",
@@ -891,8 +902,10 @@
     sort = lambda values: lax.dot_general(
         sort_rows, values, (((1,), (1,)), ((), ())), preferred_element_type=F32
     ).astype(BF)
-    out_rel, second_rel = [sort(order.now(v)) for v in (grad_out16, second16)]
-    order.close(second_core, shared_far, shared_core, out_rel, second_rel)
+    out_rel, second_rel, first_rel, context_rel = [
+        sort(order.now(v)) for v in (grad_out16, second16, first16, context16)
+    ]
+    order.close(second_core, shared_far, shared_core, out_rel, second_rel, first_rel, context_rel)
     shared_core.append(permute_core(order.now(shared_far)))
     shared_all = [p for both in zip((shared_cut, *shared_near, shared_far), shared_core) for p in both]
     shared16 = place_rows([shared_all], me, [(0, j, 0, shared_weight.shape[2]) for j in range(3)])
@@ -909,8 +922,7 @@
     shared_sum = piece_sum(shared_even, shared_odd, is_core0)
     shared_core = shared_sum.core(order)
     results[0][0] = pair(0, 0, None, None)
-    first_rel, context_rel = [sort(after(v, results[0][0][1])) for v in (first16, context16)]
-    order.close(second_core, results[0][0][1], second_far, shared_core, grad_far, first_rel, context_rel)
+    order.close(second_core, results[0][0][1], second_far, shared_core, grad_far)
     grad_core.append(permute_core(order.now(grad_far)))
     seconds_even.append(second_far)
     second_core.append(permute_core(order.now(second_far)))

time: 693 us -> 697 us (level)
    all_gather x2, waiting for transfers between devices: 3.7 us -> 14.1 us  [local(): lax.all_gather(low, 'dp', axis=0, tiled=False)]
    ppermute x61, waiting for transfers between devices: 65.9 us -> 55.6 us  [permute(): return lax.ppermute(values, 'expert', pairs)]
    unnamed x187 -> x185, local copies, waits for them, and re-layouts: 15.9 us -> 16 us
  transfers between devices with their start and end apart: 83 -> 83, of which waited for: 23 -> 23; matrix products, arithmetic and copies ran while one was open for 16% -> 15% of each run, Pallas kernels for 50% -> 50%
where the time goes in v5:
time: 697 us; the launch traced here: 687 us
  Pallas kernels  344 us (49%)
  waiting for transfers between devices  116 us (17%)
  starting transfers between devices  82.1 us (12%)
  other arithmetic  74.3 us (11%)
  local copies, waits for them, and re-layouts  37.8 us (5%)
  between operations  18.6 us (3%)
  matrix products  14.2 us (2%)
    pallas_call x8, Pallas kernels, expert_pair_call(): pl.pallas_call(functools.partial(expert_pair_kernel, prev is None), out_s...  159 us
    ppermute x61, waiting for transfers between devices, permute(): return lax.ppermute(values, 'expert', pairs)  55.6 us
    pallas_call x2, Pallas kernels, weight_grad_call(): pl.pallas_call(functools.partial(weight_grad_kernel, count), out_shape=ja...  45.8 us
    ppermute x61, starting transfers between devices, permute(): return lax.ppermute(values, 'expert', pairs)  39.7 us
    ppermute x12, waiting for transfers between devices, send_dp(): lax.ppermute(values, 'dp', [(i, i ^ k) for i in range(lax.axis_size('dp'))])  30.1 us
    pallas_call x1, Pallas kernels, attention_call(): pl.pallas_call(functools.partial(attention_kernel, scale), out_shape=[hal...  23.5 us
    pallas_call x1, Pallas kernels, heads_back_call(): pl.pallas_call(functools.partial(heads_back_kernel, scale), out_shape=[ha...  23.2 us
    pallas_call x2, Pallas kernels, update_call(): pl.pallas_call(functools.partial(update_kernel, rate), grid=(kinds, cuts)...  22 us
  transfers between devices with their start and end apart: 83, of which 23 were waited for; matrix products, arithmetic and copies ran while one was open for 15% of the time, Pallas kernels for 50%

profile of v5, /device:TPU:0, one launch (start us, length us, event | category | flops | bytes accessed | tf_op | source)
XLA Modules:
  0.0 687.0 jit_solution(13780664366503154162)
XLA Ops:
  9.6 3.0 collective-permute-start.3
  16.9 2.6 collective-permute-start.1
  19.7 6.0 collective-permute-done.refs_1_
  25.7 10.2 %collective-permute-done.1.refs_2_ = bf16[2,40,1408]{2,1,0:T(8,128)(2,1)S(1)} collective-permute-done((bf16[2,40,1408]{2,1,0:T(8,128)(2,1)S(1)}, bf16[2,40,1408]{2,1,0:T(8,128)(2,1)S(1)}, u32[]{:S(2)}, u32[]{:S(2)}) %collective-permute-start.1) | collective-permute-done | bytes 225312 | tf_op jit(solution)/shard_map/ppermute | solution.py:625
  36.6 2.3 stack_dp.2.refs_0_
  38.9 2.6 collective-permute-done.3.refs_7_.refs_8_
  46.6 2.6 collective-permute-start.8
  49.4 3.3 collective-permute-done.7.refs_1_
  52.7 10.6 %collective-permute-done.8.refs_2_ = bf16[2,40,1280]{2,1,0:T(8,128)(2,1)S(1)} collective-permute-done((bf16[2,40,1280]{2,1,0:T(8,128)(2,1)S(1)}, bf16[2,40,1280]{2,1,0:T(8,128)(2,1)S(1)}, u32[]{:S(2)}, u32[]{:S(2)}) %collective-permute-start.8) | collective-permute-done | bytes 204832 | tf_op jit(solution)/shard_map/ppermute | solution.py:625
  69.4 4.4 all-to-all-start
  75.5 12.9 %collective-permute-done.14.refs_10_ = bf16[4,2,40,1280]{3,2,1,0:T(8,128)(2,1)} collective-permute-done((bf16[4,2,40,1280]{3,2,1,0:T(8,128)(2,1)}, bf16[4,2,40,1280]{3,2,1,0:T(8,128)(2,1)}, u32[]{:S(2)}, u32[]{:S(2)}) %collective-permute-start.14) | collective-permute-done | bytes 819232 | tf_op jit(solution)/shard_map/ppermute | solution.py:598
  89.0 3.4 convert.49
  94.4 10.3 %collective-permute-done.15.refs_12_ = bf16[4,2,40,1280]{3,2,1,0:T(8,128)(2,1)S(1)} collective-permute-done((bf16[4,2,40,1280]{3,2,1,0:T(8,128)(2,1)S(1)}, bf16[4,2,40,1280]{3,2,1,0:T(8,128)(2,1)S(1)}, u32[]{:S(2)}, u32[]{:S(2)}) %collective-permute-start.15) | collective-permute-done | bytes 819232 | tf_op jit(solution)/shard_map/ppermute | solution.py:598
  110.6 11.3 %collective-permute-done.20.refs_14_ = bf16[4,2,40,1280]{3,2,1,0:T(8,128)(2,1)S(1)} collective-permute-done((bf16[4,2,40,1280]{3,2,1,0:T(8,128)(2,1)S(1)}, bf16[4,2,40,1280]{3,2,1,0:T(8,128)(2,1)S(1)}, u32[]{:S(2)}, u32[]{:S(2)}) %collective-permute-start.20) | collective-permute-done | bytes 819232 | tf_op jit(solution)/shard_map/ppermute | solution.py:598
  128.7 10.1 %place_rows.2 = (bf16[4,8,40,1280]{3,2,1,0:T(8,128)(2,1)}, bf16[4,8,40,1280]{3,2,1,0:T(8,128)(2,1)}, bf16[4,8,40,1280]{3,2,1,0:T(8,128)(2,1)}, bf16[4,8,40,1280]{3,2,1,0:T(8,128)(2,1)}, bf16[4,8,40,128]{3,2,1,0:T(8,128)(2,1)}) custom-call(s32[1]{0:T(128)} %bitcast.at_ref, bf16[4,2,40,1408]{3,2,1,0:T(8,128)(2,1)} %stack_dp.2.refs_0_, ...), custom_call_target="tpu_custom_call" | custom-call | bytes 1 | tf_op jit(solution)/shard_map/place_rows/pallas_call | solution.py:743
  140.6 23.5 %attention_forward.1 = (bf16[512,1280]{1,0:T(8,128)(2,1)}, bf16[512,1280]{1,0:T(8,128)(2,1)}, bf16[512,1280]{1,0:T(8,128)(2,1)}, bf16[512,1280]{1,0:T(8,128)(2,1...) custom-call(bf16[512,1280]{1,0:T(8,128)(2,1)} %tok_ref.3, ...), custom_call_target="tpu_custom_call" | custom-call | bytes 1 | tf_op jit(solution)/shard_map/attention_forward/pallas_call | solution.py:347
  168.7 3.0 fusion.11.ctx_ref
  171.7 3.0 fusion.10.first_ref
  176.6 3.0 fusion.9.second_rel_ref
  179.6 3.0 fusion.8.dout_rel_ref
  183.4 3.4 all-to-all-start.1
  188.0 6.1 place_rows.3
  194.1 20.3 %shared_expert.1 = (f32[512,1280]{1,0:T(8,128)}, f32[512,1280]{1,0:T(8,128)}, bf16[4,3,160,896]{3,2,1,0:T(8,128)(2,1)}, bf16[4,3,160,896]{3,2,1,0:T(8,128)(2,1)}) custom-call(bf16[512,1280]{1,0:T(8,128)(2,1)} %get-tuple-element.443.second_ref.refs_5_.refs_6_, bf16[1280,512]{1,0:T(8,128)(2,1)} %fusion.9.second_rel_ref, bf16[512,1280]{1,0:T(8,128)(2,1)} %copy-done.3, ...), custom_call_target="tpu_custom_call" | custom-call | bytes 1 | tf_op jit(solution)/shard_map/shared_expert/pallas_call | solution.py:557
  216.5 2.5 broadcast_select_fusion
  219.0 2.5 broadcast_select_fusion.1
  228.2 3.7 all-gather.5.cloned.1.call-done
  231.9 20.7 %expert_pair.8 = (bf16[512,1280]{1,0:T(8,128)(2,1)}, bf16[512,1280]{1,0:T(8,128)(2,1)}, bf16[512,1280]{1,0:T(8,128)(2,1)}, bf16[512,1280]{1,0:T(8,128)(2,1)}, f3...) custom-call(s32[1]{0:T(128)} %get-tuple-element.720.refs_0_, ...), custom_call_target="tpu_custom_call" | custom-call | flops 5284823040 | bytes 1 | tf_op jit(solution)/shard_map/expert_pair/pallas_call | solution.py:180
  255.7 2.9 collective-permute-done.40.refs_6_.refs_7_
  260.2 18.9 %expert_pair.9 = (bf16[512,1280]{1,0:T(8,128)(2,1)}, bf16[512,1280]{1,0:T(8,128)(2,1)}, bf16[512,1280]{1,0:T(8,128)(2,1)}, bf16[512,1280]{1,0:T(8,128)(2,1)}, f3...) custom-call(s32[1]{0:T(128)} %get-tuple-element.720.refs_0_, ...), custom_call_target="tpu_custom_call" | custom-call | flops 5284823040 | bytes 1 | tf_op jit(solution)/shard_map/expert_pair/pallas_call | solution.py:180
  283.9 18.8 %expert_pair.10 = (bf16[512,1280]{1,0:T(8,128)(2,1)}, bf16[512,1280]{1,0:T(8,128)(2,1)}, bf16[512,1280]{1,0:T(8,128)(2,1)}, bf16[512,1280]{1,0:T(8,128)(2,1)}, f...) custom-call(s32[1]{0:T(128)} %get-tuple-element.720.refs_0_, ...), custom_call_target="tpu_custom_call" | custom-call | flops 5284823040 | bytes 1 | tf_op jit(solution)/shard_map/expert_pair/pallas_call | solution.py:180
  302.7 18.9 %expert_pair.11 = (bf16[512,1280]{1,0:T(8,128)(2,1)}, bf16[512,1280]{1,0:T(8,128)(2,1)}, bf16[512,1280]{1,0:T(8,128)(2,1)}, bf16[512,1280]{1,0:T(8,128)(2,1)}, f...) custom-call(s32[1]{0:T(128)} %get-tuple-element.720.refs_0_, ...), custom_call_target="tpu_custom_call" | custom-call | flops 5284823040 | bytes 1 | tf_op jit(solution)/shard_map/expert_pair/pallas_call | solution.py:180
  323.5 22.9 %expert_weights.2 = bf16[4,3,320,896]{3,2,1,0:T(8,128)(2,1)} custom-call(bf16[512,1280]{1,0:T(8,128)(2,1)} %get-tuple-element.394.refs_0_, bf16[512,1280]{1,0:T(8,128)(2,1)} %get-tuple-element.395.refs_1_, bf16[512,896]{1,0:T(8,128)(2,1)} %get-tuple-element.396.refs_2_, bf16[512,1792]{1,0:T(8,128)(2,1)} %get-tuple-element.397.refs_3_, ...), custom_call_target="tpu_custom_call" | custom-call | flops 14092861440 | bytes 1 | tf_op jit(solution)/shard_map/expert_weights/pallas_call | solution.py:256
  346.4 10.4 %all-gather.7.cloned.1.call-done = bf16[12,320,896]{2,1,0:T(8,128)(2,1)} async-done(((bf16[3,320,896]{2,1,0:T(8,128)(2,1)}), bf16[12,320,896]{2,1,0:T(8,128)(2,1)}) %all-gather.7.cloned.1.call-update) | async-done | bytes 6881296 | tf_op jit(solution)/shard_map/all_gather | solution.py:841
  356.8 20.1 %expert_pair.12 = (bf16[512,1280]{1,0:T(8,128)(2,1)}, bf16[512,1280]{1,0:T(8,128)(2,1)}, bf16[512,1280]{1,0:T(8,128)(2,1)}, bf16[512,1280]{1,0:T(8,128)(2,1)}, f...) custom-call(s32[1]{0:T(128)} %get-tuple-element.721.refs_0_, ...), custom_call_target="tpu_custom_call" | custom-call | flops 5284823040 | bytes 1 | tf_op jit(solution)/shard_map/expert_pair/pallas_call | solution.py:180
  377.5 20.8 %expert_pair.13 = (bf16[512,1280]{1,0:T(8,128)(2,1)}, bf16[512,1280]{1,0:T(8,128)(2,1)}, bf16[512,1280]{1,0:T(8,128)(2,1)}, bf16[512,1280]{1,0:T(8,128)(2,1)}, f...) custom-call(s32[1]{0:T(128)} %get-tuple-element.721.refs_0_, ...), custom_call_target="tpu_custom_call" | custom-call | flops 5284823040 | bytes 1 | tf_op jit(solution)/shard_map/expert_pair/pallas_call | solution.py:180
  399.9 2.8 add_convert_fusion.1
  406.1 20.6 %expert_pair.14 = (bf16[512,1280]{1,0:T(8,128)(2,1)}, bf16[512,1280]{1,0:T(8,128)(2,1)}, bf16[512,1280]{1,0:T(8,128)(2,1)}, bf16[512,1280]{1,0:T(8,128)(2,1)}, f...) custom-call(s32[1]{0:T(128)} %get-tuple-element.721.refs_0_, ...), custom_call_target="tpu_custom_call" | custom-call | flops 5284823040 | bytes 1 | tf_op jit(solution)/shard_map/expert_pair/pallas_call | solution.py:180
  430.1 4.8 fusion.15
  437.0 20.5 %expert_pair.15 = (bf16[512,1280]{1,0:T(8,128)(2,1)}, bf16[512,1280]{1,0:T(8,128)(2,1)}, bf16[512,1280]{1,0:T(8,128)(2,1)}, bf16[512,1280]{1,0:T(8,128)(2,1)}, f...) custom-call(s32[1]{0:T(128)} %get-tuple-element.721.refs_0_, ...), custom_call_target="tpu_custom_call" | custom-call | flops 5284823040 | bytes 1 | tf_op jit(solution)/shard_map/expert_pair/pallas_call | solution.py:180
  459.6 3.3 all-to-all-start.2
  463.4 3.1 add_convert_fusion
  470.0 22.9 %expert_weights.3 = bf16[4,3,320,896]{3,2,1,0:T(8,128)(2,1)} custom-call(bf16[512,1280]{1,0:T(8,128)(2,1)} %get-tuple-element.472.refs_0_, bf16[512,1280]{1,0:T(8,128)(2,1)} %get-tuple-element.473.refs_1_, bf16[512,896]{1,0:T(8,128)(2,1)} %get-tuple-element.474.refs_2_, bf16[512,1792]{1,0:T(8,128)(2,1)} %get-tuple-element.475.refs_3_, ...), custom_call_target="tpu_custom_call" | custom-call | flops 14092861440 | bytes 1 | tf_op jit(solution)/shard_map/expert_weights/pallas_call | solution.py:256
  495.1 14.9 %hidden_backward.1 = (f32[512,1280]{1,0:T(8,128)}, bf16[512,1280]{1,0:T(8,128)(2,1)}, bf16[4,1,160,1280]{3,2,1,0:T(8,128)(2,1)}, bf16[4,1,160,1280]{3,2,1,0:T(8,128)(2,1)}, f32[1,1280]{1,0:T(1,128)}) custom-call(f32[512,1280]{1,0:T(8,128)} %get-tuple-element.345.dn_ref, f32[512,128]{1,0:T(8,128)} %pad.24.logit_ref, ...), custom_call_target="tpu_custom_call" | custom-call | flops 12582912000 | bytes 1 | tf_op jit(solution)/shard_map/hidden_backward/pallas_call | solution.py:405
  510.1 4.7 fusion.19
  516.9 23.2 %heads_backward.1 = (bf16[512,1280]{1,0:T(8,128)(2,1)}, bf16[512,1280]{1,0:T(8,128)(2,1)}, bf16[512,1280]{1,0:T(8,128)(2,1)}, bf16[4,3,160,1280]{3,2,1,0:T(8,128)(2,1)}, bf16[4,3,160,1280]{3,2,1,0:T(8,128)(2,1)}) custom-call(bf16[512,1280]{1,0:T(8,128)(2,1)} %get-tuple-element.322.q_ref, bf16[512,1280]{1,0:T(8,128)(2,1)} %get-tuple-element.323.k_ref, ...), custom_call_target="tpu_custom_call" | custom-call | flops 21810380800 | bytes 1 | tf_op jit(solution)/shard_map/heads_backward/pallas_call | solution.py:467
  540.1 6.0 collective-permute-done.58
  548.4 2.2 fusion.40
  557.2 14.9 %input_backward.1 = (f32[512,1280]{1,0:T(8,128)}, f32[1,1280]{1,0:T(1,128)}, f32[1]{0:T(128)}) custom-call(bf16[512,1280]{1,0:T(8,128)(2,1)} %get-tuple-element.513.dq_ref, bf16[512,1280]{1,0:T(8,128)(2,1)} %get-tuple-element.514.dk_ref, bf16[512,1280]{1,0:T(8,128)(2,1)} %get-tuple-element.515.dv_ref, bf16[512,1280]{1,0:T(8,128)(2,1)} %tok_ref.3, ...), custom_call_target="tpu_custom_call" | custom-call | flops 15099494400 | bytes 1 | tf_op jit(solution)/shard_map/input_backward/pallas_call | solution.py:508
  572.1 2.3 fusion.44
  576.6 2.6 fusion.28
  581.4 3.8 all-to-all-start.3
  587.6 2.3 fusion.47
  589.9 11.0 %routed_update.2 = (f32[2,3,320,896]{3,2,1,0:T(8,128)}, f32[2,3,320,896]{3,2,1,0:T(8,128)}, f32[2,3,320,896]{3,2,1,0:T(8,128)}, f32[2,3,320,896]{3,2,1,0:T(8,128)}, bf16[2,3,320,896]{3,2,1,0:T(8,128)(2,1)}) custom-call(bf16[3,320,896]{2,1,0:T(8,128)(2,1)} %bitcast.228, f32[2,3,320,896]{3,2,1,0:T(8,128)} %w_ref.3, f32[2,3,320,896]{3,2,1,0:T(8,128)} %m_ref.3, ...), custom_call_target="tpu_custom_call" | custom-call | flops 10000000000 | bytes 1 | tf_op jit(solution)/shard_map/routed_update/pallas_call | solution.py:582
  601.0 4.6 fusion.24
  608.2 4.6 fusion.20
  619.1 2.7 collective-permute-start.65
  621.8 9.1 %all-to-all-done.3 = bf16[4,3,40,896]{3,2,1,0:T(8,128)(2,1)S(1)} async-done(((bf16[4,3,40,896]{3,2,1,0:T(8,128)(2,1)}), bf16[4,3,40,896]{3,2,1,0:T(8,128)(2,1)S(1)}, u32[]{:S(2)}, u32[]{:S(2)}) %all-to-all-start.3) | async-done | bytes 860192 | tf_op jit(solution)/shard_map/all_to_all | solution.py:1016
  630.9 4.2 all-to-all-start.4
  635.1 2.6 fusion.27
  638.8 3.6 collective-permute-start.72
  643.2 3.0 all-to-all-done.4
  648.1 4.9 all-to-all-start.5
  656.3 11.0 %routed_update.3 = (f32[2,3,320,896]{3,2,1,0:T(8,128)}, f32[2,3,320,896]{3,2,1,0:T(8,128)}, f32[2,3,320,896]{3,2,1,0:T(8,128)}, f32[2,3,320,896]{3,2,1,0:T(8,128)}, bf16[2,3,320,896]{3,2,1,0:T(8,128)(2,1)}) custom-call(bf16[3,320,896]{2,1,0:T(8,128)(2,1)} %bitcast.208, ...), custom_call_target="tpu_custom_call", output_to_operand_aliasing={{0}: (4, {}), {1}: (5, {}), {2}: (6, {}), {3}: (7, {}), {4}... | custom-call | flops 10000000000 | bytes 1 | tf_op jit(solution)/shard_map/routed_update/pallas_call | solution.py:582
  668.1 2.5 all-to-all-done.5
  (434 shorter events, 125.7 us)
Async XLA Ops:
  9.6 31.9 %collective-permute-start.3 = (bf16[512,1280]{1,0:T(8,128)(2,1)S(1)}, bf16[512,1280]{1,0:T(8,128)(2,1)}, u32[]{:S(2)}, u32[]{:S(2)}) collective-permute-start(bf16[512,1280]{1,0:T(8,128)(2,1)S(1)} %multiply_convert_fusion.dout_ref.refs_7_.refs_8_), channel_id=1, source_target_pairs={{0,2},{1,3},{2,0},{3,1},{4,6},{5,7},{6,4},{7,5},{8,10},{9,11},{10,... | collective-permute-start | bytes 3932168 | tf_op jit(solution)/shard_map/ppermute | solution.py:598
  12.6 30.3 %collective-permute-start.4 = (bf16[512,1280]{1,0:T(8,128)(2,1)S(1)}, bf16[512,1280]{1,0:T(8,128)(2,1)}, u32[]{:S(2)}, u32[]{:S(2)}) collective-permute-start(bf16[512,1280]{1,0:T(8,128)(2,1)S(1)} %multiply_convert_fusion.dout_ref.refs_7_.refs_8_), channel_id=1, source_target_pairs={{0,4},{1,5},{2,6},{3,7},{4,0},{5,1},{6,2},{7,3},{8,12},{9,13},{10,... | collective-permute-start | bytes 3932168 | tf_op jit(solution)/shard_map/ppermute | solution.py:598
  16.9 19.0 %collective-permute-start.1 = (bf16[2,40,1408]{2,1,0:T(8,128)(2,1)S(1)}, bf16[2,40,1408]{2,1,0:T(8,128)(2,1)S(1)}, u32[]{:S(2)}, u32[]{:S(2)}) collective-permute-start(bf16[2,40,1408]{2,1,0:T(8,128)(2,1)S(1)} %fusion.51.refs_0_), channel_id=1, source_target_pairs={{0,16},{8,24},{16,0},{24,8},{1,17},{9,25},{17,1},{25,9},{2,18},{10... | collective-permute-start | bytes 675848 | tf_op jit(solution)/shard_map/ppermute | solution.py:625
  19.5 16.4 %collective-permute-start.2 = (bf16[2,40,1408]{2,1,0:T(8,128)(2,1)S(1)}, bf16[2,40,1408]{2,1,0:T(8,128)(2,1)S(1)}, u32[]{:S(2)}, u32[]{:S(2)}) collective-permute-start(bf16[2,40,1408]{2,1,0:T(8,128)(2,1)S(1)} %fusion.51.refs_0_), channel_id=1, source_target_pairs={{0,24},{8,16},{16,8},{24,0},{1,25},{9,17},{17,9},{25,1},{2,26},{10... | collective-permute-start | bytes 675848 | tf_op jit(solution)/shard_map/ppermute | solution.py:625
  42.9 23.9 %collective-permute-start.5 = (bf16[4,2,40,1408]{3,2,1,0:T(8,128)(2,1)}, bf16[4,2,40,1408]{3,2,1,0:T(8,128)(2,1)S(1)}, u32[]{:S(2)}, u32[]{:S(2)}) collective-permute-start(bf16[4,2,40,1408]{3,2,1,0:T(8,128)(2,1)} %stack_dp.2.refs_0_), channel_id=1, source_target_pairs={{0,2},{1,3},{2,0},{3,1},{4,6},{5,7},{6,4},{7,5},{8,10},{9,11},{10,... | collective-permute-start | bytes 2703368 | tf_op jit(solution)/shard_map/ppermute | solution.py:598
  43.3 23.6 %collective-permute-start.6 = (bf16[4,2,40,1408]{3,2,1,0:T(8,128)(2,1)}, bf16[4,2,40,1408]{3,2,1,0:T(8,128)(2,1)S(1)}, u32[]{:S(2)}, u32[]{:S(2)}) collective-permute-start(bf16[4,2,40,1408]{3,2,1,0:T(8,128)(2,1)} %stack_dp.2.refs_0_), channel_id=1, source_target_pairs={{0,4},{1,5},{2,6},{3,7},{4,0},{5,1},{6,2},{7,3},{8,12},{9,13},{10,... | collective-permute-start | bytes 2703368 | tf_op jit(solution)/shard_map/ppermute | solution.py:598
  46.6 16.7 %collective-permute-start.8 = (bf16[2,40,1280]{2,1,0:T(8,128)(2,1)S(1)}, bf16[2,40,1280]{2,1,0:T(8,128)(2,1)S(1)}, u32[]{:S(2)}, u32[]{:S(2)}) collective-permute-start(bf16[2,40,1280]{2,1,0:T(8,128)(2,1)S(1)} %copy-done.50), channel_id=1, source_target_pairs={{0,16},{8,24},{16,0},{24,8},{1,17},{9,25},{17,1},{25,9},{2,18},{10... | collective-permute-start | bytes 614408 | tf_op jit(solution)/shard_map/ppermute | solution.py:625
  66.9 21.6 %collective-permute-start.14 = (bf16[4,2,40,1280]{3,2,1,0:T(8,128)(2,1)}, bf16[4,2,40,1280]{3,2,1,0:T(8,128)(2,1)}, u32[]{:S(2)}, u32[]{:S(2)}) collective-permute-start(bf16[4,2,40,1280]{3,2,1,0:T(8,128)(2,1)} %stack_dp.3.refs_8_), channel_id=1, source_target_pairs={{0,2},{1,3},{2,0},{3,1},{4,6},{5,7},{6,4},{7,5},{8,10},{9,11},{10,... | collective-permute-start | bytes 2457608 | tf_op jit(solution)/shard_map/ppermute | solution.py:598
  69.4 37.8 %all-to-all-start = ((bf16[4,3,40,896]{3,2,1,0:T(8,128)(2,1)}), bf16[4,3,40,896]{3,2,1,0:T(8,128)(2,1)}, u32[]{:S(2)}, u32[]{:S(2)}) async-start(bf16[4,3,40,896]{3,2,1,0:T(8,128)(2,1)} %broadcast_in_dim.101), calls=%async_computation | async-start | bytes 1720320 | tf_op jit(solution)/shard_map/all_to_all | solution.py:831
  73.8 158.2 %all-gather.5.cloned.1.call-start = ((), (), s32[]{:S(2)}) async-start(), calls=%async_computation.10 | async-start | bytes 8601600 | tf_op jit(solution)/shard_map/all_gather | solution.py:841
  73.9 30.8 %collective-permute-start.13 = (bf16[4,2,40,1408]{3,2,1,0:T(8,128)(2,1)S(1)}, bf16[4,2,40,1408]{3,2,1,0:T(8,128)(2,1)S(1)}, u32[]{:S(2)}, u32[]{:S(2)}) collective-permute-start(bf16[4,2,40,1408]{3,2,1,0:T(8,128)(2,1)S(1)} %broadcast_select_fusion.2), channel_id=1, source_target_pairs={{0,4},{1,3},{2,6},{3,1},{4,0},{5,7},{6,2},{7,5},{8,12},{9,11},{10,... | collective-permute-start | bytes 2703368 | tf_op jit(solution)/shard_map/ppermute | solution.py:598
  75.0 29.8 %collective-permute-start.10 = (bf16[4,2,40,1408]{3,2,1,0:T(8,128)(2,1)S(1)}, bf16[4,2,40,1408]{3,2,1,0:T(8,128)(2,1)S(1)}, u32[]{:S(2)}, u32[]{:S(2)}) collective-permute-start(bf16[4,2,40,1408]{3,2,1,0:T(8,128)(2,1)S(1)} %copy-done.8), channel_id=1, source_target_pairs={{0,1},{1,0},{2,3},{3,2},{4,5},{5,4},{6,7},{7,6},{8,9},{9,8},{10,11... | collective-permute-start | bytes 2703368 | tf_op jit(solution)/shard_map/ppermute | solution.py:598
  75.0 29.8 %collective-permute-start.12 = (bf16[4,2,40,1408]{3,2,1,0:T(8,128)(2,1)S(1)}, bf16[4,2,40,1408]{3,2,1,0:T(8,128)(2,1)S(1)}, u32[]{:S(2)}, u32[]{:S(2)}) collective-permute-start(bf16[4,2,40,1408]{3,2,1,0:T(8,128)(2,1)S(1)} %collective-permute-done.6.refs_4_), channel_id=1, source_target_pairs={{0,1},{1,0},{2,3},{3,2},{4,5},{5,4},{6,7},{7,6},{8,9},{9,8},{10,11... | collective-permute-start | bytes 2703368 | tf_op jit(solution)/shard_map/ppermute | solution.py:598
  75.5 31.7 %collective-permute-start.11 = (bf16[4,2,40,1408]{3,2,1,0:T(8,128)(2,1)S(1)}, bf16[4,2,40,1408]{3,2,1,0:T(8,128)(2,1)}, u32[]{:S(2)}, u32[]{:S(2)}) collective-permute-start(bf16[4,2,40,1408]{3,2,1,0:T(8,128)(2,1)S(1)} %collective-permute-done.5.refs_2_), channel_id=1, source_target_pairs={{0,1},{1,0},{2,3},{3,2},{4,5},{5,4},{6,7},{7,6},{8,9},{9,8},{10,11... | collective-permute-start | bytes 2703368 | tf_op jit(solution)/shard_map/ppermute | solution.py:598
  88.4 16.3 %collective-permute-start.15 = (bf16[4,2,40,1280]{3,2,1,0:T(8,128)(2,1)S(1)}, bf16[4,2,40,1280]{3,2,1,0:T(8,128)(2,1)S(1)}, u32[]{:S(2)}, u32[]{:S(2)}) collective-permute-start(bf16[4,2,40,1280]{3,2,1,0:T(8,128)(2,1)S(1)} %copy-done.13), channel_id=1, source_target_pairs={{0,4},{1,5},{2,6},{3,7},{4,0},{5,1},{6,2},{7,3},{8,12},{9,13},{10,... | collective-permute-start | bytes 2457608 | tf_op jit(solution)/shard_map/ppermute | solution.py:598
  107.2 249.6 %all-gather.7.cloned.1.call-start = ((), (), s32[]{:S(2)}) async-start(), calls=%async_computation.11 | async-start | bytes 8601600 | tf_op jit(solution)/shard_map/all_gather | solution.py:841
  125.8 38.7 %collective-permute-start.27 = (bf16[512,1280]{1,0:T(8,128)(2,1)}, bf16[512,1280]{1,0:T(8,128)(2,1)}, u32[]{:S(2)}, u32[]{:S(2)}) collective-permute-start(bf16[512,1280]{1,0:T(8,128)(2,1)} %collective-permute-done.4.refs_7_.refs_8_), channel_id=1, source_target_pairs={{0,1},{1,0},{2,3},{3,2},{4,5},{5,4},{6,7},{7,6},{8,9},{9,8},{10,11... | collective-permute-start | bytes 3932168 | tf_op jit(solution)/shard_map/ppermute | solution.py:598
  125.9 38.6 %collective-permute-start.26 = (bf16[512,1280]{1,0:T(8,128)(2,1)}, bf16[512,1280]{1,0:T(8,128)(2,1)}, u32[]{:S(2)}, u32[]{:S(2)}) collective-permute-start(bf16[512,1280]{1,0:T(8,128)(2,1)} %collective-permute-done.3.refs_7_.refs_8_), channel_id=1, source_target_pairs={{0,1},{1,0},{2,3},{3,2},{4,5},{5,4},{6,7},{7,6},{8,9},{9,8},{10,11... | collective-permute-start | bytes 3932168 | tf_op jit(solution)/shard_map/ppermute | solution.py:598
  126.3 38.2 %collective-permute-start.25 = (bf16[512,1280]{1,0:T(8,128)(2,1)S(1)}, bf16[512,1280]{1,0:T(8,128)(2,1)S(1)}, u32[]{:S(2)}, u32[]{:S(2)}) collective-permute-start(bf16[512,1280]{1,0:T(8,128)(2,1)S(1)} %multiply_convert_fusion.dout_ref.refs_7_.refs_8_), channel_id=1, source_target_pairs={{0,1},{1,0},{2,3},{3,2},{4,5},{5,4},{6,7},{7,6},{8,9},{9,8},{10,11... | collective-permute-start | bytes 3932168 | tf_op jit(solution)/shard_map/ppermute | solution.py:598
  126.4 37.7 %collective-permute-start.23 = (bf16[4,3,40,896]{3,2,1,0:T(8,128)(2,1)}, bf16[4,3,40,896]{3,2,1,0:T(8,128)(2,1)}, u32[]{:S(2)}, u32[]{:S(2)}) collective-permute-start(bf16[4,3,40,896]{3,2,1,0:T(8,128)(2,1)} %all-to-all-done.refs_0_), channel_id=1, source_target_pairs={{0,2},{1,3},{2,0},{3,1},{4,6},{5,7},{6,4},{7,5},{8,10},{9,11},{10,... | collective-permute-start | bytes 2580488 | tf_op jit(solution)/shard_map/ppermute | solution.py:598
  128.1 36.3 %collective-permute-start.24 = (bf16[4,3,40,896]{3,2,1,0:T(8,128)(2,1)}, bf16[4,3,40,896]{3,2,1,0:T(8,128)(2,1)}, u32[]{:S(2)}, u32[]{:S(2)}) collective-permute-start(bf16[4,3,40,896]{3,2,1,0:T(8,128)(2,1)} %all-to-all-done.refs_0_), channel_id=1, source_target_pairs={{0,4},{1,5},{2,6},{3,7},{4,0},{5,1},{6,2},{7,3},{8,12},{9,13},{10,... | collective-permute-start | bytes 2580488 | tf_op jit(solution)/shard_map/ppermute | solution.py:598
  166.6 16.0 %collective-permute-start.30 = (bf16[4,3,40,896]{3,2,1,0:T(8,128)(2,1)}, bf16[4,3,40,896]{3,2,1,0:T(8,128)(2,1)}, u32[]{:S(2)}, u32[]{:S(2)}) collective-permute-start(bf16[4,3,40,896]{3,2,1,0:T(8,128)(2,1)} %collective-permute-done.23.refs_2_), channel_id=1, source_target_pairs={{0,1},{1,0},{2,3},{3,2},{4,5},{5,4},{6,7},{7,6},{8,9},{9,8},{10,11... | collective-permute-start | bytes 2580488 | tf_op jit(solution)/shard_map/ppermute | solution.py:598
  167.0 15.6 %collective-permute-start.29 = (bf16[4,3,40,896]{3,2,1,0:T(8,128)(2,1)}, bf16[4,3,40,896]{3,2,1,0:T(8,128)(2,1)}, u32[]{:S(2)}, u32[]{:S(2)}) collective-permute-start(bf16[4,3,40,896]{3,2,1,0:T(8,128)(2,1)} %all-to-all-done.refs_0_), channel_id=1, source_target_pairs={{0,1},{1,0},{2,3},{3,2},{4,5},{5,4},{6,7},{7,6},{8,9},{9,8},{10,11... | collective-permute-start | bytes 2580488 | tf_op jit(solution)/shard_map/ppermute | solution.py:598
  174.7 39.7 %collective-permute-start.33 = (bf16[512,1280]{1,0:T(8,128)(2,1)S(1)}, bf16[512,1280]{1,0:T(8,128)(2,1)}, u32[]{:S(2)}, u32[]{:S(2)}) collective-permute-start(bf16[512,1280]{1,0:T(8,128)(2,1)S(1)} %copy-done), channel_id=1, source_target_pairs={{0,2},{1,3},{2,0},{3,1},{4,6},{5,7},{6,4},{7,5},{8,10},{9,11},{10,... | collective-permute-start | bytes 3932168 | tf_op jit(solution)/shard_map/ppermute | solution.py:598
  176.1 38.3 %collective-permute-start.34 = (bf16[512,1280]{1,0:T(8,128)(2,1)S(1)}, bf16[512,1280]{1,0:T(8,128)(2,1)}, u32[]{:S(2)}, u32[]{:S(2)}) collective-permute-start(bf16[512,1280]{1,0:T(8,128)(2,1)S(1)} %copy-done), channel_id=1, source_target_pairs={{0,4},{1,5},{2,6},{3,7},{4,0},{5,1},{6,2},{7,3},{8,12},{9,13},{10,... | collective-permute-start | bytes 3932168 | tf_op jit(solution)/shard_map/ppermute | solution.py:598
  183.4 32.2 %all-to-all-start.1 = ((bf16[8,16,512]{2,1,0:T(8,128)(2,1)}), bf16[8,16,512]{2,1,0:T(8,128)(2,1)S(1)}, u32[]{:S(2)}, u32[]{:S(2)}) async-start(bf16[8,16,512]{2,1,0:T(8,128)(2,1)} %broadcast_in_dim.104), calls=%async_computation.1 | async-start | bytes 262144 | tf_op jit(solution)/shard_map/all_to_all | solution.py:825
  186.8 403.1 %reduce-scatter.3.cloned.1.call-start = ((), (), s32[]{:S(2)}) async-start(), calls=%async_computation.8 | async-start | bytes 8601600 | tf_op jit(solution)/shard_map/reduce_scatter | solution.py:941
  214.4 39.1 %collective-permute-start.38 = (bf16[4,3,4,40,896]{4,3,2,1,0:T(8,128)(2,1)}, bf16[4,3,4,40,896]{4,3,2,1,0:T(8,128)(2,1)}, u32[]{:S(2)}, u32[]{:S(2)}) collective-permute-start(bf16[4,3,4,40,896]{4,3,2,1,0:T(8,128)(2,1)} %bitcast.227), channel_id=1, source_target_pairs={{0,1},{1,0},{2,3},{3,2},{4,5},{5,4},{6,7},{7,6},{8,9},{9,8},{10,11... | collective-permute-start | bytes 10321928 | tf_op jit(solution)/shard_map/ppermute | solution.py:598
  221.5 31.1 %collective-permute-start.39 = (bf16[512,1280]{1,0:T(8,128)(2,1)}, bf16[512,1280]{1,0:T(8,128)(2,1)}, u32[]{:S(2)}, u32[]{:S(2)}) collective-permute-start(bf16[512,1280]{1,0:T(8,128)(2,1)} %broadcast_select_fusion), channel_id=1, source_target_pairs={{0,4},{1,3},{2,6},{3,1},{4,0},{5,7},{6,2},{7,5},{8,12},{9,11},{10,... | collective-permute-start | bytes 3932168 | tf_op jit(solution)/shard_map/ppermute | solution.py:598
  223.2 29.4 %collective-permute-start.36 = (bf16[512,1280]{1,0:T(8,128)(2,1)}, bf16[512,1280]{1,0:T(8,128)(2,1)}, u32[]{:S(2)}, u32[]{:S(2)}) collective-permute-start(bf16[512,1280]{1,0:T(8,128)(2,1)} %collective-permute-done.34.refs_5_.refs_6_), channel_id=1, source_target_pairs={{0,1},{1,0},{2,3},{3,2},{4,5},{5,4},{6,7},{7,6},{8,9},{9,8},{10,11... | collective-permute-start | bytes 3932168 | tf_op jit(solution)/shard_map/ppermute | solution.py:598
  223.3 29.4 %collective-permute-start.35 = (bf16[512,1280]{1,0:T(8,128)(2,1)}, bf16[512,1280]{1,0:T(8,128)(2,1)}, u32[]{:S(2)}, u32[]{:S(2)}) collective-permute-start(bf16[512,1280]{1,0:T(8,128)(2,1)} %collective-permute-done.33.refs_5_.refs_6_), channel_id=1, source_target_pairs={{0,1},{1,0},{2,3},{3,2},{4,5},{5,4},{6,7},{7,6},{8,9},{9,8},{10,11... | collective-permute-start | bytes 3932168 | tf_op jit(solution)/shard_map/ppermute | solution.py:598
  223.7 29.8 %collective-permute-start.37 = (bf16[512,1280]{1,0:T(8,128)(2,1)}, bf16[512,1280]{1,0:T(8,128)(2,1)}, u32[]{:S(2)}, u32[]{:S(2)}) collective-permute-start(bf16[512,1280]{1,0:T(8,128)(2,1)} %broadcast_select_fusion.1), channel_id=1, source_target_pairs={{0,4},{1,3},{2,6},{3,1},{4,0},{5,7},{6,2},{7,5},{8,12},{9,11},{10,... | collective-permute-start | bytes 3932168 | tf_op jit(solution)/shard_map/ppermute | solution.py:598
  253.5 25.7 %collective-permute-start.41 = (bf16[512,1280]{1,0:T(8,128)(2,1)}, bf16[512,1280]{1,0:T(8,128)(2,1)}, u32[]{:S(2)}, u32[]{:S(2)}) collective-permute-start(bf16[512,1280]{1,0:T(8,128)(2,1)} %collective-permute-done.39.refs_7_.refs_8_), channel_id=1, source_target_pairs={{0,1},{1,0},{2,3},{3,2},{4,5},{5,4},{6,7},{7,6},{8,9},{9,8},{10,11... | collective-permute-start | bytes 3932168 | tf_op jit(solution)/shard_map/ppermute | solution.py:598
  258.6 20.6 %collective-permute-start.42 = (bf16[3,4,40,896]{3,2,1,0:T(8,128)(2,1)S(1)}, bf16[3,4,40,896]{3,2,1,0:T(8,128)(2,1)S(1)}, u32[]{:S(2)}, u32[]{:S(2)}) collective-permute-start(bf16[3,4,40,896]{3,2,1,0:T(8,128)(2,1)S(1)} %fusion.36), channel_id=1, source_target_pairs={{0,4},{1,3},{2,6},{3,1},{4,0},{5,7},{6,2},{7,5},{8,12},{9,11},{10,... | collective-permute-start | bytes 2580488 | tf_op jit(solution)/shard_map/ppermute | solution.py:598
  281.3 40.3 %collective-permute-start.43 = (bf16[3,4,40,896]{3,2,1,0:T(8,128)(2,1)S(1)}, bf16[3,4,40,896]{3,2,1,0:T(8,128)(2,1)S(1)}, u32[]{:S(2)}, u32[]{:S(2)}) collective-permute-start(bf16[3,4,40,896]{3,2,1,0:T(8,128)(2,1)S(1)} %get-tuple-element.392), channel_id=1, source_target_pairs={{0,2},{1,3},{2,0},{3,1},{4,6},{5,7},{6,4},{7,5},{8,10},{9,11},{10,... | collective-permute-start | bytes 2580488 | tf_op jit(solution)/shard_map/ppermute | solution.py:598
  282.8 38.8 %collective-permute-start.44 = (bf16[3,4,40,896]{3,2,1,0:T(8,128)(2,1)S(1)}, bf16[3,4,40,896]{3,2,1,0:T(8,128)(2,1)S(1)}, u32[]{:S(2)}, u32[]{:S(2)}) collective-permute-start(bf16[3,4,40,896]{3,2,1,0:T(8,128)(2,1)S(1)} %get-tuple-element.393), channel_id=1, source_target_pairs={{0,4},{1,5},{2,6},{3,7},{4,0},{5,1},{6,2},{7,3},{8,12},{9,13},{10,... | collective-permute-start | bytes 2580488 | tf_op jit(solution)/shard_map/ppermute | solution.py:598
  376.9 21.4 %collective-permute-start.45 = (bf16[512,1280]{1,0:T(8,128)(2,1)}, bf16[512,1280]{1,0:T(8,128)(2,1)S(1)}, u32[]{:S(2)}, u32[]{:S(2)}) collective-permute-start(bf16[512,1280]{1,0:T(8,128)(2,1)} %get-tuple-element.425), channel_id=1, source_target_pairs={{0,1},{1,0},{2,3},{3,2},{4,5},{5,4},{6,7},{7,6},{8,9},{9,8},{10,11... | collective-permute-start | bytes 3932168 | tf_op jit(solution)/shard_map/ppermute | solution.py:598
  377.0 21.2 %collective-permute-start.46 = (bf16[512,1280]{1,0:T(8,128)(2,1)}, bf16[512,1280]{1,0:T(8,128)(2,1)S(1)}, u32[]{:S(2)}, u32[]{:S(2)}) collective-permute-start(bf16[512,1280]{1,0:T(8,128)(2,1)} %get-tuple-element.427), channel_id=1, source_target_pairs={{0,1},{1,0},{2,3},{3,2},{4,5},{5,4},{6,7},{7,6},{8,9},{9,8},{10,11... | collective-permute-start | bytes 3932168 | tf_op jit(solution)/shard_map/ppermute | solution.py:598
  399.4 27.4 %collective-permute-start.49 = (bf16[512,1280]{1,0:T(8,128)(2,1)}, bf16[512,1280]{1,0:T(8,128)(2,1)S(1)}, u32[]{:S(2)}, u32[]{:S(2)}) collective-permute-start(bf16[512,1280]{1,0:T(8,128)(2,1)} %get-tuple-element.441), channel_id=1, source_target_pairs={{0,1},{1,0},{2,3},{3,2},{4,5},{5,4},{6,7},{7,6},{8,9},{9,8},{10,11... | collective-permute-start | bytes 3932168 | tf_op jit(solution)/shard_map/ppermute | solution.py:598
  399.5 27.3 %collective-permute-start.48 = (bf16[512,1280]{1,0:T(8,128)(2,1)}, bf16[512,1280]{1,0:T(8,128)(2,1)}, u32[]{:S(2)}, u32[]{:S(2)}) collective-permute-start(bf16[512,1280]{1,0:T(8,128)(2,1)} %get-tuple-element.439), channel_id=1, source_target_pairs={{0,1},{1,0},{2,3},{3,2},{4,5},{5,4},{6,7},{7,6},{8,9},{9,8},{10,11... | collective-permute-start | bytes 3932168 | tf_op jit(solution)/shard_map/ppermute | solution.py:598
  402.8 24.1 %collective-permute-start.47 = (bf16[512,1280]{1,0:T(8,128)(2,1)}, bf16[512,1280]{1,0:T(8,128)(2,1)}, u32[]{:S(2)}, u32[]{:S(2)}) collective-permute-start(bf16[512,1280]{1,0:T(8,128)(2,1)} %add_convert_fusion.1), channel_id=1, source_target_pairs={{0,4},{1,3},{2,6},{3,1},{4,0},{5,7},{6,2},{7,5},{8,12},{9,11},{10,... | collective-permute-start | bytes 3932168 | tf_op jit(solution)/shard_map/ppermute | solution.py:598
  434.9 32.8 %collective-permute-start.52 = (bf16[512,1280]{1,0:T(8,128)(2,1)}, bf16[512,1280]{1,0:T(8,128)(2,1)}, u32[]{:S(2)}, u32[]{:S(2)}) collective-permute-start(bf16[512,1280]{1,0:T(8,128)(2,1)} %get-tuple-element.470), channel_id=1, source_target_pairs={{0,2},{1,3},{2,0},{3,1},{4,6},{5,7},{6,4},{7,5},{8,10},{9,11},{10,... | collective-permute-start | bytes 3932168 | tf_op jit(solution)/shard_map/ppermute | solution.py:598
  436.4 31.3 %collective-permute-start.53 = (bf16[512,1280]{1,0:T(8,128)(2,1)}, bf16[512,1280]{1,0:T(8,128)(2,1)}, u32[]{:S(2)}, u32[]{:S(2)}) collective-permute-start(bf16[512,1280]{1,0:T(8,128)(2,1)} %get-tuple-element.471), channel_id=1, source_target_pairs={{0,4},{1,5},{2,6},{3,7},{4,0},{5,1},{6,2},{7,3},{8,12},{9,13},{10,... | collective-permute-start | bytes 3932168 | tf_op jit(solution)/shard_map/ppermute | solution.py:598
  437.0 30.8 %collective-permute-start.51 = (bf16[512,1280]{1,0:T(8,128)(2,1)}, bf16[512,1280]{1,0:T(8,128)(2,1)S(1)}, u32[]{:S(2)}, u32[]{:S(2)}) collective-permute-start(bf16[512,1280]{1,0:T(8,128)(2,1)} %get-tuple-element.467), channel_id=1, source_target_pairs={{0,1},{1,0},{2,3},{3,2},{4,5},{5,4},{6,7},{7,6},{8,9},{9,8},{10,11... | collective-permute-start | bytes 3932168 | tf_op jit(solution)/shard_map/ppermute | solution.py:598
  463.0 174.8 %reduce-scatter.5.cloned.1.call-start = ((), (), s32[]{:S(2)}) async-start(), calls=%async_computation.9 | async-start | bytes 8601600 | tf_op jit(solution)/shard_map/reduce_scatter | solution.py:941
  468.8 24.1 %collective-permute-start.56 = (bf16[512,1280]{1,0:T(8,128)(2,1)}, bf16[512,1280]{1,0:T(8,128)(2,1)S(1)}, u32[]{:S(2)}, u32[]{:S(2)}) collective-permute-start(bf16[512,1280]{1,0:T(8,128)(2,1)} %get-tuple-element.493), channel_id=1, source_target_pairs={{0,1},{1,0},{2,3},{3,2},{4,5},{5,4},{6,7},{7,6},{8,9},{9,8},{10,11... | collective-permute-start | bytes 3932168 | tf_op jit(solution)/shard_map/ppermute | solution.py:598
  468.8 24.2 %collective-permute-start.54 = (bf16[512,1280]{1,0:T(8,128)(2,1)}, bf16[512,1280]{1,0:T(8,128)(2,1)}, u32[]{:S(2)}, u32[]{:S(2)}) collective-permute-start(bf16[512,1280]{1,0:T(8,128)(2,1)} %get-tuple-element.489), channel_id=1, source_target_pairs={{0,1},{1,0},{2,3},{3,2},{4,5},{5,4},{6,7},{7,6},{8,9},{9,8},{10,11... | collective-permute-start | bytes 3932168 | tf_op jit(solution)/shard_map/ppermute | solution.py:598
  469.3 23.7 %collective-permute-start.55 = (bf16[512,1280]{1,0:T(8,128)(2,1)}, bf16[512,1280]{1,0:T(8,128)(2,1)}, u32[]{:S(2)}, u32[]{:S(2)}) collective-permute-start(bf16[512,1280]{1,0:T(8,128)(2,1)} %add_convert_fusion), channel_id=1, source_target_pairs={{0,4},{1,3},{2,6},{3,1},{4,0},{5,7},{6,2},{7,5},{8,12},{9,11},{10,... | collective-permute-start | bytes 3932168 | tf_op jit(solution)/shard_map/ppermute | solution.py:598
  510.0 37.3 %collective-permute-start.57 = (bf16[4,1,4,40,1280]{4,3,2,1,0:T(8,128)(2,1)}, bf16[4,1,4,40,1280]{4,3,2,1,0:T(8,128)(2,1)S(1)}, u32[]{:S(2)}, u32[]{:S(2)}) collective-permute-start(bf16[4,1,4,40,1280]{4,3,2,1,0:T(8,128)(2,1)} %bitcast.229), channel_id=1, source_target_pairs={{0,1},{1,0},{2,3},{3,2},{4,5},{5,4},{6,7},{7,6},{8,9},{9,8},{10,11... | collective-permute-start | bytes 4915208 | tf_op jit(solution)/shard_map/ppermute | solution.py:598
  514.8 31.4 %collective-permute-start.58 = (bf16[512,1280]{1,0:T(8,128)(2,1)}, bf16[512,1280]{1,0:T(8,128)(2,1)S(1)}, u32[]{:S(2)}, u32[]{:S(2)}) collective-permute-start(bf16[512,1280]{1,0:T(8,128)(2,1)} %get-tuple-element.508), channel_id=1, source_target_pairs={{0,2},{1,3},{2,0},{3,1},{4,6},{5,7},{6,4},{7,5},{8,10},{9,11},{10,... | collective-permute-start | bytes 3932168 | tf_op jit(solution)/shard_map/ppermute | solution.py:598
  516.3 31.1 %collective-permute-start.59 = (bf16[512,1280]{1,0:T(8,128)(2,1)}, bf16[512,1280]{1,0:T(8,128)(2,1)S(1)}, u32[]{:S(2)}, u32[]{:S(2)}) collective-permute-start(bf16[512,1280]{1,0:T(8,128)(2,1)} %get-tuple-element.509), channel_id=1, source_target_pairs={{0,4},{1,5},{2,6},{3,7},{4,0},{5,1},{6,2},{7,3},{8,12},{9,13},{10,... | collective-permute-start | bytes 3932168 | tf_op jit(solution)/shard_map/ppermute | solution.py:598
  548.4 23.7 %collective-permute-start.60 = (bf16[4,3,4,40,1280]{4,3,2,1,0:T(8,128)(2,1)}, bf16[4,3,4,40,1280]{4,3,2,1,0:T(8,128)(2,1)}, u32[]{:S(2)}, u32[]{:S(2)}) collective-permute-start(bf16[4,3,4,40,1280]{4,3,2,1,0:T(8,128)(2,1)} %bitcast.226), channel_id=1, source_target_pairs={{0,1},{1,0},{2,3},{3,2},{4,5},{5,4},{6,7},{7,6},{8,9},{9,8},{10,11... | collective-permute-start | bytes 14745608 | tf_op jit(solution)/shard_map/ppermute | solution.py:598
  556.6 15.5 %collective-permute-start.61 = (bf16[1,4,40,1280]{3,2,1,0:T(8,128)(2,1)}, bf16[1,4,40,1280]{3,2,1,0:T(8,128)(2,1)S(1)}, u32[]{:S(2)}, u32[]{:S(2)}) collective-permute-start(bf16[1,4,40,1280]{3,2,1,0:T(8,128)(2,1)} %fusion.48), channel_id=1, source_target_pairs={{0,4},{1,3},{2,6},{3,1},{4,0},{5,7},{6,2},{7,5},{8,12},{9,11},{10,... | collective-permute-start | bytes 1228808 | tf_op jit(solution)/shard_map/ppermute | solution.py:598
  579.3 21.7 %collective-permute-start.62 = (bf16[3,4,40,1280]{3,2,1,0:T(8,128)(2,1)}, bf16[3,4,40,1280]{3,2,1,0:T(8,128)(2,1)}, u32[]{:S(2)}, u32[]{:S(2)}) collective-permute-start(bf16[3,4,40,1280]{3,2,1,0:T(8,128)(2,1)} %fusion.28), channel_id=1, source_target_pairs={{0,4},{1,3},{2,6},{3,1},{4,0},{5,7},{6,2},{7,5},{8,12},{9,11},{10,... | collective-permute-start | bytes 3686408 | tf_op jit(solution)/shard_map/ppermute | solution.py:598
  581.4 49.5 %all-to-all-start.3 = ((bf16[4,3,40,896]{3,2,1,0:T(8,128)(2,1)}), bf16[4,3,40,896]{3,2,1,0:T(8,128)(2,1)S(1)}, u32[]{:S(2)}, u32[]{:S(2)}) async-start(bf16[4,3,40,896]{3,2,1,0:T(8,128)(2,1)} %copy.234), calls=%async_computation.4 | async-start | bytes 1720320 | tf_op jit(solution)/shard_map/all_to_all | solution.py:1016
  605.6 29.4 %collective-permute-start.68 = (bf16[3,4,40,1280]{3,2,1,0:T(8,128)(2,1)}, bf16[3,4,40,1280]{3,2,1,0:T(8,128)(2,1)}, u32[]{:S(2)}, u32[]{:S(2)}) collective-permute-start(bf16[3,4,40,1280]{3,2,1,0:T(8,128)(2,1)} %get-tuple-element.525), channel_id=1, source_target_pairs={{0,2},{1,3},{2,0},{3,1},{4,6},{5,7},{6,4},{7,5},{8,10},{9,11},{10,... | collective-permute-start | bytes 3686408 | tf_op jit(solution)/shard_map/ppermute | solution.py:598
  606.4 28.7 %collective-permute-start.69 = (bf16[3,4,40,1280]{3,2,1,0:T(8,128)(2,1)}, bf16[3,4,40,1280]{3,2,1,0:T(8,128)(2,1)}, u32[]{:S(2)}, u32[]{:S(2)}) collective-permute-start(bf16[3,4,40,1280]{3,2,1,0:T(8,128)(2,1)} %get-tuple-element.526), channel_id=1, source_target_pairs={{0,4},{1,5},{2,6},{3,7},{4,0},{5,1},{6,2},{7,3},{8,12},{9,13},{10,... | collective-permute-start | bytes 3686408 | tf_op jit(solution)/shard_map/ppermute | solution.py:598
  617.4 25.1 %collective-permute-start.67 = (bf16[1,40,1280]{2,1,0:T(8,128)(2,1)}, bf16[1,40,1280]{2,1,0:T(8,128)(2,1)S(1)}, u32[]{:S(2)}, u32[]{:S(2)}) collective-permute-start(bf16[1,40,1280]{2,1,0:T(8,128)(2,1)} %get-tuple-element.534), channel_id=1, source_target_pairs={{0,24},{8,16},{16,8},{24,0},{1,25},{9,17},{17,9},{25,1},{2,26},{10... | collective-permute-start | bytes 307208 | tf_op jit(solution)/shard_map/ppermute | solution.py:625
  619.1 24.1 %collective-permute-start.66 = (bf16[1,40,1280]{2,1,0:T(8,128)(2,1)}, bf16[1,40,1280]{2,1,0:T(8,128)(2,1)}, u32[]{:S(2)}, u32[]{:S(2)}) collective-permute-start(bf16[1,40,1280]{2,1,0:T(8,128)(2,1)} %get-tuple-element.533), channel_id=1, source_target_pairs={{0,16},{8,24},{16,0},{24,8},{1,17},{9,25},{17,1},{25,9},{2,18},{10... | collective-permute-start | bytes 307208 | tf_op jit(solution)/shard_map/ppermute | solution.py:625
  619.1 24.1 %collective-permute-start.65 = (bf16[1,40,1280]{2,1,0:T(8,128)(2,1)}, bf16[1,40,1280]{2,1,0:T(8,128)(2,1)}, u32[]{:S(2)}, u32[]{:S(2)}) collective-permute-start(bf16[1,40,1280]{2,1,0:T(8,128)(2,1)} %get-tuple-element.532), channel_id=1, source_target_pairs={{0,8},{8,0},{16,24},{24,16},{1,9},{9,1},{17,25},{25,17},{2,10},{10... | collective-permute-start | bytes 307208 | tf_op jit(solution)/shard_map/ppermute | solution.py:625
  638.8 37.2 %collective-permute-start.72 = (bf16[3,40,1280]{2,1,0:T(8,128)(2,1)}, bf16[3,40,1280]{2,1,0:T(8,128)(2,1)}, u32[]{:S(2)}, u32[]{:S(2)}) collective-permute-start(bf16[3,40,1280]{2,1,0:T(8,128)(2,1)} %get-tuple-element.544), channel_id=1, source_target_pairs={{0,24},{8,16},{16,8},{24,0},{1,25},{9,17},{17,9},{25,1},{2,26},{10... | collective-permute-start | bytes 921608 | tf_op jit(solution)/shard_map/ppermute | solution.py:625
  642.5 33.6 %collective-permute-start.71 = (bf16[3,40,1280]{2,1,0:T(8,128)(2,1)}, bf16[3,40,1280]{2,1,0:T(8,128)(2,1)}, u32[]{:S(2)}, u32[]{:S(2)}) collective-permute-start(bf16[3,40,1280]{2,1,0:T(8,128)(2,1)} %get-tuple-element.543), channel_id=1, source_target_pairs={{0,16},{8,24},{16,0},{24,8},{1,17},{9,25},{17,1},{25,9},{2,18},{10... | collective-permute-start | bytes 921608 | tf_op jit(solution)/shard_map/ppermute | solution.py:625
  642.5 33.6 %collective-permute-start.70 = (bf16[3,40,1280]{2,1,0:T(8,128)(2,1)}, bf16[3,40,1280]{2,1,0:T(8,128)(2,1)}, u32[]{:S(2)}, u32[]{:S(2)}) collective-permute-start(bf16[3,40,1280]{2,1,0:T(8,128)(2,1)} %get-tuple-element.542), channel_id=1, source_target_pairs={{0,8},{8,0},{16,24},{24,16},{1,9},{9,1},{17,25},{25,17},{2,10},{10... | collective-permute-start | bytes 921608 | tf_op jit(solution)/shard_map/ppermute | solution.py:625
  648.1 22.5 %all-to-all-start.5 = ((f32[4,40,128]{2,1,0:T(8,128)}), f32[4,40,128]{2,1,0:T(8,128)S(1)}, u32[]{:S(2)}, u32[]{:S(2)}) async-start(f32[4,40,128]{2,1,0:T(8,128)} %add_bitcast_fusion.1), calls=%async_computation.7 | async-start | bytes 163840 | tf_op jit(solution)/shard_map/all_to_all | solution.py:1052
  (109 other events, 994.8 us)
Sparse Core Ops, SparseCore 0:
  107.3 124.6 all-gather.4
  233.5 123.2 all-gather.6
  359.7 118.5 reduce-scatter.2
  493.1 132.2 reduce-scatter.4
